TPU v7x, 32 devices: a whole 2x2x4 slice. The times are simulated.
32 devices in a mesh: row: 8 (over z, core), col: 4 (over y, x).
Axes of the slice: x: 2, y: 2, z: 4, core: 2. Of those that a mesh axis runs over, the one named last changes fastest.
Arguments:
- tokens_in: bfloat16 [8192, 2048], P(('row', 'col')), may hold values from -6 to 6
- cotangent: bfloat16 [8192, 2048], P(('row', 'col')), may hold values from -6 to 6
- target: int32 [8192], P(('row', 'col')), may hold values from 0 to 8191, as said below
- sequence_lengths: int32 [8, 2], P('row'), may hold values from 341 to 683, as said below
- sequence_adapter: int32 [8, 2], P('row'), may hold values from 0 to 7, as said below
- norm_gains: bfloat16 [2, 2048], replicated, may hold values from 0.5 to 1.5
- weight_in: bfloat16 [2048, 8240], P('row', 'col'), may hold values from -0.125 to 0.125
- conv_values: bfloat16 [5, 3072], P(None, 'col'), may hold values from -3 to 3
- conv_states: bfloat16 [5, 512], P(None, 'col'), may hold values from -3 to 3
- scan_params: float32 [3, 48], P(None, 'col'), may hold values from -4 to 2.8
- weight_mix: bfloat16 [4096, 2048], P('col', 'row'), may hold values from -3 to 3
- weight_feed: bfloat16 [2048, 8192], P('row', 'col'), may hold values from -0.125 to 0.125
- weight_down: bfloat16 [4096, 2048], P('col', 'row'), may hold values from -0.09375 to 0.09375
- in_lower: bfloat16 [2048, 128], P('row'), may hold values from -0.125 to 0.125
- in_raise: bfloat16 [128, 8240], P('row', 'col'), may hold values from -0.75 to 0.75
- mix_lower: bfloat16 [4096, 128], P('col', 'row'), may hold values from -0.001953125 to 0.001953125
- mix_raise: bfloat16 [128, 2048], P(None, 'row'), may hold values from -0.75 to 0.75
- feed_lower: bfloat16 [2048, 128], P('row'), may hold values from -0.125 to 0.125
- feed_raise: bfloat16 [128, 8192], P('row', 'col'), may hold values from -0.75 to 0.75
- down_lower: bfloat16 [4096, 128], P('col', 'row'), may hold values from -0.09375 to 0.09375
- down_raise: bfloat16 [128, 2048], P(None, 'row'), may hold values from -0.75 to 0.75
Outputs:
- block_out: bfloat16 [8192, 2048], P(('row', 'col'))
- input_grad: bfloat16 [8192, 2048], P(('row', 'col'))
- grad_in_lower: float32 [2048, 128], P(('row', 'col'))
- grad_in_raise: float32 [128, 8240], P('row', 'col')
- grad_mix_lower: float32 [4096, 128], P('col', 'row')
- grad_mix_raise: float32 [128, 2048], P(None, ('row', 'col'))
- grad_feed_lower: float32 [2048, 128], P(('row', 'col'))
- grad_feed_raise: float32 [128, 8192], P('row', 'col')
- grad_down_lower: float32 [4096, 128], P('col', 'row')
- grad_down_raise: float32 [128, 2048], P(None, ('row', 'col'))
Inputs may be any that keep to these rules, and one draw needn't show every extreme that they name: `target`: A permutation of the packed positions; packed position p lies on device p // 256; the 256 rows of one device go to every device in equal shares of 8 rows. `sequence_lengths`: each row sums to 1024. `sequence_adapter`: neighbouring sequences of a group use different adapters; every adapter is that of the first sequence of some group.
All inputs are finite; a program needn't handle non-finite values.
Results may differ from a plain program's by a relative error of at most 0.024.
Values may be sent and summed in bfloat16 or wider, within the bound.
No kernel may reach another device: no remote copies, remote signals or barrier semaphores. Data moves between devices by JAX's collectives and lax.ppermute only.
A program may use at most 256 MiB of HBM per device.

v0:
```python
import math

import jax
import jax.numpy as jnp
from jax import lax
from jax.sharding import PartitionSpec as P

NH = 48
HP = 64
NSTATE = 256
KCONV = 4
QUERY_HEADS = 8
KEY_VALUE_HEADS = 2
HEAD_SIZE = 128
RANK = 16
NADAPT = 8
SSD_BLOCK = 256
ATT_BLOCK = 512
DSSM = 3072
UNIT_IN = 1030
UNIT_FF = 512


EPSILON = 1e-05
ROPE_BASE = 10000.0
NEGATIVE = -1e30
FLOAT = jnp.float32
BFLOAT = jnp.bfloat16


def round_value(values):
    rounded = lax.optimization_barrier(values.astype(BFLOAT)).astype(FLOAT)
    return values + lax.stop_gradient(rounded - values)


def product(left, right):
    return jnp.dot(left, right, preferred_element_type=FLOAT)


def contract_last(left, right):
    return lax.dot_general(left, right, (((1,), (1,)), ((), ())), preferred_element_type=FLOAT)


def contract_first(left, right):
    return lax.dot_general(left, right, (((0,), (0,)), ((), ())), preferred_element_type=FLOAT)


def rms_norm(values, gain):
    return values * lax.rsqrt(jnp.mean(values * values, axis=-1, keepdims=True) + EPSILON) * gain


def sequence_tables(lengths, adapters, sequence_length):
    sequence_count = lengths.shape[0]
    boundary = jnp.cumsum(lengths)
    token_index = jnp.arange(sequence_length, dtype=jnp.int32)
    passed = (token_index[:, None] >= boundary[None, :]).astype(jnp.int32)
    segment = jnp.sum(passed, axis=1)
    segment_start = jnp.sum(passed * lengths[None, :], axis=1)
    position = token_index - segment_start
    member = (segment[:, None] == jnp.arange(sequence_count, dtype=jnp.int32)[None, :]).astype(
        jnp.int32
    )
    chosen = jnp.sum(member * adapters[None, :], axis=1)
    column = jnp.arange(NADAPT * RANK, dtype=jnp.int32) // RANK
    selector = (chosen[:, None] == column[None, :]).astype(FLOAT)
    return (segment, position, selector)


def causal_conv(channels, tap_table, position):
    running = tap_table[KCONV] + channels * tap_table[0]
    for lag_step in range(1, KCONV):
        shifted = jnp.concatenate(
            [jnp.zeros((lag_step, channels.shape[1]), FLOAT), channels[:-lag_step]], axis=0
        )
        running = (
            running + jnp.where((position >= lag_step)[:, None], shifted, 0.0) * tap_table[lag_step]
        )
    return jax.nn.silu(running)


def rotate(vectors, position):
    half_width = HEAD_SIZE // 2
    frequency = ROPE_BASE ** (-2.0 * jnp.arange(half_width, dtype=FLOAT) / HEAD_SIZE)
    angle_table = position.astype(FLOAT)[:, None] * frequency[None, :]
    cosine = jnp.cos(angle_table)[:, None, :]
    sine_part = jnp.sin(angle_table)[:, None, :]
    leading = vectors[..., :half_width]
    trailing = vectors[..., half_width:]
    return jnp.concatenate(
        [leading * cosine - trailing * sine_part, trailing * cosine + leading * sine_part], axis=-1
    )


def state_scan(inputs, step_size, log_decay, write_vectors, read_vectors, segment):
    sequence_length, head_count = step_size.shape
    block_count = sequence_length // SSD_BLOCK
    previous = jnp.concatenate([jnp.full((1,), -1, jnp.int32), segment[:-1]])
    first_previous = previous.reshape(block_count, SSD_BLOCK)[:, 0]
    inner_index = jnp.arange(SSD_BLOCK, dtype=jnp.int32)
    lower_mask = inner_index[:, None] >= inner_index[None, :]

    def scan_step(carry_state, block_data):
        (
            block_inputs,
            block_steps,
            block_decay,
            block_write,
            block_read,
            block_segment,
            block_previous,
        ) = block_data
        cumulative = jnp.cumsum(block_decay, axis=0)
        intersection = contract_last(block_read, block_write)
        allowed = lower_mask & (block_segment[:, None] == block_segment[None, :])
        difference = cumulative[:, None, :] - cumulative[None, :, :]
        decay_table = jnp.exp(jnp.where(allowed[:, :, None], difference, NEGATIVE))
        weights = round_value(intersection[:, :, None] * decay_table * block_steps[None, :, :])
        within = jnp.einsum("tsh,shp->thp", weights, block_inputs)
        carried = (block_segment == block_previous).astype(FLOAT)
        read_scaled = round_value(
            block_read[:, None, :] * (jnp.exp(cumulative) * carried[:, None])[:, :, None]
        )
        across = jnp.einsum("thn,hpn->thp", read_scaled, round_value(carry_state))
        tail_factor = (
            jnp.exp(cumulative[-1][None, :] - cumulative)
            * block_steps
            * (block_segment == block_segment[-1]).astype(FLOAT)[:, None]
        )
        write_scaled = round_value(block_write[:, None, :] * tail_factor[:, :, None])
        fresh_state = jnp.einsum("shp,shn->hpn", block_inputs, write_scaled)
        through = jnp.exp(cumulative[-1]) * (block_segment[-1] == block_previous).astype(FLOAT)
        return (carry_state * through[:, None, None] + fresh_state, within + across)

    sliced = (
        inputs.reshape(block_count, SSD_BLOCK, head_count, HP),
        step_size.reshape(block_count, SSD_BLOCK, head_count),
        log_decay.reshape(block_count, SSD_BLOCK, head_count),
        write_vectors.reshape(block_count, SSD_BLOCK, NSTATE),
        read_vectors.reshape(block_count, SSD_BLOCK, NSTATE),
        segment.reshape(block_count, SSD_BLOCK),
        first_previous,
    )
    zero_state = jnp.zeros((head_count, HP, NSTATE), FLOAT)
    _, outputs = lax.scan(jax.checkpoint(scan_step), zero_state, sliced)
    return outputs.reshape(sequence_length, head_count, HP)


def attention(query, key_rows, value_rows, segment):
    sequence_length, unit_count = (query.shape[0], query.shape[1])
    block_count = sequence_length // ATT_BLOCK
    token_index = jnp.arange(sequence_length, dtype=jnp.int32)
    score_scale = 1.0 / math.sqrt(HEAD_SIZE)

    def score_block(block_data):
        query_block, segment_block, token_block = block_data
        score = jnp.einsum("qud,kud->uqk", query_block, key_rows) * score_scale
        allowed = (segment_block[:, None] == segment[None, :]) & (
            token_index[None, :] <= token_block[:, None]
        )
        score = jnp.where(allowed[None], score, NEGATIVE)
        row_max = jnp.max(score, axis=2, keepdims=True)
        exponent = jnp.exp(score - row_max)
        weights = round_value(exponent / jnp.sum(exponent, axis=2, keepdims=True))
        return jnp.einsum("uqk,kud->qud", weights, value_rows)

    attended = lax.map(
        jax.checkpoint(score_block),
        (
            query.reshape(block_count, ATT_BLOCK, unit_count, HEAD_SIZE),
            segment.reshape(block_count, ATT_BLOCK),
            token_index.reshape(block_count, ATT_BLOCK),
        ),
    )
    return attended.reshape(sequence_length, unit_count, HEAD_SIZE)


def mixer_branch(
    blocks,
    state_values,
    paired_values,
    conv_values,
    scan_params,
    unit_index_list,
    segment,
    position,
):
    sequence_length, unit_count = (blocks.shape[0], blocks.shape[1])
    gate_width = DSSM // QUERY_HEADS
    per_unit = NH // QUERY_HEADS
    head_count = unit_count * per_unit
    gate_values = blocks[:, :, :gate_width].reshape(sequence_length, head_count, HP)
    conv_input = blocks[:, :, gate_width : 2 * gate_width].reshape(
        sequence_length, unit_count * gate_width
    )
    query = blocks[:, :, 2 * gate_width : 2 * gate_width + HEAD_SIZE]
    step_raw = blocks[:, :, blocks.shape[2] - per_unit :].reshape(sequence_length, head_count)
    scan_input = round_value(causal_conv(conv_input, conv_values, position)).reshape(
        sequence_length, head_count, HP
    )
    step_size = jax.nn.softplus(step_raw + scan_params[0][None, :])
    log_decay = -step_size * jnp.exp(scan_params[1])[None, :]
    scanned = state_scan(
        scan_input,
        step_size,
        log_decay,
        state_values[:, :NSTATE],
        state_values[:, NSTATE:],
        segment,
    )
    scan_output = (scanned + scan_params[2][None, :, None] * scan_input) * jax.nn.silu(gate_values)
    heads_for_keys = paired_values[:, : KEY_VALUE_HEADS * HEAD_SIZE].reshape(
        sequence_length, KEY_VALUE_HEADS, HEAD_SIZE
    )
    heads_for_values = paired_values[:, KEY_VALUE_HEADS * HEAD_SIZE :].reshape(
        sequence_length, KEY_VALUE_HEADS, HEAD_SIZE
    )
    head_selection = (
        unit_index_list[:, None] // (QUERY_HEADS // KEY_VALUE_HEADS)
        == jnp.arange(KEY_VALUE_HEADS, dtype=jnp.int32)[None, :]
    ).astype(FLOAT)
    key_rows = jnp.einsum("gjd,uj->gud", heads_for_keys, head_selection)
    value_rows = jnp.einsum("gjd,uj->gud", heads_for_values, head_selection)
    attended = attention(
        round_value(rotate(query, position)),
        round_value(rotate(key_rows, position)),
        value_rows,
        segment,
    )
    joined = jnp.concatenate(
        [scan_output.reshape(sequence_length, unit_count, gate_width), attended], axis=2
    )
    return joined.reshape(sequence_length, unit_count * (gate_width + HEAD_SIZE))


def local(
    tokens_in,
    cotangent,
    target,
    sequence_lengths,
    sequence_adapter,
    norm_gains,
    weight_in,
    conv_values,
    conv_states,
    scan_params,
    weight_mix,
    weight_feed,
    weight_down,
    in_lower,
    in_raise,
    mix_lower,
    mix_raise,
    feed_lower,
    feed_raise,
    down_lower,
    down_raise,
):
    col_devices = lax.axis_size("col")
    local_rows = tokens_in.shape[0]
    model_width = tokens_in.shape[1]
    group_rows = local_rows * col_devices
    unit_count = QUERY_HEADS // col_devices
    unit_index_list = lax.axis_index("col") * unit_count + jnp.arange(unit_count, dtype=jnp.int32)
    gate_width = DSSM // QUERY_HEADS
    paired_width = 2 * KEY_VALUE_HEADS * HEAD_SIZE // QUERY_HEADS
    state_width = 2 * NSTATE // QUERY_HEADS
    pair_offset = 2 * gate_width + HEAD_SIZE
    state_offset = pair_offset + paired_width
    destination = target // local_rows
    slot_index = target % local_rows
    sending = jnp.argsort(destination, stable=True)
    arrived_in, arrived_grad, arrived_slot = (
        lax.all_to_all(tokens_in[sending], ("row", "col"), split_axis=0, concat_axis=0, tiled=True),
        lax.all_to_all(cotangent[sending], ("row", "col"), split_axis=0, concat_axis=0, tiled=True),
        lax.all_to_all(
            slot_index[sending], ("row", "col"), split_axis=0, concat_axis=0, tiled=True
        ),
    )
    placing = jnp.argsort(arrived_slot)
    own_input = arrived_in[placing].astype(FLOAT)
    own_upstream = arrived_grad[placing].astype(FLOAT)
    segment, position, selector = sequence_tables(
        sequence_lengths[0], sequence_adapter[0], group_rows
    )
    own_selector = lax.dynamic_slice_in_dim(
        selector, lax.axis_index("col") * local_rows, local_rows, 0
    )
    norm_gain = norm_gains.astype(FLOAT)

    def fetch_inward(weight, left_factor, right_factor):
        return (
            lax.all_gather(weight, "row", axis=0, tiled=True),
            lax.all_gather(left_factor, "row", axis=0, tiled=True),
            lax.all_gather(right_factor, "row", axis=0, tiled=True),
        )

    def fetch_outward(weight, left_factor, right_factor):
        return (
            lax.all_gather(weight, "row", axis=1, tiled=True),
            lax.all_gather(left_factor, "row", axis=1, tiled=True),
            lax.all_gather(right_factor, "row", axis=1, tiled=True),
        )

    def spread_project(normed, weight, left_factor, right_factor):
        portion = lax.all_gather(normed, "col", axis=0, tiled=True)
        narrow = (selector * product(portion, left_factor)).astype(BFLOAT)
        full_part = product(portion, weight) + product(narrow, right_factor)
        return jnp.concatenate([full_part.astype(BFLOAT), narrow], axis=1)

    def reduce_forward(activations, weight, left_factor):

        def partial_rows(row_start, row_span):
            return jnp.concatenate(
                [product(activations, weight), product(activations, left_factor)], axis=1
            )

        return lax.psum_scatter(
            partial_rows(jnp.int32(0), lax.axis_size("col") * local_rows).astype(jnp.bfloat16),
            "col",
            scatter_dimension=0,
            tiled=True,
        ).astype(jnp.float32)

    def reduce_backward(gradients, weight, right_factor):

        def partial_rows(row_start, row_span):
            return jnp.concatenate(
                [contract_last(gradients, weight), contract_last(gradients, right_factor)], axis=1
            )

        return lax.psum_scatter(
            partial_rows(jnp.int32(0), lax.axis_size("col") * local_rows).astype(jnp.bfloat16),
            "col",
            scatter_dimension=0,
            tiled=True,
        ).astype(jnp.float32)

    def spread_back(branch_grad, narrow_grad, weight, left_factor, activations):
        joined = jnp.concatenate([branch_grad, narrow_grad], axis=1)
        portion = lax.all_gather(joined, "col", axis=0, tiled=True)
        main_part = portion[:, :model_width]
        narrow_part = portion[:, model_width:]
        piece_grad = contract_last(main_part, weight) + contract_last(narrow_part, left_factor)
        factor_grad = contract_first(activations, narrow_part)
        return (piece_grad, factor_grad)

    normed_one, norm_one_back = jax.vjp(lambda values: rms_norm(values, norm_gain[0]), own_input)
    normed_one = normed_one.astype(BFLOAT)
    in_weight, in_left, in_right = fetch_inward(weight_in, in_lower, in_raise)
    joined_in = spread_project(normed_one, in_weight, in_left, in_right)
    in_cols = in_weight.shape[1]
    projected = joined_in[:, :in_cols]
    inner_in = joined_in[:, in_cols:]
    blocks = projected.astype(FLOAT).reshape(group_rows, unit_count, UNIT_IN)
    pair_own = projected.reshape(group_rows, unit_count, UNIT_IN)[
        :, :, pair_offset : pair_offset + paired_width
    ].reshape(group_rows, unit_count * paired_width)
    state_own = blocks[:, :, state_offset : state_offset + state_width].reshape(
        group_rows, unit_count * state_width
    )
    conv_state_float = conv_states.astype(FLOAT)
    state_post, state_back = jax.vjp(
        lambda values: causal_conv(values, conv_state_float, position), state_own
    )
    pair_full, state_full = (
        lax.all_gather(pair_own, "col", axis=1, tiled=True),
        lax.all_gather(state_post.astype(BFLOAT), "col", axis=1, tiled=True),
    )
    conv_value_float = conv_values.astype(FLOAT)

    def mix_local(block_values, state_values, paired_values):
        return mixer_branch(
            block_values,
            state_values,
            paired_values,
            conv_value_float,
            scan_params,
            unit_index_list,
            segment,
            position,
        )

    mixed_float, mixer_back = jax.vjp(
        mix_local, blocks, state_full.astype(FLOAT), pair_full.astype(FLOAT)
    )
    mixed_out = mixed_float.astype(BFLOAT)
    out_weight, out_left, out_right = fetch_outward(weight_mix, mix_lower, mix_raise)
    summed_one = reduce_forward(mixed_out, out_weight, out_left)
    inner_out = (own_selector * summed_one[:, model_width:]).astype(BFLOAT)
    hidden = own_input + (summed_one[:, :model_width] + product(inner_out, out_right))
    normed_two, norm_two_back = jax.vjp(lambda values: rms_norm(values, norm_gain[1]), hidden)
    normed_two = normed_two.astype(BFLOAT)
    feed_weight, feed_left, feed_right = fetch_inward(weight_feed, feed_lower, feed_raise)
    joined_feed = spread_project(normed_two, feed_weight, feed_left, feed_right)
    feed_cols = feed_weight.shape[1]
    gate_up = joined_feed[:, :feed_cols].astype(FLOAT).reshape(group_rows, unit_count, 2 * UNIT_FF)
    inner_feed = joined_feed[:, feed_cols:]

    def swiglu(gate_part, up_part):
        return jax.nn.silu(gate_part) * up_part

    activated_float, swiglu_back = jax.vjp(swiglu, gate_up[:, :, :UNIT_FF], gate_up[:, :, UNIT_FF:])
    activated = activated_float.reshape(group_rows, unit_count * UNIT_FF).astype(BFLOAT)
    down_weight, down_left, down_right = fetch_outward(weight_down, down_lower, down_raise)
    summed_two = reduce_forward(activated, down_weight, down_left)
    inner_down = (own_selector * summed_two[:, model_width:]).astype(BFLOAT)
    block_out = hidden + (summed_two[:, :model_width] + product(inner_down, down_right))
    down_weight, down_left, down_right = fetch_outward(weight_down, down_lower, down_raise)
    branch_two = own_upstream.astype(BFLOAT)
    down_raise_grad = contract_first(inner_down, branch_two)
    narrow_two = (own_selector * contract_last(branch_two, down_right)).astype(BFLOAT)
    act_grad, down_lower_grad = spread_back(
        branch_two, narrow_two, down_weight, down_left, activated
    )
    act_grad = act_grad.astype(BFLOAT).astype(FLOAT).reshape(group_rows, unit_count, UNIT_FF)
    gate_grad, up_grad = swiglu_back(act_grad)
    feed_grad = (
        jnp.concatenate([gate_grad, up_grad], axis=2).reshape(group_rows, feed_cols).astype(BFLOAT)
    )
    feed_raise_grad = contract_first(inner_feed, feed_grad)
    feed_weight, feed_left, feed_right = fetch_inward(weight_feed, feed_lower, feed_raise)
    summed_three = reduce_backward(feed_grad, feed_weight, feed_right)
    narrow_feed = (own_selector * summed_three[:, model_width:]).astype(BFLOAT)
    normed_two_grad = summed_three[:, :model_width] + contract_last(narrow_feed, feed_left)
    feed_lower_grad = contract_first(normed_two, narrow_feed)
    (hidden_from_norm,) = norm_two_back(normed_two_grad)
    hidden_grad = own_upstream + hidden_from_norm
    out_weight, out_left, out_right = fetch_outward(weight_mix, mix_lower, mix_raise)
    branch_one = hidden_grad.astype(BFLOAT)
    mix_raise_grad = contract_first(inner_out, branch_one)
    narrow_one = (own_selector * contract_last(branch_one, out_right)).astype(BFLOAT)
    mixed_grad, mix_lower_grad = spread_back(
        branch_one, narrow_one, out_weight, out_left, mixed_out
    )
    block_grad, state_grad_full, pair_grad_full = mixer_back(
        mixed_grad.astype(BFLOAT).astype(FLOAT)
    )
    pair_grad, state_grad = (
        lax.psum_scatter(
            pair_grad_full.astype(jnp.bfloat16), "col", scatter_dimension=1, tiled=True
        ).astype(jnp.float32),
        lax.psum_scatter(
            state_grad_full.astype(jnp.bfloat16), "col", scatter_dimension=1, tiled=True
        ).astype(jnp.float32),
    )
    (state_pre_grad,) = state_back(state_grad)
    block_grad = block_grad.at[:, :, pair_offset : pair_offset + paired_width].set(
        pair_grad.reshape(group_rows, unit_count, paired_width)
    )
    block_grad = block_grad.at[:, :, state_offset : state_offset + state_width].set(
        state_pre_grad.reshape(group_rows, unit_count, state_width)
    )
    projected_grad = block_grad.reshape(group_rows, in_cols).astype(BFLOAT)
    in_raise_grad = contract_first(inner_in, projected_grad)
    in_weight, in_left, in_right = fetch_inward(weight_in, in_lower, in_raise)
    summed_four = reduce_backward(projected_grad, in_weight, in_right)
    narrow_in = (own_selector * summed_four[:, model_width:]).astype(BFLOAT)
    normed_one_grad = summed_four[:, :model_width] + contract_last(narrow_in, in_left)
    in_lower_grad = contract_first(normed_one, narrow_in)
    (input_from_norm,) = norm_one_back(normed_one_grad)
    input_grad = hidden_grad + input_from_norm
    grad_in_raise, grad_mix_lower, grad_feed_raise, grad_down_lower = (
        lax.psum_scatter(
            in_raise_grad.astype(jnp.bfloat16), "row", scatter_dimension=0, tiled=True
        ).astype(jnp.float32),
        lax.psum_scatter(
            mix_lower_grad.astype(jnp.bfloat16), "row", scatter_dimension=1, tiled=True
        ).astype(jnp.float32),
        lax.psum_scatter(
            feed_raise_grad.astype(jnp.bfloat16), "row", scatter_dimension=0, tiled=True
        ).astype(jnp.float32),
        lax.psum_scatter(
            down_lower_grad.astype(jnp.bfloat16), "row", scatter_dimension=1, tiled=True
        ).astype(jnp.float32),
    )
    grad_in_lower, grad_mix_raise, grad_feed_lower, grad_down_raise = (
        lax.psum_scatter(in_lower_grad, ("row", "col"), scatter_dimension=0, tiled=True),
        lax.psum_scatter(mix_raise_grad, ("row", "col"), scatter_dimension=1, tiled=True),
        lax.psum_scatter(feed_lower_grad, ("row", "col"), scatter_dimension=0, tiled=True),
        lax.psum_scatter(down_raise_grad, ("row", "col"), scatter_dimension=1, tiled=True),
    )
    returned_out, returned_grad = (
        lax.all_to_all(
            block_out.astype(BFLOAT)[arrived_slot],
            ("row", "col"),
            split_axis=0,
            concat_axis=0,
            tiled=True,
        ),
        lax.all_to_all(
            input_grad.astype(BFLOAT)[arrived_slot],
            ("row", "col"),
            split_axis=0,
            concat_axis=0,
            tiled=True,
        ),
    )
    restore = jnp.argsort(sending)
    return (
        returned_out[restore],
        returned_grad[restore],
        grad_in_lower,
        grad_in_raise,
        grad_mix_lower,
        grad_mix_raise,
        grad_feed_lower,
        grad_feed_raise,
        grad_down_lower,
        grad_down_raise,
    )


def solution(mesh):
    in_specs = (
        P(("row", "col"), None),
        P(("row", "col"), None),
        P(("row", "col")),
        P("row", None),
        P("row", None),
        P(),
        P("row", "col"),
        P(None, "col"),
        P(None, "col"),
        P(None, "col"),
        P("col", "row"),
        P("row", "col"),
        P("col", "row"),
        P("row", None),
        P("row", "col"),
        P("col", "row"),
        P(None, "row"),
        P("row", None),
        P("row", "col"),
        P("col", "row"),
        P(None, "row"),
    )
    out_specs = (
        P(("row", "col"), None),
        P(("row", "col"), None),
        P(("row", "col"), None),
        P("row", "col"),
        P("col", "row"),
        P(None, ("row", "col")),
        P(("row", "col"), None),
        P("row", "col"),
        P("col", "row"),
        P(None, ("row", "col")),
    )
    return jax.shard_map(local, mesh=mesh, in_specs=in_specs, out_specs=out_specs, check_vma=False)
```

profile of v0, /device:TPU:0, one launch (start us, length us, event | category | flops | bytes accessed | tf_op | source)
XLA Modules:
  0.0 2201.8 jit_solution(17345612813182197884)
XLA Ops:
  36.0 21.3 all-to-all-done
  91.6 20.3 all-gather.11.cloned.1.call-done
  115.4 81.2 %all-gather.13.cloned.1.call-done = bf16[2048,2060]{0,1:T(8,128)(2,1)} async-done(((bf16[256,2060]{0,1:T(8,128)(2,1)}), bf16[2048,2060]{0,1:T(8,128)(2,1)}) %all-gather.13.cloned.1.call-update) | async-done | bytes 8437776 | tf_op jit(solution)/shard_map/all_gather | solution.py:292
  322.6 154.8 %while.75 = (s32[]{:T(128)}, f32[12,64,256]{2,1,0:T(8,128)S(1)}, f32[4,256,12,64]{1,0,3,2:T(4,128)}, f32[4,12,64,256]{3,2,1,0:T(8,128)}, f32[4,256,12]{1,2,0:T(8...) while((s32[]{:T(128)}, f32[12,64,256]{2,1,0:T(8,128)S(1)}, ...), condition=%wide.region_10.11_spmd.clone, body=%wide.region_7.10_spmd.clone.sunk | while | flops 356987968 | bytes 25242344 | solution.py:144
  339.1 17.9 dynamic_update_slice.99
  377.7 17.9 dynamic_update_slice.99
  455.0 17.9 dynamic_update_slice.99
  530.8 34.4 %all_gather.81 = bf16[128,2048]{1,0:T(8,128)(2,1)S(1)} all-gather(bf16[128,256]{1,0:T(8,128)(2,1)S(1)} %copy-done.93), channel_id=1, replica_groups=mesh['row'=8,'col'=4] {'row'}, dimensions={1}, use_global_device_ids=true | all-gather | bytes 589824 | tf_op jit(solution)/shard_map/all_gather | solution.py:301
  607.5 25.6 %all_gather.77 = bf16[2048,128]{1,0:T(8,128)(2,1)} all-gather(bf16[256,128]{1,0:T(8,128)(2,1)S(1)} %copy-done.95), channel_id=1, replica_groups=mesh['row'=8,'col'=4] {'row'}, dimensions={0}, use_global_device_ids=true | all-gather | bytes 589824 | tf_op jit(solution)/shard_map/all_gather | solution.py:293
  649.6 50.4 %all-gather.27.cloned.1.call-done = bf16[1024,2176]{1,0:T(8,128)(2,1)} async-done(((bf16[256,2176]{1,0:T(8,128)(2,1)}), bf16[1024,2176]{1,0:T(8,128)(2,1)}) %all-gather.27.cloned.1.call-update) | async-done | bytes 4456464 | tf_op jit(solution)/shard_map/all_gather | solution.py:340
  715.3 68.4 %all-gather.23.cloned.1.call-done = bf16[2048,2048]{1,0:T(8,128)(2,1)} async-done(((bf16[256,2048]{1,0:T(8,128)(2,1)}), bf16[2048,2048]{1,0:T(8,128)(2,1)}) %all-gather.23.cloned.1.call-update) | async-done | bytes 8388624 | tf_op jit(solution)/shard_map/all_gather | solution.py:292
  783.7 53.0 %all-gather.21.cloned.1.call-done = bf16[1024,2048]{1,0:T(8,128)(2,1)} async-done(((bf16[256,2048]{1,0:T(8,128)(2,1)}), bf16[1024,2048]{1,0:T(8,128)(2,1)}) %all-gather.21.cloned.1.call-update) | async-done | bytes 4194320 | tf_op jit(solution)/shard_map/all_gather | solution.py:305
  919.4 55.0 %reduce-scatter.21.cloned.1.call-done = bf16[256,2176]{1,0:T(8,128)(2,1)} async-done(((bf16[1024,2176]{1,0:T(8,128)(2,1)}), bf16[256,2176]{1,0:T(8,128)(2,1)}) %reduce-scatter.21.cloned.1.call-update) | async-done | bytes 1114128 | tf_op jit(solution)/shard_map/reduce_scatter | solution.py:331
  990.4 46.2 %all-gather.29.cloned.1.call-done = bf16[1024,2176]{1,0:T(8,128)(2,1)} async-done(((bf16[256,2176]{1,0:T(8,128)(2,1)}), bf16[1024,2176]{1,0:T(8,128)(2,1)}) %all-gather.29.cloned.1.call-update) | async-done | bytes 4456464 | tf_op jit(solution)/shard_map/all_gather | solution.py:340
  1064.3 244.7 %while.76 = (s32[]{:T(128)}, f32[12,64,256]{2,1,0:T(8,128)S(1)}, f32[4,256,12,64]{1,0,3,2:T(4,128)}, f32[4,256,12]{1,0,2:T(4,128)}, f32[4,256,12]{1,0,2:T(4,128)...) while((s32[]{:T(128)}, f32[12,64,256]{2,1,0:T(8,128)S(1)}, ...), condition=%wide.region_36.37_spmd.clone, body=%wide.region_21.36_spmd.clone.sunk | while | flops 740616320 | bytes 54135152 | solution.py:144
  1313.6 42.0 %while.77 = (s32[]{:T(128)}, f32[1024,2,128]{2,0,1:T(8,128)}, f32[1024,2,128]{0,2,1:T(8,128)}, f32[2,512,2,128]{3,1,0,2:T(8,128)}, bf16[2,512,2,128]{3,1,2,0:T(8...) while((s32[]{:T(128)}, f32[1024,2,128]{2,0,1:T(8,128)}, ...), condition=%wide.region_43.44_spmd.clone, body=%wide.region_37.43_spmd.clone.sunk | while | flops 1386741760 | bytes 128565680 | solution.py:166
  1502.2 28.2 %reduce-scatter.25.cloned.1.call-done = bf16[256,2176]{1,0:T(8,128)(2,1)} async-done(((bf16[1024,2176]{1,0:T(8,128)(2,1)}), bf16[256,2176]{1,0:T(8,128)(2,1)}) %reduce-scatter.25.cloned.1.call-update) | async-done | bytes 1114128 | tf_op jit(solution)/shard_map/reduce_scatter | solution.py:331
  1565.1 29.8 %reduce-scatter.37.cloned.1.call-done = bf16[16,2048]{1,0:T(8,128)(2,1)} async-done(((bf16[128,2048]{1,0:T(8,128)(2,1)}), bf16[16,2048]{1,0:T(8,128)(2,1)}) %reduce-scatter.37.cloned.1.call-update) | async-done | bytes 65552 | tf_op jit(solution)/shard_map/reduce_scatter | solution.py:469
  1598.7 27.0 %reduce-scatter.31.cloned.1.call-done = bf16[1024,16]{0,1:T(8,128)(2,1)} async-done(((bf16[1024,128]{0,1:T(8,128)(2,1)}), bf16[1024,16]{0,1:T(8,128)(2,1)}) %reduce-scatter.31.cloned.1.call-update) | async-done | bytes 32784 | tf_op jit(solution)/shard_map/reduce_scatter | solution.py:466
  1627.1 30.1 %reduce-scatter.29.cloned.1.call-done = bf16[16,2060]{1,0:T(8,128)(2,1)} async-done(((bf16[128,2060]{1,0:T(8,128)(2,1)}), bf16[16,2060]{1,0:T(8,128)(2,1)}) %reduce-scatter.29.cloned.1.call-update) | async-done | bytes 65936 | tf_op jit(solution)/shard_map/reduce_scatter | solution.py:463
  1661.1 132.0 %reduce-scatter.35.cloned.1.call-done = f32[64,128]{1,0:T(8,128)} async-done(((f32[2048,128]{1,0:T(8,128)}), f32[64,128]{1,0:T(8,128)}) %reduce-scatter.35.cloned.1.call-update) | async-done | bytes 32784 | tf_op jit(solution)/shard_map/reduce_scatter | solution.py:479
  1793.1 133.8 %reduce-scatter.33.cloned.1.call-done = f32[128,64]{0,1:T(8,128)} async-done(((f32[128,2048]{0,1:T(8,128)}), f32[128,64]{0,1:T(8,128)}) %reduce-scatter.33.cloned.1.call-update) | async-done | bytes 32784 | tf_op jit(solution)/shard_map/reduce_scatter | solution.py:478
  1927.0 133.9 %reduce-scatter.41.cloned.1.call-done = f32[128,64]{0,1:T(8,128)} async-done(((f32[128,2048]{0,1:T(8,128)}), f32[128,64]{0,1:T(8,128)}) %reduce-scatter.41.cloned.1.call-update) | async-done | bytes 32784 | tf_op jit(solution)/shard_map/reduce_scatter | solution.py:480
  2060.9 133.9 %reduce-scatter.27.cloned.1.call-done = f32[64,128]{1,0:T(8,128)} async-done(((f32[2048,128]{1,0:T(8,128)}), f32[64,128]{1,0:T(8,128)}) %reduce-scatter.27.cloned.1.call-update) | async-done | bytes 32784 | tf_op jit(solution)/shard_map/reduce_scatter | solution.py:477
  (1125 shorter events, 1022.8 us)
Async XLA Ops:
  60.4 136.3 %all-gather.13.cloned.1.call-start = ((), (), s32[]{:S(2)}) async-start(), calls=%async_computation.20 | async-start | bytes 9510912 | tf_op jit(solution)/shard_map/all_gather | solution.py:292
  61.1 256.6 %all-gather.15.cloned.1.call-start = ((), (), s32[]{:S(2)}) async-start(), calls=%async_computation.21 | async-start | bytes 1310720 | tf_op jit(solution)/shard_map/all_gather | solution.py:367
  242.6 243.6 %all-gather.17.cloned.1.call-start = ((), (), s32[]{:S(2)}) async-start(), calls=%async_computation.22 | async-start | bytes 1310720 | tf_op jit(solution)/shard_map/all_gather | solution.py:366
  243.6 270.8 %all-gather.19.cloned.1.call-start = ((), (), s32[]{:S(2)}) async-start(), calls=%async_computation.23 | async-start | bytes 4718592 | tf_op jit(solution)/shard_map/all_gather | solution.py:299
  244.1 344.2 %reduce-scatter.17.cloned.1.call-start = ((), (), s32[]{:S(2)}) async-start(), calls=%async_computation.24 | async-start | bytes 5570560 | tf_op jit(solution)/shard_map/reduce_scatter | solution.py:317
  524.0 125.6 %all-gather.25.cloned.1.call-start = ((), (), s32[]{:S(2)}) async-start(), calls=%async_computation.27 | async-start | bytes 4718592 | tf_op jit(solution)/shard_map/all_gather | solution.py:299
  530.5 169.6 %all-gather.27.cloned.1.call-start = ((), (), s32[]{:S(2)}) async-start(), calls=%async_computation.29 | async-start | bytes 5570560 | tf_op jit(solution)/shard_map/all_gather | solution.py:340
  568.3 215.5 %all-gather.23.cloned.1.call-start = ((), (), s32[]{:S(2)}) async-start(), calls=%async_computation.26 | async-start | bytes 9437184 | tf_op jit(solution)/shard_map/all_gather | solution.py:292
  569.0 267.7 %all-gather.21.cloned.1.call-start = ((), (), s32[]{:S(2)}) async-start(), calls=%async_computation.25 | async-start | bytes 5242880 | tf_op jit(solution)/shard_map/all_gather | solution.py:305
  592.5 381.8 %reduce-scatter.21.cloned.1.call-start = ((), (), s32[]{:S(2)}) async-start(), calls=%async_computation.30 | async-start | bytes 5570560 | tf_op jit(solution)/shard_map/reduce_scatter | solution.py:331
  919.3 117.3 %all-gather.29.cloned.1.call-start = ((), (), s32[]{:S(2)}) async-start(), calls=%async_computation.31 | async-start | bytes 5570560 | tf_op jit(solution)/shard_map/all_gather | solution.py:340
  981.6 438.0 %reduce-scatter.43.cloned.1.call-start = ((), (), s32[]{:S(2)}) async-start(), calls=%async_computation.42 | async-start | bytes 1310720
  1312.1 111.1 %reduce-scatter.23.cloned.1.call-start = ((), (), s32[]{:S(2)}) async-start(), calls=%async_computation.32 | async-start | bytes 1310720 | tf_op jit(solution)/shard_map/reduce_scatter | solution.py:439
  1370.4 117.6 %reduce-scatter.19.cloned.1.call-start = ((), (), s32[]{:S(2)}) async-start(), calls=%async_computation.28 | async-start | bytes 5570560 | tf_op jit(solution)/shard_map/reduce_scatter | solution.py:317
  1383.8 146.6 %reduce-scatter.25.cloned.1.call-start = ((), (), s32[]{:S(2)}) async-start(), calls=%async_computation.33 | async-start | bytes 5570560 | tf_op jit(solution)/shard_map/reduce_scatter | solution.py:331
  1467.8 95.9 %reduce-scatter.39.cloned.1.call-start = ((), (), s32[]{:S(2)}) async-start(), calls=%async_computation.40 | async-start | bytes 294912 | tf_op jit(solution)/shard_map/reduce_scatter | solution.py:472
  1470.4 124.5 %reduce-scatter.37.cloned.1.call-start = ((), (), s32[]{:S(2)}) async-start(), calls=%async_computation.39 | async-start | bytes 589824 | tf_op jit(solution)/shard_map/reduce_scatter | solution.py:469
  1475.2 150.5 %reduce-scatter.31.cloned.1.call-start = ((), (), s32[]{:S(2)}) async-start(), calls=%async_computation.36 | async-start | bytes 294912 | tf_op jit(solution)/shard_map/reduce_scatter | solution.py:466
  1477.8 179.4 %reduce-scatter.29.cloned.1.call-start = ((), (), s32[]{:S(2)}) async-start(), calls=%async_computation.35 | async-start | bytes 626688 | tf_op jit(solution)/shard_map/reduce_scatter | solution.py:463
  1482.7 310.4 %reduce-scatter.35.cloned.1.call-start = ((), (), s32[]{:S(2)}) async-start(), calls=%async_computation.38 | async-start | bytes 1081344 | tf_op jit(solution)/shard_map/reduce_scatter | solution.py:479
  1485.3 441.7 %reduce-scatter.33.cloned.1.call-start = ((), (), s32[]{:S(2)}) async-start(), calls=%async_computation.37 | async-start | bytes 1081344 | tf_op jit(solution)/shard_map/reduce_scatter | solution.py:478
  1487.9 573.0 %reduce-scatter.41.cloned.1.call-start = ((), (), s32[]{:S(2)}) async-start(), calls=%async_computation.41 | async-start | bytes 1081344 | tf_op jit(solution)/shard_map/reduce_scatter | solution.py:480
  1502.1 692.6 %reduce-scatter.27.cloned.1.call-start = ((), (), s32[]{:S(2)}) async-start(), calls=%async_computation.34 | async-start | bytes 1081344 | tf_op jit(solution)/shard_map/reduce_scatter | solution.py:477
  1542.5 116.3 %all-to-all-start.4 = ((bf16[32,8,2048]{2,1,0:T(8,128)(2,1)}), bf16[32,8,2048]{2,1,0:T(8,128)(2,1)S(1)}, u32[]{:S(2)}, u32[]{:S(2)}) async-start(bf16[32,8,2048]{2,1,0:T(8,128)(2,1)} %bitcast.64), calls=%async_computation.9 | async-start | bytes 2097152 | tf_op jit(solution)/shard_map/all_to_all | solution.py:490
  (207 other events, 6109.0 us)
Sparse Core Ops, SparseCore 0:
  60.5 51.4 all-gather.10
  113.6 83.0 all-gather.12
  242.7 24.6 all-gather.14
  269.1 26.4 all-gather.16
  297.1 47.8 all-gather.18
  524.1 64.1 reduce-scatter.16
  589.9 54.9 all-gather.24
  646.8 53.1 all-gather.26
  701.6 82.0 all-gather.22
  785.4 51.2 all-gather.20
  919.4 54.8 reduce-scatter.20
  981.7 54.8 all-gather.28
  1312.2 27.7 reduce-scatter.42
  1370.5 27.7 reduce-scatter.22
  1401.2 54.8 reduce-scatter.18
  1468.0 62.3 reduce-scatter.24
  1532.5 31.1 reduce-scatter.38
  1565.9 28.9 reduce-scatter.36
  1597.1 28.5 reduce-scatter.30
  1627.9 29.2 reduce-scatter.28
  1660.1 132.9 reduce-scatter.34
  1795.9 130.9 reduce-scatter.32
  1929.9 130.9 reduce-scatter.40
  2063.5 131.1 reduce-scatter.26
where the time goes:
time: 2220 us; the launch traced here: 2200 us
  waiting for transfers between devices  1070 us (48%)
  local copies, waits for them, and re-layouts  465 us (21%)
  matrix products  277 us (12%)
  other arithmetic  184 us (8%)
  blocking collectives  153 us (7%)
  starting transfers between devices  22.7 us (1%)
    dynamic_update_slice x32, local copies, waits for them, and re-layouts, state_scan(): _, outputs = lax.scan(jax.checkpoint(scan_step), zero_state, sliced)  161 us
    all_gather x2, waiting for transfers between devices, fetch_inward(): lax.all_gather(weight, 'row', axis=0, tiled=True)  150 us
    reduce_scatter x1, waiting for transfers between devices, local(): lax.psum_scatter(down_raise_grad, ('row', 'col'), scatter_dimension=1, ti...  134 us
    reduce_scatter x1, waiting for transfers between devices, local(): lax.psum_scatter(in_lower_grad, ('row', 'col'), scatter_dimension=0, tile...  134 us
    reduce_scatter x1, waiting for transfers between devices, local(): lax.psum_scatter(mix_raise_grad, ('row', 'col'), scatter_dimension=1, til...  134 us
    reduce_scatter x1, waiting for transfers between devices, local(): lax.psum_scatter(feed_lower_grad, ('row', 'col'), scatter_dimension=0, ti...  132 us
    all_gather x2, waiting for transfers between devices, spread_back(): portion = lax.all_gather(joined, 'col', axis=0, tiled=True)  96.7 us
    reduce_scatter x2, waiting for transfers between devices, reduce_backward(): lax.psum_scatter(partial_rows(jnp.int32(0), lax.axis_size('col') * local_...  83.2 us
  transfers between devices with their start and end apart: 29, of which 19 were waited for; matrix products, arithmetic and copies ran while one was open for 22% of the time, Pallas kernels for 0%

commit v1 on v0

v1 whole, which is shorter than its diff:
```python
import math

import jax
import jax.numpy as jnp
from jax import lax
from jax.sharding import PartitionSpec as P

NH = 48
HP = 64
NSTATE = 256
KCONV = 4
QUERY_HEADS = 8
KEY_VALUE_HEADS = 2
HEAD_SIZE = 128
RANK = 16
NADAPT = 8
SSD_BLOCK = 256
ATT_BLOCK = 512
DSSM = 3072
UNIT_IN = 1030
UNIT_FF = 512


EPSILON = 1e-05
ROPE_BASE = 10000.0
NEGATIVE = -1e30
FLOAT = jnp.float32
BFLOAT = jnp.bfloat16


def round_value(values):
    rounded = lax.optimization_barrier(values.astype(BFLOAT)).astype(FLOAT)
    return values + lax.stop_gradient(rounded - values)


def product(left, right):
    return jnp.dot(left, right, preferred_element_type=FLOAT)


def contract_last(left, right):
    return lax.dot_general(left, right, (((1,), (1,)), ((), ())), preferred_element_type=FLOAT)


def contract_first(left, right):
    return lax.dot_general(left, right, (((0,), (0,)), ((), ())), preferred_element_type=FLOAT)


def rms_norm(values, gain):
    return values * lax.rsqrt(jnp.mean(values * values, axis=-1, keepdims=True) + EPSILON) * gain


def sequence_tables(lengths, adapters, sequence_length):
    sequence_count = lengths.shape[0]
    boundary = jnp.cumsum(lengths)
    token_index = jnp.arange(sequence_length, dtype=jnp.int32)
    passed = (token_index[:, None] >= boundary[None, :]).astype(jnp.int32)
    segment = jnp.sum(passed, axis=1)
    segment_start = jnp.sum(passed * lengths[None, :], axis=1)
    position = token_index - segment_start
    member = (segment[:, None] == jnp.arange(sequence_count, dtype=jnp.int32)[None, :]).astype(
        jnp.int32
    )
    chosen = jnp.sum(member * adapters[None, :], axis=1)
    column = jnp.arange(NADAPT * RANK, dtype=jnp.int32) // RANK
    selector = (chosen[:, None] == column[None, :]).astype(FLOAT)
    return (segment, position, selector)


def causal_conv(channels, tap_table, position):
    running = tap_table[KCONV] + channels * tap_table[0]
    for lag_step in range(1, KCONV):
        shifted = jnp.concatenate(
            [jnp.zeros((lag_step, channels.shape[1]), FLOAT), channels[:-lag_step]], axis=0
        )
        running = (
            running + jnp.where((position >= lag_step)[:, None], shifted, 0.0) * tap_table[lag_step]
        )
    return jax.nn.silu(running)


def rotate(vectors, position):
    half_width = HEAD_SIZE // 2
    frequency = ROPE_BASE ** (-2.0 * jnp.arange(half_width, dtype=FLOAT) / HEAD_SIZE)
    angle_table = position.astype(FLOAT)[:, None] * frequency[None, :]
    cosine = jnp.cos(angle_table)[:, None, :]
    sine_part = jnp.sin(angle_table)[:, None, :]
    leading = vectors[..., :half_width]
    trailing = vectors[..., half_width:]
    return jnp.concatenate(
        [leading * cosine - trailing * sine_part, trailing * cosine + leading * sine_part], axis=-1
    )


def state_scan(inputs, step_size, log_decay, write_vectors, read_vectors, segment):
    sequence_length, head_count = step_size.shape
    block_count = sequence_length // SSD_BLOCK
    previous = jnp.concatenate([jnp.full((1,), -1, jnp.int32), segment[:-1]])
    first_previous = previous.reshape(block_count, SSD_BLOCK)[:, 0]
    inner_index = jnp.arange(SSD_BLOCK, dtype=jnp.int32)
    lower_mask = inner_index[:, None] >= inner_index[None, :]

    def scan_step(carry_state, block_data):
        (
            block_inputs,
            block_steps,
            block_decay,
            block_write,
            block_read,
            block_segment,
            block_previous,
        ) = block_data
        cumulative = jnp.cumsum(block_decay, axis=0)
        intersection = contract_last(block_read, block_write)
        allowed = lower_mask & (block_segment[:, None] == block_segment[None, :])
        difference = cumulative[:, None, :] - cumulative[None, :, :]
        decay_table = jnp.exp(jnp.where(allowed[:, :, None], difference, NEGATIVE))
        weights = round_value(intersection[:, :, None] * decay_table * block_steps[None, :, :])
        within = jnp.einsum("tsh,shp->thp", weights, block_inputs)
        carried = (block_segment == block_previous).astype(FLOAT)
        read_scaled = round_value(
            block_read[:, None, :] * (jnp.exp(cumulative) * carried[:, None])[:, :, None]
        )
        across = jnp.einsum("thn,hpn->thp", read_scaled, round_value(carry_state))
        tail_factor = (
            jnp.exp(cumulative[-1][None, :] - cumulative)
            * block_steps
            * (block_segment == block_segment[-1]).astype(FLOAT)[:, None]
        )
        write_scaled = round_value(block_write[:, None, :] * tail_factor[:, :, None])
        fresh_state = jnp.einsum("shp,shn->hpn", block_inputs, write_scaled)
        through = jnp.exp(cumulative[-1]) * (block_segment[-1] == block_previous).astype(FLOAT)
        return (carry_state * through[:, None, None] + fresh_state, within + across)

    sliced = (
        inputs.reshape(block_count, SSD_BLOCK, head_count, HP),
        step_size.reshape(block_count, SSD_BLOCK, head_count),
        log_decay.reshape(block_count, SSD_BLOCK, head_count),
        write_vectors.reshape(block_count, SSD_BLOCK, NSTATE),
        read_vectors.reshape(block_count, SSD_BLOCK, NSTATE),
        segment.reshape(block_count, SSD_BLOCK),
        first_previous,
    )
    zero_state = jnp.zeros((head_count, HP, NSTATE), FLOAT)
    _, outputs = lax.scan(jax.checkpoint(scan_step), zero_state, sliced)
    return outputs.reshape(sequence_length, head_count, HP)


def attention(query, key_rows, value_rows, segment):
    sequence_length, unit_count = (query.shape[0], query.shape[1])
    block_count = sequence_length // ATT_BLOCK
    token_index = jnp.arange(sequence_length, dtype=jnp.int32)
    score_scale = 1.0 / math.sqrt(HEAD_SIZE)

    def score_block(block_data):
        query_block, segment_block, token_block = block_data
        score = jnp.einsum("qud,kud->uqk", query_block, key_rows) * score_scale
        allowed = (segment_block[:, None] == segment[None, :]) & (
            token_index[None, :] <= token_block[:, None]
        )
        score = jnp.where(allowed[None], score, NEGATIVE)
        row_max = jnp.max(score, axis=2, keepdims=True)
        exponent = jnp.exp(score - row_max)
        weights = round_value(exponent / jnp.sum(exponent, axis=2, keepdims=True))
        return jnp.einsum("uqk,kud->qud", weights, value_rows)

    attended = lax.map(
        jax.checkpoint(score_block),
        (
            query.reshape(block_count, ATT_BLOCK, unit_count, HEAD_SIZE),
            segment.reshape(block_count, ATT_BLOCK),
            token_index.reshape(block_count, ATT_BLOCK),
        ),
    )
    return attended.reshape(sequence_length, unit_count, HEAD_SIZE)


def mixer_branch(gate_in, conv_in, query_in, step_in, state_values, key_in, value_in, conv_values, scan_params, segment, position):
    rows = gate_in.shape[0]
    head_count = step_in.shape[1]
    unit_count = head_count * QUERY_HEADS // NH
    scan_input = round_value(causal_conv(conv_in, conv_values, position)).reshape(rows, head_count, HP)
    step_size = jax.nn.softplus(step_in + scan_params[0][None, :])
    log_decay = -step_size * jnp.exp(scan_params[1])[None, :]
    scanned = state_scan(
        scan_input, step_size, log_decay, state_values[:, :NSTATE], state_values[:, NSTATE:], segment
    )
    scan_output = (scanned + scan_params[2][None, :, None] * scan_input) * jax.nn.silu(
        gate_in.reshape(rows, head_count, HP)
    )
    attended = attention(
        round_value(rotate(query_in.reshape(rows, unit_count, HEAD_SIZE), position)),
        jnp.broadcast_to(round_value(rotate(key_in[:, None, :], position)), (rows, unit_count, HEAD_SIZE)),
        jnp.broadcast_to(value_in[:, None, :], (rows, unit_count, HEAD_SIZE)),
        segment,
    )
    return jnp.concatenate(
        [scan_output.reshape(rows, head_count * HP), attended.reshape(rows, unit_count * HEAD_SIZE)], axis=1
    )


GATE_WIDTH = DSSM // QUERY_HEADS
PAIR_WIDTH = 2 * KEY_VALUE_HEADS * HEAD_SIZE // QUERY_HEADS
STATE_WIDTH = 2 * NSTATE // QUERY_HEADS
STEP_WIDTH = NH // QUERY_HEADS
LANES = 128
ALL_AXES = ("row", "col")


def pad_columns(values, width):
    return jnp.pad(values, ((0, 0), (0, width - values.shape[1])))


def align_units(values, units):
    cuts = [0, GATE_WIDTH, 2 * GATE_WIDTH, 2 * GATE_WIDTH + HEAD_SIZE]
    cuts += [cuts[-1] + PAIR_WIDTH, cuts[-1] + PAIR_WIDTH + STATE_WIDTH, UNIT_IN]
    parts = [
        values[:, unit * UNIT_IN + low : unit * UNIT_IN + high]
        for low, high in zip(cuts[:-1], cuts[1:])
        for unit in range(units)
    ]
    joined = jnp.concatenate(parts, axis=1)
    return pad_columns(joined, -(-joined.shape[1] // LANES) * LANES)


def restore_units(values, units):
    widths = [GATE_WIDTH, GATE_WIDTH, HEAD_SIZE, PAIR_WIDTH, STATE_WIDTH, STEP_WIDTH]
    parts = []
    for unit in range(units):
        start = 0
        for width in widths:
            parts.append(values[:, start + unit * width : start + (unit + 1) * width])
            start += units * width
    return jnp.concatenate(parts, axis=1)


def split_halves(values, units, first, axis):
    block = values.shape[axis] // units
    take = lambda low, high: lax.slice_in_dim(values, low, high, axis=axis)
    parts = [take(unit * block, unit * block + first) for unit in range(units)]
    parts += [take(unit * block + first, (unit + 1) * block) for unit in range(units)]
    return jnp.concatenate(parts, axis=axis)


def join_halves(values, units, first, axis):
    block = values.shape[axis] // units
    rest = block - first
    take = lambda low, high: lax.slice_in_dim(values, low, high, axis=axis)
    parts = []
    for unit in range(units):
        parts.append(take(unit * first, (unit + 1) * first))
        parts.append(take(units * first + unit * rest, units * first + (unit + 1) * rest))
    return jnp.concatenate(parts, axis=axis)


def flip(values, mask):
    return lax.ppermute(values, "col", [(i, i ^ mask) for i in range(4)])


def gather_blocks(own):
    col = lax.axis_index("col")
    half = own.shape[-1] // 2
    near = flip(own, 1)
    far = flip(own, 2)
    corner = jnp.concatenate([flip(far[..., :half], 1), flip(near[..., half:], 2)], axis=-1)
    return [(col, own), (col ^ 1, near), (col ^ 2, far), (col ^ 3, corner)]


def reduce_blocks(piece):
    col = lax.axis_index("col")
    wide = lambda values: values.astype(FLOAT)
    send = lambda values, mask: flip(values.astype(BFLOAT), mask)
    corner_a = send(piece(col ^ 3, 0), 1)
    corner_b = send(piece(col ^ 3, 1), 2)
    near_a = send(piece(col ^ 1, 0), 1)
    far_b = send(piece(col ^ 2, 1), 2)
    far_a = send(piece(col ^ 2, 0) + wide(corner_a), 2)
    near_b = send(piece(col ^ 1, 1) + wide(corner_b), 1)
    first = piece(col, 0) + wide(near_a) + wide(far_a)
    second = piece(col, 1) + wide(far_b) + wide(near_b)
    return first, second


def rows_of(values, block, rows):
    return lax.dynamic_slice_in_dim(values, block * rows, rows, 0)


def spread_project(own, wide, narrow_factor, selector):
    rows = own.shape[0]
    width = narrow_factor.shape[1]

    def project(values, chosen):
        both = product(values, wide)
        narrow = (chosen * both[:, width:]).astype(BFLOAT)
        return (both[:, :width] + product(narrow, narrow_factor)).astype(BFLOAT), narrow

    if lax.axis_size("col") != 4:
        return project(lax.all_gather(own, "col", axis=0, tiled=True), selector)
    total = rows * 4
    result = jnp.zeros((total, width), BFLOAT)
    narrow_result = jnp.zeros((total, LANES), BFLOAT)
    for block, values in gather_blocks(own):
        part, narrow = project(values, rows_of(selector, block, rows))
        result = lax.dynamic_update_slice_in_dim(result, part, block * rows, 0)
        narrow_result = lax.dynamic_update_slice_in_dim(narrow_result, narrow, block * rows, 0)
    return result, narrow_result


def collect_project(values, wide, narrow_factor, own_selector):
    rows = own_selector.shape[0]
    width = narrow_factor.shape[1]
    model = wide.shape[0]
    weight = wide[:, :width]
    if lax.axis_size("col") != 4:
        partial = jnp.concatenate(
            [contract_last(values, weight), contract_last(values, narrow_factor)], axis=1
        ).astype(BFLOAT)
        summed = lax.psum_scatter(partial, "col", scatter_dimension=0, tiled=True).astype(FLOAT)
        base, narrow = summed[:, :model], summed[:, model:]
    else:
        half = model // 2

        def piece(block, side):
            taken = rows_of(values, block, rows)
            if side:
                return contract_last(taken, weight[half:])
            return jnp.concatenate(
                [contract_last(taken, weight[:half]), contract_last(taken, narrow_factor)], axis=1
            )

        first, second = reduce_blocks(piece)
        base = jnp.concatenate([first[:, :half], second], axis=1)
        narrow = first[:, half:]
    inner = (own_selector * narrow).astype(BFLOAT)
    return base + contract_last(inner, wide[:, width:]), inner


def local(
    tokens_in,
    cotangent,
    target,
    sequence_lengths,
    sequence_adapter,
    norm_gains,
    weight_in,
    conv_values,
    conv_states,
    scan_params,
    weight_mix,
    weight_feed,
    weight_down,
    in_lower,
    in_raise,
    mix_lower,
    mix_raise,
    feed_lower,
    feed_raise,
    down_lower,
    down_raise,
):
    cols = lax.axis_size("col")
    rows_axis = lax.axis_size("row")
    col = lax.axis_index("col")
    devices = cols * rows_axis
    rows = tokens_in.shape[0]
    model = tokens_in.shape[1]
    total = rows * cols
    units = QUERY_HEADS // cols
    heads = units * STEP_WIDTH
    peer = rows // devices
    lengths, adapters = sequence_lengths[0], sequence_adapter[0]
    sequences = lengths.shape[0]

    gather = lambda values: lax.all_gather(values, "row", axis=0, tiled=True)
    wide_in = gather(jnp.concatenate([align_units(weight_in, units), in_lower], axis=1))
    small_parts = [
        align_units(in_raise, units),
        split_halves(mix_lower, units, GATE_WIDTH, 0).T,
        split_halves(feed_raise, units, UNIT_FF, 1),
        down_lower.T,
    ]
    small_cuts = [0]
    for part in small_parts:
        small_cuts.append(small_cuts[-1] + part.shape[1])
    small = gather(jnp.concatenate(small_parts, axis=1))
    narrow_in, narrow_mix, narrow_feed, narrow_down = [
        small[:, low:high] for low, high in zip(small_cuts[:-1], small_cuts[1:])
    ]
    wide_mix = gather(
        jnp.concatenate([split_halves(weight_mix, units, GATE_WIDTH, 0), mix_raise], axis=0).T
    )
    wide_feed = gather(
        jnp.concatenate([split_halves(weight_feed, units, UNIT_FF, 1), feed_lower], axis=1)
    )
    wide_down = gather(jnp.concatenate([weight_down, down_raise], axis=0).T)

    destination = target // rows
    index = jnp.arange(rows, dtype=jnp.int32)
    same = (destination[:, None] == destination[None, :]) & (index[None, :] < index[:, None])
    place_sent = destination * peer + jnp.sum(same.astype(jnp.int32), axis=1)
    send_matrix = (index[:, None] == place_sent[None, :]).astype(BFLOAT)
    notes = jnp.concatenate([(target % rows)[:, None], jnp.broadcast_to(adapters[None, :], (rows, sequences))], axis=1)
    notes = pad_columns(notes.astype(BFLOAT), LANES)
    exchange = lambda values: lax.all_to_all(values, ALL_AXES, split_axis=0, concat_axis=0, tiled=True)
    arrived = exchange(product(send_matrix, jnp.concatenate([tokens_in, notes], axis=1)).astype(BFLOAT))
    arrived_grad = exchange(product(send_matrix, cotangent).astype(BFLOAT))
    arrived_slot = arrived[:, model].astype(jnp.int32)
    place_matrix = (index[:, None] == arrived_slot[None, :]).astype(BFLOAT)
    source_adapters = arrived[::peer, model + 1 : model + 1 + sequences].astype(jnp.int32)
    own_input = product(place_matrix, arrived[:, :model])
    branch_two = product(place_matrix, arrived_grad).astype(BFLOAT)
    own_upstream = branch_two.astype(FLOAT)

    segment, position, selector = sequence_tables(lengths, adapters, total)
    own_selector = rows_of(selector, col, rows)
    own_segment = rows_of(segment, col, rows)
    norm_gain = norm_gains.astype(FLOAT)

    def compact_grad(narrow, values):
        parts = [
            lax.dynamic_slice_in_dim(narrow, adapters[at] * RANK, RANK, 1)
            * (own_segment == at).astype(BFLOAT)[:, None]
            for at in range(sequences)
        ]
        grad = contract_first(jnp.concatenate(parts, axis=1), values).astype(BFLOAT)
        kept = sequences * RANK
        grad = grad.reshape(kept, devices, model // devices).transpose(1, 0, 2)
        return pad_columns(grad.reshape(devices, kept * model // devices), model)

    def expand_grad(dealt):
        kept = sequences * RANK
        dealt = dealt[:, : kept * model // devices].reshape(devices * kept, model // devices)
        adapter_row = (source_adapters[:, :, None] * RANK + jnp.arange(RANK, dtype=jnp.int32)).reshape(-1)
        chosen = (jnp.arange(NADAPT * RANK, dtype=jnp.int32)[:, None] == adapter_row[None, :]).astype(BFLOAT)
        return product(chosen, dealt)

    def send_back(values, grads):
        back = product(place_matrix.T, values.astype(BFLOAT)).astype(BFLOAT).reshape(devices, peer, model)
        joined = jnp.concatenate([back] + [grad[:, None, :] for grad in grads], axis=1)
        dealt = exchange(joined)
        returned = product(send_matrix.T, dealt[:, :peer].reshape(rows, model)).astype(BFLOAT)
        return returned, [expand_grad(dealt[:, peer + at]) for at in range(len(grads))]

    normed_one, norm_one_back = jax.vjp(lambda values: rms_norm(values, norm_gain[0]), own_input)
    normed_one = normed_one.astype(BFLOAT)
    projected, inner_in = spread_project(normed_one, wide_in, narrow_in, selector)
    cuts = [0]
    for width in (GATE_WIDTH, GATE_WIDTH, HEAD_SIZE, PAIR_WIDTH, STATE_WIDTH, STEP_WIDTH):
        cuts.append(cuts[-1] + units * width)
    gate_in, conv_in, query_in, pair_own, state_own, step_in = [
        projected[:, low:high] for low, high in zip(cuts[:-1], cuts[1:])
    ]
    conv_state_float = conv_states.astype(FLOAT)
    state_post, state_back = jax.vjp(
        lambda values: causal_conv(values, conv_state_float, position), state_own.astype(FLOAT)
    )
    shared = jnp.concatenate([pair_own, state_post.astype(BFLOAT)], axis=1)
    if cols == 4:
        held = jnp.zeros((cols,) + shared.shape, BFLOAT)
        for block, values in gather_blocks(shared):
            held = lax.dynamic_update_index_in_dim(held, values, block, 0)
    else:
        held = lax.all_gather(shared, "col", axis=0)
    pair_width = units * PAIR_WIDTH
    state_full = jnp.concatenate([held[at, :, pair_width:] for at in range(cols)], axis=1)
    pair_full = jnp.concatenate([held[at, :, :pair_width] for at in range(cols)], axis=1)
    key_head = col * units // (QUERY_HEADS // KEY_VALUE_HEADS)
    pick = lambda start: lax.select_n(
        key_head,
        *[pair_full[:, start + at * HEAD_SIZE : start + (at + 1) * HEAD_SIZE] for at in range(KEY_VALUE_HEADS)],
    )
    keys, values = pick(0), pick(KEY_VALUE_HEADS * HEAD_SIZE)
    conv_value_float = conv_values.astype(FLOAT)

    def mix_local(*parts):
        return mixer_branch(*parts, conv_value_float, scan_params, segment, position)

    mixed_float, mixer_back = jax.vjp(
        mix_local, *[part.astype(FLOAT) for part in (gate_in, conv_in, query_in, step_in, state_full, keys, values)]
    )
    mixed_out = mixed_float.astype(BFLOAT)
    branch_sum, inner_out = collect_project(mixed_out, wide_mix, narrow_mix, own_selector)
    hidden = own_input + branch_sum
    normed_two, norm_two_back = jax.vjp(lambda values: rms_norm(values, norm_gain[1]), hidden)
    normed_two = normed_two.astype(BFLOAT)
    gate_up, inner_feed = spread_project(normed_two, wide_feed, narrow_feed, selector)
    act_grad, narrow_two = spread_project(branch_two, wide_down, narrow_down, selector)
    half_feed = units * UNIT_FF

    def swiglu(gate_part, up_part):
        return jax.nn.silu(gate_part) * up_part

    activated, swiglu_back = jax.vjp(
        swiglu, gate_up[:, :half_feed].astype(FLOAT), gate_up[:, half_feed:].astype(FLOAT)
    )
    activated = activated.astype(BFLOAT)
    feed_grad = jnp.concatenate(swiglu_back(act_grad.astype(FLOAT)), axis=1).astype(BFLOAT)
    normed_two_grad, narrow_three = collect_project(feed_grad, wide_feed, narrow_feed, own_selector)
    (hidden_from_norm,) = norm_two_back(normed_two_grad)
    hidden_grad = own_upstream + hidden_from_norm
    branch_one = hidden_grad.astype(BFLOAT)
    mixed_grad, narrow_one = spread_project(branch_one, wide_mix, narrow_mix, selector)

    down_sum, inner_down = collect_project(activated, wide_down, narrow_down, own_selector)
    block_out, (grad_down_raise, grad_feed_lower, grad_mix_raise) = send_back(
        hidden + down_sum,
        [
            compact_grad(inner_down, branch_two),
            compact_grad(narrow_three, normed_two),
            compact_grad(inner_out, branch_one),
        ],
    )

    def sum_rows(values):
        return lax.psum_scatter(values.astype(BFLOAT), "row", scatter_dimension=0, tiled=True).astype(FLOAT)

    early = sum_rows(
        jnp.concatenate(
            [
                contract_first(narrow_one, mixed_out),
                contract_first(inner_feed, feed_grad),
                contract_first(narrow_two, activated),
            ],
            axis=1,
        )
    )
    early_cuts = [cut - small_cuts[1] for cut in small_cuts[1:]]
    mix_lower_part, feed_raise_part, down_lower_part = [
        early[:, low:high] for low, high in zip(early_cuts[:-1], early_cuts[1:])
    ]
    grad_mix_lower = join_halves(mix_lower_part, units, GATE_WIDTH, 1).T
    grad_feed_raise = join_halves(feed_raise_part, units, UNIT_FF, 1)
    grad_down_lower = down_lower_part.T

    gate_grad, conv_grad, query_grad, step_grad, state_grad, key_grad, value_grad = mixer_back(
        mixed_grad.astype(FLOAT)
    )
    mine = [(key_head == at).astype(FLOAT) for at in range(KEY_VALUE_HEADS)]
    pair_grad = jnp.concatenate([grad * here for grad in (key_grad, value_grad) for here in mine], axis=1)
    state_width = units * STATE_WIDTH
    stacked = jnp.stack(
        [
            jnp.concatenate(
                [
                    pair_grad[:, at * pair_width : (at + 1) * pair_width],
                    state_grad[:, at * state_width : (at + 1) * state_width],
                ],
                axis=1,
            )
            for at in range(cols)
        ]
    )
    if cols == 4:
        part = total // 2
        shared_grad = jnp.concatenate(
            reduce_blocks(
                lambda block, side: lax.dynamic_index_in_dim(stacked, block, 0, False)[
                    side * part : (side + 1) * part
                ]
            ),
            axis=0,
        )
    else:
        shared_grad = lax.psum_scatter(
            stacked.astype(BFLOAT).reshape(cols * total, -1), "col", scatter_dimension=0, tiled=True
        ).astype(FLOAT)
    (state_pre_grad,) = state_back(shared_grad[:, pair_width:])
    projected_grad = jnp.concatenate(
        [gate_grad, conv_grad, query_grad, shared_grad[:, :pair_width], state_pre_grad, step_grad], axis=1
    ).astype(BFLOAT)
    projected_grad = pad_columns(projected_grad, narrow_in.shape[1])
    grad_in_raise = restore_units(sum_rows(contract_first(inner_in, projected_grad)), units)
    normed_one_grad, narrow_four = collect_project(projected_grad, wide_in, narrow_in, own_selector)
    (input_from_norm,) = norm_one_back(normed_one_grad)
    input_grad, (grad_in_lower,) = send_back(
        hidden_grad + input_from_norm, [compact_grad(narrow_four, normed_one)]
    )
    return (
        block_out,
        input_grad,
        grad_in_lower.T,
        grad_in_raise,
        grad_mix_lower,
        grad_mix_raise,
        grad_feed_lower.T,
        grad_feed_raise,
        grad_down_lower,
        grad_down_raise,
    )


def solution(mesh):
    in_specs = (
        P(("row", "col"), None),
        P(("row", "col"), None),
        P(("row", "col")),
        P("row", None),
        P("row", None),
        P(),
        P("row", "col"),
        P(None, "col"),
        P(None, "col"),
        P(None, "col"),
        P("col", "row"),
        P("row", "col"),
        P("col", "row"),
        P("row", None),
        P("row", "col"),
        P("col", "row"),
        P(None, "row"),
        P("row", None),
        P("row", "col"),
        P("col", "row"),
        P(None, "row"),
    )
    out_specs = (
        P(("row", "col"), None),
        P(("row", "col"), None),
        P(("row", "col"), None),
        P("row", "col"),
        P("col", "row"),
        P(None, ("row", "col")),
        P(("row", "col"), None),
        P("row", "col"),
        P("col", "row"),
        P(None, ("row", "col")),
    )
    return jax.shard_map(local, mesh=mesh, in_specs=in_specs, out_specs=out_specs, check_vma=False)
```

time: 2220 us -> 1360 us (0.61)
  waiting for transfers between devices: 1070 us -> 241 us
  blocking collectives: 153 us -> 0 us
  matrix products: 277 us -> 357 us
  starting transfers between devices: 22.7 us -> 100 us
  local copies, waits for them, and re-layouts: 465 us -> 416 us
    reduce_scatter x13 -> x2, waiting for transfers between devices: 721 us -> 0.01 us  [sum_rows(): lax.psum_scatter(values.astype(BFLOAT), 'row', scatter_dimension=0, tiled...]
    all_gather x10 -> x5, waiting for transfers between devices: 320 us -> 0.03 us  [local(): gather = lambda values: lax.all_gather(values, 'row', axis=0, tiled=True)]
    all_gather x8 -> x0, blocking collectives: 153 us -> none  [the longest x2 50.2 us: fetch_outward(): lax.all_gather(right_factor, 'row', axis=1, tiled=True)]
    all_to_all x5 -> x4, waiting for transfers between devices: 26 us -> 137 us  [local(): lax.all_to_all(values, ALL_AXES, split_axis=0, concat_axis=0, tiled=True)]
    ppermute x0 -> x50, waiting for transfers between devices: none -> 104 us  [flip(): return lax.ppermute(values, 'col', [(i, i ^ mask) for i in range(4)])]
    dot_general x12 -> x44, matrix products: 56.2 us -> 128 us  [product(): return jnp.dot(left, right, preferred_element_type=FLOAT)]
    ppermute x0 -> x50, starting transfers between devices: none -> 66.3 us  [flip(): return lax.ppermute(values, 'col', [(i, i ^ mask) for i in range(4)])]
    reshape x18 -> x11, local copies, waits for them, and re-layouts: 50 us -> 16.6 us  [the longest x1 5.32 us: mixer_branch(): gate_in.reshape(rows, head_count, HP)]
  transfers between devices with their start and end apart: 29 -> 61, of which waited for: 19 -> 22; matrix products, arithmetic and copies ran while one was open for 22% -> 67% of each run, Pallas kernels for 0% -> 0%
where the time goes in v1:
time: 1360 us; the launch traced here: 1350 us
  local copies, waits for them, and re-layouts  416 us (31%)
  matrix products  357 us (26%)
  waiting for transfers between devices  241 us (18%)
  other arithmetic  201 us (15%)
  starting transfers between devices  100 us (7%)
  between operations  19.1 us (1%)
    dynamic_update_slice x16, local copies, waits for them, and re-layouts, state_scan(): _, outputs = lax.scan(jax.checkpoint(scan_step), zero_state, sliced)  149 us
    all_to_all x4, waiting for transfers between devices, local(): lax.all_to_all(values, ALL_AXES, split_axis=0, concat_axis=0, tiled=True)  137 us
    dot_general x44, matrix products, product(): return jnp.dot(left, right, preferred_element_type=FLOAT)  128 us
    ppermute x50, waiting for transfers between devices, flip(): return lax.ppermute(values, 'col', [(i, i ^ mask) for i in range(4)])  104 us
    dot_general x67, matrix products, contract_last(): lax.dot_general(left, right, (((1,), (1,)), ((), ())), preferred_element_...  83.3 us
    ppermute x50, starting transfers between devices, flip(): return lax.ppermute(values, 'col', [(i, i ^ mask) for i in range(4)])  66.3 us
    unnamed x386, local copies, waits for them, and re-layouts  58.6 us
    dot_general x12, matrix products, scan_step(): within = jnp.einsum('tsh,shp->thp', weights, block_inputs)  44.7 us
  transfers between devices with their start and end apart: 61, of which 22 were waited for; matrix products, arithmetic and copies ran while one was open for 67% of the time, Pallas kernels for 0%

profile of v1, /device:TPU:0, one launch (start us, length us, event | category | flops | bytes accessed | tf_op | source)
XLA Modules:
  0.0 1346.8 jit_solution(3580008760612466372)
XLA Ops:
  26.6 7.3 all-to-all-start
  50.4 35.3 %all-to-all-done = bf16[32,8,2176]{2,1,0:T(8,128)(2,1)S(1)} async-done(((bf16[32,8,2176]{2,1,0:T(8,128)(2,1)}), bf16[32,8,2176]{2,1,0:T(8,128)(2,1)S(1)}, u32[]{:S(2)}, u32[]{:S(2)}) %all-to-all-start) | async-done | bytes 1114144 | tf_op jit(solution)/shard_map/all_to_all | solution.py:403
  101.2 34.2 %all-to-all-done.1 = bf16[32,8,2048]{2,1,0:T(8,128)(2,1)S(1)} async-done(((bf16[32,8,2048]{2,1,0:T(8,128)(2,1)}), bf16[32,8,2048]{2,1,0:T(8,128)(2,1)S(1)}, u32[]{:S(2)}, u32[]{:S(2)}) %all-to-all-start.1) | async-done | bytes 1048608 | tf_op jit(solution)/shard_map/all_to_all | solution.py:403
  137.2 14.5 %collective-permute-start.25 = (bf16[256,2048]{0,1:T(8,128)(2,1)S(1)}, bf16[256,2048]{0,1:T(8,128)(2,1)}, u32[]{:S(2)}, u32[]{:S(2)}) collective-permute-start(bf16[256,2048]{0,1:T(8,128)(2,1)S(1)} %convolution_convert_fusion.6), channel_id=1, source_target_pairs={{0,2},{1,3},{2,0},{3,1},{4,6},{5,7},{6,4},{7,5},{8,10},{9,11},{10,... | collective-permute-start | bytes 3145736 | tf_op jit(solution)/shard_map/ppermute | solution.py:256
  159.2 12.0 collective-permute-done.25
  209.3 7.2 fusion.639
  291.0 167.3 %while.73 = (s32[]{:T(128)}, f32[12,64,256]{2,1,0:T(8,128)S(1)}, f32[4,256,12,64]{1,0,3,2:T(4,128)}, f32[4,12,64,256]{3,2,1,0:T(8,128)}, f32[4,256,12]{1,2,0:T(8...) while((s32[]{:T(128)}, f32[12,64,256]{2,1,0:T(8,128)S(1)}, ...), condition=%wide.region_9.10_spmd.clone, body=%wide.region_6.9_spmd.clone.sunk | while | flops 356987968 | bytes 25242344 | solution.py:144
  308.7 17.9 %dynamic_update_slice.281 = f32[4,256,12,64]{1,0,3,2:T(4,128)} dynamic-update-slice(f32[4,256,12,64]{1,0,3,2:T(4,128)} %get-tuple-element.2027, f32[1,256,12,64]{1,0,3,2:T(1,128)S(1)} %copy.724, s32[]{:T(128)} %get-tuple-element.2025, s32[]{:T(128)} %constant.367.clone.1..sunk, s32[]{:T(128)} %constant.367.clone.1..sunk, s32[]{:T(128)} %constant.367.clone.1..sunk) | dynamic-update-slice | bytes 1572868 | tf_op jit(solution)/shard_map/jvp()/while/body/jit(dynamic_update_index_in_dim)/dynamic_update_slice | solution.py:144
  350.6 17.9 %dynamic_update_slice.281 = f32[4,256,12,64]{1,0,3,2:T(4,128)} dynamic-update-slice(f32[4,256,12,64]{1,0,3,2:T(4,128)} %get-tuple-element.2027, f32[1,256,12,64]{1,0,3,2:T(1,128)S(1)} %copy.724, s32[]{:T(128)} %get-tuple-element.2025, s32[]{:T(128)} %constant.367.clone.1..sunk, s32[]{:T(128)} %constant.367.clone.1..sunk, s32[]{:T(128)} %constant.367.clone.1..sunk) | dynamic-update-slice | bytes 1572868 | tf_op jit(solution)/shard_map/jvp()/while/body/jit(dynamic_update_index_in_dim)/dynamic_update_slice | solution.py:144
  392.4 17.9 %dynamic_update_slice.281 = f32[4,256,12,64]{1,0,3,2:T(4,128)} dynamic-update-slice(f32[4,256,12,64]{1,0,3,2:T(4,128)} %get-tuple-element.2027, f32[1,256,12,64]{1,0,3,2:T(1,128)S(1)} %copy.724, s32[]{:T(128)} %get-tuple-element.2025, s32[]{:T(128)} %constant.367.clone.1..sunk, s32[]{:T(128)} %constant.367.clone.1..sunk, s32[]{:T(128)} %constant.367.clone.1..sunk) | dynamic-update-slice | bytes 1572868 | tf_op jit(solution)/shard_map/jvp()/while/body/jit(dynamic_update_index_in_dim)/dynamic_update_slice | solution.py:144
  434.2 17.9 %dynamic_update_slice.281 = f32[4,256,12,64]{1,0,3,2:T(4,128)} dynamic-update-slice(f32[4,256,12,64]{1,0,3,2:T(4,128)} %get-tuple-element.2027, f32[1,256,12,64]{1,0,3,2:T(1,128)S(1)} %copy.724, s32[]{:T(128)} %get-tuple-element.2025, s32[]{:T(128)} %constant.367.clone.1..sunk, s32[]{:T(128)} %constant.367.clone.1..sunk, s32[]{:T(128)} %constant.367.clone.1..sunk) | dynamic-update-slice | bytes 1572868 | tf_op jit(solution)/shard_map/jvp()/while/body/jit(dynamic_update_index_in_dim)/dynamic_update_slice | solution.py:144
  463.2 13.8 %while.72 = (s32[]{:T(128)}, bf16[2,512,2,128]{3,1,2,0:T(8,128)(2,1)S(1)}, s32[2,512]{1,0:T(2,128)S(1)}, s32[1,1024]{1,0:T(1,128)S(1)}, s32[2,512]{1,0:T(2,128)S...) while((s32[]{:T(128)}, ...), condition=%wide.region_13.14_spmd.clone, body=%wide.region_10.13_spmd.clone.sunk | while | flops 551027712 | bytes 27292260 | solution.py:166
  512.9 16.9 %collective-permute-done.9 = bf16[256,1152]{0,1:T(8,128)(2,1)S(1)} collective-permute-done((bf16[256,1152]{0,1:T(8,128)(2,1)S(1)}, bf16[256,1152]{0,1:T(8,128)(2,1)S(1)}, u32[]{:S(2)}, u32[]{:S(2)}) %collective-permute-start.9) | collective-permute-done | bytes 589856 | tf_op jit(solution)/shard_map/ppermute | solution.py:256
  648.7 16.4 %collective-permute-done.19 = bf16[256,1152]{0,1:T(8,128)(2,1)S(1)} collective-permute-done((bf16[256,1152]{0,1:T(8,128)(2,1)S(1)}, bf16[256,1152]{0,1:T(8,128)(2,1)S(1)}, u32[]{:S(2)}, u32[]{:S(2)}) %collective-permute-start.19) | collective-permute-done | bytes 589856 | tf_op jit(solution)/shard_map/ppermute | solution.py:256
  702.4 12.9 collective-permute-done.35
  756.1 49.0 %while.75 = (s32[]{:T(128)}, f32[1024,2,128]{2,0,1:T(8,128)}, f32[1024,2,128]{0,2,1:T(8,128)}, f32[2,512,2,128]{3,1,0,2:T(8,128)}, bf16[2,512,2,128]{3,1,2,0:T(8...) while((s32[]{:T(128)}, f32[1024,2,128]{2,0,1:T(8,128)}, ...), condition=%wide.region_38.39_spmd.clone, body=%wide.region_32.38_spmd.clone.sunk | while | flops 1386741760 | bytes 132235656 | solution.py:166
  844.0 242.3 %while.74 = (s32[]{:T(128)}, f32[12,64,256]{2,1,0:T(8,128)S(1)}, f32[4,256,12,64]{1,0,3,2:T(4,128)}, f32[4,256,12]{1,2,0:T(8,128)}, f32[4,256,12]{1,2,0:T(8,128)...) while((s32[]{:T(128)}, f32[12,64,256]{2,1,0:T(8,128)S(1)}, ...), condition=%wide.region_31.32_spmd.clone, body=%wide.region_16.31_spmd.clone.sunk | while | flops 740622464 | bytes 54521716 | solution.py:144
  884.5 17.9 %dynamic_update_slice.285 = f32[4,256,12,64]{1,0,3,2:T(4,128)} dynamic-update-slice(f32[4,256,12,64]{1,0,3,2:T(4,128)} %get-tuple-element.2104, f32[1,256,12,64]{1,0,3,2:T(1,128)S(1)} %copy.732, s32[]{:T(128)S(6)} %sub.576, s32[]{:T(128)} %constant.367.clone.1..sunk.1, s32[]{:T(128)} %constant.367.clone.1..sunk.1, s32[]{:T(128)} %constant.367.clone.1..sunk.1) | dynamic-update-slice | bytes 1572868 | tf_op jit(solution)/shard_map/transpose(jvp())/while/body/jit(dynamic_update_index_in_dim)/dynamic_update_slice | solution.py:144
  945.0 17.9 %dynamic_update_slice.285 = f32[4,256,12,64]{1,0,3,2:T(4,128)} dynamic-update-slice(f32[4,256,12,64]{1,0,3,2:T(4,128)} %get-tuple-element.2104, f32[1,256,12,64]{1,0,3,2:T(1,128)S(1)} %copy.732, s32[]{:T(128)S(6)} %sub.576, s32[]{:T(128)} %constant.367.clone.1..sunk.1, s32[]{:T(128)} %constant.367.clone.1..sunk.1, s32[]{:T(128)} %constant.367.clone.1..sunk.1) | dynamic-update-slice | bytes 1572868 | tf_op jit(solution)/shard_map/transpose(jvp())/while/body/jit(dynamic_update_index_in_dim)/dynamic_update_slice | solution.py:144
  1005.5 17.9 %dynamic_update_slice.285 = f32[4,256,12,64]{1,0,3,2:T(4,128)} dynamic-update-slice(f32[4,256,12,64]{1,0,3,2:T(4,128)} %get-tuple-element.2104, f32[1,256,12,64]{1,0,3,2:T(1,128)S(1)} %copy.732, s32[]{:T(128)S(6)} %sub.576, s32[]{:T(128)} %constant.367.clone.1..sunk.1, s32[]{:T(128)} %constant.367.clone.1..sunk.1, s32[]{:T(128)} %constant.367.clone.1..sunk.1) | dynamic-update-slice | bytes 1572868 | tf_op jit(solution)/shard_map/transpose(jvp())/while/body/jit(dynamic_update_index_in_dim)/dynamic_update_slice | solution.py:144
  1066.0 17.9 %dynamic_update_slice.285 = f32[4,256,12,64]{1,0,3,2:T(4,128)} dynamic-update-slice(f32[4,256,12,64]{1,0,3,2:T(4,128)} %get-tuple-element.2104, f32[1,256,12,64]{1,0,3,2:T(1,128)S(1)} %copy.732, s32[]{:T(128)S(6)} %sub.576, s32[]{:T(128)} %constant.367.clone.1..sunk.1, s32[]{:T(128)} %constant.367.clone.1..sunk.1, s32[]{:T(128)} %constant.367.clone.1..sunk.1) | dynamic-update-slice | bytes 1572868 | tf_op jit(solution)/shard_map/transpose(jvp())/while/body/jit(dynamic_update_index_in_dim)/dynamic_update_slice | solution.py:144
  1199.0 19.1 %all-to-all-start.3 = ((bf16[32,9,2048]{2,1,0:T(8,128)(2,1)}), bf16[32,9,2048]{2,1,0:T(8,128)(2,1)}, u32[]{:S(2)}, u32[]{:S(2)}) async-start(bf16[32,9,2048]{2,1,0:T(8,128)(2,1)} %pad_maximum_fusion.8), calls=%async_computation.3 | async-start | bytes 4194304 | tf_op jit(solution)/shard_map/all_to_all | solution.py:403
  1243.4 33.2 %all-to-all-done.3 = bf16[32,9,2048]{2,1,0:T(8,128)(2,1)} async-done(((bf16[32,9,2048]{2,1,0:T(8,128)(2,1)}), bf16[32,9,2048]{2,1,0:T(8,128)(2,1)}, u32[]{:S(2)}, u32[]{:S(2)}) %all-to-all-start.3) | async-done | bytes 1179680 | tf_op jit(solution)/shard_map/all_to_all | solution.py:403
  1295.5 34.4 %all-to-all-done.2 = bf16[32,11,2048]{2,1,0:T(8,128)(2,1)S(1)} async-done(((bf16[32,11,2048]{2,1,0:T(8,128)(2,1)}), bf16[32,11,2048]{2,1,0:T(8,128)(2,1)S(1)}, u32[]{:S(2)}, u32[]{:S(2)}) %all-to-all-start.2) | async-done | bytes 1441824 | tf_op jit(solution)/shard_map/all_to_all | solution.py:403
  (1406 shorter events, 928.7 us)
Async XLA Ops:
  7.2 170.7 %all-gather.14.cloned.1.call-start = ((), (), s32[]{:S(2)}) async-start(), calls=%async_computation.10 | async-start | bytes 5308416 | tf_op jit(solution)/shard_map/all_gather | solution.py:373
  9.3 191.7 %all-gather.6.cloned.1.call-start = ((), (), s32[]{:S(2)}) async-start(), calls=%async_computation.6 | async-start | bytes 10616832 | tf_op jit(solution)/shard_map/all_gather | solution.py:373
  20.9 214.5 %all-gather.8.cloned.1.call-start = ((), (), s32[]{:S(2)}) async-start(), calls=%async_computation.7 | async-start | bytes 1806336 | tf_op jit(solution)/shard_map/all_gather | solution.py:373
  22.2 470.6 %all-gather.10.cloned.1.call-start = ((), (), s32[]{:S(2)}) async-start(), calls=%async_computation.8 | async-start | bytes 5308416 | tf_op jit(solution)/shard_map/all_gather | solution.py:373
  26.6 59.2 %all-to-all-start = ((bf16[32,8,2176]{2,1,0:T(8,128)(2,1)}), bf16[32,8,2176]{2,1,0:T(8,128)(2,1)S(1)}, u32[]{:S(2)}, u32[]{:S(2)}) async-start(bf16[32,8,2176]{2,1,0:T(8,128)(2,1)} %fusion.151), calls=%async_computation | async-start | bytes 2228224 | tf_op jit(solution)/shard_map/all_to_all | solution.py:403
  33.9 514.5 %all-gather.12.cloned.1.call-start = ((), (), s32[]{:S(2)}) async-start(), calls=%async_computation.9 | async-start | bytes 10027008 | tf_op jit(solution)/shard_map/all_gather | solution.py:373
  85.7 49.7 %all-to-all-start.1 = ((bf16[32,8,2048]{2,1,0:T(8,128)(2,1)}), bf16[32,8,2048]{2,1,0:T(8,128)(2,1)S(1)}, u32[]{:S(2)}, u32[]{:S(2)}) async-start(bf16[32,8,2048]{2,1,0:T(8,128)(2,1)} %fusion.197), calls=%async_computation.1 | async-start | bytes 2097152 | tf_op jit(solution)/shard_map/all_to_all | solution.py:403
  88.5 1192.9 %reduce-scatter.3.cloned.1.call-start = ((), (), s32[]{:S(2)}) async-start(), calls=%async_computation.11 | async-start | bytes 626688 | tf_op jit(solution)/shard_map/reduce_scatter | solution.py:514
  98.0 59.9 %collective-permute-start = (bf16[256,2048]{0,1:T(8,128)(2,1)}, bf16[256,2048]{0,1:T(8,128)(2,1)}, u32[]{:S(2)}, u32[]{:S(2)}) collective-permute-start(bf16[256,2048]{0,1:T(8,128)(2,1)} %multiply_convert_fusion.6), channel_id=1, source_target_pairs={{0,1},{1,0},{2,3},{3,2},{4,5},{5,4},{6,7},{7,6},{8,9},{9,8},{10,11... | collective-permute-start | bytes 3145736 | tf_op jit(solution)/shard_map/ppermute | solution.py:256
  99.7 56.9 %collective-permute-start.1 = (bf16[256,2048]{0,1:T(8,128)(2,1)}, bf16[256,2048]{0,1:T(8,128)(2,1)}, u32[]{:S(2)}, u32[]{:S(2)}) collective-permute-start(bf16[256,2048]{0,1:T(8,128)(2,1)} %multiply_convert_fusion.6), channel_id=1, source_target_pairs={{0,2},{1,3},{2,0},{3,1},{4,6},{5,7},{6,4},{7,5},{8,10},{9,11},{10,... | collective-permute-start | bytes 3145736 | tf_op jit(solution)/shard_map/ppermute | solution.py:256
  136.0 37.5 %collective-permute-start.24 = (bf16[256,2048]{0,1:T(8,128)(2,1)S(1)}, bf16[256,2048]{0,1:T(8,128)(2,1)}, u32[]{:S(2)}, u32[]{:S(2)}) collective-permute-start(bf16[256,2048]{0,1:T(8,128)(2,1)S(1)} %convolution_convert_fusion.6), channel_id=1, source_target_pairs={{0,1},{1,0},{2,3},{3,2},{4,5},{5,4},{6,7},{7,6},{8,9},{9,8},{10,11... | collective-permute-start | bytes 3145736 | tf_op jit(solution)/shard_map/ppermute | solution.py:256
  137.2 34.0 %collective-permute-start.25 = (bf16[256,2048]{0,1:T(8,128)(2,1)S(1)}, bf16[256,2048]{0,1:T(8,128)(2,1)}, u32[]{:S(2)}, u32[]{:S(2)}) collective-permute-start(bf16[256,2048]{0,1:T(8,128)(2,1)S(1)} %convolution_convert_fusion.6), channel_id=1, source_target_pairs={{0,2},{1,3},{2,0},{3,1},{4,6},{5,7},{6,4},{7,5},{8,10},{9,11},{10,... | collective-permute-start | bytes 3145736 | tf_op jit(solution)/shard_map/ppermute | solution.py:256
  157.7 68.6 %collective-permute-start.2 = (bf16[256,1024]{0,1:T(8,128)(2,1)S(1)}, bf16[256,1024]{0,1:T(8,128)(2,1)}, u32[]{:S(2)}, u32[]{:S(2)}) collective-permute-start(bf16[256,1024]{0,1:T(8,128)(2,1)S(1)} %slice.971), channel_id=1, source_target_pairs={{0,1},{1,0},{2,3},{3,2},{4,5},{5,4},{6,7},{7,6},{8,9},{9,8},{10,11... | collective-permute-start | bytes 1572872 | tf_op jit(solution)/shard_map/ppermute | solution.py:256
  159.0 67.3 %collective-permute-start.3 = (bf16[256,1024]{0,1:T(8,128)(2,1)S(1)}, bf16[256,1024]{0,1:T(8,128)(2,1)}, u32[]{:S(2)}, u32[]{:S(2)}) collective-permute-start(bf16[256,1024]{0,1:T(8,128)(2,1)S(1)} %slice.972), channel_id=1, source_target_pairs={{0,2},{1,3},{2,0},{3,1},{4,6},{5,7},{6,4},{7,5},{8,10},{9,11},{10,... | collective-permute-start | bytes 1572872 | tf_op jit(solution)/shard_map/ppermute | solution.py:256
  243.9 34.7 %collective-permute-start.4 = (bf16[1024,256]{1,0:T(8,128)(2,1)}, bf16[1024,256]{1,0:T(8,128)(2,1)}, u32[]{:S(2)}, u32[]{:S(2)}) collective-permute-start(bf16[1024,256]{1,0:T(8,128)(2,1)} %pad_maximum_fusion.22), channel_id=1, source_target_pairs={{0,1},{1,0},{2,3},{3,2},{4,5},{5,4},{6,7},{7,6},{8,9},{9,8},{10,11... | collective-permute-start | bytes 1572872 | tf_op jit(solution)/shard_map/ppermute | solution.py:256
  501.8 33.8 %collective-permute-start.8 = (bf16[256,1152]{0,1:T(8,128)(2,1)S(1)}, bf16[256,1152]{0,1:T(8,128)(2,1)S(1)}, u32[]{:S(2)}, u32[]{:S(2)}) collective-permute-start(bf16[256,1152]{0,1:T(8,128)(2,1)S(1)} %pad_maximum_fusion.13), channel_id=1, source_target_pairs={{0,1},{1,0},{2,3},{3,2},{4,5},{5,4},{6,7},{7,6},{8,9},{9,8},{10,11... | collective-permute-start | bytes 1769480 | tf_op jit(solution)/shard_map/ppermute | solution.py:256
  614.7 52.1 %collective-permute-start.31 = (bf16[256,1024]{0,1:T(8,128)(2,1)S(1)}, bf16[256,1024]{0,1:T(8,128)(2,1)S(1)}, u32[]{:S(2)}, u32[]{:S(2)}) collective-permute-start(bf16[256,1024]{0,1:T(8,128)(2,1)S(1)} %fusion.299), channel_id=1, source_target_pairs={{0,2},{1,3},{2,0},{3,1},{4,6},{5,7},{6,4},{7,5},{8,10},{9,11},{10,... | collective-permute-start | bytes 1572872 | tf_op jit(solution)/shard_map/ppermute | solution.py:256
  617.9 57.9 %collective-permute-start.28 = (bf16[256,1152]{0,1:T(8,128)(2,1)S(1)}, bf16[256,1152]{0,1:T(8,128)(2,1)S(1)}, u32[]{:S(2)}, u32[]{:S(2)}) collective-permute-start(bf16[256,1152]{0,1:T(8,128)(2,1)S(1)} %pad_maximum_fusion.17), channel_id=1, source_target_pairs={{0,1},{1,0},{2,3},{3,2},{4,5},{5,4},{6,7},{7,6},{8,9},{9,8},{10,11... | collective-permute-start | bytes 1769480 | tf_op jit(solution)/shard_map/ppermute | solution.py:256
  642.0 52.0 %collective-permute-start.18 = (bf16[256,1152]{0,1:T(8,128)(2,1)}, bf16[256,1152]{0,1:T(8,128)(2,1)}, u32[]{:S(2)}, u32[]{:S(2)}) collective-permute-start(bf16[256,1152]{0,1:T(8,128)(2,1)} %pad_maximum_fusion.15), channel_id=1, source_target_pairs={{0,1},{1,0},{2,3},{3,2},{4,5},{5,4},{6,7},{7,6},{8,9},{9,8},{10,11... | collective-permute-start | bytes 1769480 | tf_op jit(solution)/shard_map/ppermute | solution.py:256
  666.8 551.4 %collective-permute-start.21 = (bf16[256,1024]{0,1:T(8,128)(2,1)}, bf16[256,1024]{0,1:T(8,128)(2,1)}, u32[]{:S(2)}, u32[]{:S(2)}) collective-permute-start(bf16[256,1024]{0,1:T(8,128)(2,1)} %fusion.283), channel_id=1, source_target_pairs={{0,2},{1,3},{2,0},{3,1},{4,6},{5,7},{6,4},{7,5},{8,10},{9,11},{10,... | collective-permute-start | bytes 1572872 | tf_op jit(solution)/shard_map/ppermute | solution.py:256
  1180.1 38.0 %collective-permute-start.23 = (bf16[256,1024]{0,1:T(8,128)(2,1)}, bf16[256,1024]{0,1:T(8,128)(2,1)}, u32[]{:S(2)}, u32[]{:S(2)}) collective-permute-start(bf16[256,1024]{0,1:T(8,128)(2,1)} %add_convert_fusion.4), channel_id=1, source_target_pairs={{0,1},{1,0},{2,3},{3,2},{4,5},{5,4},{6,7},{7,6},{8,9},{9,8},{10,11... | collective-permute-start | bytes 1572872 | tf_op jit(solution)/shard_map/ppermute | solution.py:256
  1199.0 77.6 %all-to-all-start.3 = ((bf16[32,9,2048]{2,1,0:T(8,128)(2,1)}), bf16[32,9,2048]{2,1,0:T(8,128)(2,1)}, u32[]{:S(2)}, u32[]{:S(2)}) async-start(bf16[32,9,2048]{2,1,0:T(8,128)(2,1)} %pad_maximum_fusion.8), calls=%async_computation.3 | async-start | bytes 4194304 | tf_op jit(solution)/shard_map/all_to_all | solution.py:403
  1218.1 67.2 %reduce-scatter.5.cloned.1.call-start = ((), (), s32[]{:S(2)}) async-start(), calls=%async_computation.12 | async-start | bytes 1179648 | tf_op jit(solution)/shard_map/reduce_scatter | solution.py:514
  1276.6 53.3 %all-to-all-start.2 = ((bf16[32,11,2048]{2,1,0:T(8,128)(2,1)}), bf16[32,11,2048]{2,1,0:T(8,128)(2,1)S(1)}, u32[]{:S(2)}, u32[]{:S(2)}) async-start(bf16[32,11,2048]{2,1,0:T(8,128)(2,1)} %pad_maximum_fusion.7), calls=%async_computation.2 | async-start | bytes 4194304 | tf_op jit(solution)/shard_map/all_to_all | solution.py:403
  (276 other events, 3864.6 us)
Sparse Core Ops, SparseCore 0:
  9.6 78.6 all-gather.13
  89.9 105.6 all-gather.5
  197.3 25.1 all-gather.7
  224.0 51.6 all-gather.9
  277.2 84.5 all-gather.11
  1137.8 42.4 reduce-scatter.2
  1223.2 39.2 reduce-scatter.4

commit v2 on v1

--- a/solution.py
+++ b/solution.py
@@ -3,6 +3,8 @@
 import jax
 import jax.numpy as jnp
 from jax import lax
+from jax.experimental import pallas as pl
+from jax.experimental.pallas import tpu as pltpu
 from jax.sharding import PartitionSpec as P
 
 NH = 48
@@ -15,7 +17,6 @@
 RANK = 16
 NADAPT = 8
 SSD_BLOCK = 256
-ATT_BLOCK = 512
 DSSM = 3072
 UNIT_IN = 1030
 UNIT_FF = 512
@@ -26,11 +27,6 @@
 NEGATIVE = -1e30
 FLOAT = jnp.float32
 BFLOAT = jnp.bfloat16
-
-
-def round_value(values):
-    rounded = lax.optimization_barrier(values.astype(BFLOAT)).astype(FLOAT)
-    return values + lax.stop_gradient(rounded - values)
 
 
 def product(left, right):
@@ -78,123 +74,491 @@
     return jax.nn.silu(running)
 
 
-def rotate(vectors, position):
+VMEM_BYTES = 56 * 1024 * 1024
+LANES = 128
+
+
+def whole(shape):
+    return pl.BlockSpec(shape, lambda *_: (0,) * len(shape))
+
+
+def dot(left, right, contract):
+    return lax.dot_general(left, right, ((contract[:1], contract[1:]), ((), ())), preferred_element_type=FLOAT)
+
+
+def parts_of(values, count):
+    parts = []
+    for _ in range(count):
+        part = values.astype(BFLOAT)
+        parts.append(part)
+        values = values - part.astype(FLOAT)
+    return parts
+
+
+def running_sum(values, triangle, contract):
+    width = values.shape[1]
+    split = dot(triangle, jnp.concatenate(parts_of(values, 3), axis=1), contract)
+    return split[:, :width] + split[:, width : 2 * width] + split[:, 2 * width :]
+
+
+def head_spread(values, expand):
+    return dot(jnp.concatenate(parts_of(values, 2), axis=1), expand, (1, 0))
+
+
+def head_sum(values, expand):
+    high, low = parts_of(values, 2)
+    single = expand[:LANES]
+    return dot(high, single, (1, 1)) + dot(low, single, (1, 1))
+
+
+def silu_parts(values):
+    gate = 1.0 / (1.0 + jnp.exp(-values))
+    return values * gate, gate
+
+
+def expand_table(channels):
+    row = lax.broadcasted_iota(jnp.int32, (2 * LANES, channels), 0) % LANES
+    channel = lax.broadcasted_iota(jnp.int32, (2 * LANES, channels), 1) // HP
+    return (row == channel).astype(BFLOAT)
+
+
+def scan_block(gate_ref, conv_ref, before_ref, step_ref, write_ref, read_ref, meta_ref, segment_ref, taps_ref, head_ref):
+    rows = SSD_BLOCK
+    channels = conv_ref.shape[1]
+    meta = meta_ref[...]
+    current = conv_ref[...].astype(FLOAT)
+    window = jnp.concatenate([before_ref[8:16, :].astype(FLOAT), current], axis=0)
+    summed = taps_ref[KCONV : KCONV + 1, :] + current * taps_ref[0:1, :]
+    for lag in range(1, KCONV):
+        shifted = window[8 - lag : 8 - lag + rows]
+        summed = summed + jnp.where(meta[:, 1:2] >= lag, shifted, 0.0) * taps_ref[lag : lag + 1, :]
+    activated, conv_gate = silu_parts(summed)
+    inputs = activated.astype(BFLOAT)
+    wide_inputs = inputs.astype(FLOAT)
+    raw = step_ref[...].astype(FLOAT) + head_ref[0:1, :]
+    steps = jnp.maximum(raw, 0.0) + jnp.log1p(jnp.exp(-jnp.abs(raw)))
+    row = lax.broadcasted_iota(jnp.int32, (rows, rows), 0)
+    column = lax.broadcasted_iota(jnp.int32, (rows, rows), 1)
+    triangle = (row >= column).astype(BFLOAT)
+    total = running_sum(steps * head_ref[1:2, :], triangle, (1, 0))
+    entered = jnp.exp(total) * meta[:, 3:4]
+    leaving = jnp.exp(total[rows - 1 : rows] - total) * meta[:, 4:5]
+    expand = expand_table(channels)
+    spread = head_spread(jnp.concatenate([steps, entered, leaving * steps], axis=0), expand)
+    blocked = jnp.where((row >= column) & (meta[:, 0:1] == segment_ref[0:1, :]), 0.0, NEGATIVE)
+    crossing = dot(read_ref[...], write_ref[...], (1, 1))
+    return dict(
+        summed=summed,
+        conv_gate=conv_gate,
+        wide_inputs=wide_inputs,
+        raw=raw,
+        steps=steps,
+        triangle=triangle,
+        total=total,
+        total_rows=total.T,
+        leaving=leaving,
+        expand=expand,
+        steps_wide=spread[:rows],
+        entered_wide=spread[rows : 2 * rows],
+        tail_wide=spread[2 * rows :],
+        stepped=(wide_inputs * spread[:rows]).astype(BFLOAT),
+        tailed=(wide_inputs * spread[2 * rows :]).astype(BFLOAT),
+        blocked=blocked,
+        crossing=crossing,
+    )
+
+
+def decay_of(block, head):
+    return jnp.exp(
+        block["total"][:, head : head + 1] - block["total_rows"][head : head + 1, :] + block["blocked"]
+    )
+
+
+def scan_forward_kernel(
+    gate_ref, conv_ref, before_ref, step_ref, write_ref, read_ref, meta_ref, segment_ref, taps_ref, head_ref,
+    skip_ref, out_ref, scanned_ref, states_ref, state,
+):
+    @pl.when(pl.program_id(0) == 0)
+    def _():
+        state[...] = jnp.zeros_like(state)
+
+    block = scan_block(
+        gate_ref, conv_ref, before_ref, step_ref, write_ref, read_ref, meta_ref, segment_ref, taps_ref, head_ref
+    )
+    heads = conv_ref.shape[1] // HP
+    carried = state[...].astype(BFLOAT)
+    states_ref[0] = carried
+    across = dot(read_ref[...], carried, (1, 0)) * block["entered_wide"]
+    within = []
+    for head in range(heads):
+        weights = (block["crossing"] * decay_of(block, head)).astype(BFLOAT)
+        within.append(dot(weights, block["stepped"][:, head * HP : (head + 1) * HP], (1, 0)))
+    scanned = across + jnp.concatenate(within, axis=1)
+    scanned_ref[...] = scanned
+    gated, _ = silu_parts(gate_ref[...].astype(FLOAT))
+    out_ref[...] = ((scanned + skip_ref[0:1, :] * block["wide_inputs"]) * gated).astype(BFLOAT)
+    state[...] = state[...] * block["entered_wide"][SSD_BLOCK - 1 : SSD_BLOCK, :] + dot(
+        write_ref[...], block["tailed"], (0, 0)
+    )
+
+
+def scan_backward_kernel(
+    gate_ref, conv_ref, before_ref, step_ref, write_ref, read_ref, meta_ref, segment_ref, taps_ref, head_ref,
+    skip_ref, scanned_ref, states_ref, grad_ref, query_grad_ref, out_ref, shared_ref, state_grad, later,
+):
+    @pl.when(pl.program_id(0) == 0)
+    def _():
+        state_grad[...] = jnp.zeros_like(state_grad)
+        later[...] = jnp.zeros_like(later)
+
+    block = scan_block(
+        gate_ref, conv_ref, before_ref, step_ref, write_ref, read_ref, meta_ref, segment_ref, taps_ref, head_ref
+    )
+    rows = SSD_BLOCK
+    channels = conv_ref.shape[1]
+    heads = channels // HP
+    meta = meta_ref[...]
+    read, write = read_ref[...], write_ref[...]
+    inputs = block["wide_inputs"]
+    scanned = scanned_ref[...]
+    skip = skip_ref[0:1, :]
+    gate_values = gate_ref[...].astype(FLOAT)
+    gated, gate = silu_parts(gate_values)
+    grad = grad_ref[...].astype(FLOAT)
+    gate_grad = grad * (scanned + skip * inputs) * (gate * (1.0 + gate_values * (1.0 - gate)))
+    out_grad = grad * gated
+    inputs_grad = skip * out_grad
+    rounded = out_grad.astype(BFLOAT)
+    wide_rounded = rounded.astype(FLOAT)
+    carried = states_ref[0]
+    after = state_grad[...]
+    after_rounded = after.astype(BFLOAT)
+
+    from_state = dot(write, after_rounded, (1, 0))
+    entering = (wide_rounded * block["entered_wide"]).astype(BFLOAT)
+    write_grad = dot(block["tailed"], after_rounded, (1, 1))
+    read_grad = dot(entering, carried, (1, 1))
+    last_entered = block["entered_wide"][rows - 1 : rows, :]
+    through = jnp.sum(after * carried.astype(FLOAT), axis=0, keepdims=True) * last_entered
+    state_grad[...] = after * last_entered + dot(read, entering, (0, 0))
+
+    crossing_grad = jnp.zeros((rows, rows), FLOAT)
+    pulled = []
+    for head in range(heads):
+        span = slice(head * HP, (head + 1) * HP)
+        decay = decay_of(block, head)
+        weights = (block["crossing"] * decay).astype(BFLOAT)
+        pulled.append(dot(weights, rounded[:, span], (0, 0)))
+        crossing_grad = crossing_grad + dot(rounded[:, span], block["stepped"][:, span], (1, 1)) * decay
+    pulled = jnp.concatenate(pulled, axis=1)
+    crossing_rounded = crossing_grad.astype(BFLOAT)
+    read_grad = read_grad + dot(crossing_rounded, write, (1, 0))
+    write_grad = write_grad + dot(crossing_rounded, read, (0, 0))
+    shared_ref[:, :NSTATE] = write_grad.astype(BFLOAT)
+    shared_ref[:, NSTATE:] = read_grad.astype(BFLOAT)
+
+    inputs_grad = inputs_grad + block["steps_wide"] * pulled + block["tail_wide"] * from_state
+    sums = head_sum(
+        jnp.concatenate(
+            [
+                wide_rounded * scanned - block["stepped"].astype(FLOAT) * pulled,
+                inputs * pulled,
+                inputs * from_state,
+                jnp.broadcast_to(through, (8, channels)),
+            ],
+            axis=0,
+        ),
+        block["expand"],
+    )
+    leaving_grad = sums[2 * rows : 3 * rows] * block["leaving"]
+    leaving_total = leaving_grad * block["steps"]
+    last = sums[3 * rows : 3 * rows + 1] + jnp.sum(leaving_total, axis=0, keepdims=True)
+    total_grad = sums[:rows] - leaving_total
+    total_grad = total_grad + jnp.where(
+        lax.broadcasted_iota(jnp.int32, total_grad.shape, 0) == rows - 1, last, 0.0
+    )
+    decay_grad = running_sum(total_grad, block["triangle"], (0, 0))
+    steps_grad = sums[rows : 2 * rows] + leaving_grad + decay_grad * head_ref[1:2, :]
+    raw_grad = steps_grad / (1.0 + jnp.exp(-block["raw"]))
+    raw_grad = jnp.where(lax.broadcasted_iota(jnp.int32, raw_grad.shape, 1) < heads, raw_grad, 0.0)
+
+    summed, conv_gate = block["summed"], block["conv_gate"]
+    summed_grad = inputs_grad * (conv_gate * (1.0 + summed * (1.0 - conv_gate)))
+    window = jnp.concatenate([summed_grad, later[...]], axis=0)
+    conv_grad = summed_grad * taps_ref[0:1, :]
+    for lag in range(1, KCONV):
+        conv_grad = conv_grad + jnp.where(meta[:, 2:3] >= lag, window[lag : lag + rows], 0.0) * taps_ref[lag : lag + 1, :]
+    later[...] = summed_grad[:8]
+
+    out_ref[:, :channels] = gate_grad.astype(BFLOAT)
+    out_ref[:, channels : 2 * channels] = conv_grad.astype(BFLOAT)
+    query_width = query_grad_ref.shape[1]
+    out_ref[:, 2 * channels : 2 * channels + query_width] = query_grad_ref[...]
+    rest = out_ref.shape[1] - LANES
+    out_ref[:, 2 * channels + query_width : rest] = jnp.zeros((rows, rest - 2 * channels - query_width), BFLOAT)
+    out_ref[:, rest:] = raw_grad.astype(BFLOAT)
+
+
+def scan_specs(tokens, channels, width, order):
+    half = SSD_BLOCK // 16
+    return [
+        pl.BlockSpec((SSD_BLOCK, channels), lambda i: (order(i), 0)),
+        pl.BlockSpec((SSD_BLOCK, channels), lambda i: (order(i), 1)),
+        pl.BlockSpec((16, channels), lambda i: (jnp.maximum(order(i) * half - 1, 0), 1)),
+        pl.BlockSpec((SSD_BLOCK, LANES), lambda i: (order(i), width // LANES - 1)),
+        pl.BlockSpec((SSD_BLOCK, NSTATE), lambda i: (order(i), 0)),
+        pl.BlockSpec((SSD_BLOCK, NSTATE), lambda i: (order(i), 1)),
+        pl.BlockSpec((SSD_BLOCK, LANES), lambda i: (order(i), 0)),
+        pl.BlockSpec((8, SSD_BLOCK), lambda i: (0, order(i))),
+        whole((8, channels)),
+        whole((8, LANES)),
+        whole((8, channels)),
+    ]
+
+
+def scan_cost(tokens, channels, factor):
+    heads = channels // HP
+    return pl.CostEstimate(
+        flops=factor * 2 * tokens * SSD_BLOCK * (3 * channels + NSTATE),
+        bytes_accessed=factor * tokens * channels * 12,
+        transcendentals=tokens * SSD_BLOCK * heads,
+    )
+
+
+def scan_forward(projected, states, tables):
+    tokens, width = projected.shape
+    channels = tables["taps"].shape[1]
+    blocks = tokens // SSD_BLOCK
+    order = lambda i: i
+    return pl.pallas_call(
+        scan_forward_kernel,
+        grid=(blocks,),
+        in_specs=scan_specs(tokens, channels, width, order),
+        out_specs=[
+            pl.BlockSpec((SSD_BLOCK, channels), lambda i: (i, 0)),
+            pl.BlockSpec((SSD_BLOCK, channels), lambda i: (i, 0)),
+            pl.BlockSpec((1, NSTATE, channels), lambda i: (i, 0, 0)),
+        ],
+        out_shape=[
+            jax.ShapeDtypeStruct((tokens, channels), BFLOAT),
+            jax.ShapeDtypeStruct((tokens, channels), FLOAT),
+            jax.ShapeDtypeStruct((blocks, NSTATE, channels), BFLOAT),
+        ],
+        scratch_shapes=[pltpu.VMEM((NSTATE, channels), FLOAT)],
+        compiler_params=pltpu.CompilerParams(vmem_limit_bytes=VMEM_BYTES),
+        cost_estimate=scan_cost(tokens, channels, 1),
+        name="scan_forward",
+    )(
+        projected, projected, projected, projected, states, states,
+        tables["meta"], tables["segment_row"], tables["taps"], tables["head"], tables["skip"],
+    )
+
+
+def scan_backward(projected, states, tables, scanned, carried, mixed_grad, query_grad):
+    tokens, width = projected.shape
+    channels = tables["taps"].shape[1]
+    blocks = tokens // SSD_BLOCK
+    order = lambda i: blocks - 1 - i
+    back = lambda i: (blocks - 1 - i, 0)
+    return pl.pallas_call(
+        scan_backward_kernel,
+        grid=(blocks,),
+        in_specs=scan_specs(tokens, channels, width, order)
+        + [
+            pl.BlockSpec((SSD_BLOCK, channels), back),
+            pl.BlockSpec((1, NSTATE, channels), lambda i: (blocks - 1 - i, 0, 0)),
+            pl.BlockSpec((SSD_BLOCK, channels), back),
+            pl.BlockSpec((SSD_BLOCK, query_grad.shape[1]), back),
+        ],
+        out_specs=[
+            pl.BlockSpec((SSD_BLOCK, width), back),
+            pl.BlockSpec((SSD_BLOCK, 2 * NSTATE), back),
+        ],
+        out_shape=[
+            jax.ShapeDtypeStruct((tokens, width), BFLOAT),
+            jax.ShapeDtypeStruct((tokens, 2 * NSTATE), BFLOAT),
+        ],
+        scratch_shapes=[pltpu.VMEM((NSTATE, channels), FLOAT), pltpu.VMEM((8, channels), FLOAT)],
+        compiler_params=pltpu.CompilerParams(vmem_limit_bytes=VMEM_BYTES),
+        cost_estimate=scan_cost(tokens, channels, 2),
+        name="scan_backward",
+    )(
+        projected, projected, projected, projected, states, states,
+        tables["meta"], tables["segment_row"], tables["taps"], tables["head"], tables["skip"],
+        scanned, carried, mixed_grad, query_grad,
+    )
+
+
+def turned(values, cosine, sine):
+    return (values * cosine + pltpu.roll(values, HEAD_SIZE // 2, 1) * sine).astype(BFLOAT)
+
+
+def turned_back(values, cosine, sine):
+    return values * cosine + pltpu.roll(values * sine, HEAD_SIZE // 2, 1)
+
+
+ATT_ROWS = 256
+
+
+def attention_mask(meta_ref, segment_ref, start, extent):
+    row = start + lax.broadcasted_iota(jnp.int32, (ATT_ROWS, extent), 0)
+    column = lax.broadcasted_iota(jnp.int32, (ATT_ROWS, extent), 1)
+    return (row >= column) & (meta_ref[start : start + ATT_ROWS, 0:1] == segment_ref[0:1, :extent])
+
+
+def probabilities(query, keys, allowed):
+    score = dot(query, keys, (1, 1)) * (1.0 / math.sqrt(HEAD_SIZE))
+    score = jnp.where(allowed, score, NEGATIVE)
+    exponent = jnp.exp(score - jnp.max(score, axis=1, keepdims=True))
+    return exponent / jnp.sum(exponent, axis=1, keepdims=True)
+
+
+def attention_forward_kernel(query_ref, key_ref, value_ref, cosine_ref, sine_ref, meta_ref, segment_ref, out_ref, keys):
+    tokens = key_ref.shape[0]
+    keys[...] = turned(key_ref[...].astype(FLOAT), cosine_ref[...], sine_ref[...])
+    for start in range(0, tokens, ATT_ROWS):
+        extent = start + ATT_ROWS
+        here = slice(start, extent)
+        allowed = attention_mask(meta_ref, segment_ref, start, extent)
+        for unit in range(query_ref.shape[1] // HEAD_SIZE):
+            span = slice(unit * HEAD_SIZE, (unit + 1) * HEAD_SIZE)
+            query = turned(query_ref[here, span].astype(FLOAT), cosine_ref[here], sine_ref[here])
+            weights = probabilities(query, keys[:extent], allowed).astype(BFLOAT)
+            out_ref[here, span] = dot(weights, value_ref[:extent], (1, 0)).astype(BFLOAT)
+
+
+def attention_backward_kernel(
+    query_ref, key_ref, value_ref, cosine_ref, sine_ref, meta_ref, segment_ref, grad_ref,
+    query_grad_ref, key_grad_ref, value_grad_ref, keys, key_sum, value_sum,
+):
+    tokens = key_ref.shape[0]
+    scale = 1.0 / math.sqrt(HEAD_SIZE)
+    keys[...] = turned(key_ref[...].astype(FLOAT), cosine_ref[...], sine_ref[...])
+    key_sum[...] = jnp.zeros_like(key_sum)
+    value_sum[...] = jnp.zeros_like(value_sum)
+    for start in range(0, tokens, ATT_ROWS):
+        extent = start + ATT_ROWS
+        here = slice(start, extent)
+        allowed = attention_mask(meta_ref, segment_ref, start, extent)
+        for unit in range(query_ref.shape[1] // HEAD_SIZE):
+            span = slice(unit * HEAD_SIZE, (unit + 1) * HEAD_SIZE)
+            query = turned(query_ref[here, span].astype(FLOAT), cosine_ref[here], sine_ref[here])
+            weights = probabilities(query, keys[:extent], allowed)
+            grad = grad_ref[here, span]
+            weights_grad = dot(grad, value_ref[:extent], (1, 1))
+            value_sum[:extent] += dot(weights.astype(BFLOAT), grad, (0, 0))
+            mean_grad = jnp.sum(weights * weights_grad, axis=1, keepdims=True)
+            score_grad = (weights * (weights_grad - mean_grad) * scale).astype(BFLOAT)
+            query_grad = dot(score_grad, keys[:extent], (1, 0))
+            key_sum[:extent] += dot(score_grad, query, (0, 0))
+            query_grad_ref[here, span] = turned_back(query_grad, cosine_ref[here], sine_ref[here]).astype(BFLOAT)
+    key_grad_ref[...] = turned_back(key_sum[...], cosine_ref[...], sine_ref[...]).astype(BFLOAT)
+    value_grad_ref[...] = value_sum[...].astype(BFLOAT)
+
+
+def attention_cost(tokens, width, factor):
+    return pl.CostEstimate(
+        flops=factor * 2 * tokens * tokens * width,
+        bytes_accessed=factor * tokens * width * 8,
+        transcendentals=tokens * tokens * width // (2 * HEAD_SIZE),
+    )
+
+
+def attention_specs(projected, channels, units):
+    tokens = projected.shape[0]
+    query_width = units * HEAD_SIZE
+    narrow = whole((tokens, HEAD_SIZE))
+    return [
+        pl.BlockSpec((tokens, query_width), lambda *_: (0, 2 * channels // query_width)),
+        narrow,
+        narrow,
+        narrow,
+        narrow,
+        whole((tokens, LANES)),
+        whole((8, tokens)),
+    ]
+
+
+def attention_forward(projected, keys, values, tables):
+    tokens = projected.shape[0]
+    channels = tables["taps"].shape[1]
+    units = channels // (DSSM // QUERY_HEADS)
+    width = units * HEAD_SIZE
+    return pl.pallas_call(
+        attention_forward_kernel,
+        grid=(1,),
+        in_specs=attention_specs(projected, channels, units),
+        out_specs=whole((tokens, width)),
+        out_shape=jax.ShapeDtypeStruct((tokens, width), BFLOAT),
+        scratch_shapes=[pltpu.VMEM((tokens, HEAD_SIZE), BFLOAT)],
+        compiler_params=pltpu.CompilerParams(vmem_limit_bytes=VMEM_BYTES),
+        cost_estimate=attention_cost(tokens, width, 1),
+        name="attention_forward",
+    )(projected, keys, values, tables["cosine"], tables["sine"], tables["meta"], tables["segment_row"])
+
+
+def attention_backward(projected, keys, values, tables, mixed_grad):
+    tokens = projected.shape[0]
+    channels = tables["taps"].shape[1]
+    units = channels // (DSSM // QUERY_HEADS)
+    width = units * HEAD_SIZE
+    narrow = whole((tokens, HEAD_SIZE))
+    return pl.pallas_call(
+        attention_backward_kernel,
+        grid=(1,),
+        in_specs=attention_specs(projected, channels, units)
+        + [pl.BlockSpec((tokens, width), lambda *_: (0, channels // width))],
+        out_specs=[whole((tokens, width)), narrow, narrow],
+        out_shape=[
+            jax.ShapeDtypeStruct((tokens, width), BFLOAT),
+            jax.ShapeDtypeStruct((tokens, HEAD_SIZE), BFLOAT),
+            jax.ShapeDtypeStruct((tokens, HEAD_SIZE), BFLOAT),
+        ],
+        scratch_shapes=[
+            pltpu.VMEM((tokens, HEAD_SIZE), BFLOAT),
+            pltpu.VMEM((tokens, HEAD_SIZE), FLOAT),
+            pltpu.VMEM((tokens, HEAD_SIZE), FLOAT),
+        ],
+        compiler_params=pltpu.CompilerParams(vmem_limit_bytes=VMEM_BYTES),
+        cost_estimate=attention_cost(tokens, width, 3),
+        name="attention_backward",
+    )(
+        projected, keys, values, tables["cosine"], tables["sine"], tables["meta"], tables["segment_row"], mixed_grad
+    )
+
+
+def mixer_tables(lengths, segment, position, conv_values, scan_params):
+    tokens = segment.shape[0]
+    block = jnp.arange(tokens, dtype=jnp.int32) // SSD_BLOCK
+    previous = jnp.concatenate([jnp.full((1,), -1, jnp.int32), segment[:-1]])
+    first_previous = jnp.repeat(previous[::SSD_BLOCK], SSD_BLOCK)
+    last_segment = jnp.repeat(segment[SSD_BLOCK - 1 :: SSD_BLOCK], SSD_BLOCK)
+    length = jnp.sum(
+        jnp.where(segment[:, None] == jnp.arange(lengths.shape[0], dtype=jnp.int32)[None, :], lengths[None, :], 0),
+        axis=1,
+    )
+    columns = [
+        segment,
+        position,
+        length - 1 - position,
+        segment == first_previous,
+        segment == last_segment,
+    ]
+    meta = jnp.stack([column.astype(FLOAT) for column in columns], axis=1)
     half_width = HEAD_SIZE // 2
     frequency = ROPE_BASE ** (-2.0 * jnp.arange(half_width, dtype=FLOAT) / HEAD_SIZE)
-    angle_table = position.astype(FLOAT)[:, None] * frequency[None, :]
-    cosine = jnp.cos(angle_table)[:, None, :]
-    sine_part = jnp.sin(angle_table)[:, None, :]
-    leading = vectors[..., :half_width]
-    trailing = vectors[..., half_width:]
-    return jnp.concatenate(
-        [leading * cosine - trailing * sine_part, trailing * cosine + leading * sine_part], axis=-1
-    )
-
-
-def state_scan(inputs, step_size, log_decay, write_vectors, read_vectors, segment):
-    sequence_length, head_count = step_size.shape
-    block_count = sequence_length // SSD_BLOCK
-    previous = jnp.concatenate([jnp.full((1,), -1, jnp.int32), segment[:-1]])
-    first_previous = previous.reshape(block_count, SSD_BLOCK)[:, 0]
-    inner_index = jnp.arange(SSD_BLOCK, dtype=jnp.int32)
-    lower_mask = inner_index[:, None] >= inner_index[None, :]
-
-    def scan_step(carry_state, block_data):
-        (
-            block_inputs,
-            block_steps,
-            block_decay,
-            block_write,
-            block_read,
-            block_segment,
-            block_previous,
-        ) = block_data
-        cumulative = jnp.cumsum(block_decay, axis=0)
-        intersection = contract_last(block_read, block_write)
-        allowed = lower_mask & (block_segment[:, None] == block_segment[None, :])
-        difference = cumulative[:, None, :] - cumulative[None, :, :]
-        decay_table = jnp.exp(jnp.where(allowed[:, :, None], difference, NEGATIVE))
-        weights = round_value(intersection[:, :, None] * decay_table * block_steps[None, :, :])
-        within = jnp.einsum("tsh,shp->thp", weights, block_inputs)
-        carried = (block_segment == block_previous).astype(FLOAT)
-        read_scaled = round_value(
-            block_read[:, None, :] * (jnp.exp(cumulative) * carried[:, None])[:, :, None]
-        )
-        across = jnp.einsum("thn,hpn->thp", read_scaled, round_value(carry_state))
-        tail_factor = (
-            jnp.exp(cumulative[-1][None, :] - cumulative)
-            * block_steps
-            * (block_segment == block_segment[-1]).astype(FLOAT)[:, None]
-        )
-        write_scaled = round_value(block_write[:, None, :] * tail_factor[:, :, None])
-        fresh_state = jnp.einsum("shp,shn->hpn", block_inputs, write_scaled)
-        through = jnp.exp(cumulative[-1]) * (block_segment[-1] == block_previous).astype(FLOAT)
-        return (carry_state * through[:, None, None] + fresh_state, within + across)
-
-    sliced = (
-        inputs.reshape(block_count, SSD_BLOCK, head_count, HP),
-        step_size.reshape(block_count, SSD_BLOCK, head_count),
-        log_decay.reshape(block_count, SSD_BLOCK, head_count),
-        write_vectors.reshape(block_count, SSD_BLOCK, NSTATE),
-        read_vectors.reshape(block_count, SSD_BLOCK, NSTATE),
-        segment.reshape(block_count, SSD_BLOCK),
-        first_previous,
-    )
-    zero_state = jnp.zeros((head_count, HP, NSTATE), FLOAT)
-    _, outputs = lax.scan(jax.checkpoint(scan_step), zero_state, sliced)
-    return outputs.reshape(sequence_length, head_count, HP)
-
-
-def attention(query, key_rows, value_rows, segment):
-    sequence_length, unit_count = (query.shape[0], query.shape[1])
-    block_count = sequence_length // ATT_BLOCK
-    token_index = jnp.arange(sequence_length, dtype=jnp.int32)
-    score_scale = 1.0 / math.sqrt(HEAD_SIZE)
-
-    def score_block(block_data):
-        query_block, segment_block, token_block = block_data
-        score = jnp.einsum("qud,kud->uqk", query_block, key_rows) * score_scale
-        allowed = (segment_block[:, None] == segment[None, :]) & (
-            token_index[None, :] <= token_block[:, None]
-        )
-        score = jnp.where(allowed[None], score, NEGATIVE)
-        row_max = jnp.max(score, axis=2, keepdims=True)
-        exponent = jnp.exp(score - row_max)
-        weights = round_value(exponent / jnp.sum(exponent, axis=2, keepdims=True))
-        return jnp.einsum("uqk,kud->qud", weights, value_rows)
-
-    attended = lax.map(
-        jax.checkpoint(score_block),
-        (
-            query.reshape(block_count, ATT_BLOCK, unit_count, HEAD_SIZE),
-            segment.reshape(block_count, ATT_BLOCK),
-            token_index.reshape(block_count, ATT_BLOCK),
-        ),
-    )
-    return attended.reshape(sequence_length, unit_count, HEAD_SIZE)
-
-
-def mixer_branch(gate_in, conv_in, query_in, step_in, state_values, key_in, value_in, conv_values, scan_params, segment, position):
-    rows = gate_in.shape[0]
-    head_count = step_in.shape[1]
-    unit_count = head_count * QUERY_HEADS // NH
-    scan_input = round_value(causal_conv(conv_in, conv_values, position)).reshape(rows, head_count, HP)
-    step_size = jax.nn.softplus(step_in + scan_params[0][None, :])
-    log_decay = -step_size * jnp.exp(scan_params[1])[None, :]
-    scanned = state_scan(
-        scan_input, step_size, log_decay, state_values[:, :NSTATE], state_values[:, NSTATE:], segment
-    )
-    scan_output = (scanned + scan_params[2][None, :, None] * scan_input) * jax.nn.silu(
-        gate_in.reshape(rows, head_count, HP)
-    )
-    attended = attention(
-        round_value(rotate(query_in.reshape(rows, unit_count, HEAD_SIZE), position)),
-        jnp.broadcast_to(round_value(rotate(key_in[:, None, :], position)), (rows, unit_count, HEAD_SIZE)),
-        jnp.broadcast_to(value_in[:, None, :], (rows, unit_count, HEAD_SIZE)),
-        segment,
-    )
-    return jnp.concatenate(
-        [scan_output.reshape(rows, head_count * HP), attended.reshape(rows, unit_count * HEAD_SIZE)], axis=1
+    angle = position.astype(FLOAT)[:, None] * frequency[None, :]
+    cosine, sine = jnp.cos(angle), jnp.sin(angle)
+    heads = scan_params.shape[1]
+    head = jnp.stack([scan_params[0], -jnp.exp(scan_params[1]), scan_params[2]])
+    return dict(
+        meta=jnp.pad(meta, ((0, 0), (0, LANES - meta.shape[1]))),
+        segment_row=jnp.broadcast_to(segment.astype(FLOAT)[None, :], (8, tokens)),
+        taps=jnp.pad(conv_values.astype(FLOAT), ((0, 3), (0, 0))),
+        head=jnp.pad(head, ((0, 5), (0, LANES - heads))),
+        skip=jnp.broadcast_to(jnp.repeat(scan_params[2], HP)[None, :], (8, heads * HP)),
+        cosine=jnp.concatenate([cosine, cosine], axis=1),
+        sine=jnp.concatenate([-sine, sine], axis=1),
     )
 
 
@@ -202,7 +566,6 @@
 PAIR_WIDTH = 2 * KEY_VALUE_HEADS * HEAD_SIZE // QUERY_HEADS
 STATE_WIDTH = 2 * NSTATE // QUERY_HEADS
 STEP_WIDTH = NH // QUERY_HEADS
-LANES = 128
 ALL_AXES = ("row", "col")
 
 
@@ -469,15 +832,10 @@
         *[pair_full[:, start + at * HEAD_SIZE : start + (at + 1) * HEAD_SIZE] for at in range(KEY_VALUE_HEADS)],
     )
     keys, values = pick(0), pick(KEY_VALUE_HEADS * HEAD_SIZE)
-    conv_value_float = conv_values.astype(FLOAT)
-
-    def mix_local(*parts):
-        return mixer_branch(*parts, conv_value_float, scan_params, segment, position)
-
-    mixed_float, mixer_back = jax.vjp(
-        mix_local, *[part.astype(FLOAT) for part in (gate_in, conv_in, query_in, step_in, state_full, keys, values)]
-    )
-    mixed_out = mixed_float.astype(BFLOAT)
+    tables = mixer_tables(lengths, segment, position, conv_values, scan_params)
+    scan_out, scanned, carried = scan_forward(projected, state_full, tables)
+    attended = attention_forward(projected, keys, values, tables)
+    mixed_out = jnp.concatenate([scan_out, attended], axis=1)
     branch_sum, inner_out = collect_project(mixed_out, wide_mix, narrow_mix, own_selector)
     hidden = own_input + branch_sum
     normed_two, norm_two_back = jax.vjp(lambda values: rms_norm(values, norm_gain[1]), hidden)
@@ -531,10 +889,11 @@
     grad_feed_raise = join_halves(feed_raise_part, units, UNIT_FF, 1)
     grad_down_lower = down_lower_part.T
 
-    gate_grad, conv_grad, query_grad, step_grad, state_grad, key_grad, value_grad = mixer_back(
-        mixed_grad.astype(FLOAT)
-    )
-    mine = [(key_head == at).astype(FLOAT) for at in range(KEY_VALUE_HEADS)]
+    query_grad, key_grad, value_grad = attention_backward(projected, keys, values, tables, mixed_grad)
+    projected_grad, state_grad = scan_backward(
+        projected, state_full, tables, scanned, carried, mixed_grad, query_grad
+    )
+    mine = [(key_head == at).astype(BFLOAT) for at in range(KEY_VALUE_HEADS)]
     pair_grad = jnp.concatenate([grad * here for grad in (key_grad, value_grad) for here in mine], axis=1)
     state_width = units * STATE_WIDTH
     stacked = jnp.stack(
@@ -564,10 +923,8 @@
             stacked.astype(BFLOAT).reshape(cols * total, -1), "col", scatter_dimension=0, tiled=True
         ).astype(FLOAT)
     (state_pre_grad,) = state_back(shared_grad[:, pair_width:])
-    projected_grad = jnp.concatenate(
-        [gate_grad, conv_grad, query_grad, shared_grad[:, :pair_width], state_pre_grad, step_grad], axis=1
-    ).astype(BFLOAT)
-    projected_grad = pad_columns(projected_grad, narrow_in.shape[1])
+    shared_back = jnp.concatenate([shared_grad[:, :pair_width], state_pre_grad], axis=1).astype(BFLOAT)
+    projected_grad = lax.dynamic_update_slice(projected_grad, shared_back, (0, cuts[3]))
     grad_in_raise = restore_units(sum_rows(contract_first(inner_in, projected_grad)), units)
     normed_one_grad, narrow_four = collect_project(projected_grad, wide_in, narrow_in, own_selector)
     (input_from_norm,) = norm_one_back(normed_one_grad)

time: 1360 us -> 847 us (0.62)
  local copies, waits for them, and re-layouts: 416 us -> 106 us
  matrix products: 357 us -> 209 us
  other arithmetic: 201 us -> 59.2 us
  waiting for transfers between devices: 241 us -> 318 us
  Pallas kernels: 0 us -> 56.6 us
  starting transfers between devices: 100 us -> 72.7 us
    dynamic_update_slice x16 -> x0, local copies, waits for them, and re-layouts: 149 us -> none  [state_scan(): _, outputs = lax.scan(jax.checkpoint(scan_step), zero_state, sliced)]
    dot_general x50 -> x0, matrix products: 133 us -> none  [the longest x12 44.7 us: scan_step(): within = jnp.einsum('tsh,shp->thp', weights, block_inputs)]
    pallas_call x0 -> x4, Pallas kernels: none -> 56.6 us  [the longest x1 26.1 us: scan_backward(): pl.pallas_call(scan_backward_kernel, grid=(blocks,), in_specs=scan_specs(...]
    convert_element_type x36 -> x5, other arithmetic: 47.1 us -> 0.04 us  [mixer_tables(): meta = jnp.stack([column.astype(FLOAT) for column in columns], axis=1)]
    ppermute x50, waiting for transfers between devices: 104 us -> 147 us  [flip(): return lax.ppermute(values, 'col', [(i, i ^ mask) for i in range(4)])]
    dynamic_slice x48 -> x0, local copies, waits for them, and re-layouts: 39.3 us -> none  [the longest x40 36.7 us: state_scan(): _, outputs = lax.scan(jax.checkpoint(scan_step), zero_state, sliced)]
    all_gather x5, waiting for transfers between devices: 0.03 us -> 30.8 us  [local(): gather = lambda values: lax.all_gather(values, 'row', axis=0, tiled=True)]
    reshape x14 -> x0, local copies, waits for them, and re-layouts: 25.6 us -> none  [the longest x2 7.47 us: state_scan(): inputs.reshape(block_count, SSD_BLOCK, head_count, HP)]
  transfers between devices with their start and end apart: 61 -> 61, of which waited for: 22 -> 27; matrix products, arithmetic and copies ran while one was open for 67% -> 35% of each run, Pallas kernels for 0% -> 7%
where the time goes in v2:
time: 847 us; the launch traced here: 839 us
  waiting for transfers between devices  318 us (38%)
  matrix products  209 us (25%)
  local copies, waits for them, and re-layouts  106 us (13%)
  starting transfers between devices  72.7 us (9%)
  other arithmetic  59.2 us (7%)
  Pallas kernels  56.6 us (7%)
  between operations  18.7 us (2%)
    ppermute x50, waiting for transfers between devices, flip(): return lax.ppermute(values, 'col', [(i, i ^ mask) for i in range(4)])  147 us
    all_to_all x4, waiting for transfers between devices, local(): lax.all_to_all(values, ALL_AXES, split_axis=0, concat_axis=0, tiled=True)  140 us
    dot_general x44, matrix products, product(): return jnp.dot(left, right, preferred_element_type=FLOAT)  130 us
    dot_general x51, matrix products, contract_last(): lax.dot_general(left, right, (((1,), (1,)), ((), ())), preferred_element_...  67.4 us
    ppermute x50, starting transfers between devices, flip(): return lax.ppermute(values, 'col', [(i, i ^ mask) for i in range(4)])  54.1 us
    unnamed x297, local copies, waits for them, and re-layouts  52.6 us
    all_gather x5, waiting for transfers between devices, local(): gather = lambda values: lax.all_gather(values, 'row', axis=0, tiled=True)  30.8 us
    pallas_call x1, Pallas kernels, scan_backward(): pl.pallas_call(scan_backward_kernel, grid=(blocks,), in_specs=scan_specs(...  26.1 us
  transfers between devices with their start and end apart: 61, of which 27 were waited for; matrix products, arithmetic and copies ran while one was open for 35% of the time, Pallas kernels for 7%

profile of v2, /device:TPU:0, one launch (start us, length us, event | category | flops | bytes accessed | tf_op | source)
XLA Modules:
  0.0 839.4 jit_solution(6890390925934911940)
XLA Ops:
  19.3 7.4 all-to-all-start
  40.5 39.0 %all-to-all-done = bf16[32,8,2176]{2,1,0:T(8,128)(2,1)S(1)} async-done(((bf16[32,8,2176]{2,1,0:T(8,128)(2,1)}), bf16[32,8,2176]{2,1,0:T(8,128)(2,1)S(1)}, u32[]{:S(2)}, u32[]{:S(2)}) %all-to-all-start) | async-done | bytes 1114144 | tf_op jit(solution)/shard_map/all_to_all | solution.py:766
  91.8 33.1 %all-to-all-done.1 = bf16[32,8,2048]{2,1,0:T(8,128)(2,1)S(1)} async-done(((bf16[32,8,2048]{2,1,0:T(8,128)(2,1)}), bf16[32,8,2048]{2,1,0:T(8,128)(2,1)S(1)}, u32[]{:S(2)}, u32[]{:S(2)}) %all-to-all-start.1) | async-done | bytes 1048608 | tf_op jit(solution)/shard_map/all_to_all | solution.py:766
  140.3 13.8 %collective-permute-done.25 = bf16[256,2048]{0,1:T(8,128)(2,1)S(1)} collective-permute-done((bf16[256,2048]{0,1:T(8,128)(2,1)}, bf16[256,2048]{0,1:T(8,128)(2,1)S(1)}, u32[]{:S(2)}, u32[]{:S(2)}) %collective-permute-start.25) | collective-permute-done | bytes 1048608 | tf_op jit(solution)/shard_map/ppermute | solution.py:619
  175.5 14.4 %all-gather.6.cloned.1.call-done = bf16[2048,2304]{0,1:T(8,128)(2,1)} async-done(((bf16[256,2304]{0,1:T(8,128)(2,1)}), bf16[2048,2304]{0,1:T(8,128)(2,1)}) %all-gather.6.cloned.1.call-update) | async-done | bytes 9437200 | tf_op jit(solution)/shard_map/all_gather | solution.py:736
  189.9 6.7 fusion.468
  198.1 7.1 fusion.469
  206.7 6.7 fusion.470
  215.1 6.7 fusion.188
  260.1 6.9 attention_forward.1
  268.7 13.5 %scan_forward.1 = (bf16[1024,768]{1,0:T(8,128)(2,1)}, f32[1024,768]{1,0:T(8,128)}, bf16[4,256,768]{2,1,0:T(8,128)(2,1)}) custom-call(bf16[1024,2176]{1,0:T(8,128)(2,1)} %copy-done.2, bf16[1024,2176]{1,0:T(8,128)(2,1)} %copy-done.2, bf16[1024,2176]{1,0:T(8,128)(2,1)} %copy-done.2, bf16[1024,2176]{1,0:T(8,128)(2,1)} %copy-done.2, ...), custom_call_target="tpu_custom_call" | custom-call | flops 1342177280 | bytes 9437184 | tf_op jit(solution)/shard_map/scan_forward/pallas_call | solution.py:333
  305.2 17.6 %collective-permute-done.9 = bf16[256,1152]{0,1:T(8,128)(2,1)S(1)} collective-permute-done((bf16[256,1152]{0,1:T(8,128)(2,1)S(1)}, bf16[256,1152]{0,1:T(8,128)(2,1)S(1)}, u32[]{:S(2)}, u32[]{:S(2)}) %collective-permute-start.9) | collective-permute-done | bytes 589856 | tf_op jit(solution)/shard_map/ppermute | solution.py:619
  339.6 16.5 %all-gather.12.cloned.1.call-done = bf16[2048,2176]{1,0:T(8,128)(2,1)} async-done(((bf16[256,2176]{1,0:T(8,128)(2,1)}), bf16[2048,2176]{1,0:T(8,128)(2,1)}) %all-gather.12.cloned.1.call-update) | async-done | bytes 8912912 | tf_op jit(solution)/shard_map/all_gather | solution.py:736
  356.0 6.7 fusion.471
  367.6 8.0 fusion.472
  465.5 19.8 %collective-permute-done.33 = bf16[256,1024]{0,1:T(8,128)(2,1)S(1)} collective-permute-done((bf16[256,1024]{0,1:T(8,128)(2,1)S(1)}, bf16[256,1024]{0,1:T(8,128)(2,1)S(1)}, u32[]{:S(2)}, u32[]{:S(2)}) %collective-permute-start.33) | collective-permute-done | bytes 524320 | tf_op jit(solution)/shard_map/ppermute | solution.py:619
  500.9 16.4 %collective-permute-done.35 = bf16[256,2048]{0,1:T(8,128)(2,1)} collective-permute-done((bf16[256,2048]{0,1:T(8,128)(2,1)}, bf16[256,2048]{0,1:T(8,128)(2,1)}, u32[]{:S(2)}, u32[]{:S(2)}) %collective-permute-start.35) | collective-permute-done | bytes 1048608 | tf_op jit(solution)/shard_map/ppermute | solution.py:619
  554.1 10.1 %attention_backward.1 = (bf16[1024,256]{1,0:T(8,128)(2,1)}, bf16[1024,128]{1,0:T(8,128)(2,1)}, bf16[1024,128]{1,0:T(8,128)(2,1)}) custom-call(bf16[1024,2176]{1,0:T(8,128)(2,1)} %copy-done.2, bf16[1024,128]{1,0:T(8,128)(2,1)} %get-tuple-element.86.key_ref, bf16[1024,128]{1,0:T(8,128)(2,1)} %get-tuple-element.85.value_ref, ...), custom_call_target="tpu_custom_call" | custom-call | flops 1610612736 | bytes 6291456 | tf_op jit(solution)/shard_map/attention_backward/pallas_call | solution.py:506
  564.1 26.1 %scan_backward.1 = (bf16[1024,2176]{1,0:T(8,128)(2,1)}, bf16[1024,512]{1,0:T(8,128)(2,1)}) custom-call(bf16[1024,2176]{1,0:T(8,128)(2,1)} %copy-done.2, bf16[1024,2176]{1,0:T(8,128)(2,1)} %copy-done.2, bf16[1024,2176]{1,0:T(8,128)(2,1)} %copy-done.2, bf16[1024,2176]{1,0:T(8,128)(2,1)} %copy-done.2, bf16[1024,512]{1,0:T(8,128)(2,1)} %pad_maximum_fusion.11.write_ref.read_ref, ...), custom_call_target="tpu_custom_call" | custom-call | flops 2684354560 | bytes 18874368 | tf_op jit(solution)/shard_map/scan_backward/pallas_call | solution.py:363
  605.4 11.3 %collective-permute-done.42 = bf16[512,256]{1,0:T(8,128)(2,1)S(1)} collective-permute-done((bf16[512,256]{1,0:T(8,128)(2,1)S(1)}, bf16[512,256]{1,0:T(8,128)(2,1)S(1)}, u32[]{:S(2)}, u32[]{:S(2)}) %collective-permute-start.42) | collective-permute-done | bytes 262176 | tf_op jit(solution)/shard_map/ppermute | solution.py:619
  625.9 7.1 collective-permute-done.41
  666.7 17.2 %collective-permute-done.45 = bf16[256,1152]{0,1:T(8,128)(2,1)S(1)} collective-permute-done((bf16[256,1152]{0,1:T(8,128)(2,1)S(1)}, bf16[256,1152]{0,1:T(8,128)(2,1)S(1)}, u32[]{:S(2)}, u32[]{:S(2)}) %collective-permute-start.45) | collective-permute-done | bytes 589856 | tf_op jit(solution)/shard_map/ppermute | solution.py:619
  735.6 33.8 %all-to-all-done.3 = bf16[32,9,2048]{2,1,0:T(8,128)(2,1)} async-done(((bf16[32,9,2048]{2,1,0:T(8,128)(2,1)}), bf16[32,9,2048]{2,1,0:T(8,128)(2,1)}, u32[]{:S(2)}, u32[]{:S(2)}) %all-to-all-start.3) | async-done | bytes 1179680 | tf_op jit(solution)/shard_map/all_to_all | solution.py:766
  788.3 34.0 %all-to-all-done.2 = bf16[32,11,2048]{2,1,0:T(8,128)(2,1)S(1)} async-done(((bf16[32,11,2048]{2,1,0:T(8,128)(2,1)}), bf16[32,11,2048]{2,1,0:T(8,128)(2,1)S(1)}, u32[]{:S(2)}, u32[]{:S(2)}) %all-to-all-start.2) | async-done | bytes 1441824 | tf_op jit(solution)/shard_map/all_to_all | solution.py:766
  (732 shorter events, 440.8 us)
Async XLA Ops:
  7.2 151.6 %all-gather.14.cloned.1.call-start = ((), (), s32[]{:S(2)}) async-start(), calls=%async_computation.10 | async-start | bytes 5308416 | tf_op jit(solution)/shard_map/all_gather | solution.py:736
  9.4 180.5 %all-gather.6.cloned.1.call-start = ((), (), s32[]{:S(2)}) async-start(), calls=%async_computation.6 | async-start | bytes 10616832 | tf_op jit(solution)/shard_map/all_gather | solution.py:736
  13.7 209.7 %all-gather.8.cloned.1.call-start = ((), (), s32[]{:S(2)}) async-start(), calls=%async_computation.7 | async-start | bytes 1806336 | tf_op jit(solution)/shard_map/all_gather | solution.py:736
  15.1 269.8 %all-gather.10.cloned.1.call-start = ((), (), s32[]{:S(2)}) async-start(), calls=%async_computation.8 | async-start | bytes 5308416 | tf_op jit(solution)/shard_map/all_gather | solution.py:736
  19.3 60.2 %all-to-all-start = ((bf16[32,8,2176]{2,1,0:T(8,128)(2,1)}), bf16[32,8,2176]{2,1,0:T(8,128)(2,1)S(1)}, u32[]{:S(2)}, u32[]{:S(2)}) async-start(bf16[32,8,2176]{2,1,0:T(8,128)(2,1)} %fusion.11), calls=%async_computation | async-start | bytes 2228224 | tf_op jit(solution)/shard_map/all_to_all | solution.py:766
  26.7 329.3 %all-gather.12.cloned.1.call-start = ((), (), s32[]{:S(2)}) async-start(), calls=%async_computation.9 | async-start | bytes 10027008 | tf_op jit(solution)/shard_map/all_gather | solution.py:736
  79.5 45.4 %all-to-all-start.1 = ((bf16[32,8,2048]{2,1,0:T(8,128)(2,1)}), bf16[32,8,2048]{2,1,0:T(8,128)(2,1)S(1)}, u32[]{:S(2)}, u32[]{:S(2)}) async-start(bf16[32,8,2048]{2,1,0:T(8,128)(2,1)} %fusion.46), calls=%async_computation.1 | async-start | bytes 2097152 | tf_op jit(solution)/shard_map/all_to_all | solution.py:766
  82.7 690.9 %reduce-scatter.3.cloned.1.call-start = ((), (), s32[]{:S(2)}) async-start(), calls=%async_computation.11 | async-start | bytes 626688 | tf_op jit(solution)/shard_map/reduce_scatter | solution.py:872
  88.6 49.8 %collective-permute-start = (bf16[256,2048]{0,1:T(8,128)(2,1)}, bf16[256,2048]{0,1:T(8,128)(2,1)}, u32[]{:S(2)}, u32[]{:S(2)}) collective-permute-start(bf16[256,2048]{0,1:T(8,128)(2,1)} %multiply_convert_fusion.1), channel_id=1, source_target_pairs={{0,1},{1,0},{2,3},{3,2},{4,5},{5,4},{6,7},{7,6},{8,9},{9,8},{10,11... | collective-permute-start | bytes 3145736 | tf_op jit(solution)/shard_map/ppermute | solution.py:619
  90.3 46.4 %collective-permute-start.1 = (bf16[256,2048]{0,1:T(8,128)(2,1)}, bf16[256,2048]{0,1:T(8,128)(2,1)}, u32[]{:S(2)}, u32[]{:S(2)}) collective-permute-start(bf16[256,2048]{0,1:T(8,128)(2,1)} %multiply_convert_fusion.1), channel_id=1, source_target_pairs={{0,2},{1,3},{2,0},{3,1},{4,6},{5,7},{6,4},{7,5},{8,10},{9,11},{10,... | collective-permute-start | bytes 3145736 | tf_op jit(solution)/shard_map/ppermute | solution.py:619
  137.8 77.2 %collective-permute-start.2 = (bf16[256,1024]{0,1:T(8,128)(2,1)S(1)}, bf16[256,1024]{0,1:T(8,128)(2,1)}, u32[]{:S(2)}, u32[]{:S(2)}) collective-permute-start(bf16[256,1024]{0,1:T(8,128)(2,1)S(1)} %slice.806), channel_id=1, source_target_pairs={{0,1},{1,0},{2,3},{3,2},{4,5},{5,4},{6,7},{7,6},{8,9},{9,8},{10,11... | collective-permute-start | bytes 1572872 | tf_op jit(solution)/shard_map/ppermute | solution.py:619
  139.5 75.6 %collective-permute-start.3 = (bf16[256,1024]{0,1:T(8,128)(2,1)S(1)}, bf16[256,1024]{0,1:T(8,128)(2,1)}, u32[]{:S(2)}, u32[]{:S(2)}) collective-permute-start(bf16[256,1024]{0,1:T(8,128)(2,1)S(1)} %slice.807), channel_id=1, source_target_pairs={{0,2},{1,3},{2,0},{3,1},{4,6},{5,7},{6,4},{7,5},{8,10},{9,11},{10,... | collective-permute-start | bytes 1572872 | tf_op jit(solution)/shard_map/ppermute | solution.py:619
  154.9 82.2 %collective-permute-start.26 = (bf16[256,1024]{0,1:T(8,128)(2,1)}, bf16[256,1024]{0,1:T(8,128)(2,1)}, u32[]{:S(2)}, u32[]{:S(2)}) collective-permute-start(bf16[256,1024]{0,1:T(8,128)(2,1)} %slice.857), channel_id=1, source_target_pairs={{0,1},{1,0},{2,3},{3,2},{4,5},{5,4},{6,7},{7,6},{8,9},{9,8},{10,11... | collective-permute-start | bytes 1572872 | tf_op jit(solution)/shard_map/ppermute | solution.py:619
  157.5 79.6 %collective-permute-start.27 = (bf16[256,1024]{0,1:T(8,128)(2,1)}, bf16[256,1024]{0,1:T(8,128)(2,1)}, u32[]{:S(2)}, u32[]{:S(2)}) collective-permute-start(bf16[256,1024]{0,1:T(8,128)(2,1)} %slice.858), channel_id=1, source_target_pairs={{0,2},{1,3},{2,0},{3,1},{4,6},{5,7},{6,4},{7,5},{8,10},{9,11},{10,... | collective-permute-start | bytes 1572872 | tf_op jit(solution)/shard_map/ppermute | solution.py:619
  338.1 39.7 %collective-permute-start.15 = (bf16[256,2048]{0,1:T(8,128)(2,1)}, bf16[256,2048]{0,1:T(8,128)(2,1)}, u32[]{:S(2)}, u32[]{:S(2)}) collective-permute-start(bf16[256,2048]{0,1:T(8,128)(2,1)} %multiply_convert_fusion), channel_id=1, source_target_pairs={{0,2},{1,3},{2,0},{3,1},{4,6},{5,7},{6,4},{7,5},{8,10},{9,11},{10,... | collective-permute-start | bytes 3145736 | tf_op jit(solution)/shard_map/ppermute | solution.py:619
  432.4 54.5 %collective-permute-start.28 = (bf16[256,1152]{0,1:T(8,128)(2,1)S(1)}, bf16[256,1152]{0,1:T(8,128)(2,1)S(1)}, u32[]{:S(2)}, u32[]{:S(2)}) collective-permute-start(bf16[256,1152]{0,1:T(8,128)(2,1)S(1)} %pad_maximum_fusion.17), channel_id=1, source_target_pairs={{0,1},{1,0},{2,3},{3,2},{4,5},{5,4},{6,7},{7,6},{8,9},{9,8},{10,11... | collective-permute-start | bytes 1769480 | tf_op jit(solution)/shard_map/ppermute | solution.py:619
  441.3 182.3 %collective-permute-start.18 = (bf16[256,1152]{0,1:T(8,128)(2,1)}, bf16[256,1152]{0,1:T(8,128)(2,1)}, u32[]{:S(2)}, u32[]{:S(2)}) collective-permute-start(bf16[256,1152]{0,1:T(8,128)(2,1)} %pad_maximum_fusion.15), channel_id=1, source_target_pairs={{0,1},{1,0},{2,3},{3,2},{4,5},{5,4},{6,7},{7,6},{8,9},{9,8},{10,11... | collective-permute-start | bytes 1769480 | tf_op jit(solution)/shard_map/ppermute | solution.py:619
  464.9 128.1 %collective-permute-start.19 = (bf16[256,1152]{0,1:T(8,128)(2,1)}, bf16[256,1152]{0,1:T(8,128)(2,1)}, u32[]{:S(2)}, u32[]{:S(2)}) collective-permute-start(bf16[256,1152]{0,1:T(8,128)(2,1)} %pad_maximum_fusion.16), channel_id=1, source_target_pairs={{0,1},{1,0},{2,3},{3,2},{4,5},{5,4},{6,7},{7,6},{8,9},{9,8},{10,11... | collective-permute-start | bytes 1769480 | tf_op jit(solution)/shard_map/ppermute | solution.py:619
  485.3 114.5 %collective-permute-start.22 = (bf16[256,1024]{0,1:T(8,128)(2,1)}, bf16[256,1024]{0,1:T(8,128)(2,1)}, u32[]{:S(2)}, u32[]{:S(2)}) collective-permute-start(bf16[256,1024]{0,1:T(8,128)(2,1)} %fusion.132), channel_id=1, source_target_pairs={{0,2},{1,3},{2,0},{3,1},{4,6},{5,7},{6,4},{7,5},{8,10},{9,11},{10,... | collective-permute-start | bytes 1572872 | tf_op jit(solution)/shard_map/ppermute | solution.py:619
  604.6 106.4 %collective-permute-start.21 = (bf16[256,1024]{0,1:T(8,128)(2,1)}, bf16[256,1024]{0,1:T(8,128)(2,1)}, u32[]{:S(2)}, u32[]{:S(2)}) collective-permute-start(bf16[256,1024]{0,1:T(8,128)(2,1)} %fusion.129), channel_id=1, source_target_pairs={{0,2},{1,3},{2,0},{3,1},{4,6},{5,7},{6,4},{7,5},{8,10},{9,11},{10,... | collective-permute-start | bytes 1572872 | tf_op jit(solution)/shard_map/ppermute | solution.py:619
  655.0 38.5 %collective-permute-start.44 = (bf16[256,1152]{0,1:T(8,128)(2,1)S(1)}, bf16[256,1152]{0,1:T(8,128)(2,1)S(1)}, u32[]{:S(2)}, u32[]{:S(2)}) collective-permute-start(bf16[256,1152]{0,1:T(8,128)(2,1)S(1)} %pad_maximum_fusion.19), channel_id=1, source_target_pairs={{0,1},{1,0},{2,3},{3,2},{4,5},{5,4},{6,7},{7,6},{8,9},{9,8},{10,11... | collective-permute-start | bytes 1769480 | tf_op jit(solution)/shard_map/ppermute | solution.py:619
  707.4 62.0 %all-to-all-start.3 = ((bf16[32,9,2048]{2,1,0:T(8,128)(2,1)}), bf16[32,9,2048]{2,1,0:T(8,128)(2,1)}, u32[]{:S(2)}, u32[]{:S(2)}) async-start(bf16[32,9,2048]{2,1,0:T(8,128)(2,1)} %pad_maximum_fusion.8), calls=%async_computation.3 | async-start | bytes 4194304 | tf_op jit(solution)/shard_map/all_to_all | solution.py:766
  710.9 66.7 %reduce-scatter.5.cloned.1.call-start = ((), (), s32[]{:S(2)}) async-start(), calls=%async_computation.12 | async-start | bytes 1179648 | tf_op jit(solution)/shard_map/reduce_scatter | solution.py:872
  769.4 53.0 %all-to-all-start.2 = ((bf16[32,11,2048]{2,1,0:T(8,128)(2,1)}), bf16[32,11,2048]{2,1,0:T(8,128)(2,1)S(1)}, u32[]{:S(2)}, u32[]{:S(2)}) async-start(bf16[32,11,2048]{2,1,0:T(8,128)(2,1)} %pad_maximum_fusion.6), calls=%async_computation.2 | async-start | bytes 4194304 | tf_op jit(solution)/shard_map/all_to_all | solution.py:766
  (169 other events, 1774.1 us)
Sparse Core Ops, SparseCore 0:
  9.6 80.5 all-gather.13
  91.8 98.0 all-gather.5
  191.5 25.2 all-gather.7
  218.2 51.7 all-gather.9
  271.4 84.5 all-gather.11
  639.3 27.8 reduce-scatter.2
  716.1 39.1 reduce-scatter.4

commit v3 on v2

v3 whole, which is shorter than its diff:
```python
import functools
import math

import jax
import jax.numpy as jnp
from jax import lax
from jax.experimental import pallas as pl
from jax.experimental.pallas import tpu as pltpu
from jax.sharding import PartitionSpec as P

NH = 48
HP = 64
NSTATE = 256
KCONV = 4
QUERY_HEADS = 8
KEY_VALUE_HEADS = 2
HEAD_SIZE = 128
RANK = 16
NADAPT = 8
SSD_BLOCK = 256
DSSM = 3072
UNIT_IN = 1030
UNIT_FF = 512


EPSILON = 1e-05
ROPE_BASE = 10000.0
NEGATIVE = -1e30
FLOAT = jnp.float32
BFLOAT = jnp.bfloat16


def product(left, right):
    return jnp.dot(left, right, preferred_element_type=FLOAT)


def contract_last(left, right):
    return lax.dot_general(left, right, (((1,), (1,)), ((), ())), preferred_element_type=FLOAT)


def contract_first(left, right):
    return lax.dot_general(left, right, (((0,), (0,)), ((), ())), preferred_element_type=FLOAT)


def rms_norm(values, gain):
    return values * lax.rsqrt(jnp.mean(values * values, axis=-1, keepdims=True) + EPSILON) * gain


def sequence_tables(lengths, adapters, sequence_length):
    sequence_count = lengths.shape[0]
    boundary = jnp.cumsum(lengths)
    token_index = jnp.arange(sequence_length, dtype=jnp.int32)
    passed = (token_index[:, None] >= boundary[None, :]).astype(jnp.int32)
    segment = jnp.sum(passed, axis=1)
    segment_start = jnp.sum(passed * lengths[None, :], axis=1)
    position = token_index - segment_start
    member = (segment[:, None] == jnp.arange(sequence_count, dtype=jnp.int32)[None, :]).astype(
        jnp.int32
    )
    chosen = jnp.sum(member * adapters[None, :], axis=1)
    column = jnp.arange(NADAPT * RANK, dtype=jnp.int32) // RANK
    selector = (chosen[:, None] == column[None, :]).astype(FLOAT)
    return (segment, position, selector)


SCAN_BYTES = 32 * 1024 * 1024
DENSE_BYTES = 16 * 1024 * 1024
LANES = 128


def whole(shape):
    return pl.BlockSpec(shape, lambda *_: (0,) * len(shape))


def dot(left, right, contract):
    return lax.dot_general(left, right, ((contract[:1], contract[1:]), ((), ())), preferred_element_type=FLOAT)


def parts_of(values, count):
    parts = []
    for _ in range(count):
        part = values.astype(BFLOAT)
        parts.append(part)
        values = values - part.astype(FLOAT)
    return parts


def running_sum(values, triangle, contract):
    width = values.shape[1]
    split = dot(triangle, jnp.concatenate(parts_of(values, 3), axis=1), contract)
    return split[:, :width] + split[:, width : 2 * width] + split[:, 2 * width :]


def head_spread(values, expand):
    return dot(jnp.concatenate(parts_of(values, 2), axis=1), expand, (1, 0))


def head_sum(values, expand):
    high, low = parts_of(values, 2)
    single = expand[:LANES]
    return dot(high, single, (1, 1)) + dot(low, single, (1, 1))


def silu_parts(values):
    gate = 1.0 / (1.0 + jnp.exp(-values))
    return values * gate, gate


def expand_table(channels):
    row = lax.broadcasted_iota(jnp.int32, (2 * LANES, channels), 0) % LANES
    channel = lax.broadcasted_iota(jnp.int32, (2 * LANES, channels), 1) // HP
    return (row == channel).astype(BFLOAT)


def conv_sum(current_ref, before_ref, taps_ref, meta):
    rows = SSD_BLOCK
    current = current_ref[...].astype(FLOAT)
    window = jnp.concatenate([before_ref[...].astype(FLOAT)[8:16], current], axis=0)
    summed = taps_ref[KCONV : KCONV + 1, :] + current * taps_ref[0:1, :]
    for lag in range(1, KCONV):
        shifted = window[8 - lag : 8 - lag + rows]
        summed = summed + jnp.where(meta[:, 1:2] >= lag, shifted, 0.0) * taps_ref[lag : lag + 1, :]
    return summed


def conv_back(summed_grad, later, taps_ref, meta):
    rows = SSD_BLOCK
    window = jnp.concatenate([summed_grad, later[...]], axis=0)
    grad = summed_grad * taps_ref[0:1, :]
    for lag in range(1, KCONV):
        grad = grad + jnp.where(meta[:, 2:3] >= lag, window[lag : lag + rows], 0.0) * taps_ref[lag : lag + 1, :]
    later[...] = summed_grad[:8]
    return grad


def silu_slope(values, gate):
    return gate * (1.0 + values * (1.0 - gate))


def scan_block(
    conv_ref, before_ref, state_ref, state_before_ref, step_ref, meta_ref, segment_ref, taps_ref, state_taps_ref, head_ref
):
    rows = SSD_BLOCK
    channels = conv_ref.shape[1]
    meta = meta_ref[...]
    summed = conv_sum(conv_ref, before_ref, taps_ref, meta)
    activated, conv_gate = silu_parts(summed)
    wide_inputs = activated.astype(BFLOAT).astype(FLOAT)
    state_summed = conv_sum(state_ref, state_before_ref, state_taps_ref, meta)
    state_values, state_gate = silu_parts(state_summed)
    write = state_values[:, :NSTATE].astype(BFLOAT)
    read = state_values[:, NSTATE:].astype(BFLOAT)
    raw = step_ref[...].astype(FLOAT) + head_ref[0:1, :]
    steps = jnp.maximum(raw, 0.0) + jnp.log1p(jnp.exp(-jnp.abs(raw)))
    row = lax.broadcasted_iota(jnp.int32, (rows, rows), 0)
    column = lax.broadcasted_iota(jnp.int32, (rows, rows), 1)
    triangle = (row >= column).astype(BFLOAT)
    total = running_sum(steps * head_ref[1:2, :], triangle, (1, 0))
    entered = jnp.exp(total) * meta[:, 3:4]
    leaving = jnp.exp(total[rows - 1 : rows] - total) * meta[:, 4:5]
    expand = expand_table(channels)
    spread = head_spread(jnp.concatenate([steps, entered, leaving * steps], axis=0), expand)
    blocked = jnp.where((row >= column) & (meta[:, 0:1] == segment_ref[0:1, :]), 0.0, NEGATIVE)
    return dict(
        summed=summed,
        conv_gate=conv_gate,
        state_summed=state_summed,
        state_gate=state_gate,
        write=write,
        read=read,
        wide_inputs=wide_inputs,
        raw=raw,
        steps=steps,
        triangle=triangle,
        total=total,
        total_rows=total.T,
        leaving=leaving,
        expand=expand,
        steps_wide=spread[:rows],
        entered_wide=spread[rows : 2 * rows],
        tail_wide=spread[2 * rows :],
        stepped=(wide_inputs * spread[:rows]).astype(BFLOAT),
        tailed=(wide_inputs * spread[2 * rows :]).astype(BFLOAT),
        blocked=blocked,
        crossing=dot(read, write, (1, 1)),
    )


def decay_of(block, head):
    return jnp.exp(
        block["total"][:, head : head + 1] - block["total_rows"][head : head + 1, :] + block["blocked"]
    )


def scan_forward_kernel(
    gate_ref, conv_ref, before_ref, state_ref, state_before_ref, step_ref, meta_ref, segment_ref, taps_ref,
    state_taps_ref, head_ref, skip_ref, mixed_ref, out_ref, scanned_ref, states_ref, state,
):
    del mixed_ref

    @pl.when(pl.program_id(0) == 0)
    def _():
        state[...] = jnp.zeros_like(state)

    block = scan_block(
        conv_ref, before_ref, state_ref, state_before_ref, step_ref, meta_ref, segment_ref, taps_ref, state_taps_ref,
        head_ref,
    )
    heads = conv_ref.shape[1] // HP
    carried = state[...].astype(BFLOAT)
    states_ref[0] = carried
    across = dot(block["read"], carried, (1, 0)) * block["entered_wide"]
    within = []
    for head in range(heads):
        weights = (block["crossing"] * decay_of(block, head)).astype(BFLOAT)
        within.append(dot(weights, block["stepped"][:, head * HP : (head + 1) * HP], (1, 0)))
    scanned = across + jnp.concatenate(within, axis=1)
    scanned_ref[...] = scanned
    gated, _ = silu_parts(gate_ref[...].astype(FLOAT))
    out_ref[...] = ((scanned + skip_ref[0:1, :] * block["wide_inputs"]) * gated).astype(BFLOAT)
    state[...] = state[...] * block["entered_wide"][SSD_BLOCK - 1 : SSD_BLOCK, :] + dot(
        block["write"], block["tailed"], (0, 0)
    )


def scan_backward_kernel(
    gate_ref, conv_ref, before_ref, state_ref, state_before_ref, step_ref, meta_ref, segment_ref, taps_ref,
    state_taps_ref, head_ref, skip_ref, scanned_ref, states_ref, grad_ref, query_grad_ref, key_grad_ref,
    value_grad_ref, out_ref, state_grad, later, state_later,
):
    @pl.when(pl.program_id(0) == 0)
    def _():
        state_grad[...] = jnp.zeros_like(state_grad)
        later[...] = jnp.zeros_like(later)
        state_later[...] = jnp.zeros_like(state_later)

    block = scan_block(
        conv_ref, before_ref, state_ref, state_before_ref, step_ref, meta_ref, segment_ref, taps_ref, state_taps_ref,
        head_ref,
    )
    rows = SSD_BLOCK
    channels = conv_ref.shape[1]
    heads = channels // HP
    meta = meta_ref[...]
    read, write = block["read"], block["write"]
    inputs = block["wide_inputs"]
    scanned = scanned_ref[...]
    skip = skip_ref[0:1, :]
    gate_values = gate_ref[...].astype(FLOAT)
    gated, gate = silu_parts(gate_values)
    grad = grad_ref[...].astype(FLOAT)
    gate_grad = grad * (scanned + skip * inputs) * silu_slope(gate_values, gate)
    out_grad = grad * gated
    inputs_grad = skip * out_grad
    rounded = out_grad.astype(BFLOAT)
    wide_rounded = rounded.astype(FLOAT)
    carried = states_ref[0]
    after = state_grad[...]
    after_rounded = after.astype(BFLOAT)

    from_state = dot(write, after_rounded, (1, 0))
    entering = (wide_rounded * block["entered_wide"]).astype(BFLOAT)
    write_grad = dot(block["tailed"], after_rounded, (1, 1))
    read_grad = dot(entering, carried, (1, 1))
    last_entered = block["entered_wide"][rows - 1 : rows, :]
    through = jnp.sum(after * carried.astype(FLOAT), axis=0, keepdims=True) * last_entered
    state_grad[...] = after * last_entered + dot(read, entering, (0, 0))

    crossing_grad = jnp.zeros((rows, rows), FLOAT)
    pulled = []
    for head in range(heads):
        span = slice(head * HP, (head + 1) * HP)
        decay = decay_of(block, head)
        weights = (block["crossing"] * decay).astype(BFLOAT)
        pulled.append(dot(weights, rounded[:, span], (0, 0)))
        crossing_grad = crossing_grad + dot(rounded[:, span], block["stepped"][:, span], (1, 1)) * decay
    pulled = jnp.concatenate(pulled, axis=1)
    crossing_rounded = crossing_grad.astype(BFLOAT)
    read_grad = read_grad + dot(crossing_rounded, write, (1, 0))
    write_grad = write_grad + dot(crossing_rounded, read, (0, 0))

    inputs_grad = inputs_grad + block["steps_wide"] * pulled + block["tail_wide"] * from_state
    sums = head_sum(
        jnp.concatenate(
            [
                wide_rounded * scanned - block["stepped"].astype(FLOAT) * pulled,
                inputs * pulled,
                inputs * from_state,
                jnp.broadcast_to(through, (8, channels)),
            ],
            axis=0,
        ),
        block["expand"],
    )
    leaving_grad = sums[2 * rows : 3 * rows] * block["leaving"]
    leaving_total = leaving_grad * block["steps"]
    last = sums[3 * rows : 3 * rows + 1] + jnp.sum(leaving_total, axis=0, keepdims=True)
    total_grad = sums[:rows] - leaving_total
    total_grad = total_grad + jnp.where(
        lax.broadcasted_iota(jnp.int32, total_grad.shape, 0) == rows - 1, last, 0.0
    )
    decay_grad = running_sum(total_grad, block["triangle"], (0, 0))
    steps_grad = sums[rows : 2 * rows] + leaving_grad + decay_grad * head_ref[1:2, :]
    raw_grad = steps_grad / (1.0 + jnp.exp(-block["raw"]))
    raw_grad = jnp.where(lax.broadcasted_iota(jnp.int32, raw_grad.shape, 1) < heads, raw_grad, 0.0)

    state_slope = silu_slope(block["state_summed"], block["state_gate"])
    state_pre = conv_back(
        jnp.concatenate([write_grad, read_grad], axis=1) * state_slope, state_later, state_taps_ref, meta
    )
    conv_pre = conv_back(inputs_grad * silu_slope(block["summed"], block["conv_gate"]), later, taps_ref, meta)
    start = 0
    for values in (
        state_pre, key_grad_ref[...], value_grad_ref[...], gate_grad, conv_pre, query_grad_ref[...], raw_grad
    ):
        out_ref[:, start : start + values.shape[1]] = values.astype(BFLOAT)
        start += values.shape[1]


STATES = 2 * NSTATE
PAIR = 2 * HEAD_SIZE


def scan_specs(channels, order):
    half = SSD_BLOCK // 16
    before = lambda i: jnp.maximum(order(i) * half - 1, 0)
    gate_at = (STATES + PAIR) // channels
    step_at = (STATES + PAIR + 2 * channels + channels * QUERY_HEADS // DSSM * HEAD_SIZE) // LANES
    return [
        pl.BlockSpec((SSD_BLOCK, channels), lambda i: (order(i), gate_at)),
        pl.BlockSpec((SSD_BLOCK, channels), lambda i: (order(i), gate_at + 1)),
        pl.BlockSpec((16, channels), lambda i: (before(i), gate_at + 1)),
        pl.BlockSpec((SSD_BLOCK, STATES), lambda i: (order(i), 0)),
        pl.BlockSpec((16, STATES), lambda i: (before(i), 0)),
        pl.BlockSpec((SSD_BLOCK, LANES), lambda i: (order(i), step_at)),
        pl.BlockSpec((SSD_BLOCK, LANES), lambda i: (order(i), 0)),
        pl.BlockSpec((8, SSD_BLOCK), lambda i: (0, order(i))),
        whole((8, channels)),
        whole((8, STATES)),
        whole((8, LANES)),
        whole((8, channels)),
    ]


def scan_operands(projected, tables):
    return [projected] * 6 + [
        tables[name] for name in ("meta", "segment_row", "taps", "state_taps", "head", "skip")
    ]


def scan_cost(tokens, channels, factor):
    heads = channels // HP
    return pl.CostEstimate(
        flops=factor * 2 * tokens * SSD_BLOCK * (3 * channels + NSTATE),
        bytes_accessed=factor * tokens * channels * 12,
        transcendentals=tokens * SSD_BLOCK * heads,
    )


def scan_forward(projected, tables, mixed):
    tokens = projected.shape[0]
    channels = tables["taps"].shape[1]
    blocks = tokens // SSD_BLOCK
    return pl.pallas_call(
        scan_forward_kernel,
        grid=(blocks,),
        in_specs=scan_specs(channels, lambda i: i) + [pl.BlockSpec(memory_space=pl.ANY)],
        out_specs=[
            pl.BlockSpec((SSD_BLOCK, channels), lambda i: (i, 0)),
            pl.BlockSpec((SSD_BLOCK, channels), lambda i: (i, 0)),
            pl.BlockSpec((1, NSTATE, channels), lambda i: (i, 0, 0)),
        ],
        out_shape=[
            jax.ShapeDtypeStruct(mixed.shape, BFLOAT),
            jax.ShapeDtypeStruct((tokens, channels), FLOAT),
            jax.ShapeDtypeStruct((blocks, NSTATE, channels), BFLOAT),
        ],
        scratch_shapes=[pltpu.VMEM((NSTATE, channels), FLOAT)],
        input_output_aliases={12: 0},
        compiler_params=pltpu.CompilerParams(vmem_limit_bytes=SCAN_BYTES),
        cost_estimate=scan_cost(tokens, channels, 1),
        name="scan_forward",
    )(*scan_operands(projected, tables), mixed)


def scan_backward(projected, tables, scanned, carried, mixed_grad, query_grad, key_grad, value_grad):
    tokens, width = projected.shape
    channels = tables["taps"].shape[1]
    blocks = tokens // SSD_BLOCK
    back = lambda i: (blocks - 1 - i, 0)
    return pl.pallas_call(
        scan_backward_kernel,
        grid=(blocks,),
        in_specs=scan_specs(channels, lambda i: blocks - 1 - i)
        + [
            pl.BlockSpec((SSD_BLOCK, channels), back),
            pl.BlockSpec((1, NSTATE, channels), lambda i: (blocks - 1 - i, 0, 0)),
            pl.BlockSpec((SSD_BLOCK, channels), back),
            pl.BlockSpec((SSD_BLOCK, query_grad.shape[1]), back),
            pl.BlockSpec((SSD_BLOCK, HEAD_SIZE), back),
            pl.BlockSpec((SSD_BLOCK, HEAD_SIZE), back),
        ],
        out_specs=pl.BlockSpec((SSD_BLOCK, width), back),
        out_shape=jax.ShapeDtypeStruct((tokens, width), BFLOAT),
        scratch_shapes=[
            pltpu.VMEM((NSTATE, channels), FLOAT),
            pltpu.VMEM((8, channels), FLOAT),
            pltpu.VMEM((8, STATES), FLOAT),
        ],
        compiler_params=pltpu.CompilerParams(vmem_limit_bytes=SCAN_BYTES),
        cost_estimate=scan_cost(tokens, channels, 2),
        name="scan_backward",
    )(*scan_operands(projected, tables), scanned, carried, mixed_grad, query_grad, key_grad, value_grad)


def turned(values, cosine, sine):
    return (values * cosine + pltpu.roll(values, HEAD_SIZE // 2, 1) * sine).astype(BFLOAT)


def turned_back(values, cosine, sine):
    return values * cosine + pltpu.roll(values * sine, HEAD_SIZE // 2, 1)


ATT_ROWS = 256


def attention_mask(meta_ref, segment_ref, start, extent):
    row = start + lax.broadcasted_iota(jnp.int32, (ATT_ROWS, extent), 0)
    column = lax.broadcasted_iota(jnp.int32, (ATT_ROWS, extent), 1)
    return (row >= column) & (meta_ref[start : start + ATT_ROWS, 0:1] == segment_ref[0:1, :extent])


def probabilities(query, keys, allowed):
    score = dot(query, keys, (1, 1)) * (1.0 / math.sqrt(HEAD_SIZE))
    score = jnp.where(allowed, score, NEGATIVE)
    exponent = jnp.exp(score - jnp.max(score, axis=1, keepdims=True))
    return exponent / jnp.sum(exponent, axis=1, keepdims=True)


def attention_forward_kernel(query_ref, key_ref, value_ref, cosine_ref, sine_ref, meta_ref, segment_ref, out_ref, keys):
    tokens = key_ref.shape[0]
    keys[...] = turned(key_ref[...].astype(FLOAT), cosine_ref[...], sine_ref[...])
    for start in range(0, tokens, ATT_ROWS):
        extent = start + ATT_ROWS
        here = slice(start, extent)
        allowed = attention_mask(meta_ref, segment_ref, start, extent)
        for unit in range(query_ref.shape[1] // HEAD_SIZE):
            span = slice(unit * HEAD_SIZE, (unit + 1) * HEAD_SIZE)
            query = turned(query_ref[here, span].astype(FLOAT), cosine_ref[here], sine_ref[here])
            weights = probabilities(query, keys[:extent], allowed).astype(BFLOAT)
            out_ref[here, span] = dot(weights, value_ref[:extent], (1, 0)).astype(BFLOAT)


def attention_backward_kernel(
    query_ref, key_ref, value_ref, cosine_ref, sine_ref, meta_ref, segment_ref, grad_ref,
    query_grad_ref, key_grad_ref, value_grad_ref, keys, key_sum, value_sum,
):
    tokens = key_ref.shape[0]
    scale = 1.0 / math.sqrt(HEAD_SIZE)
    keys[...] = turned(key_ref[...].astype(FLOAT), cosine_ref[...], sine_ref[...])
    key_sum[...] = jnp.zeros_like(key_sum)
    value_sum[...] = jnp.zeros_like(value_sum)
    for start in range(0, tokens, ATT_ROWS):
        extent = start + ATT_ROWS
        here = slice(start, extent)
        allowed = attention_mask(meta_ref, segment_ref, start, extent)
        for unit in range(query_ref.shape[1] // HEAD_SIZE):
            span = slice(unit * HEAD_SIZE, (unit + 1) * HEAD_SIZE)
            query = turned(query_ref[here, span].astype(FLOAT), cosine_ref[here], sine_ref[here])
            weights = probabilities(query, keys[:extent], allowed)
            grad = grad_ref[here, span]
            weights_grad = dot(grad, value_ref[:extent], (1, 1))
            value_sum[:extent] += dot(weights.astype(BFLOAT), grad, (0, 0))
            mean_grad = jnp.sum(weights * weights_grad, axis=1, keepdims=True)
            score_grad = (weights * (weights_grad - mean_grad) * scale).astype(BFLOAT)
            query_grad = dot(score_grad, keys[:extent], (1, 0))
            key_sum[:extent] += dot(score_grad, query, (0, 0))
            query_grad_ref[here, span] = turned_back(query_grad, cosine_ref[here], sine_ref[here]).astype(BFLOAT)
    key_grad_ref[...] = turned_back(key_sum[...], cosine_ref[...], sine_ref[...]).astype(BFLOAT)
    value_grad_ref[...] = value_sum[...].astype(BFLOAT)


def attention_cost(tokens, width, factor):
    return pl.CostEstimate(
        flops=factor * 2 * tokens * tokens * width,
        bytes_accessed=factor * tokens * width * 8,
        transcendentals=tokens * tokens * width // (2 * HEAD_SIZE),
    )


def attention_specs(tokens, channels):
    width = channels * QUERY_HEADS // DSSM * HEAD_SIZE
    narrow = whole((tokens, HEAD_SIZE))
    return [
        pl.BlockSpec((tokens, width), lambda *_: (0, (STATES + PAIR + 2 * channels) // width)),
        pl.BlockSpec((tokens, HEAD_SIZE), lambda *_: (0, STATES // HEAD_SIZE)),
        pl.BlockSpec((tokens, HEAD_SIZE), lambda *_: (0, STATES // HEAD_SIZE + 1)),
        narrow,
        narrow,
        whole((tokens, LANES)),
        whole((8, tokens)),
    ]


def attention_operands(projected, tables):
    return [projected] * 3 + [tables[name] for name in ("cosine", "sine", "meta", "segment_row")]


def attention_forward(projected, tables):
    tokens = projected.shape[0]
    channels = tables["taps"].shape[1]
    width = channels * QUERY_HEADS // DSSM * HEAD_SIZE
    return pl.pallas_call(
        attention_forward_kernel,
        grid=(1,),
        in_specs=attention_specs(tokens, channels),
        out_specs=pl.BlockSpec((tokens, width), lambda *_: (0, channels // width)),
        out_shape=jax.ShapeDtypeStruct((tokens, channels + width), BFLOAT),
        scratch_shapes=[pltpu.VMEM((tokens, HEAD_SIZE), BFLOAT)],
        compiler_params=pltpu.CompilerParams(vmem_limit_bytes=SCAN_BYTES),
        cost_estimate=attention_cost(tokens, width, 1),
        name="attention_forward",
    )(*attention_operands(projected, tables))


def attention_backward(projected, tables, mixed_grad):
    tokens = projected.shape[0]
    channels = tables["taps"].shape[1]
    width = channels * QUERY_HEADS // DSSM * HEAD_SIZE
    narrow = whole((tokens, HEAD_SIZE))
    return pl.pallas_call(
        attention_backward_kernel,
        grid=(1,),
        in_specs=attention_specs(tokens, channels)
        + [pl.BlockSpec((tokens, width), lambda *_: (0, channels // width))],
        out_specs=[whole((tokens, width)), narrow, narrow],
        out_shape=[
            jax.ShapeDtypeStruct((tokens, width), BFLOAT),
            jax.ShapeDtypeStruct((tokens, HEAD_SIZE), BFLOAT),
            jax.ShapeDtypeStruct((tokens, HEAD_SIZE), BFLOAT),
        ],
        scratch_shapes=[
            pltpu.VMEM((tokens, HEAD_SIZE), BFLOAT),
            pltpu.VMEM((tokens, HEAD_SIZE), FLOAT),
            pltpu.VMEM((tokens, HEAD_SIZE), FLOAT),
        ],
        compiler_params=pltpu.CompilerParams(vmem_limit_bytes=SCAN_BYTES),
        cost_estimate=attention_cost(tokens, width, 3),
        name="attention_backward",
    )(*attention_operands(projected, tables), mixed_grad)


def mixer_tables(lengths, segment, position, conv_values, conv_states, scan_params):
    tokens = segment.shape[0]
    block = jnp.arange(tokens, dtype=jnp.int32) // SSD_BLOCK
    previous = jnp.concatenate([jnp.full((1,), -1, jnp.int32), segment[:-1]])
    first_previous = jnp.repeat(previous[::SSD_BLOCK], SSD_BLOCK)
    last_segment = jnp.repeat(segment[SSD_BLOCK - 1 :: SSD_BLOCK], SSD_BLOCK)
    length = jnp.sum(
        jnp.where(segment[:, None] == jnp.arange(lengths.shape[0], dtype=jnp.int32)[None, :], lengths[None, :], 0),
        axis=1,
    )
    columns = [
        segment,
        position,
        length - 1 - position,
        segment == first_previous,
        segment == last_segment,
    ]
    meta = jnp.stack([column.astype(FLOAT) for column in columns], axis=1)
    half_width = HEAD_SIZE // 2
    frequency = ROPE_BASE ** (-2.0 * jnp.arange(half_width, dtype=FLOAT) / HEAD_SIZE)
    angle = position.astype(FLOAT)[:, None] * frequency[None, :]
    cosine, sine = jnp.cos(angle), jnp.sin(angle)
    heads = scan_params.shape[1]
    head = jnp.stack([scan_params[0], -jnp.exp(scan_params[1]), scan_params[2]])
    return dict(
        meta=jnp.pad(meta, ((0, 0), (0, LANES - meta.shape[1]))),
        segment_row=jnp.broadcast_to(segment.astype(FLOAT)[None, :], (8, tokens)),
        taps=jnp.pad(conv_values.astype(FLOAT), ((0, 3), (0, 0))),
        state_taps=jnp.pad(conv_states.astype(FLOAT), ((0, 3), (0, 0))),
        head=jnp.pad(head, ((0, 5), (0, LANES - heads))),
        skip=jnp.broadcast_to(jnp.repeat(scan_params[2], HP)[None, :], (8, heads * HP)),
        cosine=jnp.concatenate([cosine, cosine], axis=1),
        sine=jnp.concatenate([-sine, sine], axis=1),
    )


HALVES = 2


def matrix_rows(values):
    return values.reshape(values.shape[0] * values.shape[1], values.shape[2])


def cut_tiles(width, tile):
    return [(low, min(low + tile, width)) for low in range(0, width, tile)]


def spread_kernel(mask, count, left_ref, right_ref, chosen_ref, *rest):
    weights, (out_ref, narrow_ref, out_tile, narrow, sems) = rest[:count], rest[-5:]
    rows = left_ref.shape[0]
    shards = weights[0].shape[0]
    depth = shards // HALVES
    start = pl.multiple_of((lax.axis_index("col") ^ mask) * rows, rows)
    here = pl.ds(start, rows)

    def through(ref, low, high):
        return dot(left_ref[...], matrix_rows(ref[:depth, :rows, low:high]), (1, 0)) + dot(
            right_ref[...], matrix_rows(ref[depth:, :rows, low:high]), (1, 0)
        )

    lower = weights[-1].shape[2] - LANES
    narrow[...] = (chosen_ref[here, :] * through(weights[-1], lower, lower + LANES)).astype(BFLOAT)
    copies = [pltpu.make_async_copy(narrow, narrow_ref.at[here, :], sems.at[0])]
    copies[0].start()
    column = 0
    for ref in weights:
        for low, high in cut_tiles(ref.shape[2] - (LANES if ref is weights[-1] else 0), 512):
            span = slice(column, column + high - low)
            column += high - low
            raised = matrix_rows(ref[:, rows : rows + NADAPT * RANK // shards, low:high])
            out_tile[:, span] = (through(ref, low, high) + dot(narrow[...], raised, (1, 0))).astype(BFLOAT)
            copies.append(
                pltpu.make_async_copy(out_tile.at[:, span], out_ref.at[here, span], sems.at[len(copies)])
            )
            copies[-1].start()
    for copy in copies:
        copy.wait()


def weights_width(gathered):
    return sum(part.shape[2] for part in gathered) - LANES


def spread_block(mask, halves, gathered, selector, held):
    rows, half = halves[0].shape
    width = weights_width(gathered)
    total = selector.shape[0]
    fast, free = pl.BlockSpec(memory_space=pltpu.VMEM), pl.BlockSpec(memory_space=pl.ANY)
    operands = [*halves, selector, *gathered]
    in_specs = [fast] * len(operands)
    aliases = {}
    if held is not None:
        aliases = {len(operands): 0, len(operands) + 1: 1}
        operands += list(held)
        in_specs += [free] * 2
    copies = 1 + sum(-(-part.shape[2] // 512) for part in gathered)
    return pl.pallas_call(
        functools.partial(spread_kernel, mask, len(gathered)),
        in_specs=in_specs,
        out_specs=[free] * 2,
        out_shape=[
            jax.ShapeDtypeStruct((total, width), BFLOAT),
            jax.ShapeDtypeStruct((total, LANES), BFLOAT),
        ],
        scratch_shapes=[
            pltpu.VMEM((rows, width), BFLOAT),
            pltpu.VMEM((rows, LANES), BFLOAT),
            pltpu.SemaphoreType.DMA((copies,)),
        ],
        input_output_aliases=aliases,
        compiler_params=pltpu.CompilerParams(vmem_limit_bytes=DENSE_BYTES),
        cost_estimate=pl.CostEstimate(
            flops=4 * rows * half * (width + LANES), bytes_accessed=2 * rows * (2 * half + width), transcendentals=0
        ),
        name="spread_block",
    )(*operands)


def collect_kernel(masks, count, values_ref, *refs):
    weights, outs = refs[:count], refs[count:]
    rows = values_ref.shape[0] // 4
    shards = weights[0].shape[0]
    half = shards // HALVES * rows
    width = values_ref.shape[1]
    starts, column = [], 0
    for ref in weights:
        high = min(column + ref.shape[2], width)
        starts.append((column, high))
        column = high
    for at, mask in enumerate(masks):
        here = pl.ds(pl.multiple_of((lax.axis_index("col") ^ mask) * rows, rows), rows)
        first, second = outs[2 * at], outs[2 * at + 1]

        def through(cut):
            total = None
            for (low, high), ref in zip(starts, weights):
                part = dot(values_ref[here, low:high], cut(ref, high - low), (1, 1))
                total = part if total is None else total + part
            return total

        for shard in range(shards):
            out_ref = first if shard < shards // HALVES else second
            column = shard * rows % half
            out_ref[:, column : column + rows] = through(lambda ref, wide: ref[shard, :rows, :wide]).astype(
                out_ref.dtype
            )
        first[:, half:] = through(
            lambda ref, wide: matrix_rows(ref[:, rows : rows + NADAPT * RANK // shards, :wide])
        ).astype(first.dtype)


def collect_blocks(masks, values, gathered, types):
    rows = values.shape[0] // 4
    half = gathered[0].shape[0] // HALVES * rows
    fast = pl.BlockSpec(memory_space=pltpu.VMEM)
    out_shape = []
    for pair in types:
        out_shape.append(jax.ShapeDtypeStruct((rows, half + LANES), pair[0]))
        out_shape.append(jax.ShapeDtypeStruct((rows, half), pair[1]))
    outs = pl.pallas_call(
        functools.partial(collect_kernel, masks, len(gathered)),
        in_specs=[fast] * (1 + len(gathered)),
        out_specs=[fast] * len(out_shape),
        out_shape=out_shape,
        compiler_params=pltpu.CompilerParams(vmem_limit_bytes=DENSE_BYTES),
        cost_estimate=pl.CostEstimate(
            flops=4 * len(masks) * rows * half * values.shape[1],
            bytes_accessed=2 * len(masks) * rows * (values.shape[1] + 4 * half),
            transcendentals=0,
        ),
        name="collect_blocks",
    )(values, *gathered)
    return [tuple(outs[2 * at : 2 * at + 2]) for at in range(len(masks))]


def root_mean(values):
    return lax.rsqrt(jnp.mean(values * values, axis=1, keepdims=True) + EPSILON)


def finish_kernel(kind, first_own, first_near, first_far, second_own, second_near, second_far, lower_ref, chosen_ref,
                  *refs):
    half = second_own.shape[1]
    wide = lambda ref: ref[...].astype(FLOAT)
    first = wide(first_own) + wide(first_near) + wide(first_far)
    second = wide(second_own) + wide(second_near) + wide(second_far)
    inner = (chosen_ref[...] * first[:, half:]).astype(BFLOAT)
    shards, tall, _ = lower_ref.shape
    rows = tall - NADAPT * RANK // shards
    summed = jnp.concatenate([first[:, :half], second], axis=1) + dot(
        inner, matrix_rows(lower_ref[:, :rows, :]), (1, 1)
    )
    if kind == "output":
        residual_ref, out_ref, inner_ref = refs
        inner_ref[...] = inner
        out_ref[...] = (residual_ref[...] + summed).astype(BFLOAT)
        return
    if kind == "forward":
        residual_ref, gain_ref, out_ref, inner_ref, left_ref, right_ref = refs
        hidden = residual_ref[...] + summed
        normed = (hidden * root_mean(hidden) * gain_ref[0:1, :]).astype(BFLOAT)
        out_ref[...] = hidden
    else:
        values_ref, upstream_ref, gain_ref = refs[:3]
        values = values_ref[...]
        scale = root_mean(values)
        weighted = summed * gain_ref[0:1, :]
        mean = jnp.mean(weighted * values, axis=1, keepdims=True)
        hidden = upstream_ref[...].astype(FLOAT) + scale * weighted - values * (scale * scale * scale * mean)
        normed = hidden.astype(BFLOAT)
        if kind == "input":
            out_ref, inner_ref = refs[3:]
            inner_ref[...] = inner
            out_ref[...] = normed
            return
        out_ref, inner_ref, left_ref, right_ref = refs[3:]
        out_ref[...] = hidden
    inner_ref[...] = inner
    left_ref[...] = normed[:, :half]
    right_ref[...] = normed[:, half:]


def finish(kind, parts, gathered, own_selector, *operands):
    rows = own_selector.shape[0]
    half = parts[3].shape[1]
    shards, tall, full = gathered[-1].shape
    model = HALVES * half
    result = BFLOAT if kind in ("output", "input") else FLOAT
    out_shape = [jax.ShapeDtypeStruct((rows, model), result), jax.ShapeDtypeStruct((rows, LANES), BFLOAT)]
    if kind in ("forward", "backward"):
        out_shape += [jax.ShapeDtypeStruct((rows, half), BFLOAT)] * 2
    given = [*parts, gathered[-1], own_selector, *operands]
    in_specs = [whole(value.shape) for value in given]
    in_specs[6] = pl.BlockSpec((shards, tall, LANES), lambda *_: (0, 0, full // LANES - 1))
    return pl.pallas_call(
        functools.partial(finish_kernel, kind),
        grid=(1,),
        in_specs=in_specs,
        out_specs=[whole(shape.shape) for shape in out_shape],
        out_shape=out_shape,
        compiler_params=pltpu.CompilerParams(vmem_limit_bytes=DENSE_BYTES),
        cost_estimate=pl.CostEstimate(
            flops=2 * rows * model * LANES, bytes_accessed=rows * model * 20, transcendentals=0
        ),
        name="finish_" + kind,
    )(*given)


def send_kernel(target_column, target_row, tokens_ref, adapter_ref, sent_ref, matrix_ref):
    rows = tokens_ref.shape[0]
    model = tokens_ref.shape[1]
    peer = adapter_ref.shape[0]
    column, row = target_column[:, 0:1], target_row[0:1, :]
    earlier = lax.broadcasted_iota(jnp.int32, (rows, rows), 0) < lax.broadcasted_iota(jnp.int32, (rows, rows), 1)
    same = jnp.where((column // rows == row // rows) & earlier, 1.0, 0.0)
    place = (row // rows) * peer + jnp.sum(same, axis=0, keepdims=True).astype(jnp.int32)
    matrix = (lax.broadcasted_iota(jnp.int32, (rows, rows), 0) == place).astype(BFLOAT)
    matrix_ref[...] = matrix
    sent_ref[:, :model] = dot(matrix, tokens_ref[...], (1, 0)).astype(BFLOAT)
    lane = lax.broadcasted_iota(jnp.int32, (rows, LANES), 1)
    slots = jnp.where(lane == 0, column % rows, 0).astype(FLOAT).astype(BFLOAT)
    notes = dot(matrix, slots, (1, 0))
    sent_ref[:, model:] = jnp.where(lane == 0, notes, adapter_ref[0:1, :]).astype(BFLOAT)


def send_tokens(target, tokens, adapters, peer):
    rows, model = tokens.shape
    notes = jnp.pad(adapters.astype(FLOAT), (1, LANES - 1 - adapters.shape[0]))
    return pl.pallas_call(
        send_kernel,
        in_specs=[pl.BlockSpec(memory_space=pltpu.VMEM)] * 4,
        out_specs=[pl.BlockSpec(memory_space=pltpu.VMEM)] * 2,
        out_shape=[
            jax.ShapeDtypeStruct((rows, model + LANES), BFLOAT),
            jax.ShapeDtypeStruct((rows, rows), BFLOAT),
        ],
        compiler_params=pltpu.CompilerParams(vmem_limit_bytes=DENSE_BYTES),
        name="send_tokens",
    )(
        jnp.broadcast_to(target[:, None], (rows, LANES)),
        jnp.broadcast_to(target[None, :], (8, rows)),
        tokens,
        jnp.broadcast_to(notes[None, :], (peer, LANES)),
    )


def arrive_kernel(arrived_ref, gain_ref, own_ref, matrix_ref, left_ref, right_ref):
    rows, model = own_ref.shape
    slots = arrived_ref[:, model:].astype(FLOAT).T[0:1, :]
    row = lax.broadcasted_iota(jnp.int32, (rows, rows), 0).astype(FLOAT)
    matrix = (row == slots).astype(BFLOAT)
    matrix_ref[...] = matrix
    own = dot(matrix, arrived_ref[:, :model], (1, 0))
    own_ref[...] = own
    normed = (own * root_mean(own) * gain_ref[0:1, :]).astype(BFLOAT)
    left_ref[...] = normed[:, : model // HALVES]
    right_ref[...] = normed[:, model // HALVES :]


def arrive_tokens(arrived, gain):
    rows, model = arrived.shape[0], arrived.shape[1] - LANES
    return pl.pallas_call(
        arrive_kernel,
        in_specs=[pl.BlockSpec(memory_space=pltpu.VMEM)] * 2,
        out_specs=[pl.BlockSpec(memory_space=pltpu.VMEM)] * 4,
        out_shape=[
            jax.ShapeDtypeStruct((rows, model), FLOAT),
            jax.ShapeDtypeStruct((rows, rows), BFLOAT),
            jax.ShapeDtypeStruct((rows, model // HALVES), BFLOAT),
            jax.ShapeDtypeStruct((rows, model // HALVES), BFLOAT),
        ],
        compiler_params=pltpu.CompilerParams(vmem_limit_bytes=DENSE_BYTES),
        name="arrive_tokens",
    )(arrived, gain)


GATE_WIDTH = DSSM // QUERY_HEADS
PAIR_WIDTH = 2 * KEY_VALUE_HEADS * HEAD_SIZE // QUERY_HEADS
STATE_WIDTH = 2 * NSTATE // QUERY_HEADS
STEP_WIDTH = NH // QUERY_HEADS
ALL_AXES = ("row", "col")


def pad_columns(values, width):
    return jnp.pad(values, ((0, 0), (0, width - values.shape[1])))


def after(values, *earlier):
    return lax.optimization_barrier((values, *earlier))[0]


def unit_parts(values, units):
    cuts = [0]
    for width in (GATE_WIDTH, GATE_WIDTH, HEAD_SIZE, PAIR_WIDTH, STATE_WIDTH, STEP_WIDTH):
        cuts.append(cuts[-1] + width)
    return [
        jnp.concatenate(
            [values[:, unit * UNIT_IN + low : unit * UNIT_IN + high] for unit in range(units)], axis=1
        )
        for low, high in zip(cuts[:-1], cuts[1:])
    ]


def restore_units(parts, units):
    ordered = []
    for unit in range(units):
        for part in parts:
            width = part.shape[1] // units
            ordered.append(part[:, unit * width : (unit + 1) * width])
    return jnp.concatenate(ordered, axis=1)


def split_halves(values, units, first, axis):
    block = values.shape[axis] // units
    take = lambda low, high: lax.slice_in_dim(values, low, high, axis=axis)
    parts = [take(unit * block, unit * block + first) for unit in range(units)]
    parts += [take(unit * block + first, (unit + 1) * block) for unit in range(units)]
    return jnp.concatenate(parts, axis=axis)


def join_halves(values, units, first, axis):
    block = values.shape[axis] // units
    rest = block - first
    take = lambda low, high: lax.slice_in_dim(values, low, high, axis=axis)
    parts = []
    for unit in range(units):
        parts.append(take(unit * first, (unit + 1) * first))
        parts.append(take(units * first + unit * rest, units * first + (unit + 1) * rest))
    return jnp.concatenate(parts, axis=axis)


def quick(rows):
    return lax.axis_size("col") == 4 and lax.axis_size("row") == 8 and rows == 256


def flip(values, mask):
    return lax.ppermute(values, "col", [(i, i ^ mask) for i in range(4)])


def gather_blocks(halves):
    left, right = halves
    far_left, near_right = flip(left, 2), flip(right, 1)
    near_left, far_right = flip(left, 1), flip(right, 2)
    corner_left, corner_right = flip(far_left, 1), flip(near_right, 2)
    return [
        (0, (left, right)),
        (1, (near_left, near_right)),
        (2, (far_left, far_right)),
        (3, (corner_left, corner_right)),
    ]


def rows_of(values, block, rows):
    return lax.dynamic_slice_in_dim(values, block * rows, rows, 0)


def spread_project(halves, gathered, selector):
    rows = halves[0].shape[0]
    if quick(rows):
        held = None
        for mask, values in gather_blocks(halves):
            held = spread_block(mask, values, gathered, selector, held)
        return held
    wide, narrow_factor = gathered
    width = narrow_factor.shape[1]
    both = product(lax.all_gather(jnp.concatenate(halves, axis=1), "col", axis=0, tiled=True), wide)
    narrow = (selector * both[:, width:]).astype(BFLOAT)
    return (both[:, :width] + product(narrow, narrow_factor)).astype(BFLOAT), narrow


def collect_project(values, gathered, kind, own_selector, *operands):
    rows, model = own_selector.shape[0], operands[0].shape[1]
    if quick(rows):
        wide = lambda part: part.astype(FLOAT)
        (corner,) = collect_blocks([3], values, gathered, [(BFLOAT, BFLOAT)])
        corner_first, corner_second = flip(corner[0], 1), flip(corner[1], 2)
        near, far = collect_blocks([1, 2], values, gathered, [(BFLOAT, FLOAT), (FLOAT, BFLOAT)])
        near_first, far_second = flip(near[0], 1), flip(far[1], 2)
        (own,) = collect_blocks([0], values, gathered, [(FLOAT, FLOAT)])
        far_first = flip((far[0] + wide(corner_first)).astype(BFLOAT), 2)
        near_second = flip((near[1] + wide(corner_second)).astype(BFLOAT), 1)
        parts = [own[0], near_first, far_first, own[1], far_second, near_second]
        return finish(kind, parts, gathered, own_selector, *operands)
    wide, narrow_factor = gathered
    width = narrow_factor.shape[1]
    partial = jnp.concatenate(
        [contract_last(values, wide[:, :width]), contract_last(values, narrow_factor)], axis=1
    ).astype(BFLOAT)
    summed = lax.psum_scatter(partial, "col", scatter_dimension=0, tiled=True).astype(FLOAT)
    inner = (own_selector * summed[:, model:]).astype(BFLOAT)
    summed = summed[:, :model] + contract_last(inner, wide[:, width:])
    if kind == "output":
        return (operands[0] + summed).astype(BFLOAT), inner
    if kind == "forward":
        residual, gain = operands
        hidden = residual + summed
        return hidden, inner, *cut_halves(rms_norm(hidden, gain[0]).astype(BFLOAT))
    values, upstream, gain = operands
    _, back = jax.vjp(lambda given: rms_norm(given, gain[0]), values)
    hidden = upstream.astype(FLOAT) + back(summed)[0]
    if kind == "input":
        return hidden.astype(BFLOAT), inner
    return hidden, inner, *cut_halves(hidden.astype(BFLOAT))


def cut_halves(values):
    half = values.shape[1] // HALVES
    return values[:, :half], values[:, half:]


def local(
    tokens_in,
    cotangent,
    target,
    sequence_lengths,
    sequence_adapter,
    norm_gains,
    weight_in,
    conv_values,
    conv_states,
    scan_params,
    weight_mix,
    weight_feed,
    weight_down,
    in_lower,
    in_raise,
    mix_lower,
    mix_raise,
    feed_lower,
    feed_raise,
    down_lower,
    down_raise,
):
    cols = lax.axis_size("col")
    rows_axis = lax.axis_size("row")
    col = lax.axis_index("col")
    devices = cols * rows_axis
    rows = tokens_in.shape[0]
    model = tokens_in.shape[1]
    total = rows * cols
    units = QUERY_HEADS // cols
    channels = units * GATE_WIDTH
    peer = rows // devices
    lengths, adapters = sequence_lengths[0], sequence_adapter[0]
    sequences = lengths.shape[0]
    fast = quick(rows)
    key_head = col * units // (QUERY_HEADS // KEY_VALUE_HEADS)
    exchange = lambda values: lax.all_to_all(values, ALL_AXES, split_axis=0, concat_axis=0, tiled=True)

    sent, send_matrix = send_tokens(target, tokens_in, adapters, peer)
    arrived = exchange(sent)

    def gather_weight(weight, lower, raised):
        top = jnp.concatenate([weight, lower], axis=1)
        if fast:
            bottom = pad_columns(raised, top.shape[1])
            return (lax.all_gather(jnp.concatenate([top, bottom], axis=0), "row", axis=0),)
        wide = lax.all_gather(top, "row", axis=0, tiled=True)
        return wide, lax.all_gather(raised, "row", axis=0, tiled=True)

    depth = weight_in.shape[0]
    height = depth + in_raise.shape[0]
    given = after(jnp.concatenate([weight_in, in_raise], axis=0), send_matrix)
    gates, convs, queries, pairs, states, steps = unit_parts(given, units)
    pair_width, state_width = pairs.shape[1], states.shape[1]
    taps = jnp.concatenate([jnp.zeros((KCONV + 1, pair_width), BFLOAT), conv_states], axis=1)
    taps = jnp.pad(taps, ((0, 16 - KCONV - 1), (0, 0)))
    shared = jnp.concatenate([jnp.concatenate([pairs, states], axis=1), taps], axis=0)
    if fast:
        shared = lax.all_gather(shared, "row", axis=0)
        held = jnp.zeros((cols,) + shared.shape, BFLOAT)
        near, far = flip(shared, 1), flip(shared, 2)
        for block, values in ((col, shared), (col ^ 1, near), (col ^ 2, far)):
            held = lax.dynamic_update_index_in_dim(held, values, block, 0)
        split = shared.shape[0] // 2
        corner = jnp.concatenate([flip(near[:split], 2), flip(far[split:], 1)], axis=0)
        held = lax.dynamic_update_index_in_dim(held, corner, col ^ 3, 0)
    else:
        held = lax.all_gather(shared, "col", axis=0)
    all_pairs = jnp.concatenate([held[at, ..., :height, :pair_width] for at in range(cols)], axis=-1)
    pick = lambda start: lax.select_n(
        key_head,
        *[all_pairs[..., start + at * HEAD_SIZE : start + (at + 1) * HEAD_SIZE] for at in range(KEY_VALUE_HEADS)],
    )
    shared_columns = jnp.concatenate(
        [held[at, ..., :height, pair_width:] for at in range(cols)]
        + [pick(0), pick(KEY_VALUE_HEADS * HEAD_SIZE)],
        axis=-1,
    )
    tap_rows = held[:, 0] if fast else held
    all_taps = jnp.concatenate(
        [tap_rows[at, height : height + KCONV + 1, pair_width:] for at in range(cols)], axis=1
    )
    own_columns = [gates, convs, queries, pad_columns(steps, LANES)]
    if fast:
        own_columns = jnp.concatenate(own_columns, axis=1)
        weights_in = (shared_columns, *gather_weight(own_columns[:depth], in_lower, own_columns[depth:]))
    else:
        columns = jnp.concatenate([shared_columns, *own_columns], axis=1)
        weights_in = gather_weight(columns[:depth], in_lower, columns[depth:])
    weights_mix = gather_weight(
        after(split_halves(weight_mix, units, GATE_WIDTH, 0).T, send_matrix),
        mix_raise.T,
        split_halves(mix_lower, units, GATE_WIDTH, 0).T,
    )
    weights_feed = gather_weight(
        after(split_halves(weight_feed, units, UNIT_FF, 1), arrived),
        feed_lower,
        split_halves(feed_raise, units, UNIT_FF, 1),
    )

    gains = jnp.broadcast_to(norm_gains.astype(FLOAT)[:, None, :], (2, 8, model))
    own_input, place_matrix, *normed_one = arrive_tokens(arrived.reshape(rows, model + LANES), gains[0])
    source_adapters = arrived.reshape(rows, model + LANES)[::peer, model + 1 : model + 1 + sequences].astype(jnp.int32)
    segment, position, selector = sequence_tables(lengths, adapters, total)
    own_selector = rows_of(selector, col, rows)
    own_segment = rows_of(segment, col, rows)
    tables = mixer_tables(lengths, segment, position, conv_values, all_taps, scan_params)

    def compact_grad(narrow, values):
        parts = [
            lax.dynamic_slice_in_dim(narrow, adapters[at] * RANK, RANK, 1)
            * (own_segment == at).astype(BFLOAT)[:, None]
            for at in range(sequences)
        ]
        grad = contract_first(jnp.concatenate(parts, axis=1), values).astype(BFLOAT)
        kept = sequences * RANK
        grad = grad.reshape(kept, devices, model // devices).transpose(1, 0, 2)
        return grad.reshape(devices, peer, kept * model // devices // peer)

    def expand_grad(dealt):
        kept = sequences * RANK
        dealt = dealt.reshape(devices * kept, model // devices)
        adapter_row = (source_adapters[:, :, None] * RANK + jnp.arange(RANK, dtype=jnp.int32)).reshape(-1)
        chosen = (jnp.arange(NADAPT * RANK, dtype=jnp.int32)[:, None] == adapter_row[None, :]).astype(BFLOAT)
        return product(chosen, dealt)

    def send_back(values, grads):
        back = contract_first(place_matrix, values).astype(BFLOAT).reshape(devices, peer, model)
        return exchange(jnp.concatenate([back, *grads], axis=2))

    def take_back(dealt, count):
        returned = contract_first(send_matrix, dealt[:, :, :model].reshape(rows, model)).astype(BFLOAT)
        width = (dealt.shape[2] - model) // max(count, 1)
        return returned, [
            expand_grad(dealt[:, :, model + at * width : model + (at + 1) * width]) for at in range(count)
        ]

    projected, inner_in = spread_project(normed_one, weights_in, selector)

    sent_grad = product(send_matrix, cotangent).astype(BFLOAT).reshape(devices, peer, model)
    arrived_grad = exchange(after(sent_grad, normed_one[0])).reshape(rows, model)
    branch_two = product(place_matrix, arrived_grad).astype(BFLOAT)
    weights_down = gather_weight(after(weight_down.T, normed_one[0]), down_raise.T, down_lower.T)

    mixed_out = attention_forward(projected, tables)
    mixed_out, scanned, carried = scan_forward(projected, tables, mixed_out)
    hidden, inner_out, *normed_two = collect_project(mixed_out, weights_mix, "forward", own_selector, own_input, gains[1])
    gate_up, inner_feed = spread_project(normed_two, weights_feed, selector)
    act_grad, narrow_two = spread_project(cut_halves(after(branch_two, projected)), weights_down, selector)
    half_feed = units * UNIT_FF
    gate_part, up_part = gate_up[:, :half_feed].astype(FLOAT), gate_up[:, half_feed:].astype(FLOAT)
    gate = jax.nn.sigmoid(gate_part)
    silu = gate_part * gate
    activated = (silu * up_part).astype(BFLOAT)
    wide_grad = act_grad.astype(FLOAT)
    feed_grad = jnp.concatenate(
        [wide_grad * up_part * (gate * (1.0 + gate_part * (1.0 - gate))), wide_grad * silu], axis=1
    ).astype(BFLOAT)
    hidden_grad, narrow_three, *branch_one = collect_project(
        feed_grad, weights_feed, "backward", own_selector, hidden, branch_two, gains[1]
    )
    mixed_grad, narrow_one = spread_project(branch_one, weights_mix, selector)

    block_out, inner_down = collect_project(
        after(activated, mixed_grad), weights_down, "output", own_selector, hidden
    )
    query_grad, key_grad, value_grad = attention_backward(projected, tables, mixed_grad)
    projected_grad = scan_backward(
        projected, tables, scanned, carried, mixed_grad, query_grad, key_grad, value_grad
    )
    dealt_out = send_back(
        block_out,
        [
            compact_grad(inner_down, branch_two),
            compact_grad(narrow_three, jnp.concatenate(normed_two, axis=1)),
            compact_grad(inner_out, jnp.concatenate(branch_one, axis=1)),
        ],
    )

    def sum_rows(values):
        return lax.psum_scatter(values.astype(BFLOAT), "row", scatter_dimension=0, tiled=True).astype(FLOAT)

    early_parts = [
        contract_first(narrow_one, mixed_out),
        contract_first(inner_feed, feed_grad),
        contract_first(narrow_two, activated),
    ]
    early = sum_rows(jnp.concatenate(early_parts, axis=1))
    early_cuts = [0, early_parts[0].shape[1]]
    early_cuts.append(early_cuts[1] + early_parts[1].shape[1])
    grad_mix_lower = join_halves(early[:, : early_cuts[1]], units, GATE_WIDTH, 1).T
    grad_feed_raise = join_halves(early[:, early_cuts[1] : early_cuts[2]], units, UNIT_FF, 1)
    grad_down_lower = early[:, early_cuts[2] :].T

    raise_grad = contract_first(inner_in, projected_grad)
    key_columns = raise_grad[:, STATES : STATES + HEAD_SIZE]
    value_columns = raise_grad[:, STATES + HEAD_SIZE : STATES + PAIR]
    mine = [(key_head == at).astype(FLOAT) for at in range(KEY_VALUE_HEADS)]
    pair_grad = jnp.concatenate([part * here for part in (key_columns, value_columns) for here in mine], axis=1)
    stacked = jnp.stack(
        [
            jnp.concatenate(
                [
                    pair_grad[:, at * pair_width : (at + 1) * pair_width],
                    raise_grad[:, at * state_width : (at + 1) * state_width],
                ],
                axis=1,
            )
            for at in range(cols)
        ]
    )
    if fast:
        to_send = stacked.astype(BFLOAT)
        piece = lambda block: lax.dynamic_index_in_dim(to_send, block, 0, False)
        near_sum = lambda block: lax.dynamic_index_in_dim(stacked, block, 0, False)
        pair_sums = flip(jnp.stack([piece(col ^ 1), piece(col ^ 3)]), 1).astype(FLOAT)
        far_sum = (near_sum(col ^ 2) + pair_sums[1]).astype(BFLOAT)
        shared_sum = near_sum(col) + pair_sums[0] + flip(far_sum, 2).astype(FLOAT)
    else:
        shared_sum = lax.psum_scatter(
            stacked.astype(BFLOAT).reshape(cols * NADAPT * RANK, -1), "col", scatter_dimension=0, tiled=True
        ).astype(FLOAT)
    late = sum_rows(jnp.concatenate([shared_sum, raise_grad[:, STATES + PAIR :]], axis=1))
    shared_width = pair_width + state_width
    cuts = [shared_width]
    for width in (channels, channels, units * HEAD_SIZE, units * STEP_WIDTH):
        cuts.append(cuts[-1] + width)
    gate_columns, conv_columns, query_columns, step_columns = [
        late[:, low:high] for low, high in zip(cuts[:-1], cuts[1:])
    ]
    grad_in_raise = restore_units(
        [
            gate_columns,
            conv_columns,
            query_columns,
            late[:, :pair_width],
            late[:, pair_width:shared_width],
            step_columns,
        ],
        units,
    )

    input_grad, narrow_four = collect_project(
        after(projected_grad, dealt_out), weights_in, "input", own_selector, own_input, hidden_grad, gains[0]
    )
    dealt_grad = send_back(input_grad, [compact_grad(narrow_four, jnp.concatenate(normed_one, axis=1))])
    returned_out, (grad_down_raise, grad_feed_lower, grad_mix_raise) = take_back(dealt_out, 3)
    returned_grad, (grad_in_lower,) = take_back(dealt_grad, 1)
    return (
        returned_out,
        returned_grad,
        grad_in_lower.T,
        grad_in_raise,
        grad_mix_lower,
        grad_mix_raise,
        grad_feed_lower.T,
        grad_feed_raise,
        grad_down_lower,
        grad_down_raise,
    )


def solution(mesh):
    in_specs = (
        P(("row", "col"), None),
        P(("row", "col"), None),
        P(("row", "col")),
        P("row", None),
        P("row", None),
        P(),
        P("row", "col"),
        P(None, "col"),
        P(None, "col"),
        P(None, "col"),
        P("col", "row"),
        P("row", "col"),
        P("col", "row"),
        P("row", None),
        P("row", "col"),
        P("col", "row"),
        P(None, "row"),
        P("row", None),
        P("row", "col"),
        P("col", "row"),
        P(None, "row"),
    )
    out_specs = (
        P(("row", "col"), None),
        P(("row", "col"), None),
        P(("row", "col"), None),
        P("row", "col"),
        P("col", "row"),
        P(None, ("row", "col")),
        P(("row", "col"), None),
        P("row", "col"),
        P("col", "row"),
        P(None, ("row", "col")),
    )
    return jax.shard_map(local, mesh=mesh, in_specs=in_specs, out_specs=out_specs, check_vma=False)
```

time: 847 us -> 720 us (0.85)
  matrix products: 209 us -> 21.9 us
  Pallas kernels: 56.6 us -> 190 us
  waiting for transfers between devices: 318 us -> 242 us
  other arithmetic: 59.2 us -> 48.2 us
  starting transfers between devices: 72.7 us -> 82.5 us
    pallas_call x1 -> x35, Pallas kernels: 13.5 us -> 152 us  [the longest x16 89.8 us: spread_block(): pl.pallas_call(functools.partial(spread_kernel, mask, len(gathered)), in_...]
    dot_general x44 -> x6, matrix products: 130 us -> 6.57 us  [product(): return jnp.dot(left, right, preferred_element_type=FLOAT)]
    all_to_all x4, waiting for transfers between devices: 140 us -> 52 us  [local(): lax.all_to_all(values, ALL_AXES, split_axis=0, concat_axis=0, tiled=True)]
    dot_general x51 -> x0, matrix products: 67.4 us -> none  [contract_last(): lax.dot_general(left, right, (((1,), (1,)), ((), ())), preferred_element_...]
    reduce_scatter x2, waiting for transfers between devices: 0.02 us -> 29.4 us  [sum_rows(): lax.psum_scatter(values.astype(BFLOAT), 'row', scatter_dimension=0, tiled...]
    ppermute x50 -> x54, waiting for transfers between devices: 147 us -> 129 us  [flip(): return lax.ppermute(values, 'col', [(i, i ^ mask) for i in range(4)])]
    unnamed x297 -> x254, local copies, waits for them, and re-layouts: 52.6 us -> 66.8 us
    slice x49 -> x16, local copies, waits for them, and re-layouts: 24.5 us -> 12.5 us  [the longest x4 2.83 us: restore_units(): ordered.append(part[:, unit * width:(unit + 1) * width])]
  transfers between devices with their start and end apart: 61 -> 65, of which waited for: 27 -> 25; matrix products, arithmetic and copies ran while one was open for 35% -> 13% of each run, Pallas kernels for 7% -> 23%
where the time goes in v3:
time: 720 us; the launch traced here: 710 us
  waiting for transfers between devices  242 us (34%)
  Pallas kernels  190 us (26%)
  local copies, waits for them, and re-layouts  107 us (15%)
  starting transfers between devices  82.5 us (11%)
  other arithmetic  48.2 us (7%)
  matrix products  21.9 us (3%)
  between operations  17.9 us (2%)
    ppermute x54, waiting for transfers between devices, flip(): return lax.ppermute(values, 'col', [(i, i ^ mask) for i in range(4)])  129 us
    pallas_call x16, Pallas kernels, spread_block(): pl.pallas_call(functools.partial(spread_kernel, mask, len(gathered)), in_...  89.8 us
    unnamed x254, local copies, waits for them, and re-layouts  66.8 us
    ppermute x54, starting transfers between devices, flip(): return lax.ppermute(values, 'col', [(i, i ^ mask) for i in range(4)])  62 us
    all_to_all x4, waiting for transfers between devices, local(): lax.all_to_all(values, ALL_AXES, split_axis=0, concat_axis=0, tiled=True)  52 us
    pallas_call x12, Pallas kernels, collect_blocks(): pl.pallas_call(functools.partial(collect_kernel, masks, len(gathered)), i...  37.7 us
    all_gather x4, waiting for transfers between devices, gather_weight(): lax.all_gather(jnp.concatenate([top, bottom], axis=0), 'row', axis=0)  31 us
    reduce_scatter x2, waiting for transfers between devices, sum_rows(): lax.psum_scatter(values.astype(BFLOAT), 'row', scatter_dimension=0, tiled...  29.4 us
  transfers between devices with their start and end apart: 65, of which 25 were waited for; matrix products, arithmetic and copies ran while one was open for 13% of the time, Pallas kernels for 23%

profile of v3, /device:TPU:0, one launch (start us, length us, event | category | flops | bytes accessed | tf_op | source)
XLA Modules:
  0.0 709.8 jit_solution(8602641086130864483)
XLA Ops:
  18.7 7.3 %all-to-all-start = ((bf16[32,8,2176]{2,1,0:T(8,128)(2,1)}), bf16[32,8,2176]{2,1,0:T(8,128)(2,1)S(1)}, u32[]{:S(2)}, u32[]{:S(2)}) async-start(bf16[32,8,2176]{2,1,0:T(8,128)(2,1)} %bitcast.1), calls=%async_computation | async-start | bytes 2228224 | tf_op jit(solution)/shard_map/all_to_all | solution.py:1039
  27.0 35.0 %all-to-all-done = bf16[32,8,2176]{2,1,0:T(8,128)(2,1)S(1)} async-done(((bf16[32,8,2176]{2,1,0:T(8,128)(2,1)}), bf16[32,8,2176]{2,1,0:T(8,128)(2,1)S(1)}, u32[]{:S(2)}, u32[]{:S(2)}) %all-to-all-start) | async-done | bytes 1114144 | tf_op jit(solution)/shard_map/all_to_all | solution.py:1039
  83.7 15.0 %collective-permute-done.4 = bf16[8,288,256]{2,1,0:T(8,128)(2,1)} collective-permute-done((bf16[8,288,256]{2,1,0:T(8,128)(2,1)}, bf16[8,288,256]{2,1,0:T(8,128)(2,1)}, u32[]{:S(2)}, u32[]{:S(2)}) %collective-permute-start.4) | collective-permute-done | bytes 1179680 | tf_op jit(solution)/shard_map/ppermute | solution.py:928
  120.4 15.3 %collective-permute-done.2.right_ref = bf16[256,1024]{1,0:T(8,128)(2,1)S(1)} collective-permute-done((bf16[256,1024]{1,0:T(8,128)(2,1)}, bf16[256,1024]{1,0:T(8,128)(2,1)S(1)}, u32[]{:S(2)}, u32[]{:S(2)}) %collective-permute-start.2) | collective-permute-done | bytes 524320 | tf_op jit(solution)/shard_map/ppermute | solution.py:928
  137.7 8.6 %collective-permute-done.left_ref = bf16[256,1024]{1,0:T(8,128)(2,1)S(1)} collective-permute-done((bf16[256,1024]{1,0:T(8,128)(2,1)}, bf16[256,1024]{1,0:T(8,128)(2,1)S(1)}, u32[]{:S(2)}, u32[]{:S(2)}) %collective-permute-start) | collective-permute-done | bytes 524320 | tf_op jit(solution)/shard_map/ppermute | solution.py:928
  168.3 8.9 %spread_block.16 = (bf16[1024,2688]{1,0:T(8,128)(2,1)S(1)}, bf16[1024,128]{1,0:T(8,128)(2,1)S(1)}) custom-call(bf16[256,1024]{1,0:T(8,128)(2,1)} %get-tuple-element.109.left_ref, bf16[256,1024]{1,0:T(8,128)(2,1)} %get-tuple-element.110.right_ref, f32[1024,128]{1,0:T(8,128)S(1)} %compare_convert_fusion.chosen_ref, bf16[8,272,768]{2,1,0:T(8,128)(2,1)S(1)} %copy-done.16, ...), custom_call_target="tpu_custom_call" | custom-call | flops 2952790016 | bytes 2424832 | tf_op jit(solution)/shard_map/spread_block/pallas_call | solution.py:649
  177.3 8.6 %spread_block.17 = (bf16[1024,2688]{1,0:T(8,128)(2,1)S(1)}, bf16[1024,128]{1,0:T(8,128)(2,1)S(1)}) custom-call(bf16[256,1024]{1,0:T(8,128)(2,1)} %collective-permute-done.9.left_ref, bf16[256,1024]{1,0:T(8,128)(2,1)S(1)} %collective-permute-done.2.right_ref, ...), custom_call_target="tpu_custom_call", output_to_operand_aliasing={{0}: (5, {}), {1}: (6, {})} | custom-call | flops 2952790016 | bytes 2424832 | tf_op jit(solution)/shard_map/spread_block/pallas_call | solution.py:649
  185.9 18.9 %spread_block.18 = (bf16[1024,2688]{1,0:T(8,128)(2,1)S(1)}, bf16[1024,128]{1,0:T(8,128)(2,1)S(1)}) custom-call(bf16[256,1024]{1,0:T(8,128)(2,1)S(1)} %collective-permute-done.left_ref, bf16[256,1024]{1,0:T(8,128)(2,1)S(1)} %collective-permute-done.8.right_ref, ...), custom_call_target="tpu_custom_call", output_to_operand_aliasing={{0}: (5, {}), {1}: (6, {})} | custom-call | flops 2952790016 | bytes 2424832 | tf_op jit(solution)/shard_map/spread_block/pallas_call | solution.py:649
  204.8 8.6 %spread_block.19 = (bf16[1024,2688]{1,0:T(8,128)(2,1)S(1)}, bf16[1024,128]{1,0:T(8,128)(2,1)S(1)}) custom-call(bf16[256,1024]{1,0:T(8,128)(2,1)} %collective-permute-done.1.left_ref, bf16[256,1024]{1,0:T(8,128)(2,1)S(1)} %collective-permute-done.3.right_ref, ...), custom_call_target="tpu_custom_call", output_to_operand_aliasing={{0}: (5, {}), {1}: (6, {})} | custom-call | flops 2952790016 | bytes 2424832 | tf_op jit(solution)/shard_map/spread_block/pallas_call | solution.py:649
  218.1 13.1 %scan_forward.1 = (bf16[1024,1024]{1,0:T(8,128)(2,1)S(1)}, f32[1024,768]{1,0:T(8,128)S(1)}, bf16[4,256,768]{2,1,0:T(8,128)(2,1)S(1)}) custom-call(bf16[1024,2688]{1,0:T(8,128)(2,1)S(1)} %get-tuple-element.118.query_ref.key_ref.value_ref.gate_ref.conv_ref.before_ref.state_ref.state_before_ref.step_ref, ...), custom_call_target="tpu_custom_call", output_to_operand_aliasing={{0}: (12, {})} | custom-call | flops 1342177280 | bytes 9437184 | tf_op jit(solution)/shard_map/scan_forward/pallas_call | solution.py:364
  261.1 9.3 %collective-permute-done.24.right_ref = bf16[256,1024]{1,0:T(8,128)(2,1)} collective-permute-done((bf16[256,1024]{1,0:T(8,128)(2,1)}, bf16[256,1024]{1,0:T(8,128)(2,1)}, u32[]{:S(2)}, u32[]{:S(2)}) %collective-permute-start.24) | collective-permute-done | bytes 524320 | tf_op jit(solution)/shard_map/ppermute | solution.py:928
  272.5 6.0 collective-permute-done.13.second_near
  285.1 9.2 %collective-permute-done.15.second_far = bf16[256,1024]{1,0:T(8,128)(2,1)} collective-permute-done((bf16[256,1024]{1,0:T(8,128)(2,1)}, bf16[256,1024]{1,0:T(8,128)(2,1)}, u32[]{:S(2)}, u32[]{:S(2)}) %collective-permute-start.15) | collective-permute-done | bytes 524320 | tf_op jit(solution)/shard_map/ppermute | solution.py:928
  330.0 30.9 %all-gather.17.cloned.1.call-done = bf16[2176,2176]{1,0:T(8,128)(2,1)} async-done(((bf16[272,2176]{1,0:T(8,128)(2,1)}), bf16[2176,2176]{1,0:T(8,128)(2,1)}) %all-gather.17.cloned.1.call-update) | async-done | bytes 9469968 | tf_op jit(solution)/shard_map/all_gather | solution.py:1048
  402.8 7.0 collective-permute-done.29
  422.4 10.6 %collective-permute-done.33.second_far = bf16[256,1024]{1,0:T(8,128)(2,1)S(1)} collective-permute-done((bf16[256,1024]{1,0:T(8,128)(2,1)S(1)}, bf16[256,1024]{1,0:T(8,128)(2,1)S(1)}, u32[]{:S(2)}, u32[]{:S(2)}) %collective-permute-start.33) | collective-permute-done | bytes 524320 | tf_op jit(solution)/shard_map/ppermute | solution.py:928
  477.3 7.3 %attention_backward.1 = (bf16[1024,256]{1,0:T(8,128)(2,1)S(1)}, bf16[1024,128]{1,0:T(8,128)(2,1)S(1)}, bf16[1024,128]{1,0:T(8,128)(2,1)S(1)}) custom-call(bf16[1024,2688]{1,0:T(8,128)(2,1)S(1)} %bitcast.144, bf16[1024,2688]{1,0:T(8,128)(2,1)S(1)} %bitcast.144, bf16[1024,2688]{1,0:T(8,128)(2,1)S(1)} %bitcast.144, f32[1024,128]{1,0:T(8,128)S(1)} %copy-done.36, ...), custom_call_target="tpu_custom_call" | custom-call | flops 1610612736 | bytes 6291456 | tf_op jit(solution)/shard_map/attention_backward/pallas_call | solution.py:531
  492.9 26.7 %scan_backward.1.values_ref = bf16[1024,2688]{1,0:T(8,128)(2,1)S(1)} custom-call(bf16[1024,2688]{1,0:T(8,128)(2,1)S(1)} %bitcast.144, bf16[1024,2688]{1,0:T(8,128)(2,1)S(1)} %bitcast.144, bf16[1024,2688]{1,0:T(8,128)(2,1)S(1)} %bitcast.144, bf16[1024,2688]{1,0:T(8,128)(2,1)S(1)} %bitcast.144, bf16[1024,2688]{1,0:T(8,128)(2,1)S(1)} %bitcast.144, ...), custom_call_target="tpu_custom_call" | custom-call | flops 2684354560 | bytes 18874368 | tf_op jit(solution)/shard_map/scan_backward/pallas_call | solution.py:391
  529.4 9.0 %collective-permute-done.52 = bf16[2,128,256]{2,1,0:T(8,128)(2,1)S(1)} collective-permute-done((bf16[2,128,256]{2,1,0:T(8,128)(2,1)S(1)}, bf16[2,128,256]{2,1,0:T(8,128)(2,1)S(1)}, u32[]{:S(2)}, u32[]{:S(2)}) %collective-permute-start.52) | collective-permute-done | bytes 131104 | tf_op jit(solution)/shard_map/ppermute | solution.py:928
  562.1 7.0 collective-permute-done.53
  576.9 29.4 %reduce-scatter.3.cloned.1.call-done = bf16[16,2176]{1,0:T(8,128)(2,1)} async-done(((bf16[128,2176]{1,0:T(8,128)(2,1)}), bf16[16,2176]{1,0:T(8,128)(2,1)}) %reduce-scatter.3.cloned.1.call-update) | async-done | bytes 69648 | tf_op jit(solution)/shard_map/reduce_scatter | solution.py:1183
  621.3 7.6 %collect_blocks.22 = (bf16[256,1152]{1,0:T(8,128)(2,1)}, f32[256,1024]{1,0:T(8,128)S(1)}, f32[256,1152]{1,0:T(8,128)S(1)}, bf16[256,1024]{1,0:T(8,128)(2,1)}) custom-call(bf16[1024,2688]{1,0:T(8,128)(2,1)S(1)} %copy-done.19, bf16[8,272,768]{2,1,0:T(8,128)(2,1)S(1)} %copy-done.17, bf16[8,272,2048]{2,1,0:T(8,128)(2,1)S(1)} %bitcast.158), custom_call_target="tpu_custom_call" | custom-call | flops 5637144576 | bytes 6946816 | tf_op jit(solution)/shard_map/collect_blocks/pallas_call | solution.py:712
  648.4 6.7 collective-permute-done.51.second_far
  683.0 17.1 %all-to-all-done.3 = bf16[32,8,2304]{2,1,0:T(8,128)(2,1)S(1)} async-done(((bf16[32,8,2304]{2,1,0:T(8,128)(2,1)}), bf16[32,8,2304]{2,1,0:T(8,128)(2,1)S(1)}, u32[]{:S(2)}, u32[]{:S(2)}) %all-to-all-start.3) | async-done | bytes 1179680 | tf_op jit(solution)/shard_map/all_to_all | solution.py:1039
  (568 shorter events, 368.8 us)
Async XLA Ops:
  7.2 63.2 %all-gather.11.cloned.1.call-start = ((), (), s32[]{:S(2)}) async-start(), calls=%async_computation.8 | async-start | bytes 1327104 | tf_op jit(solution)/shard_map/all_gather | solution.py:1061
  14.7 147.9 %all-gather.13.cloned.1.call-start = ((), (), s32[]{:S(2)}) async-start(), calls=%async_computation.9 | async-start | bytes 10027008 | tf_op jit(solution)/shard_map/all_gather | solution.py:1048
  16.8 217.9 %all-gather.15.cloned.1.call-start = ((), (), s32[]{:S(2)}) async-start(), calls=%async_computation.10 | async-start | bytes 5640192 | tf_op jit(solution)/shard_map/all_gather | solution.py:1048
  18.7 43.3 %all-to-all-start = ((bf16[32,8,2176]{2,1,0:T(8,128)(2,1)}), bf16[32,8,2176]{2,1,0:T(8,128)(2,1)S(1)}, u32[]{:S(2)}, u32[]{:S(2)}) async-start(bf16[32,8,2176]{2,1,0:T(8,128)(2,1)} %bitcast.1), calls=%async_computation | async-start | bytes 2228224 | tf_op jit(solution)/shard_map/all_to_all | solution.py:1039
  26.0 280.9 %all-gather.19.cloned.1.call-start = ((), (), s32[]{:S(2)}) async-start(), calls=%async_computation.12 | async-start | bytes 5640192 | tf_op jit(solution)/shard_map/all_gather | solution.py:1048
  66.7 294.2 %all-gather.17.cloned.1.call-start = ((), (), s32[]{:S(2)}) async-start(), calls=%async_computation.11 | async-start | bytes 10653696 | tf_op jit(solution)/shard_map/all_gather | solution.py:1048
  100.6 47.4 %collective-permute-start.6 = (bf16[4,288,256]{2,1,0:T(8,128)(2,1)}, bf16[4,288,256]{2,1,0:T(8,128)(2,1)}, u32[]{:S(2)}, u32[]{:S(2)}) collective-permute-start(bf16[4,288,256]{2,1,0:T(8,128)(2,1)} %slice.428), channel_id=1, source_target_pairs={{0,2},{1,3},{2,0},{3,1},{4,6},{5,7},{6,4},{7,5},{8,10},{9,11},{10,... | collective-permute-start | bytes 1769480 | tf_op jit(solution)/shard_map/ppermute | solution.py:928
  104.0 45.7 %collective-permute-start.7 = (bf16[4,288,256]{2,1,0:T(8,128)(2,1)}, bf16[4,288,256]{2,1,0:T(8,128)(2,1)}, u32[]{:S(2)}, u32[]{:S(2)}) collective-permute-start(bf16[4,288,256]{2,1,0:T(8,128)(2,1)} %slice.429), channel_id=1, source_target_pairs={{0,1},{1,0},{2,3},{3,2},{4,5},{5,4},{6,7},{7,6},{8,9},{9,8},{10,11... | collective-permute-start | bytes 1769480 | tf_op jit(solution)/shard_map/ppermute | solution.py:928
  109.3 76.6 %collective-permute-start.8 = (bf16[256,1024]{1,0:T(8,128)(2,1)}, bf16[256,1024]{1,0:T(8,128)(2,1)S(1)}, u32[]{:S(2)}, u32[]{:S(2)}) collective-permute-start(bf16[256,1024]{1,0:T(8,128)(2,1)} %get-tuple-element.110.right_ref), channel_id=1, source_target_pairs={{0,2},{1,3},{2,0},{3,1},{4,6},{5,7},{6,4},{7,5},{8,10},{9,11},{10,... | collective-permute-start | bytes 1572872 | tf_op jit(solution)/shard_map/ppermute | solution.py:928
  110.4 35.9 %collective-permute-start = (bf16[256,1024]{1,0:T(8,128)(2,1)}, bf16[256,1024]{1,0:T(8,128)(2,1)S(1)}, u32[]{:S(2)}, u32[]{:S(2)}) collective-permute-start(bf16[256,1024]{1,0:T(8,128)(2,1)} %get-tuple-element.109.left_ref), channel_id=1, source_target_pairs={{0,2},{1,3},{2,0},{3,1},{4,6},{5,7},{6,4},{7,5},{8,10},{9,11},{10,... | collective-permute-start | bytes 1572872 | tf_op jit(solution)/shard_map/ppermute | solution.py:928
  111.9 129.1 %all-to-all-start.1 = ((bf16[32,8,2048]{2,1,0:T(8,128)(2,1)}), bf16[32,8,2048]{2,1,0:T(8,128)(2,1)}, u32[]{:S(2)}, u32[]{:S(2)}) async-start(bf16[32,8,2048]{2,1,0:T(8,128)(2,1)} %fusion.9), calls=%async_computation.1 | async-start | bytes 2097152 | tf_op jit(solution)/shard_map/all_to_all | solution.py:1039
  135.7 41.6 %collective-permute-start.9 = (bf16[256,1024]{1,0:T(8,128)(2,1)}, bf16[256,1024]{1,0:T(8,128)(2,1)}, u32[]{:S(2)}, u32[]{:S(2)}) collective-permute-start(bf16[256,1024]{1,0:T(8,128)(2,1)} %get-tuple-element.109.left_ref), channel_id=1, source_target_pairs={{0,1},{1,0},{2,3},{3,2},{4,5},{5,4},{6,7},{7,6},{8,9},{9,8},{10,11... | collective-permute-start | bytes 1572872 | tf_op jit(solution)/shard_map/ppermute | solution.py:928
  146.3 58.4 %collective-permute-start.3 = (bf16[256,1024]{1,0:T(8,128)(2,1)S(1)}, bf16[256,1024]{1,0:T(8,128)(2,1)S(1)}, u32[]{:S(2)}, u32[]{:S(2)}) collective-permute-start(bf16[256,1024]{1,0:T(8,128)(2,1)S(1)} %collective-permute-done.2.right_ref), channel_id=1, source_target_pairs={{0,2},{1,3},{2,0},{3,1},{4,6},{5,7},{6,4},{7,5},{8,10},{9,11},{10,... | collective-permute-start | bytes 1572872 | tf_op jit(solution)/shard_map/ppermute | solution.py:928
  148.0 56.7 %collective-permute-start.1 = (bf16[256,1024]{1,0:T(8,128)(2,1)S(1)}, bf16[256,1024]{1,0:T(8,128)(2,1)}, u32[]{:S(2)}, u32[]{:S(2)}) collective-permute-start(bf16[256,1024]{1,0:T(8,128)(2,1)S(1)} %collective-permute-done.left_ref), channel_id=1, source_target_pairs={{0,1},{1,0},{2,3},{3,2},{4,5},{5,4},{6,7},{7,6},{8,9},{9,8},{10,11... | collective-permute-start | bytes 1572872 | tf_op jit(solution)/shard_map/ppermute | solution.py:928
  283.1 36.5 %collective-permute-start.25 = (bf16[256,1024]{1,0:T(8,128)(2,1)}, bf16[256,1024]{1,0:T(8,128)(2,1)}, u32[]{:S(2)}, u32[]{:S(2)}) collective-permute-start(bf16[256,1024]{1,0:T(8,128)(2,1)} %collective-permute-done.24.right_ref), channel_id=1, source_target_pairs={{0,2},{1,3},{2,0},{3,1},{4,6},{5,7},{6,4},{7,5},{8,10},{9,11},{10,... | collective-permute-start | bytes 1572872 | tf_op jit(solution)/shard_map/ppermute | solution.py:928
  312.8 55.6 %collective-permute-start.21 = (bf16[256,1024]{1,0:T(8,128)(2,1)S(1)}, bf16[256,1024]{1,0:T(8,128)(2,1)}, u32[]{:S(2)}, u32[]{:S(2)}) collective-permute-start(bf16[256,1024]{1,0:T(8,128)(2,1)S(1)} %get-tuple-element.130.left_ref), channel_id=1, source_target_pairs={{0,1},{1,0},{2,3},{3,2},{4,5},{5,4},{6,7},{7,6},{8,9},{9,8},{10,11... | collective-permute-start | bytes 1572872 | tf_op jit(solution)/shard_map/ppermute | solution.py:928
  319.6 53.7 %collective-permute-start.20 = (bf16[256,1024]{1,0:T(8,128)(2,1)S(1)}, bf16[256,1024]{1,0:T(8,128)(2,1)}, u32[]{:S(2)}, u32[]{:S(2)}) collective-permute-start(bf16[256,1024]{1,0:T(8,128)(2,1)S(1)} %get-tuple-element.131.right_ref), channel_id=1, source_target_pairs={{0,2},{1,3},{2,0},{3,1},{4,6},{5,7},{6,4},{7,5},{8,10},{9,11},{10,... | collective-permute-start | bytes 1572872 | tf_op jit(solution)/shard_map/ppermute | solution.py:928
  325.7 52.4 %collective-permute-start.17 = (bf16[256,1024]{1,0:T(8,128)(2,1)S(1)}, bf16[256,1024]{1,0:T(8,128)(2,1)}, u32[]{:S(2)}, u32[]{:S(2)}) collective-permute-start(bf16[256,1024]{1,0:T(8,128)(2,1)S(1)} %collective-permute-done.16.left_ref), channel_id=1, source_target_pairs={{0,1},{1,0},{2,3},{3,2},{4,5},{5,4},{6,7},{7,6},{8,9},{9,8},{10,11... | collective-permute-start | bytes 1572872 | tf_op jit(solution)/shard_map/ppermute | solution.py:928
  327.9 50.2 %collective-permute-start.19 = (bf16[256,1024]{1,0:T(8,128)(2,1)S(1)}, bf16[256,1024]{1,0:T(8,128)(2,1)}, u32[]{:S(2)}, u32[]{:S(2)}) collective-permute-start(bf16[256,1024]{1,0:T(8,128)(2,1)S(1)} %collective-permute-done.18.right_ref), channel_id=1, source_target_pairs={{0,2},{1,3},{2,0},{3,1},{4,6},{5,7},{6,4},{7,5},{8,10},{9,11},{10,... | collective-permute-start | bytes 1572872 | tf_op jit(solution)/shard_map/ppermute | solution.py:928
  490.8 48.4 %collective-permute-start.43 = (bf16[256,1024]{1,0:T(8,128)(2,1)S(1)}, bf16[256,1024]{1,0:T(8,128)(2,1)S(1)}, u32[]{:S(2)}, u32[]{:S(2)}) collective-permute-start(bf16[256,1024]{1,0:T(8,128)(2,1)S(1)} %get-tuple-element.174), channel_id=1, source_target_pairs={{0,2},{1,3},{2,0},{3,1},{4,6},{5,7},{6,4},{7,5},{8,10},{9,11},{10,... | collective-permute-start | bytes 1572872 | tf_op jit(solution)/shard_map/ppermute | solution.py:928
  492.3 46.9 %collective-permute-start.40 = (bf16[256,1152]{1,0:T(8,128)(2,1)S(1)}, bf16[256,1152]{1,0:T(8,128)(2,1)S(1)}, u32[]{:S(2)}, u32[]{:S(2)}) collective-permute-start(bf16[256,1152]{1,0:T(8,128)(2,1)S(1)} %get-tuple-element.170), channel_id=1, source_target_pairs={{0,1},{1,0},{2,3},{3,2},{4,5},{5,4},{6,7},{7,6},{8,9},{9,8},{10,11... | collective-permute-start | bytes 1769480 | tf_op jit(solution)/shard_map/ppermute | solution.py:928
  553.8 54.6 %all-to-all-start.2 = ((bf16[32,8,2816]{2,1,0:T(8,128)(2,1)}), bf16[32,8,2816]{2,1,0:T(8,128)(2,1)}, u32[]{:S(2)}, u32[]{:S(2)}) async-start(bf16[32,8,2816]{2,1,0:T(8,128)(2,1)} %pad_maximum_fusion.1), calls=%async_computation.2 | async-start | bytes 2883584 | tf_op jit(solution)/shard_map/all_to_all | solution.py:1039
  557.4 48.9 %reduce-scatter.3.cloned.1.call-start = ((), (), s32[]{:S(2)}) async-start(), calls=%async_computation.6 | async-start | bytes 626688 | tf_op jit(solution)/shard_map/reduce_scatter | solution.py:1183
  571.0 100.0 %reduce-scatter.5.cloned.1.call-start = ((), (), s32[]{:S(2)}) async-start(), calls=%async_computation.7 | async-start | bytes 1179648 | tf_op jit(solution)/shard_map/reduce_scatter | solution.py:1183
  (157 other events, 2017.1 us)
Sparse Core Ops, SparseCore 0:
  14.8 34.8 all-gather.10
  51.3 109.2 all-gather.12
  162.2 52.2 all-gather.14
  216.7 52.9 all-gather.18
  271.1 89.7 all-gather.16
  571.1 35.1 reduce-scatter.2
  609.1 30.7 reduce-scatter.4

commit v4 on v3

--- a/solution.py
+++ b/solution.py
@@ -138,7 +138,8 @@
 
 
 def scan_block(
-    conv_ref, before_ref, state_ref, state_before_ref, step_ref, meta_ref, segment_ref, taps_ref, state_taps_ref, head_ref
+    conv_ref, before_ref, state_ref, state_before_ref, step_ref, meta_ref, segment_ref, taps_ref, state_taps_ref, head_ref,
+    turned_over,
 ):
     rows = SSD_BLOCK
     channels = conv_ref.shape[1]
@@ -160,7 +161,8 @@
     leaving = jnp.exp(total[rows - 1 : rows] - total) * meta[:, 4:5]
     expand = expand_table(channels)
     spread = head_spread(jnp.concatenate([steps, entered, leaving * steps], axis=0), expand)
-    blocked = jnp.where((row >= column) & (meta[:, 0:1] == segment_ref[0:1, :]), 0.0, NEGATIVE)
+    ordered = row <= column if turned_over else row >= column
+    blocked = jnp.where(ordered & (meta[:, 0:1] == segment_ref[0:1, :]), 0.0, NEGATIVE)
     return dict(
         summed=summed,
         conv_gate=conv_gate,
@@ -182,14 +184,18 @@
         stepped=(wide_inputs * spread[:rows]).astype(BFLOAT),
         tailed=(wide_inputs * spread[2 * rows :]).astype(BFLOAT),
         blocked=blocked,
-        crossing=dot(read, write, (1, 1)),
+        crossing=dot(write, read, (1, 1)) if turned_over else dot(read, write, (1, 1)),
     )
 
 
 def decay_of(block, head):
-    return jnp.exp(
-        block["total"][:, head : head + 1] - block["total_rows"][head : head + 1, :] + block["blocked"]
-    )
+    difference = block["total"][:, head : head + 1] - block["total_rows"][head : head + 1, :]
+    return jnp.exp(difference + block["blocked"])
+
+
+def turned_decay_of(block, head):
+    difference = block["total_rows"][head : head + 1, :] - block["total"][:, head : head + 1]
+    return jnp.exp(difference + block["blocked"])
 
 
 def scan_forward_kernel(
@@ -204,7 +210,7 @@
 
     block = scan_block(
         conv_ref, before_ref, state_ref, state_before_ref, step_ref, meta_ref, segment_ref, taps_ref, state_taps_ref,
-        head_ref,
+        head_ref, False,
     )
     heads = conv_ref.shape[1] // HP
     carried = state[...].astype(BFLOAT)
@@ -225,8 +231,7 @@
 
 def scan_backward_kernel(
     gate_ref, conv_ref, before_ref, state_ref, state_before_ref, step_ref, meta_ref, segment_ref, taps_ref,
-    state_taps_ref, head_ref, skip_ref, scanned_ref, states_ref, grad_ref, query_grad_ref, key_grad_ref,
-    value_grad_ref, out_ref, state_grad, later, state_later,
+    state_taps_ref, head_ref, skip_ref, scanned_ref, states_ref, grad_ref, out_ref, state_grad, later, state_later,
 ):
     @pl.when(pl.program_id(0) == 0)
     def _():
@@ -236,7 +241,7 @@
 
     block = scan_block(
         conv_ref, before_ref, state_ref, state_before_ref, step_ref, meta_ref, segment_ref, taps_ref, state_taps_ref,
-        head_ref,
+        head_ref, True,
     )
     rows = SSD_BLOCK
     channels = conv_ref.shape[1]
@@ -270,14 +275,14 @@
     pulled = []
     for head in range(heads):
         span = slice(head * HP, (head + 1) * HP)
-        decay = decay_of(block, head)
+        decay = turned_decay_of(block, head)
         weights = (block["crossing"] * decay).astype(BFLOAT)
-        pulled.append(dot(weights, rounded[:, span], (0, 0)))
-        crossing_grad = crossing_grad + dot(rounded[:, span], block["stepped"][:, span], (1, 1)) * decay
+        pulled.append(dot(weights, rounded[:, span], (1, 0)))
+        crossing_grad = crossing_grad + dot(block["stepped"][:, span], rounded[:, span], (1, 1)) * decay
     pulled = jnp.concatenate(pulled, axis=1)
     crossing_rounded = crossing_grad.astype(BFLOAT)
-    read_grad = read_grad + dot(crossing_rounded, write, (1, 0))
-    write_grad = write_grad + dot(crossing_rounded, read, (0, 0))
+    read_grad = read_grad + dot(crossing_rounded, write, (0, 0))
+    write_grad = write_grad + dot(crossing_rounded, read, (1, 0))
 
     inputs_grad = inputs_grad + block["steps_wide"] * pulled + block["tail_wide"] * from_state
     sums = head_sum(
@@ -309,12 +314,11 @@
         jnp.concatenate([write_grad, read_grad], axis=1) * state_slope, state_later, state_taps_ref, meta
     )
     conv_pre = conv_back(inputs_grad * silu_slope(block["summed"], block["conv_gate"]), later, taps_ref, meta)
-    start = 0
-    for values in (
-        state_pre, key_grad_ref[...], value_grad_ref[...], gate_grad, conv_pre, query_grad_ref[...], raw_grad
-    ):
-        out_ref[:, start : start + values.shape[1]] = values.astype(BFLOAT)
-        start += values.shape[1]
+    out_ref[:, : 2 * NSTATE] = state_pre.astype(BFLOAT)
+    start = 2 * NSTATE + 2 * HEAD_SIZE
+    out_ref[:, start : start + channels] = gate_grad.astype(BFLOAT)
+    out_ref[:, start + channels : start + 2 * channels] = conv_pre.astype(BFLOAT)
+    out_ref[:, out_ref.shape[1] - LANES :] = raw_grad.astype(BFLOAT)
 
 
 STATES = 2 * NSTATE
@@ -383,7 +387,7 @@
     )(*scan_operands(projected, tables), mixed)
 
 
-def scan_backward(projected, tables, scanned, carried, mixed_grad, query_grad, key_grad, value_grad):
+def scan_backward(projected, tables, scanned, carried, mixed_grad):
     tokens, width = projected.shape
     channels = tables["taps"].shape[1]
     blocks = tokens // SSD_BLOCK
@@ -396,9 +400,6 @@
             pl.BlockSpec((SSD_BLOCK, channels), back),
             pl.BlockSpec((1, NSTATE, channels), lambda i: (blocks - 1 - i, 0, 0)),
             pl.BlockSpec((SSD_BLOCK, channels), back),
-            pl.BlockSpec((SSD_BLOCK, query_grad.shape[1]), back),
-            pl.BlockSpec((SSD_BLOCK, HEAD_SIZE), back),
-            pl.BlockSpec((SSD_BLOCK, HEAD_SIZE), back),
         ],
         out_specs=pl.BlockSpec((SSD_BLOCK, width), back),
         out_shape=jax.ShapeDtypeStruct((tokens, width), BFLOAT),
@@ -410,7 +411,7 @@
         compiler_params=pltpu.CompilerParams(vmem_limit_bytes=SCAN_BYTES),
         cost_estimate=scan_cost(tokens, channels, 2),
         name="scan_backward",
-    )(*scan_operands(projected, tables), scanned, carried, mixed_grad, query_grad, key_grad, value_grad)
+    )(*scan_operands(projected, tables), scanned, carried, mixed_grad)
 
 
 def turned(values, cosine, sine):
@@ -452,9 +453,10 @@
 
 
 def attention_backward_kernel(
-    query_ref, key_ref, value_ref, cosine_ref, sine_ref, meta_ref, segment_ref, grad_ref,
-    query_grad_ref, key_grad_ref, value_grad_ref, keys, key_sum, value_sum,
+    query_ref, key_ref, value_ref, cosine_ref, sine_ref, meta_ref, segment_ref, grad_ref, held_ref,
+    out_ref, keys, key_sum, value_sum, query_grad_ref, shared_grad_ref, sems,
 ):
+    del held_ref
     tokens = key_ref.shape[0]
     scale = 1.0 / math.sqrt(HEAD_SIZE)
     keys[...] = turned(key_ref[...].astype(FLOAT), cosine_ref[...], sine_ref[...])
@@ -476,8 +478,18 @@
             query_grad = dot(score_grad, keys[:extent], (1, 0))
             key_sum[:extent] += dot(score_grad, query, (0, 0))
             query_grad_ref[here, span] = turned_back(query_grad, cosine_ref[here], sine_ref[here]).astype(BFLOAT)
-    key_grad_ref[...] = turned_back(key_sum[...], cosine_ref[...], sine_ref[...]).astype(BFLOAT)
-    value_grad_ref[...] = value_sum[...].astype(BFLOAT)
+    shared_grad_ref[:, :HEAD_SIZE] = turned_back(key_sum[...], cosine_ref[...], sine_ref[...]).astype(BFLOAT)
+    shared_grad_ref[:, HEAD_SIZE:] = value_sum[...].astype(BFLOAT)
+    end = out_ref.shape[1] - LANES
+    width = query_grad_ref.shape[1]
+    copies = [
+        pltpu.make_async_copy(query_grad_ref, out_ref.at[:, end - width : end], sems.at[0]),
+        pltpu.make_async_copy(shared_grad_ref, out_ref.at[:, STATES : STATES + PAIR], sems.at[1]),
+    ]
+    for copy in copies:
+        copy.start()
+    for copy in copies:
+        copy.wait()
 
 
 def attention_cost(tokens, width, factor):
@@ -523,31 +535,30 @@
     )(*attention_operands(projected, tables))
 
 
-def attention_backward(projected, tables, mixed_grad):
+def attention_backward(projected, tables, mixed_grad, projected_grad):
     tokens = projected.shape[0]
     channels = tables["taps"].shape[1]
     width = channels * QUERY_HEADS // DSSM * HEAD_SIZE
-    narrow = whole((tokens, HEAD_SIZE))
     return pl.pallas_call(
         attention_backward_kernel,
         grid=(1,),
         in_specs=attention_specs(tokens, channels)
-        + [pl.BlockSpec((tokens, width), lambda *_: (0, channels // width))],
-        out_specs=[whole((tokens, width)), narrow, narrow],
-        out_shape=[
-            jax.ShapeDtypeStruct((tokens, width), BFLOAT),
-            jax.ShapeDtypeStruct((tokens, HEAD_SIZE), BFLOAT),
-            jax.ShapeDtypeStruct((tokens, HEAD_SIZE), BFLOAT),
-        ],
+        + [pl.BlockSpec((tokens, width), lambda *_: (0, channels // width)), pl.BlockSpec(memory_space=pl.ANY)],
+        out_specs=pl.BlockSpec(memory_space=pl.ANY),
+        out_shape=jax.ShapeDtypeStruct(projected_grad.shape, BFLOAT),
         scratch_shapes=[
             pltpu.VMEM((tokens, HEAD_SIZE), BFLOAT),
             pltpu.VMEM((tokens, HEAD_SIZE), FLOAT),
             pltpu.VMEM((tokens, HEAD_SIZE), FLOAT),
+            pltpu.VMEM((tokens, width), BFLOAT),
+            pltpu.VMEM((tokens, PAIR), BFLOAT),
+            pltpu.SemaphoreType.DMA((2,)),
         ],
+        input_output_aliases={8: 0},
         compiler_params=pltpu.CompilerParams(vmem_limit_bytes=SCAN_BYTES),
         cost_estimate=attention_cost(tokens, width, 3),
         name="attention_backward",
-    )(*attention_operands(projected, tables), mixed_grad)
+    )(*attention_operands(projected, tables), mixed_grad, projected_grad)
 
 
 def mixer_tables(lengths, segment, position, conv_values, conv_states, scan_params):
@@ -880,6 +891,10 @@
     return lax.optimization_barrier((values, *earlier))[0]
 
 
+def after_all(values, *earlier):
+    return lax.optimization_barrier((*values, *earlier))[: len(values)]
+
+
 def unit_parts(values, units):
     cuts = [0]
     for width in (GATE_WIDTH, GATE_WIDTH, HEAD_SIZE, PAIR_WIDTH, STATE_WIDTH, STEP_WIDTH):
@@ -945,13 +960,17 @@
     return lax.dynamic_slice_in_dim(values, block * rows, rows, 0)
 
 
+def spread_gathered(blocks, gathered, selector):
+    held = None
+    for mask, values in blocks:
+        held = spread_block(mask, values, gathered, selector, held)
+    return held
+
+
 def spread_project(halves, gathered, selector):
     rows = halves[0].shape[0]
     if quick(rows):
-        held = None
-        for mask, values in gather_blocks(halves):
-            held = spread_block(mask, values, gathered, selector, held)
-        return held
+        return spread_gathered(gather_blocks(halves), gathered, selector)
     wide, narrow_factor = gathered
     width = narrow_factor.shape[1]
     both = product(lax.all_gather(jnp.concatenate(halves, axis=1), "col", axis=0, tiled=True), wide)
@@ -959,19 +978,37 @@
     return (both[:, :width] + product(narrow, narrow_factor)).astype(BFLOAT), narrow
 
 
+def collect_start(values, gathered, earlier=()):
+    (corner,) = collect_blocks([3], values, gathered, [(BFLOAT, BFLOAT)])
+    arriving = flip(corner[0], 1), flip(corner[1], 2)
+    values = after(values, *earlier) if earlier else values
+    near, far, own = collect_blocks([1, 2, 0], values, gathered, [(BFLOAT, FLOAT), (FLOAT, BFLOAT), (FLOAT, FLOAT)])
+    return own, flip(near[0], 1), flip(far[1], 2), far[0], near[1], arriving
+
+
+def collect_middle(started):
+    own, near_first, far_second, far_first, near_second, arriving = started
+    onward = [
+        (kept + part.astype(FLOAT)).astype(BFLOAT) for kept, part in zip((far_first, near_second), arriving)
+    ]
+    return (own, near_first, far_second), onward
+
+
+def collect_onward(onward):
+    return flip(onward[0], 2), flip(onward[1], 1)
+
+
+def collect_end(kept, last, kind, gathered, own_selector, *operands):
+    own, near_first, far_second = kept
+    parts = [own[0], near_first, last[0], own[1], far_second, last[1]]
+    return finish(kind, parts, gathered, own_selector, *operands)
+
+
 def collect_project(values, gathered, kind, own_selector, *operands):
     rows, model = own_selector.shape[0], operands[0].shape[1]
     if quick(rows):
-        wide = lambda part: part.astype(FLOAT)
-        (corner,) = collect_blocks([3], values, gathered, [(BFLOAT, BFLOAT)])
-        corner_first, corner_second = flip(corner[0], 1), flip(corner[1], 2)
-        near, far = collect_blocks([1, 2], values, gathered, [(BFLOAT, FLOAT), (FLOAT, BFLOAT)])
-        near_first, far_second = flip(near[0], 1), flip(far[1], 2)
-        (own,) = collect_blocks([0], values, gathered, [(FLOAT, FLOAT)])
-        far_first = flip((far[0] + wide(corner_first)).astype(BFLOAT), 2)
-        near_second = flip((near[1] + wide(corner_second)).astype(BFLOAT), 1)
-        parts = [own[0], near_first, far_first, own[1], far_second, near_second]
-        return finish(kind, parts, gathered, own_selector, *operands)
+        kept, onward = collect_middle(collect_start(values, gathered))
+        return collect_end(kept, collect_onward(onward), kind, gathered, own_selector, *operands)
     wide, narrow_factor = gathered
     width = narrow_factor.shape[1]
     partial = jnp.concatenate(
@@ -1039,13 +1076,14 @@
     exchange = lambda values: lax.all_to_all(values, ALL_AXES, split_axis=0, concat_axis=0, tiled=True)
 
     sent, send_matrix = send_tokens(target, tokens_in, adapters, peer)
-    arrived = exchange(sent)
+    shards = []
 
     def gather_weight(weight, lower, raised):
         top = jnp.concatenate([weight, lower], axis=1)
         if fast:
             bottom = pad_columns(raised, top.shape[1])
-            return (lax.all_gather(jnp.concatenate([top, bottom], axis=0), "row", axis=0),)
+            shards.append(jnp.concatenate([top, bottom], axis=0))
+            return (lax.all_gather(shards[-1], "row", axis=0),)
         wide = lax.all_gather(top, "row", axis=0, tiled=True)
         return wide, lax.all_gather(raised, "row", axis=0, tiled=True)
 
@@ -1057,10 +1095,21 @@
     taps = jnp.concatenate([jnp.zeros((KCONV + 1, pair_width), BFLOAT), conv_states], axis=1)
     taps = jnp.pad(taps, ((0, 16 - KCONV - 1), (0, 0)))
     shared = jnp.concatenate([jnp.concatenate([pairs, states], axis=1), taps], axis=0)
+    own_columns = jnp.concatenate([gates, convs, queries, pad_columns(steps, LANES)], axis=1)
     if fast:
-        shared = lax.all_gather(shared, "row", axis=0)
+        shared_shard = shared
+        shared = lax.all_gather(shared_shard, "row", axis=0)
+        weights_own = gather_weight(own_columns[:depth], in_lower, own_columns[depth:])
+        sent = after(sent, shared_shard, shards[0])
+    arrived = exchange(sent)
+    gains = jnp.broadcast_to(norm_gains.astype(FLOAT)[:, None, :], (2, 8, model))
+    if fast:
+        near, far = flip(shared, 1), flip(shared, 2)
+        arrived = after(arrived, near, far)
+    own_input, place_matrix, *normed_one = arrive_tokens(arrived.reshape(rows, model + LANES), gains[0])
+    blocks_one = gather_blocks(normed_one) if fast else normed_one
+    if fast:
         held = jnp.zeros((cols,) + shared.shape, BFLOAT)
-        near, far = flip(shared, 1), flip(shared, 2)
         for block, values in ((col, shared), (col ^ 1, near), (col ^ 2, far)):
             held = lax.dynamic_update_index_in_dim(held, values, block, 0)
         split = shared.shape[0] // 2
@@ -1082,15 +1131,13 @@
     all_taps = jnp.concatenate(
         [tap_rows[at, height : height + KCONV + 1, pair_width:] for at in range(cols)], axis=1
     )
-    own_columns = [gates, convs, queries, pad_columns(steps, LANES)]
     if fast:
-        own_columns = jnp.concatenate(own_columns, axis=1)
-        weights_in = (shared_columns, *gather_weight(own_columns[:depth], in_lower, own_columns[depth:]))
+        weights_in = (shared_columns, *weights_own)
     else:
-        columns = jnp.concatenate([shared_columns, *own_columns], axis=1)
+        columns = jnp.concatenate([shared_columns, own_columns], axis=1)
         weights_in = gather_weight(columns[:depth], in_lower, columns[depth:])
     weights_mix = gather_weight(
-        after(split_halves(weight_mix, units, GATE_WIDTH, 0).T, send_matrix),
+        after(split_halves(weight_mix, units, GATE_WIDTH, 0).T, sent),
         mix_raise.T,
         split_halves(mix_lower, units, GATE_WIDTH, 0).T,
     )
@@ -1100,8 +1147,6 @@
         split_halves(feed_raise, units, UNIT_FF, 1),
     )
 
-    gains = jnp.broadcast_to(norm_gains.astype(FLOAT)[:, None, :], (2, 8, model))
-    own_input, place_matrix, *normed_one = arrive_tokens(arrived.reshape(rows, model + LANES), gains[0])
     source_adapters = arrived.reshape(rows, model + LANES)[::peer, model + 1 : model + 1 + sequences].astype(jnp.int32)
     segment, position, selector = sequence_tables(lengths, adapters, total)
     own_selector = rows_of(selector, col, rows)
@@ -1126,9 +1171,14 @@
         chosen = (jnp.arange(NADAPT * RANK, dtype=jnp.int32)[:, None] == adapter_row[None, :]).astype(BFLOAT)
         return product(chosen, dealt)
 
-    def send_back(values, grads):
+    def send_back(values, grads, earlier=()):
         back = contract_first(place_matrix, values).astype(BFLOAT).reshape(devices, peer, model)
-        return exchange(jnp.concatenate([back, *grads], axis=2))
+        payload = jnp.concatenate([back, *grads], axis=2)
+        payload = after(payload, *earlier) if earlier else payload
+        payloads.append(payload)
+        return exchange(payload)
+
+    payloads = []
 
     def take_back(dealt, count):
         returned = contract_first(send_matrix, dealt[:, :, :model].reshape(rows, model)).astype(BFLOAT)
@@ -1137,12 +1187,12 @@
             expand_grad(dealt[:, :, model + at * width : model + (at + 1) * width]) for at in range(count)
         ]
 
-    projected, inner_in = spread_project(normed_one, weights_in, selector)
+    projected, inner_in = (spread_gathered if fast else spread_project)(blocks_one, weights_in, selector)
 
     sent_grad = product(send_matrix, cotangent).astype(BFLOAT).reshape(devices, peer, model)
     arrived_grad = exchange(after(sent_grad, normed_one[0])).reshape(rows, model)
     branch_two = product(place_matrix, arrived_grad).astype(BFLOAT)
-    weights_down = gather_weight(after(weight_down.T, normed_one[0]), down_raise.T, down_lower.T)
+    weights_down = gather_weight(after(weight_down.T, projected), down_raise.T, down_lower.T)
 
     mixed_out = attention_forward(projected, tables)
     mixed_out, scanned, carried = scan_forward(projected, tables, mixed_out)
@@ -1163,13 +1213,23 @@
     )
     mixed_grad, narrow_one = spread_project(branch_one, weights_mix, selector)
 
-    block_out, inner_down = collect_project(
-        after(activated, mixed_grad), weights_down, "output", own_selector, hidden
-    )
-    query_grad, key_grad, value_grad = attention_backward(projected, tables, mixed_grad)
-    projected_grad = scan_backward(
-        projected, tables, scanned, carried, mixed_grad, query_grad, key_grad, value_grad
-    )
+    if fast:
+        started = collect_start(after(activated, mixed_grad), weights_down)
+        projected_grad = scan_backward(
+            projected, tables, scanned, carried, after(mixed_grad, started[0][0], started[3])
+        )
+        kept, onward = collect_middle((*started[:5], [after(part, projected_grad) for part in started[5]]))
+        projected_grad = attention_backward(projected, tables, mixed_grad, after(projected_grad, *onward))
+        last = collect_onward(onward)
+        started_in = collect_start(projected_grad, weights_in, last)
+        kept_in, onward_in = collect_middle(started_in)
+        block_out, inner_down = collect_end(
+            kept, last, "output", weights_down, own_selector, after(hidden, *onward_in, *kept_in[1:])
+        )
+    else:
+        block_out, inner_down = collect_project(activated, weights_down, "output", own_selector, hidden)
+        projected_grad = scan_backward(projected, tables, scanned, carried, mixed_grad)
+        projected_grad = attention_backward(projected, tables, mixed_grad, projected_grad)
     dealt_out = send_back(
         block_out,
         [
@@ -1188,11 +1248,6 @@
         contract_first(narrow_two, activated),
     ]
     early = sum_rows(jnp.concatenate(early_parts, axis=1))
-    early_cuts = [0, early_parts[0].shape[1]]
-    early_cuts.append(early_cuts[1] + early_parts[1].shape[1])
-    grad_mix_lower = join_halves(early[:, : early_cuts[1]], units, GATE_WIDTH, 1).T
-    grad_feed_raise = join_halves(early[:, early_cuts[1] : early_cuts[2]], units, UNIT_FF, 1)
-    grad_down_lower = early[:, early_cuts[2] :].T
 
     raise_grad = contract_first(inner_in, projected_grad)
     key_columns = raise_grad[:, STATES : STATES + HEAD_SIZE]
@@ -1223,6 +1278,31 @@
             stacked.astype(BFLOAT).reshape(cols * NADAPT * RANK, -1), "col", scatter_dimension=0, tiled=True
         ).astype(FLOAT)
     late = sum_rows(jnp.concatenate([shared_sum, raise_grad[:, STATES + PAIR :]], axis=1))
+    if fast:
+        input_grad, narrow_four = collect_end(
+            kept_in,
+            collect_onward(onward_in),
+            "input",
+            weights_in,
+            own_selector,
+            own_input,
+            after(hidden_grad, payloads[0]),
+            gains[0],
+        )
+    else:
+        input_grad, narrow_four = collect_project(
+            projected_grad, weights_in, "input", own_selector, own_input, hidden_grad, gains[0]
+        )
+    dealt_grad = send_back(
+        input_grad, [compact_grad(narrow_four, jnp.concatenate(normed_one, axis=1))], [dealt_out]
+    )
+    dealt_out, early, late = after_all((dealt_out, early, late), payloads[-1])
+    early_cuts = [0, early_parts[0].shape[1]]
+    early_cuts.append(early_cuts[1] + early_parts[1].shape[1])
+    grad_mix_lower = join_halves(early[:, : early_cuts[1]], units, GATE_WIDTH, 1).T
+    grad_feed_raise = join_halves(early[:, early_cuts[1] : early_cuts[2]], units, UNIT_FF, 1)
+    grad_down_lower = early[:, early_cuts[2] :].T
+
     shared_width = pair_width + state_width
     cuts = [shared_width]
     for width in (channels, channels, units * HEAD_SIZE, units * STEP_WIDTH):
@@ -1242,10 +1322,6 @@
         units,
     )
 
-    input_grad, narrow_four = collect_project(
-        after(projected_grad, dealt_out), weights_in, "input", own_selector, own_input, hidden_grad, gains[0]
-    )
-    dealt_grad = send_back(input_grad, [compact_grad(narrow_four, jnp.concatenate(normed_one, axis=1))])
     returned_out, (grad_down_raise, grad_feed_lower, grad_mix_raise) = take_back(dealt_out, 3)
     returned_grad, (grad_in_lower,) = take_back(dealt_grad, 1)
     return (

time: 720 us -> 685 us (0.951)
  other arithmetic: 48.2 us -> 33.3 us
    reduce_scatter x2, waiting for transfers between devices: 29.4 us -> 0.02 us  [sum_rows(): lax.psum_scatter(values.astype(BFLOAT), 'row', scatter_dimension=0, tiled...]
    ppermute x54, waiting for transfers between devices: 129 us -> 152 us  [flip(): return lax.ppermute(values, 'col', [(i, i ^ mask) for i in range(4)])]
    unnamed x254 -> x266, local copies, waits for them, and re-layouts: 66.8 us -> 82.3 us
    pallas_call x16, Pallas kernels: 89.8 us -> 79.8 us  [spread_block(): pl.pallas_call(functools.partial(spread_kernel, mask, len(gathered)), in_...]
    pallas_call x12 -> x8, Pallas kernels: 37.7 us -> 37.8 us  [collect_blocks(): pl.pallas_call(functools.partial(collect_kernel, masks, len(gathered)), i...]
  transfers between devices with their start and end apart: 65 -> 65, of which waited for: 25 -> 27; matrix products, arithmetic and copies ran while one was open for 13% -> 11% of each run, Pallas kernels for 23% -> 24%
where the time goes in v4:
time: 685 us; the launch traced here: 676 us
  waiting for transfers between devices  235 us (34%)
  Pallas kernels  183 us (27%)
  local copies, waits for them, and re-layouts  103 us (15%)
  starting transfers between devices  80.7 us (12%)
  other arithmetic  33.3 us (5%)
  matrix products  23.6 us (3%)
  between operations  17.6 us (3%)
    ppermute x54, waiting for transfers between devices, flip(): return lax.ppermute(values, 'col', [(i, i ^ mask) for i in range(4)])  152 us
    unnamed x266, local copies, waits for them, and re-layouts  82.3 us
    pallas_call x16, Pallas kernels, spread_block(): pl.pallas_call(functools.partial(spread_kernel, mask, len(gathered)), in_...  79.8 us
    ppermute x54, starting transfers between devices, flip(): return lax.ppermute(values, 'col', [(i, i ^ mask) for i in range(4)])  60.8 us
    all_to_all x4, waiting for transfers between devices, local(): lax.all_to_all(values, ALL_AXES, split_axis=0, concat_axis=0, tiled=True)  51.9 us
    pallas_call x8, Pallas kernels, collect_blocks(): pl.pallas_call(functools.partial(collect_kernel, masks, len(gathered)), i...  37.8 us
    pallas_call x1, Pallas kernels, scan_backward(): pl.pallas_call(scan_backward_kernel, grid=(blocks,), in_specs=scan_specs(...  28.4 us
    all_gather x4, waiting for transfers between devices, gather_weight(): return (lax.all_gather(shards[-1], 'row', axis=0),)  23 us
  transfers between devices with their start and end apart: 65, of which 27 were waited for; matrix products, arithmetic and copies ran while one was open for 11% of the time, Pallas kernels for 24%

profile of v4, /device:TPU:0, one launch (start us, length us, event | category | flops | bytes accessed | tf_op | source)
XLA Modules:
  0.0 676.3 jit_solution(3205346109961221715)
XLA Ops:
  24.8 7.3 %all-to-all-start = ((bf16[32,8,2176]{2,1,0:T(8,128)(2,1)}), bf16[32,8,2176]{2,1,0:T(8,128)(2,1)S(1)}, u32[]{:S(2)}, u32[]{:S(2)}) async-start(bf16[32,8,2176]{2,1,0:T(8,128)(2,1)} %bitcast.181), calls=%async_computation | async-start | bytes 2228224 | tf_op jit(solution)/shard_map/all_to_all | solution.py:1076
  32.1 7.9 %all-gather.11.cloned.1.call-done = bf16[2304,256]{1,0:T(8,128)(2,1)} async-done(((bf16[288,256]{1,0:T(8,128)(2,1)}), bf16[2304,256]{1,0:T(8,128)(2,1)}) %all-gather.11.cloned.1.call-update) | async-done | bytes 1179664 | tf_op jit(solution)/shard_map/all_gather | solution.py:1101
  45.8 32.6 %all-to-all-done = bf16[32,8,2176]{2,1,0:T(8,128)(2,1)S(1)} async-done(((bf16[32,8,2176]{2,1,0:T(8,128)(2,1)}), bf16[32,8,2176]{2,1,0:T(8,128)(2,1)S(1)}, u32[]{:S(2)}, u32[]{:S(2)}) %all-to-all-start) | async-done | bytes 1114144 | tf_op jit(solution)/shard_map/all_to_all | solution.py:1076
  96.4 14.4 %collective-permute-done.4.right_ref = bf16[256,1024]{1,0:T(8,128)(2,1)S(1)} collective-permute-done((bf16[256,1024]{1,0:T(8,128)(2,1)}, bf16[256,1024]{1,0:T(8,128)(2,1)S(1)}, u32[]{:S(2)}, u32[]{:S(2)}) %collective-permute-start.4) | collective-permute-done | bytes 524320 | tf_op jit(solution)/shard_map/ppermute | solution.py:943
  112.1 12.2 %collective-permute-done.2.left_ref = bf16[256,1024]{1,0:T(8,128)(2,1)S(1)} collective-permute-done((bf16[256,1024]{1,0:T(8,128)(2,1)}, bf16[256,1024]{1,0:T(8,128)(2,1)S(1)}, u32[]{:S(2)}, u32[]{:S(2)}) %collective-permute-start.2) | collective-permute-done | bytes 524320 | tf_op jit(solution)/shard_map/ppermute | solution.py:943
  139.9 8.8 %spread_block.16 = (bf16[1024,2688]{1,0:T(8,128)(2,1)S(1)}, bf16[1024,128]{1,0:T(8,128)(2,1)S(1)}) custom-call(bf16[256,1024]{1,0:T(8,128)(2,1)} %get-tuple-element.121.left_ref, bf16[256,1024]{1,0:T(8,128)(2,1)} %get-tuple-element.122.right_ref, f32[1024,128]{1,0:T(8,128)S(1)} %compare_convert_fusion.chosen_ref, bf16[8,272,768]{2,1,0:T(8,128)(2,1)S(1)} %copy-done.16, ...), custom_call_target="tpu_custom_call" | custom-call | flops 2952790016 | bytes 2424832 | tf_op jit(solution)/shard_map/spread_block/pallas_call | solution.py:660
  148.8 8.5 %spread_block.17 = (bf16[1024,2688]{1,0:T(8,128)(2,1)S(1)}, bf16[1024,128]{1,0:T(8,128)(2,1)S(1)}) custom-call(bf16[256,1024]{1,0:T(8,128)(2,1)} %collective-permute-done.9.left_ref, bf16[256,1024]{1,0:T(8,128)(2,1)S(1)} %collective-permute-done.4.right_ref, ...), custom_call_target="tpu_custom_call", output_to_operand_aliasing={{0}: (5, {}), {1}: (6, {})} | custom-call | flops 2952790016 | bytes 2424832 | tf_op jit(solution)/shard_map/spread_block/pallas_call | solution.py:660
  157.3 7.9 %spread_block.18 = (bf16[1024,2688]{1,0:T(8,128)(2,1)S(1)}, bf16[1024,128]{1,0:T(8,128)(2,1)S(1)}) custom-call(bf16[256,1024]{1,0:T(8,128)(2,1)S(1)} %collective-permute-done.2.left_ref, bf16[256,1024]{1,0:T(8,128)(2,1)S(1)} %collective-permute-done.8.right_ref, ...), custom_call_target="tpu_custom_call", output_to_operand_aliasing={{0}: (5, {}), {1}: (6, {})} | custom-call | flops 2952790016 | bytes 2424832 | tf_op jit(solution)/shard_map/spread_block/pallas_call | solution.py:660
  165.3 8.7 %spread_block.19 = (bf16[1024,2688]{1,0:T(8,128)(2,1)S(1)}, bf16[1024,128]{1,0:T(8,128)(2,1)S(1)}) custom-call(bf16[256,1024]{1,0:T(8,128)(2,1)} %collective-permute-done.3.left_ref, bf16[256,1024]{1,0:T(8,128)(2,1)} %collective-permute-done.5.right_ref, ...), custom_call_target="tpu_custom_call", output_to_operand_aliasing={{0}: (5, {}), {1}: (6, {})} | custom-call | flops 2952790016 | bytes 2424832 | tf_op jit(solution)/shard_map/spread_block/pallas_call | solution.py:660
  195.3 12.9 %scan_forward.1 = (bf16[1024,1024]{1,0:T(8,128)(2,1)S(1)}, f32[1024,768]{1,0:T(8,128)S(1)}, bf16[4,256,768]{2,1,0:T(8,128)(2,1)S(1)}) custom-call(bf16[1024,2688]{1,0:T(8,128)(2,1)S(1)} %copy-done.3, bf16[1024,2688]{1,0:T(8,128)(2,1)S(1)} %copy-done.3, bf16[1024,2688]{1,0:T(8,128)(2,1)S(1)} %copy-done.3, ...), custom_call_target="tpu_custom_call", output_to_operand_aliasing={{0}: (12, {})} | custom-call | flops 1342177280 | bytes 9437184 | tf_op jit(solution)/shard_map/scan_forward/pallas_call | solution.py:368
  226.6 7.8 %collective-permute-done.11 = bf16[256,1152]{1,0:T(8,128)(2,1)S(1)} collective-permute-done((bf16[256,1152]{1,0:T(8,128)(2,1)S(1)}, bf16[256,1152]{1,0:T(8,128)(2,1)S(1)}, u32[]{:S(2)}, u32[]{:S(2)}) %collective-permute-start.11) | collective-permute-done | bytes 589856 | tf_op jit(solution)/shard_map/ppermute | solution.py:943
  247.1 10.8 %collective-permute-done.15.second_far = bf16[256,1024]{1,0:T(8,128)(2,1)} collective-permute-done((bf16[256,1024]{1,0:T(8,128)(2,1)}, bf16[256,1024]{1,0:T(8,128)(2,1)}, u32[]{:S(2)}, u32[]{:S(2)}) %collective-permute-start.15) | collective-permute-done | bytes 524320 | tf_op jit(solution)/shard_map/ppermute | solution.py:943
  276.7 7.5 %collective-permute-done.21.left_ref = bf16[256,1024]{1,0:T(8,128)(2,1)} collective-permute-done((bf16[256,1024]{1,0:T(8,128)(2,1)}, bf16[256,1024]{1,0:T(8,128)(2,1)}, u32[]{:S(2)}, u32[]{:S(2)}) %collective-permute-start.21) | collective-permute-done | bytes 524320 | tf_op jit(solution)/shard_map/ppermute | solution.py:943
  287.0 8.5 %collective-permute-done.18.right_ref = bf16[256,1024]{1,0:T(8,128)(2,1)} collective-permute-done((bf16[256,1024]{1,0:T(8,128)(2,1)}, bf16[256,1024]{1,0:T(8,128)(2,1)}, u32[]{:S(2)}, u32[]{:S(2)}) %collective-permute-start.18) | collective-permute-done | bytes 524320 | tf_op jit(solution)/shard_map/ppermute | solution.py:943
  327.6 18.8 %all-gather.19.cloned.1.call-done = bf16[2176,1152]{1,0:T(8,128)(2,1)} async-done(((bf16[272,1152]{1,0:T(8,128)(2,1)}), bf16[2176,1152]{1,0:T(8,128)(2,1)}) %all-gather.19.cloned.1.call-update) | async-done | bytes 5013520 | tf_op jit(solution)/shard_map/all_gather | solution.py:1086
  374.8 7.5 %collect_blocks.10 = (bf16[256,1152]{1,0:T(8,128)(2,1)S(1)}, f32[256,1024]{1,0:T(8,128)S(1)}, f32[256,1152]{1,0:T(8,128)S(1)}, bf16[256,1024]{1,0:T(8,128)(2,1)S...) custom-call(bf16[1024,2048]{1,0:T(8,128)(2,1)S(1)} %pad_maximum_fusion.values_ref, bf16[8,272,2176]{2,1,0:T(8,128)(2,1)S(1)} %bitcast.152), custom_call_target="tpu_custom_call" | custom-call | flops 6442450944 | bytes 9437184 | tf_op jit(solution)/shard_map/collect_blocks/pallas_call | solution.py:723
  402.2 10.2 %collective-permute-done.33.second_far = bf16[256,1024]{1,0:T(8,128)(2,1)S(1)} collective-permute-done((bf16[256,1024]{1,0:T(8,128)(2,1)S(1)}, bf16[256,1024]{1,0:T(8,128)(2,1)S(1)}, u32[]{:S(2)}, u32[]{:S(2)}) %collective-permute-start.33) | collective-permute-done | bytes 524320 | tf_op jit(solution)/shard_map/ppermute | solution.py:943
  422.6 8.8 %collective-permute-done.34.left_ref = bf16[256,1024]{1,0:T(8,128)(2,1)S(1)} collective-permute-done((bf16[256,1024]{1,0:T(8,128)(2,1)S(1)}, bf16[256,1024]{1,0:T(8,128)(2,1)S(1)}, u32[]{:S(2)}, u32[]{:S(2)}) %collective-permute-start.34) | collective-permute-done | bytes 524320 | tf_op jit(solution)/shard_map/ppermute | solution.py:943
  466.6 28.4 %scan_backward.1.held_ref = bf16[1024,2688]{1,0:T(8,128)(2,1)S(1)} custom-call(bf16[1024,2688]{1,0:T(8,128)(2,1)S(1)} %bitcast.144, bf16[1024,2688]{1,0:T(8,128)(2,1)S(1)} %bitcast.144, bf16[1024,2688]{1,0:T(8,128)(2,1)S(1)} %bitcast.144, bf16[1024,2688]{1,0:T(8,128)(2,1)S(1)} %bitcast.144, bf16[1024,2688]{1,0:T(8,128)(2,1)S(1)} %bitcast.144, ...), custom_call_target="tpu_custom_call" | custom-call | flops 2684354560 | bytes 18874368 | tf_op jit(solution)/shard_map/scan_backward/pallas_call | solution.py:395
  499.4 7.5 %attention_backward.1.values_ref = bf16[1024,2688]{1,0:T(8,128)(2,1)S(1)} custom-call(bf16[1024,2688]{1,0:T(8,128)(2,1)S(1)} %bitcast.144, bf16[1024,2688]{1,0:T(8,128)(2,1)S(1)} %bitcast.144, bf16[1024,2688]{1,0:T(8,128)(2,1)S(1)} %bitcast.144, f32[1024,128]{1,0:T(8,128)S(1)} %copy-done.38, ...), custom_call_target="tpu_custom_call", output_to_operand_aliasing={{}: (8, {})} | custom-call | flops 1610612736 | bytes 6291456 | tf_op jit(solution)/shard_map/attention_backward/pallas_call | solution.py:542
  520.4 15.9 %collective-permute-done.51 = bf16[128,256]{1,0:T(8,128)(2,1)S(1)} collective-permute-done((bf16[128,256]{1,0:T(8,128)(2,1)S(1)}, bf16[128,256]{1,0:T(8,128)(2,1)S(1)}, u32[]{:S(2)}, u32[]{:S(2)}) %collective-permute-start.51) | collective-permute-done | bytes 65568 | tf_op jit(solution)/shard_map/ppermute | solution.py:943
  547.1 10.4 %collect_blocks.14 = (bf16[256,1152]{1,0:T(8,128)(2,1)S(1)}, f32[256,1024]{1,0:T(8,128)S(1)}, f32[256,1152]{1,0:T(8,128)S(1)}, bf16[256,1024]{1,0:T(8,128)(2,1)S...) custom-call(bf16[1024,2688]{1,0:T(8,128)(2,1)S(1)} %copy-done.20, bf16[8,272,768]{2,1,0:T(8,128)(2,1)S(1)} %copy-done.18, ...), custom_call_target="tpu_custom_call" | custom-call | flops 8455716864 | bytes 10420224 | tf_op jit(solution)/shard_map/collect_blocks/pallas_call | solution.py:723
  592.9 20.1 %collective-permute-done.53.second_far = bf16[256,1024]{1,0:T(8,128)(2,1)} collective-permute-done((bf16[256,1024]{1,0:T(8,128)(2,1)}, bf16[256,1024]{1,0:T(8,128)(2,1)}, u32[]{:S(2)}, u32[]{:S(2)}) %collective-permute-start.53) | collective-permute-done | bytes 524320 | tf_op jit(solution)/shard_map/ppermute | solution.py:943
  647.5 19.3 %all-to-all-done.3 = bf16[32,8,2304]{2,1,0:T(8,128)(2,1)S(1)} async-done(((bf16[32,8,2304]{2,1,0:T(8,128)(2,1)}), bf16[32,8,2304]{2,1,0:T(8,128)(2,1)S(1)}, u32[]{:S(2)}, u32[]{:S(2)}) %all-to-all-start.3) | async-done | bytes 1179680 | tf_op jit(solution)/shard_map/all_to_all | solution.py:1076
  (579 shorter events, 355.9 us)
Async XLA Ops:
  12.9 121.6 %all-gather.13.cloned.1.call-start = ((), (), s32[]{:S(2)}) async-start(), calls=%async_computation.9 | async-start | bytes 10027008 | tf_op jit(solution)/shard_map/all_gather | solution.py:1086
  21.5 190.9 %all-gather.15.cloned.1.call-start = ((), (), s32[]{:S(2)}) async-start(), calls=%async_computation.10 | async-start | bytes 5640192 | tf_op jit(solution)/shard_map/all_gather | solution.py:1086
  24.8 53.6 %all-to-all-start = ((bf16[32,8,2176]{2,1,0:T(8,128)(2,1)}), bf16[32,8,2176]{2,1,0:T(8,128)(2,1)S(1)}, u32[]{:S(2)}, u32[]{:S(2)}) async-start(bf16[32,8,2176]{2,1,0:T(8,128)(2,1)} %bitcast.181), calls=%async_computation | async-start | bytes 2228224 | tf_op jit(solution)/shard_map/all_to_all | solution.py:1076
  32.1 264.7 %all-gather.17.cloned.1.call-start = ((), (), s32[]{:S(2)}) async-start(), calls=%async_computation.11 | async-start | bytes 10653696 | tf_op jit(solution)/shard_map/all_gather | solution.py:1086
  40.0 38.4 %collective-permute-start.1 = (bf16[8,288,256]{2,1,0:T(8,128)(2,1)}, bf16[8,288,256]{2,1,0:T(8,128)(2,1)}, u32[]{:S(2)}, u32[]{:S(2)}) collective-permute-start(bf16[8,288,256]{2,1,0:T(8,128)(2,1)} %bitcast.183), channel_id=1, source_target_pairs={{0,2},{1,3},{2,0},{3,1},{4,6},{5,7},{6,4},{7,5},{8,10},{9,11},{10,... | collective-permute-start | bytes 3538952 | tf_op jit(solution)/shard_map/ppermute | solution.py:943
  81.2 265.3 %all-gather.19.cloned.1.call-start = ((), (), s32[]{:S(2)}) async-start(), calls=%async_computation.12 | async-start | bytes 5640192 | tf_op jit(solution)/shard_map/all_gather | solution.py:1086
  84.1 41.8 %collective-permute-start.7 = (bf16[4,288,256]{2,1,0:T(8,128)(2,1)S(1)}, bf16[4,288,256]{2,1,0:T(8,128)(2,1)S(1)}, u32[]{:S(2)}, u32[]{:S(2)}) collective-permute-start(bf16[4,288,256]{2,1,0:T(8,128)(2,1)S(1)} %slice.431), channel_id=1, source_target_pairs={{0,1},{1,0},{2,3},{3,2},{4,5},{5,4},{6,7},{7,6},{8,9},{9,8},{10,11... | collective-permute-start | bytes 1769480 | tf_op jit(solution)/shard_map/ppermute | solution.py:943
  86.6 39.5 %collective-permute-start.6 = (bf16[4,288,256]{2,1,0:T(8,128)(2,1)S(1)}, bf16[4,288,256]{2,1,0:T(8,128)(2,1)S(1)}, u32[]{:S(2)}, u32[]{:S(2)}) collective-permute-start(bf16[4,288,256]{2,1,0:T(8,128)(2,1)S(1)} %slice.430), channel_id=1, source_target_pairs={{0,2},{1,3},{2,0},{3,1},{4,6},{5,7},{6,4},{7,5},{8,10},{9,11},{10,... | collective-permute-start | bytes 1769480 | tf_op jit(solution)/shard_map/ppermute | solution.py:943
  91.3 66.0 %collective-permute-start.8 = (bf16[256,1024]{1,0:T(8,128)(2,1)}, bf16[256,1024]{1,0:T(8,128)(2,1)S(1)}, u32[]{:S(2)}, u32[]{:S(2)}) collective-permute-start(bf16[256,1024]{1,0:T(8,128)(2,1)} %get-tuple-element.122.right_ref), channel_id=1, source_target_pairs={{0,2},{1,3},{2,0},{3,1},{4,6},{5,7},{6,4},{7,5},{8,10},{9,11},{10,... | collective-permute-start | bytes 1572872 | tf_op jit(solution)/shard_map/ppermute | solution.py:943
  110.8 38.0 %collective-permute-start.9 = (bf16[256,1024]{1,0:T(8,128)(2,1)}, bf16[256,1024]{1,0:T(8,128)(2,1)}, u32[]{:S(2)}, u32[]{:S(2)}) collective-permute-start(bf16[256,1024]{1,0:T(8,128)(2,1)} %get-tuple-element.121.left_ref), channel_id=1, source_target_pairs={{0,1},{1,0},{2,3},{3,2},{4,5},{5,4},{6,7},{7,6},{8,9},{9,8},{10,11... | collective-permute-start | bytes 1572872 | tf_op jit(solution)/shard_map/ppermute | solution.py:943
  124.3 40.9 %collective-permute-start.5 = (bf16[256,1024]{1,0:T(8,128)(2,1)S(1)}, bf16[256,1024]{1,0:T(8,128)(2,1)}, u32[]{:S(2)}, u32[]{:S(2)}) collective-permute-start(bf16[256,1024]{1,0:T(8,128)(2,1)S(1)} %collective-permute-done.4.right_ref), channel_id=1, source_target_pairs={{0,2},{1,3},{2,0},{3,1},{4,6},{5,7},{6,4},{7,5},{8,10},{9,11},{10,... | collective-permute-start | bytes 1572872 | tf_op jit(solution)/shard_map/ppermute | solution.py:943
  125.9 39.4 %collective-permute-start.3 = (bf16[256,1024]{1,0:T(8,128)(2,1)S(1)}, bf16[256,1024]{1,0:T(8,128)(2,1)}, u32[]{:S(2)}, u32[]{:S(2)}) collective-permute-start(bf16[256,1024]{1,0:T(8,128)(2,1)S(1)} %collective-permute-done.2.left_ref), channel_id=1, source_target_pairs={{0,1},{1,0},{2,3},{3,2},{4,5},{5,4},{6,7},{7,6},{8,9},{9,8},{10,11... | collective-permute-start | bytes 1572872 | tf_op jit(solution)/shard_map/ppermute | solution.py:943
  182.9 89.5 %all-to-all-start.1 = ((bf16[32,8,2048]{2,1,0:T(8,128)(2,1)}), bf16[32,8,2048]{2,1,0:T(8,128)(2,1)}, u32[]{:S(2)}, u32[]{:S(2)}) async-start(bf16[32,8,2048]{2,1,0:T(8,128)(2,1)} %fusion.9), calls=%async_computation.1 | async-start | bytes 2097152 | tf_op jit(solution)/shard_map/all_to_all | solution.py:1076
  187.0 444.1 %reduce-scatter.5.cloned.1.call-start = ((), (), s32[]{:S(2)}) async-start(), calls=%async_computation.7 | async-start | bytes 626688 | tf_op jit(solution)/shard_map/reduce_scatter | solution.py:1243
  311.5 44.1 %collective-permute-start.26 = (bf16[256,1024]{1,0:T(8,128)(2,1)S(1)}, bf16[256,1024]{1,0:T(8,128)(2,1)}, u32[]{:S(2)}, u32[]{:S(2)}) collective-permute-start(bf16[256,1024]{1,0:T(8,128)(2,1)S(1)} %get-tuple-element.247.right_ref), channel_id=1, source_target_pairs={{0,2},{1,3},{2,0},{3,1},{4,6},{5,7},{6,4},{7,5},{8,10},{9,11},{10,... | collective-permute-start | bytes 1572872 | tf_op jit(solution)/shard_map/ppermute | solution.py:943
  311.9 40.3 %collective-permute-start.27 = (bf16[256,1024]{1,0:T(8,128)(2,1)}, bf16[256,1024]{1,0:T(8,128)(2,1)}, u32[]{:S(2)}, u32[]{:S(2)}) collective-permute-start(bf16[256,1024]{1,0:T(8,128)(2,1)} %get-tuple-element.248.left_ref), channel_id=1, source_target_pairs={{0,1},{1,0},{2,3},{3,2},{4,5},{5,4},{6,7},{7,6},{8,9},{9,8},{10,11... | collective-permute-start | bytes 1572872 | tf_op jit(solution)/shard_map/ppermute | solution.py:943
  318.1 40.8 %collective-permute-start.25 = (bf16[256,1024]{1,0:T(8,128)(2,1)}, bf16[256,1024]{1,0:T(8,128)(2,1)}, u32[]{:S(2)}, u32[]{:S(2)}) collective-permute-start(bf16[256,1024]{1,0:T(8,128)(2,1)} %collective-permute-done.24.right_ref), channel_id=1, source_target_pairs={{0,2},{1,3},{2,0},{3,1},{4,6},{5,7},{6,4},{7,5},{8,10},{9,11},{10,... | collective-permute-start | bytes 1572872 | tf_op jit(solution)/shard_map/ppermute | solution.py:943
  320.1 38.8 %collective-permute-start.23 = (bf16[256,1024]{1,0:T(8,128)(2,1)}, bf16[256,1024]{1,0:T(8,128)(2,1)}, u32[]{:S(2)}, u32[]{:S(2)}) collective-permute-start(bf16[256,1024]{1,0:T(8,128)(2,1)} %collective-permute-done.22.left_ref), channel_id=1, source_target_pairs={{0,1},{1,0},{2,3},{3,2},{4,5},{5,4},{6,7},{7,6},{8,9},{9,8},{10,11... | collective-permute-start | bytes 1572872 | tf_op jit(solution)/shard_map/ppermute | solution.py:943
  456.9 38.2 %collective-permute-start.44 = (bf16[256,1024]{1,0:T(8,128)(2,1)}, bf16[256,1024]{1,0:T(8,128)(2,1)}, u32[]{:S(2)}, u32[]{:S(2)}) collective-permute-start(bf16[256,1024]{1,0:T(8,128)(2,1)} %get-tuple-element.191), channel_id=1, source_target_pairs={{0,2},{1,3},{2,0},{3,1},{4,6},{5,7},{6,4},{7,5},{8,10},{9,11},{10,... | collective-permute-start | bytes 1572872 | tf_op jit(solution)/shard_map/ppermute | solution.py:943
  458.3 39.1 %collective-permute-start.41 = (bf16[256,1152]{1,0:T(8,128)(2,1)S(1)}, bf16[256,1152]{1,0:T(8,128)(2,1)}, u32[]{:S(2)}, u32[]{:S(2)}) collective-permute-start(bf16[256,1152]{1,0:T(8,128)(2,1)S(1)} %get-tuple-element.183), channel_id=1, source_target_pairs={{0,1},{1,0},{2,3},{3,2},{4,5},{5,4},{6,7},{7,6},{8,9},{9,8},{10,11... | collective-permute-start | bytes 1769480 | tf_op jit(solution)/shard_map/ppermute | solution.py:943
  510.3 58.7 %collective-permute-start.43 = (bf16[256,1024]{1,0:T(8,128)(2,1)}, bf16[256,1024]{1,0:T(8,128)(2,1)}, u32[]{:S(2)}, u32[]{:S(2)}) collective-permute-start(bf16[256,1024]{1,0:T(8,128)(2,1)} %get-tuple-element.189), channel_id=1, source_target_pairs={{0,2},{1,3},{2,0},{3,1},{4,6},{5,7},{6,4},{7,5},{8,10},{9,11},{10,... | collective-permute-start | bytes 1572872 | tf_op jit(solution)/shard_map/ppermute | solution.py:943
  510.8 58.1 %collective-permute-start.40 = (bf16[256,1152]{1,0:T(8,128)(2,1)}, bf16[256,1152]{1,0:T(8,128)(2,1)}, u32[]{:S(2)}, u32[]{:S(2)}) collective-permute-start(bf16[256,1152]{1,0:T(8,128)(2,1)} %get-tuple-element.181), channel_id=1, source_target_pairs={{0,1},{1,0},{2,3},{3,2},{4,5},{5,4},{6,7},{7,6},{8,9},{9,8},{10,11... | collective-permute-start | bytes 1769480 | tf_op jit(solution)/shard_map/ppermute | solution.py:943
  582.8 50.1 %all-to-all-start.2 = ((bf16[32,8,2816]{2,1,0:T(8,128)(2,1)}), bf16[32,8,2816]{2,1,0:T(8,128)(2,1)}, u32[]{:S(2)}, u32[]{:S(2)}) async-start(bf16[32,8,2816]{2,1,0:T(8,128)(2,1)} %pad_maximum_fusion.1), calls=%async_computation.2 | async-start | bytes 2883584 | tf_op jit(solution)/shard_map/all_to_all | solution.py:1076
  586.4 45.5 %reduce-scatter.3.cloned.1.call-start = ((), (), s32[]{:S(2)}) async-start(), calls=%async_computation.6 | async-start | bytes 1179648 | tf_op jit(solution)/shard_map/reduce_scatter | solution.py:1243
  (163 other events, 2421.1 us)
Sparse Core Ops, SparseCore 0:
  13.0 26.9 all-gather.10
  41.6 92.7 all-gather.12
  136.1 53.5 all-gather.14
  191.2 99.9 all-gather.16
  293.2 53.1 all-gather.18
  537.9 29.6 reduce-scatter.4
  589.5 37.5 reduce-scatter.2

commit v5 on v4

--- a/solution.py
+++ b/solution.py
@@ -63,6 +63,7 @@
     return (segment, position, selector)
 
 
+ESTIMATE = 16
 SCAN_BYTES = 32 * 1024 * 1024
 DENSE_BYTES = 16 * 1024 * 1024
 LANES = 128
@@ -70,6 +71,14 @@
 
 def whole(shape):
     return pl.BlockSpec(shape, lambda *_: (0,) * len(shape))
+
+
+def estimate(flops, bytes_accessed, transcendentals):
+    return pl.CostEstimate(
+        flops=flops // ESTIMATE,
+        bytes_accessed=bytes_accessed // ESTIMATE,
+        transcendentals=transcendentals // ESTIMATE,
+    )
 
 
 def dot(left, right, contract):
@@ -354,7 +363,7 @@
 
 def scan_cost(tokens, channels, factor):
     heads = channels // HP
-    return pl.CostEstimate(
+    return estimate(
         flops=factor * 2 * tokens * SSD_BLOCK * (3 * channels + NSTATE),
         bytes_accessed=factor * tokens * channels * 12,
         transcendentals=tokens * SSD_BLOCK * heads,
@@ -493,7 +502,7 @@
 
 
 def attention_cost(tokens, width, factor):
-    return pl.CostEstimate(
+    return estimate(
         flops=factor * 2 * tokens * tokens * width,
         bytes_accessed=factor * tokens * width * 8,
         transcendentals=tokens * tokens * width // (2 * HEAD_SIZE),
@@ -598,6 +607,7 @@
 
 
 HALVES = 2
+DENSE_TILE = 1024
 
 
 def matrix_rows(values):
@@ -627,7 +637,7 @@
     copies[0].start()
     column = 0
     for ref in weights:
-        for low, high in cut_tiles(ref.shape[2] - (LANES if ref is weights[-1] else 0), 512):
+        for low, high in cut_tiles(ref.shape[2] - (LANES if ref is weights[-1] else 0), DENSE_TILE):
             span = slice(column, column + high - low)
             column += high - low
             raised = matrix_rows(ref[:, rows : rows + NADAPT * RANK // shards, low:high])
@@ -656,7 +666,7 @@
         aliases = {len(operands): 0, len(operands) + 1: 1}
         operands += list(held)
         in_specs += [free] * 2
-    copies = 1 + sum(-(-part.shape[2] // 512) for part in gathered)
+    copies = 1 + sum(-(-part.shape[2] // DENSE_TILE) for part in gathered)
     return pl.pallas_call(
         functools.partial(spread_kernel, mask, len(gathered)),
         in_specs=in_specs,
@@ -672,7 +682,7 @@
         ],
         input_output_aliases=aliases,
         compiler_params=pltpu.CompilerParams(vmem_limit_bytes=DENSE_BYTES),
-        cost_estimate=pl.CostEstimate(
+        cost_estimate=estimate(
             flops=4 * rows * half * (width + LANES), bytes_accessed=2 * rows * (2 * half + width), transcendentals=0
         ),
         name="spread_block",
@@ -726,7 +736,7 @@
         out_specs=[fast] * len(out_shape),
         out_shape=out_shape,
         compiler_params=pltpu.CompilerParams(vmem_limit_bytes=DENSE_BYTES),
-        cost_estimate=pl.CostEstimate(
+        cost_estimate=estimate(
             flops=4 * len(masks) * rows * half * values.shape[1],
             bytes_accessed=2 * len(masks) * rows * (values.shape[1] + 4 * half),
             transcendentals=0,
@@ -747,10 +757,8 @@
     first = wide(first_own) + wide(first_near) + wide(first_far)
     second = wide(second_own) + wide(second_near) + wide(second_far)
     inner = (chosen_ref[...] * first[:, half:]).astype(BFLOAT)
-    shards, tall, _ = lower_ref.shape
-    rows = tall - NADAPT * RANK // shards
     summed = jnp.concatenate([first[:, :half], second], axis=1) + dot(
-        inner, matrix_rows(lower_ref[:, :rows, :]), (1, 1)
+        inner, matrix_rows(lower_ref[...]), (1, 1)
     )
     if kind == "output":
         residual_ref, out_ref, inner_ref = refs
@@ -785,15 +793,15 @@
 def finish(kind, parts, gathered, own_selector, *operands):
     rows = own_selector.shape[0]
     half = parts[3].shape[1]
-    shards, tall, full = gathered[-1].shape
+    shards = gathered[-1].shape[0]
     model = HALVES * half
+    lower = gathered[-1][:, : model // shards, -LANES:]
     result = BFLOAT if kind in ("output", "input") else FLOAT
     out_shape = [jax.ShapeDtypeStruct((rows, model), result), jax.ShapeDtypeStruct((rows, LANES), BFLOAT)]
     if kind in ("forward", "backward"):
         out_shape += [jax.ShapeDtypeStruct((rows, half), BFLOAT)] * 2
-    given = [*parts, gathered[-1], own_selector, *operands]
+    given = [*parts, lower, own_selector, *operands]
     in_specs = [whole(value.shape) for value in given]
-    in_specs[6] = pl.BlockSpec((shards, tall, LANES), lambda *_: (0, 0, full // LANES - 1))
     return pl.pallas_call(
         functools.partial(finish_kernel, kind),
         grid=(1,),
@@ -801,7 +809,7 @@
         out_specs=[whole(shape.shape) for shape in out_shape],
         out_shape=out_shape,
         compiler_params=pltpu.CompilerParams(vmem_limit_bytes=DENSE_BYTES),
-        cost_estimate=pl.CostEstimate(
+        cost_estimate=estimate(
             flops=2 * rows * model * LANES, bytes_accessed=rows * model * 20, transcendentals=0
         ),
         name="finish_" + kind,
@@ -978,10 +986,10 @@
     return (both[:, :width] + product(narrow, narrow_factor)).astype(BFLOAT), narrow
 
 
-def collect_start(values, gathered, earlier=()):
+def collect_start(values, gathered):
     (corner,) = collect_blocks([3], values, gathered, [(BFLOAT, BFLOAT)])
     arriving = flip(corner[0], 1), flip(corner[1], 2)
-    values = after(values, *earlier) if earlier else values
+    values = after(values, corner[0])
     near, far, own = collect_blocks([1, 2, 0], values, gathered, [(BFLOAT, FLOAT), (FLOAT, BFLOAT), (FLOAT, FLOAT)])
     return own, flip(near[0], 1), flip(far[1], 2), far[0], near[1], arriving
 
@@ -1100,12 +1108,11 @@
         shared_shard = shared
         shared = lax.all_gather(shared_shard, "row", axis=0)
         weights_own = gather_weight(own_columns[:depth], in_lower, own_columns[depth:])
-        sent = after(sent, shared_shard, shards[0])
     arrived = exchange(sent)
     gains = jnp.broadcast_to(norm_gains.astype(FLOAT)[:, None, :], (2, 8, model))
     if fast:
         near, far = flip(shared, 1), flip(shared, 2)
-        arrived = after(arrived, near, far)
+        arrived = after(arrived, near, far, shards[0])
     own_input, place_matrix, *normed_one = arrive_tokens(arrived.reshape(rows, model + LANES), gains[0])
     blocks_one = gather_blocks(normed_one) if fast else normed_one
     if fast:
@@ -1219,12 +1226,14 @@
             projected, tables, scanned, carried, after(mixed_grad, started[0][0], started[3])
         )
         kept, onward = collect_middle((*started[:5], [after(part, projected_grad) for part in started[5]]))
-        projected_grad = attention_backward(projected, tables, mixed_grad, after(projected_grad, *onward))
+        projected_grad = attention_backward(
+            projected, tables, mixed_grad, after(projected_grad, *onward, *kept[1:])
+        )
         last = collect_onward(onward)
-        started_in = collect_start(projected_grad, weights_in, last)
+        started_in = collect_start(projected_grad, weights_in)
         kept_in, onward_in = collect_middle(started_in)
         block_out, inner_down = collect_end(
-            kept, last, "output", weights_down, own_selector, after(hidden, *onward_in, *kept_in[1:])
+            kept, last, "output", weights_down, own_selector, after(hidden, started_in[0][0])
         )
     else:
         block_out, inner_down = collect_project(activated, weights_down, "output", own_selector, hidden)
@@ -1237,6 +1246,7 @@
             compact_grad(narrow_three, jnp.concatenate(normed_two, axis=1)),
             compact_grad(inner_out, jnp.concatenate(branch_one, axis=1)),
         ],
+        [*onward_in, *kept_in[1:]] if fast else (),
     )
 
     def sum_rows(values):
@@ -1249,7 +1259,7 @@
     ]
     early = sum_rows(jnp.concatenate(early_parts, axis=1))
 
-    raise_grad = contract_first(inner_in, projected_grad)
+    raise_grad = contract_first(inner_in, after(projected_grad, *onward_in) if fast else projected_grad)
     key_columns = raise_grad[:, STATES : STATES + HEAD_SIZE]
     value_columns = raise_grad[:, STATES + HEAD_SIZE : STATES + PAIR]
     mine = [(key_head == at).astype(FLOAT) for at in range(KEY_VALUE_HEADS)]

time: 685 us -> 668 us (0.975)
  waiting for transfers between devices: 235 us -> 222 us
  Pallas kernels: 183 us -> 174 us
    ppermute x54, waiting for transfers between devices: 152 us -> 139 us  [flip(): return lax.ppermute(values, 'col', [(i, i ^ mask) for i in range(4)])]
    all_to_all x4, waiting for transfers between devices: 51.9 us -> 41.2 us  [local(): lax.all_to_all(values, ALL_AXES, split_axis=0, concat_axis=0, tiled=True)]
    pallas_call x16, Pallas kernels: 79.8 us -> 71.3 us  [spread_block(): pl.pallas_call(functools.partial(spread_kernel, mask, len(gathered)), in_...]
    unnamed x266 -> x330, local copies, waits for them, and re-layouts: 82.3 us -> 78.9 us
  transfers between devices with their start and end apart: 65 -> 65, of which waited for: 27 -> 29; matrix products, arithmetic and copies ran while one was open for 11% -> 13% of each run, Pallas kernels for 24% -> 24%
where the time goes in v5:
time: 668 us; the launch traced here: 659 us
  waiting for transfers between devices  222 us (33%)
  Pallas kernels  174 us (26%)
  local copies, waits for them, and re-layouts  106 us (16%)
  starting transfers between devices  78.6 us (12%)
  other arithmetic  35.1 us (5%)
  matrix products  25.8 us (4%)
  between operations  18.3 us (3%)
    ppermute x54, waiting for transfers between devices, flip(): return lax.ppermute(values, 'col', [(i, i ^ mask) for i in range(4)])  139 us
    unnamed x330, local copies, waits for them, and re-layouts  78.9 us
    pallas_call x16, Pallas kernels, spread_block(): pl.pallas_call(functools.partial(spread_kernel, mask, len(gathered)), in_...  71.3 us
    ppermute x54, starting transfers between devices, flip(): return lax.ppermute(values, 'col', [(i, i ^ mask) for i in range(4)])  61.1 us
    all_to_all x4, waiting for transfers between devices, local(): lax.all_to_all(values, ALL_AXES, split_axis=0, concat_axis=0, tiled=True)  41.2 us
    pallas_call x8, Pallas kernels, collect_blocks(): pl.pallas_call(functools.partial(collect_kernel, masks, len(gathered)), i...  38.1 us
    pallas_call x1, Pallas kernels, scan_backward(): pl.pallas_call(scan_backward_kernel, grid=(blocks,), in_specs=scan_specs(...  27.8 us
    all_gather x4, waiting for transfers between devices, gather_weight(): return (lax.all_gather(shards[-1], 'row', axis=0),)  23.6 us
  transfers between devices with their start and end apart: 65, of which 29 were waited for; matrix products, arithmetic and copies ran while one was open for 13% of the time, Pallas kernels for 24%

profile of v5, /device:TPU:0, one launch (start us, length us, event | category | flops | bytes accessed | tf_op | source)
XLA Modules:
  0.0 659.4 jit_solution(1732734906583899581)
XLA Ops:
  23.0 7.3 %all-to-all-start = ((bf16[32,8,2176]{2,1,0:T(8,128)(2,1)}), bf16[32,8,2176]{2,1,0:T(8,128)(2,1)S(1)}, u32[]{:S(2)}, u32[]{:S(2)}) async-start(bf16[32,8,2176]{2,1,0:T(8,128)(2,1)} %bitcast.181), calls=%async_computation | async-start | bytes 2228224 | tf_op jit(solution)/shard_map/all_to_all | solution.py:1084
  30.4 12.0 %all-gather.11.cloned.1.call-done = bf16[2304,256]{1,0:T(8,128)(2,1)} async-done(((bf16[288,256]{1,0:T(8,128)(2,1)}), bf16[2304,256]{1,0:T(8,128)(2,1)}) %all-gather.11.cloned.1.call-update) | async-done | bytes 1179664 | tf_op jit(solution)/shard_map/all_gather | solution.py:1109
  48.0 21.9 %all-to-all-done = bf16[32,8,2176]{2,1,0:T(8,128)(2,1)S(1)} async-done(((bf16[32,8,2176]{2,1,0:T(8,128)(2,1)}), bf16[32,8,2176]{2,1,0:T(8,128)(2,1)S(1)}, u32[]{:S(2)}, u32[]{:S(2)}) %all-to-all-start) | async-done | bytes 1114144 | tf_op jit(solution)/shard_map/all_to_all | solution.py:1084
  69.9 6.2 collective-permute-done.1
  96.1 12.8 %collective-permute-done.4.right_ref = bf16[256,1024]{1,0:T(8,128)(2,1)S(1)} collective-permute-done((bf16[256,1024]{1,0:T(8,128)(2,1)}, bf16[256,1024]{1,0:T(8,128)(2,1)S(1)}, u32[]{:S(2)}, u32[]{:S(2)}) %collective-permute-start.4) | collective-permute-done | bytes 524320 | tf_op jit(solution)/shard_map/ppermute | solution.py:951
  109.6 12.2 %collective-permute-done.2.left_ref = bf16[256,1024]{1,0:T(8,128)(2,1)} collective-permute-done((bf16[256,1024]{1,0:T(8,128)(2,1)}, bf16[256,1024]{1,0:T(8,128)(2,1)}, u32[]{:S(2)}, u32[]{:S(2)}) %collective-permute-start.2) | collective-permute-done | bytes 524320 | tf_op jit(solution)/shard_map/ppermute | solution.py:951
  139.7 7.5 %spread_block.16 = (bf16[1024,2688]{1,0:T(8,128)(2,1)S(1)}, bf16[1024,128]{1,0:T(8,128)(2,1)S(1)}) custom-call(bf16[256,1024]{1,0:T(8,128)(2,1)} %get-tuple-element.124.left_ref, bf16[256,1024]{1,0:T(8,128)(2,1)} %get-tuple-element.125.right_ref, f32[1024,128]{1,0:T(8,128)S(1)} %compare_convert_fusion.chosen_ref, bf16[8,272,768]{2,1,0:T(8,128)(2,1)S(1)} %copy-done.15, ...), custom_call_target="tpu_custom_call" | custom-call | flops 184549376 | bytes 151552 | tf_op jit(solution)/shard_map/spread_block/pallas_call | solution.py:670
  147.2 7.1 %spread_block.17 = (bf16[1024,2688]{1,0:T(8,128)(2,1)S(1)}, bf16[1024,128]{1,0:T(8,128)(2,1)S(1)}) custom-call(bf16[256,1024]{1,0:T(8,128)(2,1)} %collective-permute-done.9.left_ref, bf16[256,1024]{1,0:T(8,128)(2,1)S(1)} %collective-permute-done.4.right_ref, ...), custom_call_target="tpu_custom_call", output_to_operand_aliasing={{0}: (5, {}), {1}: (6, {})} | custom-call | flops 184549376 | bytes 151552 | tf_op jit(solution)/shard_map/spread_block/pallas_call | solution.py:670
  154.3 7.5 %spread_block.18 = (bf16[1024,2688]{1,0:T(8,128)(2,1)S(1)}, bf16[1024,128]{1,0:T(8,128)(2,1)S(1)}) custom-call(bf16[256,1024]{1,0:T(8,128)(2,1)} %collective-permute-done.2.left_ref, bf16[256,1024]{1,0:T(8,128)(2,1)S(1)} %collective-permute-done.8.right_ref, ...), custom_call_target="tpu_custom_call", output_to_operand_aliasing={{0}: (5, {}), {1}: (6, {})} | custom-call | flops 184549376 | bytes 151552 | tf_op jit(solution)/shard_map/spread_block/pallas_call | solution.py:670
  161.9 7.3 %spread_block.19 = (bf16[1024,2688]{1,0:T(8,128)(2,1)S(1)}, bf16[1024,128]{1,0:T(8,128)(2,1)S(1)}) custom-call(bf16[256,1024]{1,0:T(8,128)(2,1)} %collective-permute-done.3.left_ref, bf16[256,1024]{1,0:T(8,128)(2,1)} %collective-permute-done.5.right_ref, ...), custom_call_target="tpu_custom_call", output_to_operand_aliasing={{0}: (5, {}), {1}: (6, {})} | custom-call | flops 184549376 | bytes 151552 | tf_op jit(solution)/shard_map/spread_block/pallas_call | solution.py:670
  189.7 12.9 %scan_forward.1 = (bf16[1024,1024]{1,0:T(8,128)(2,1)S(1)}, f32[1024,768]{1,0:T(8,128)S(1)}, bf16[4,256,768]{2,1,0:T(8,128)(2,1)S(1)}) custom-call(bf16[1024,2688]{1,0:T(8,128)(2,1)S(1)} %copy-done.3, bf16[1024,2688]{1,0:T(8,128)(2,1)S(1)} %copy-done.3, bf16[1024,2688]{1,0:T(8,128)(2,1)S(1)} %copy-done.3, ...), custom_call_target="tpu_custom_call", output_to_operand_aliasing={{0}: (12, {})} | custom-call | flops 83886080 | bytes 589824 | tf_op jit(solution)/shard_map/scan_forward/pallas_call | solution.py:377
  242.0 11.2 %collective-permute-done.15.second_far = bf16[256,1024]{1,0:T(8,128)(2,1)} collective-permute-done((bf16[256,1024]{1,0:T(8,128)(2,1)}, bf16[256,1024]{1,0:T(8,128)(2,1)}, u32[]{:S(2)}, u32[]{:S(2)}) %collective-permute-start.15) | collective-permute-done | bytes 524320 | tf_op jit(solution)/shard_map/ppermute | solution.py:951
  277.2 6.6 %collective-permute-done.22.left_ref = bf16[256,1024]{1,0:T(8,128)(2,1)} collective-permute-done((bf16[256,1024]{1,0:T(8,128)(2,1)}, bf16[256,1024]{1,0:T(8,128)(2,1)}, u32[]{:S(2)}, u32[]{:S(2)}) %collective-permute-start.22) | collective-permute-done | bytes 524320 | tf_op jit(solution)/shard_map/ppermute | solution.py:951
  325.2 17.9 %all-gather.19.cloned.1.call-done = bf16[2176,1152]{1,0:T(8,128)(2,1)} async-done(((bf16[272,1152]{1,0:T(8,128)(2,1)}), bf16[2176,1152]{1,0:T(8,128)(2,1)}) %all-gather.19.cloned.1.call-update) | async-done | bytes 5013520 | tf_op jit(solution)/shard_map/all_gather | solution.py:1094
  369.4 7.5 %collect_blocks.11 = (bf16[256,1152]{1,0:T(8,128)(2,1)S(1)}, f32[256,1024]{1,0:T(8,128)S(1)}, f32[256,1152]{1,0:T(8,128)S(1)}, bf16[256,1024]{1,0:T(8,128)(2,1)S...) custom-call(bf16[1024,2048]{1,0:T(8,128)(2,1)S(1)} %pad_maximum_fusion.values_ref, bf16[8,272,2176]{2,1,0:T(8,128)(2,1)S(1)} %bitcast.152), custom_call_target="tpu_custom_call" | custom-call | flops 402653184 | bytes 589824 | tf_op jit(solution)/shard_map/collect_blocks/pallas_call | solution.py:733
  385.7 17.2 %collective-permute-done.32 = bf16[256,1024]{1,0:T(8,128)(2,1)S(1)} collective-permute-done((bf16[256,1024]{1,0:T(8,128)(2,1)S(1)}, bf16[256,1024]{1,0:T(8,128)(2,1)S(1)}, u32[]{:S(2)}, u32[]{:S(2)}) %collective-permute-start.32) | collective-permute-done | bytes 524320 | tf_op jit(solution)/shard_map/ppermute | solution.py:951
  403.9 11.2 %collective-permute-done.33.second_far = bf16[256,1024]{1,0:T(8,128)(2,1)S(1)} collective-permute-done((bf16[256,1024]{1,0:T(8,128)(2,1)S(1)}, bf16[256,1024]{1,0:T(8,128)(2,1)S(1)}, u32[]{:S(2)}, u32[]{:S(2)}) %collective-permute-start.33) | collective-permute-done | bytes 524320 | tf_op jit(solution)/shard_map/ppermute | solution.py:951
  423.2 10.9 %collective-permute-done.34.left_ref = bf16[256,1024]{1,0:T(8,128)(2,1)} collective-permute-done((bf16[256,1024]{1,0:T(8,128)(2,1)S(1)}, bf16[256,1024]{1,0:T(8,128)(2,1)}, u32[]{:S(2)}, u32[]{:S(2)}) %collective-permute-start.34) | collective-permute-done | bytes 524320 | tf_op jit(solution)/shard_map/ppermute | solution.py:951
  474.4 27.8 %scan_backward.1.held_ref = bf16[1024,2688]{1,0:T(8,128)(2,1)S(1)} custom-call(bf16[1024,2688]{1,0:T(8,128)(2,1)S(1)} %bitcast.144, bf16[1024,2688]{1,0:T(8,128)(2,1)S(1)} %bitcast.144, bf16[1024,2688]{1,0:T(8,128)(2,1)S(1)} %bitcast.144, bf16[1024,2688]{1,0:T(8,128)(2,1)S(1)} %bitcast.144, bf16[1024,2688]{1,0:T(8,128)(2,1)S(1)} %bitcast.144, ...), custom_call_target="tpu_custom_call" | custom-call | flops 167772160 | bytes 1179648 | tf_op jit(solution)/shard_map/scan_backward/pallas_call | solution.py:404
  507.4 7.5 %attention_backward.1.values_ref = bf16[1024,2688]{1,0:T(8,128)(2,1)S(1)} custom-call(bf16[1024,2688]{1,0:T(8,128)(2,1)S(1)} %bitcast.144, bf16[1024,2688]{1,0:T(8,128)(2,1)S(1)} %bitcast.144, bf16[1024,2688]{1,0:T(8,128)(2,1)S(1)} %bitcast.144, f32[1024,128]{1,0:T(8,128)S(1)} %copy-done.34, ...), custom_call_target="tpu_custom_call", output_to_operand_aliasing={{}: (8, {})} | custom-call | flops 100663296 | bytes 393216 | tf_op jit(solution)/shard_map/attention_backward/pallas_call | solution.py:551
  530.8 10.9 %collect_blocks.15 = (bf16[256,1152]{1,0:T(8,128)(2,1)}, f32[256,1024]{1,0:T(8,128)S(1)}, f32[256,1152]{1,0:T(8,128)S(1)}, bf16[256,1024]{1,0:T(8,128)(2,1)}, f3...) custom-call(bf16[1024,2688]{1,0:T(8,128)(2,1)S(1)} %copy-done.13, bf16[8,272,768]{2,1,0:T(8,128)(2,1)S(1)} %copy-done.17, ...), custom_call_target="tpu_custom_call" | custom-call | flops 528482304 | bytes 651264 | tf_op jit(solution)/shard_map/collect_blocks/pallas_call | solution.py:733
  569.9 8.4 %collective-permute-done.50 = bf16[2,128,256]{2,1,0:T(8,128)(2,1)S(1)} collective-permute-done((bf16[2,128,256]{2,1,0:T(8,128)(2,1)S(1)}, bf16[2,128,256]{2,1,0:T(8,128)(2,1)S(1)}, u32[]{:S(2)}, u32[]{:S(2)}) %collective-permute-start.50) | collective-permute-done | bytes 131104 | tf_op jit(solution)/shard_map/ppermute | solution.py:951
  584.9 10.3 %collective-permute-done.53.second_far = bf16[256,1024]{1,0:T(8,128)(2,1)} collective-permute-done((bf16[256,1024]{1,0:T(8,128)(2,1)}, bf16[256,1024]{1,0:T(8,128)(2,1)}, u32[]{:S(2)}, u32[]{:S(2)}) %collective-permute-start.53) | collective-permute-done | bytes 524320 | tf_op jit(solution)/shard_map/ppermute | solution.py:951
  630.4 19.3 %all-to-all-done.3 = bf16[32,8,2304]{2,1,0:T(8,128)(2,1)S(1)} async-done(((bf16[32,8,2304]{2,1,0:T(8,128)(2,1)}), bf16[32,8,2304]{2,1,0:T(8,128)(2,1)S(1)}, u32[]{:S(2)}, u32[]{:S(2)}) %all-to-all-start.3) | async-done | bytes 1179680 | tf_op jit(solution)/shard_map/all_to_all | solution.py:1084
  (647 shorter events, 359.6 us)
Async XLA Ops:
  12.6 121.6 %all-gather.13.cloned.1.call-start = ((), (), s32[]{:S(2)}) async-start(), calls=%async_computation.9 | async-start | bytes 10027008 | tf_op jit(solution)/shard_map/all_gather | solution.py:1094
  21.2 185.6 %all-gather.15.cloned.1.call-start = ((), (), s32[]{:S(2)}) async-start(), calls=%async_computation.10 | async-start | bytes 5640192 | tf_op jit(solution)/shard_map/all_gather | solution.py:1094
  23.0 46.9 %all-to-all-start = ((bf16[32,8,2176]{2,1,0:T(8,128)(2,1)}), bf16[32,8,2176]{2,1,0:T(8,128)(2,1)S(1)}, u32[]{:S(2)}, u32[]{:S(2)}) async-start(bf16[32,8,2176]{2,1,0:T(8,128)(2,1)} %bitcast.181), calls=%async_computation | async-start | bytes 2228224 | tf_op jit(solution)/shard_map/all_to_all | solution.py:1084
  30.4 270.0 %all-gather.17.cloned.1.call-start = ((), (), s32[]{:S(2)}) async-start(), calls=%async_computation.11 | async-start | bytes 10653696 | tf_op jit(solution)/shard_map/all_gather | solution.py:1094
  78.8 264.4 %all-gather.19.cloned.1.call-start = ((), (), s32[]{:S(2)}) async-start(), calls=%async_computation.12 | async-start | bytes 5640192 | tf_op jit(solution)/shard_map/all_gather | solution.py:1094
  82.3 40.7 %collective-permute-start.7 = (bf16[4,288,256]{2,1,0:T(8,128)(2,1)S(1)}, bf16[4,288,256]{2,1,0:T(8,128)(2,1)S(1)}, u32[]{:S(2)}, u32[]{:S(2)}) collective-permute-start(bf16[4,288,256]{2,1,0:T(8,128)(2,1)S(1)} %slice.447), channel_id=1, source_target_pairs={{0,1},{1,0},{2,3},{3,2},{4,5},{5,4},{6,7},{7,6},{8,9},{9,8},{10,11... | collective-permute-start | bytes 1769480 | tf_op jit(solution)/shard_map/ppermute | solution.py:951
  84.3 40.1 %collective-permute-start.6 = (bf16[4,288,256]{2,1,0:T(8,128)(2,1)S(1)}, bf16[4,288,256]{2,1,0:T(8,128)(2,1)S(1)}, u32[]{:S(2)}, u32[]{:S(2)}) collective-permute-start(bf16[4,288,256]{2,1,0:T(8,128)(2,1)S(1)} %slice.446), channel_id=1, source_target_pairs={{0,2},{1,3},{2,0},{3,1},{4,6},{5,7},{6,4},{7,5},{8,10},{9,11},{10,... | collective-permute-start | bytes 1769480 | tf_op jit(solution)/shard_map/ppermute | solution.py:951
  89.9 64.4 %collective-permute-start.8 = (bf16[256,1024]{1,0:T(8,128)(2,1)}, bf16[256,1024]{1,0:T(8,128)(2,1)S(1)}, u32[]{:S(2)}, u32[]{:S(2)}) collective-permute-start(bf16[256,1024]{1,0:T(8,128)(2,1)} %get-tuple-element.125.right_ref), channel_id=1, source_target_pairs={{0,2},{1,3},{2,0},{3,1},{4,6},{5,7},{6,4},{7,5},{8,10},{9,11},{10,... | collective-permute-start | bytes 1572872 | tf_op jit(solution)/shard_map/ppermute | solution.py:951
  108.8 38.4 %collective-permute-start.9 = (bf16[256,1024]{1,0:T(8,128)(2,1)}, bf16[256,1024]{1,0:T(8,128)(2,1)}, u32[]{:S(2)}, u32[]{:S(2)}) collective-permute-start(bf16[256,1024]{1,0:T(8,128)(2,1)} %get-tuple-element.124.left_ref), channel_id=1, source_target_pairs={{0,1},{1,0},{2,3},{3,2},{4,5},{5,4},{6,7},{7,6},{8,9},{9,8},{10,11... | collective-permute-start | bytes 1572872 | tf_op jit(solution)/shard_map/ppermute | solution.py:951
  121.9 40.0 %collective-permute-start.5 = (bf16[256,1024]{1,0:T(8,128)(2,1)S(1)}, bf16[256,1024]{1,0:T(8,128)(2,1)}, u32[]{:S(2)}, u32[]{:S(2)}) collective-permute-start(bf16[256,1024]{1,0:T(8,128)(2,1)S(1)} %collective-permute-done.4.right_ref), channel_id=1, source_target_pairs={{0,2},{1,3},{2,0},{3,1},{4,6},{5,7},{6,4},{7,5},{8,10},{9,11},{10,... | collective-permute-start | bytes 1572872 | tf_op jit(solution)/shard_map/ppermute | solution.py:951
  123.0 38.9 %collective-permute-start.3 = (bf16[256,1024]{1,0:T(8,128)(2,1)}, bf16[256,1024]{1,0:T(8,128)(2,1)}, u32[]{:S(2)}, u32[]{:S(2)}) collective-permute-start(bf16[256,1024]{1,0:T(8,128)(2,1)} %collective-permute-done.2.left_ref), channel_id=1, source_target_pairs={{0,1},{1,0},{2,3},{3,2},{4,5},{5,4},{6,7},{7,6},{8,9},{9,8},{10,11... | collective-permute-start | bytes 1572872 | tf_op jit(solution)/shard_map/ppermute | solution.py:951
  176.9 58.5 %all-to-all-start.1 = ((bf16[32,8,2048]{2,1,0:T(8,128)(2,1)}), bf16[32,8,2048]{2,1,0:T(8,128)(2,1)}, u32[]{:S(2)}, u32[]{:S(2)}) async-start(bf16[32,8,2048]{2,1,0:T(8,128)(2,1)} %fusion.9), calls=%async_computation.1 | async-start | bytes 2097152 | tf_op jit(solution)/shard_map/all_to_all | solution.py:1084
  180.8 429.3 %reduce-scatter.3.cloned.1.call-start = ((), (), s32[]{:S(2)}) async-start(), calls=%async_computation.6 | async-start | bytes 1179648 | tf_op jit(solution)/shard_map/reduce_scatter | solution.py:1253
  275.7 42.4 %collective-permute-start.19 = (bf16[256,1024]{1,0:T(8,128)(2,1)}, bf16[256,1024]{1,0:T(8,128)(2,1)}, u32[]{:S(2)}, u32[]{:S(2)}) collective-permute-start(bf16[256,1024]{1,0:T(8,128)(2,1)} %collective-permute-done.18.right_ref), channel_id=1, source_target_pairs={{0,2},{1,3},{2,0},{3,1},{4,6},{5,7},{6,4},{7,5},{8,10},{9,11},{10,... | collective-permute-start | bytes 1572872 | tf_op jit(solution)/shard_map/ppermute | solution.py:951
  283.9 64.8 %collective-permute-start.27 = (bf16[256,1024]{1,0:T(8,128)(2,1)}, bf16[256,1024]{1,0:T(8,128)(2,1)}, u32[]{:S(2)}, u32[]{:S(2)}) collective-permute-start(bf16[256,1024]{1,0:T(8,128)(2,1)} %get-tuple-element.256.left_ref), channel_id=1, source_target_pairs={{0,1},{1,0},{2,3},{3,2},{4,5},{5,4},{6,7},{7,6},{8,9},{9,8},{10,11... | collective-permute-start | bytes 1572872 | tf_op jit(solution)/shard_map/ppermute | solution.py:951
  287.6 64.3 %collective-permute-start.26 = (bf16[256,1024]{1,0:T(8,128)(2,1)}, bf16[256,1024]{1,0:T(8,128)(2,1)}, u32[]{:S(2)}, u32[]{:S(2)}) collective-permute-start(bf16[256,1024]{1,0:T(8,128)(2,1)} %get-tuple-element.255.right_ref), channel_id=1, source_target_pairs={{0,2},{1,3},{2,0},{3,1},{4,6},{5,7},{6,4},{7,5},{8,10},{9,11},{10,... | collective-permute-start | bytes 1572872 | tf_op jit(solution)/shard_map/ppermute | solution.py:951
  295.8 59.2 %collective-permute-start.25 = (bf16[256,1024]{1,0:T(8,128)(2,1)}, bf16[256,1024]{1,0:T(8,128)(2,1)}, u32[]{:S(2)}, u32[]{:S(2)}) collective-permute-start(bf16[256,1024]{1,0:T(8,128)(2,1)} %collective-permute-done.24.right_ref), channel_id=1, source_target_pairs={{0,2},{1,3},{2,0},{3,1},{4,6},{5,7},{6,4},{7,5},{8,10},{9,11},{10,... | collective-permute-start | bytes 1572872 | tf_op jit(solution)/shard_map/ppermute | solution.py:951
  298.8 56.2 %collective-permute-start.23 = (bf16[256,1024]{1,0:T(8,128)(2,1)}, bf16[256,1024]{1,0:T(8,128)(2,1)}, u32[]{:S(2)}, u32[]{:S(2)}) collective-permute-start(bf16[256,1024]{1,0:T(8,128)(2,1)} %collective-permute-done.22.left_ref), channel_id=1, source_target_pairs={{0,1},{1,0},{2,3},{3,2},{4,5},{5,4},{6,7},{7,6},{8,9},{9,8},{10,11... | collective-permute-start | bytes 1572872 | tf_op jit(solution)/shard_map/ppermute | solution.py:951
  463.1 40.3 %collective-permute-start.44 = (bf16[256,1024]{1,0:T(8,128)(2,1)S(1)}, bf16[256,1024]{1,0:T(8,128)(2,1)S(1)}, u32[]{:S(2)}, u32[]{:S(2)}) collective-permute-start(bf16[256,1024]{1,0:T(8,128)(2,1)S(1)} %get-tuple-element.197), channel_id=1, source_target_pairs={{0,2},{1,3},{2,0},{3,1},{4,6},{5,7},{6,4},{7,5},{8,10},{9,11},{10,... | collective-permute-start | bytes 1572872 | tf_op jit(solution)/shard_map/ppermute | solution.py:951
  465.2 40.5 %collective-permute-start.41 = (bf16[256,1152]{1,0:T(8,128)(2,1)S(1)}, bf16[256,1152]{1,0:T(8,128)(2,1)S(1)}, u32[]{:S(2)}, u32[]{:S(2)}) collective-permute-start(bf16[256,1152]{1,0:T(8,128)(2,1)S(1)} %get-tuple-element.185), channel_id=1, source_target_pairs={{0,1},{1,0},{2,3},{3,2},{4,5},{5,4},{6,7},{7,6},{8,9},{9,8},{10,11... | collective-permute-start | bytes 1769480 | tf_op jit(solution)/shard_map/ppermute | solution.py:951
  504.4 41.4 %collective-permute-start.45 = (bf16[256,1024]{1,0:T(8,128)(2,1)}, bf16[256,1024]{1,0:T(8,128)(2,1)}, u32[]{:S(2)}, u32[]{:S(2)}) collective-permute-start(bf16[256,1024]{1,0:T(8,128)(2,1)} %add_convert_fusion.5), channel_id=1, source_target_pairs={{0,1},{1,0},{2,3},{3,2},{4,5},{5,4},{6,7},{7,6},{8,9},{9,8},{10,11... | collective-permute-start | bytes 1572872 | tf_op jit(solution)/shard_map/ppermute | solution.py:951
  506.6 39.2 %collective-permute-start.42 = (bf16[256,1152]{1,0:T(8,128)(2,1)}, bf16[256,1152]{1,0:T(8,128)(2,1)}, u32[]{:S(2)}, u32[]{:S(2)}) collective-permute-start(bf16[256,1152]{1,0:T(8,128)(2,1)} %add_convert_fusion.1), channel_id=1, source_target_pairs={{0,2},{1,3},{2,0},{3,1},{4,6},{5,7},{6,4},{7,5},{8,10},{9,11},{10,... | collective-permute-start | bytes 1769480 | tf_op jit(solution)/shard_map/ppermute | solution.py:951
  559.0 58.8 %all-to-all-start.2 = ((bf16[32,8,2816]{2,1,0:T(8,128)(2,1)}), bf16[32,8,2816]{2,1,0:T(8,128)(2,1)}, u32[]{:S(2)}, u32[]{:S(2)}) async-start(bf16[32,8,2816]{2,1,0:T(8,128)(2,1)} %pad_maximum_fusion.1), calls=%async_computation.2 | async-start | bytes 2883584 | tf_op jit(solution)/shard_map/all_to_all | solution.py:1084
  562.4 54.5 %reduce-scatter.5.cloned.1.call-start = ((), (), s32[]{:S(2)}) async-start(), calls=%async_computation.7 | async-start | bytes 626688 | tf_op jit(solution)/shard_map/reduce_scatter | solution.py:1253
  (195 other events, 2400.5 us)
Sparse Core Ops, SparseCore 0:
  12.8 29.6 all-gather.10
  44.1 90.1 all-gather.12
  136.5 57.7 all-gather.14
  195.8 93.0 all-gather.16
  290.3 52.7 all-gather.18
  521.9 30.1 reduce-scatter.2
  583.7 33.1 reduce-scatter.4

commit v6 on v5

--- a/solution.py
+++ b/solution.py
@@ -986,12 +986,22 @@
     return (both[:, :width] + product(narrow, narrow_factor)).astype(BFLOAT), narrow
 
 
-def collect_start(values, gathered):
-    (corner,) = collect_blocks([3], values, gathered, [(BFLOAT, BFLOAT)])
+PIECE_TYPES = [(BFLOAT, BFLOAT), (BFLOAT, FLOAT), (FLOAT, BFLOAT), (FLOAT, FLOAT)]
+
+
+def collect_pieces(values, gathered, at_once):
+    if at_once:
+        return collect_blocks([3, 1, 2, 0], values, gathered, PIECE_TYPES)
+    (corner,) = collect_blocks([3], values, gathered, PIECE_TYPES[:1])
+    values = after(values, corner[0])
+    return [corner, *collect_blocks([1, 2, 0], values, gathered, PIECE_TYPES[1:])]
+
+
+def collect_send(pieces, ordered=True):
+    corner, near, far, own = pieces
     arriving = flip(corner[0], 1), flip(corner[1], 2)
-    values = after(values, corner[0])
-    near, far, own = collect_blocks([1, 2, 0], values, gathered, [(BFLOAT, FLOAT), (FLOAT, BFLOAT), (FLOAT, FLOAT)])
-    return own, flip(near[0], 1), flip(far[1], 2), far[0], near[1], arriving
+    sent_near, sent_far = after_all((near[0], far[1]), *arriving) if ordered else (near[0], far[1])
+    return own, flip(sent_near, 1), flip(sent_far, 2), far[0], near[1], arriving
 
 
 def collect_middle(started):
@@ -1015,7 +1025,7 @@
 def collect_project(values, gathered, kind, own_selector, *operands):
     rows, model = own_selector.shape[0], operands[0].shape[1]
     if quick(rows):
-        kept, onward = collect_middle(collect_start(values, gathered))
+        kept, onward = collect_middle(collect_send(collect_pieces(values, gathered, False)))
         return collect_end(kept, collect_onward(onward), kind, gathered, own_selector, *operands)
     wide, narrow_factor = gathered
     width = narrow_factor.shape[1]
@@ -1215,22 +1225,46 @@
     feed_grad = jnp.concatenate(
         [wide_grad * up_part * (gate * (1.0 + gate_part * (1.0 - gate))), wide_grad * silu], axis=1
     ).astype(BFLOAT)
-    hidden_grad, narrow_three, *branch_one = collect_project(
-        feed_grad, weights_feed, "backward", own_selector, hidden, branch_two, gains[1]
-    )
-    mixed_grad, narrow_one = spread_project(branch_one, weights_mix, selector)
-
     if fast:
-        started = collect_start(after(activated, mixed_grad), weights_down)
-        projected_grad = scan_backward(
-            projected, tables, scanned, carried, after(mixed_grad, started[0][0], started[3])
+        pieces = collect_pieces(after(activated, feed_grad), weights_down, True)
+        kept, onward = collect_middle(collect_send(collect_pieces(feed_grad, weights_feed, False)))
+        hidden_grad, narrow_three, *branch_one = collect_end(
+            kept,
+            collect_onward(onward),
+            "backward",
+            weights_feed,
+            own_selector,
+            after(hidden, pieces[3][0]),
+            branch_two,
+            gains[1],
         )
+        blocks_branch = gather_blocks(branch_one)
+    else:
+        hidden_grad, narrow_three, *branch_one = collect_project(
+            feed_grad, weights_feed, "backward", own_selector, hidden, branch_two, gains[1]
+        )
+    early_grads = [
+        compact_grad(narrow_three, jnp.concatenate(normed_two, axis=1)),
+        compact_grad(inner_out, jnp.concatenate(branch_one, axis=1)),
+    ]
+    if fast:
+        blocks_branch[3] = (3, after_all(blocks_branch[3][1], *early_grads))
+        mixed_grad, narrow_one = spread_gathered(blocks_branch, weights_mix, selector)
+    else:
+        mixed_grad, narrow_one = spread_project(branch_one, weights_mix, selector)
+
+    if fast:
+        near_parts = after_all((*pieces[0], pieces[1][0], pieces[2][1]), mixed_grad)
+        started = collect_send(
+            [near_parts[:2], (near_parts[2], pieces[1][1]), (pieces[2][0], near_parts[3]), pieces[3]], False
+        )
+        projected_grad = scan_backward(projected, tables, scanned, carried, after(mixed_grad, near_parts[0]))
         kept, onward = collect_middle((*started[:5], [after(part, projected_grad) for part in started[5]]))
         projected_grad = attention_backward(
             projected, tables, mixed_grad, after(projected_grad, *onward, *kept[1:])
         )
         last = collect_onward(onward)
-        started_in = collect_start(projected_grad, weights_in)
+        started_in = collect_send(collect_pieces(projected_grad, weights_in, True))
         kept_in, onward_in = collect_middle(started_in)
         block_out, inner_down = collect_end(
             kept, last, "output", weights_down, own_selector, after(hidden, started_in[0][0])
@@ -1243,10 +1277,8 @@
         block_out,
         [
             compact_grad(inner_down, branch_two),
-            compact_grad(narrow_three, jnp.concatenate(normed_two, axis=1)),
-            compact_grad(inner_out, jnp.concatenate(branch_one, axis=1)),
+            *early_grads,
         ],
-        [*onward_in, *kept_in[1:]] if fast else (),
     )
 
     def sum_rows(values):
@@ -1260,34 +1292,8 @@
     early = sum_rows(jnp.concatenate(early_parts, axis=1))
 
     raise_grad = contract_first(inner_in, after(projected_grad, *onward_in) if fast else projected_grad)
-    key_columns = raise_grad[:, STATES : STATES + HEAD_SIZE]
-    value_columns = raise_grad[:, STATES + HEAD_SIZE : STATES + PAIR]
-    mine = [(key_head == at).astype(FLOAT) for at in range(KEY_VALUE_HEADS)]
-    pair_grad = jnp.concatenate([part * here for part in (key_columns, value_columns) for here in mine], axis=1)
-    stacked = jnp.stack(
-        [
-            jnp.concatenate(
-                [
-                    pair_grad[:, at * pair_width : (at + 1) * pair_width],
-                    raise_grad[:, at * state_width : (at + 1) * state_width],
-                ],
-                axis=1,
-            )
-            for at in range(cols)
-        ]
-    )
-    if fast:
-        to_send = stacked.astype(BFLOAT)
-        piece = lambda block: lax.dynamic_index_in_dim(to_send, block, 0, False)
-        near_sum = lambda block: lax.dynamic_index_in_dim(stacked, block, 0, False)
-        pair_sums = flip(jnp.stack([piece(col ^ 1), piece(col ^ 3)]), 1).astype(FLOAT)
-        far_sum = (near_sum(col ^ 2) + pair_sums[1]).astype(BFLOAT)
-        shared_sum = near_sum(col) + pair_sums[0] + flip(far_sum, 2).astype(FLOAT)
-    else:
-        shared_sum = lax.psum_scatter(
-            stacked.astype(BFLOAT).reshape(cols * NADAPT * RANK, -1), "col", scatter_dimension=0, tiled=True
-        ).astype(FLOAT)
-    late = sum_rows(jnp.concatenate([shared_sum, raise_grad[:, STATES + PAIR :]], axis=1))
+    late = sum_rows(raise_grad)
+
     if fast:
         input_grad, narrow_four = collect_end(
             kept_in,
@@ -1313,6 +1319,30 @@
     grad_feed_raise = join_halves(early[:, early_cuts[1] : early_cuts[2]], units, UNIT_FF, 1)
     grad_down_lower = early[:, early_cuts[2] :].T
 
+    key_columns = late[:, STATES : STATES + HEAD_SIZE]
+    value_columns = late[:, STATES + HEAD_SIZE : STATES + PAIR]
+    mine = [(key_head == at).astype(FLOAT) for at in range(KEY_VALUE_HEADS)]
+    pair_grad = jnp.concatenate([part * here for part in (key_columns, value_columns) for here in mine], axis=1)
+    stacked = jnp.stack(
+        [
+            jnp.concatenate(
+                [
+                    pair_grad[:, at * pair_width : (at + 1) * pair_width],
+                    late[:, at * state_width : (at + 1) * state_width],
+                ],
+                axis=1,
+            )
+            for at in range(cols)
+        ]
+    )
+    if fast:
+        piece = lambda mask: lax.dynamic_index_in_dim(stacked, col ^ mask, 0, False)
+        shared_sum = piece(0) + flip(piece(1), 1) + flip(piece(2), 2) + flip(piece(3), 3)
+    else:
+        shared_sum = lax.psum_scatter(
+            stacked.reshape(stacked.shape[0] * stacked.shape[1], -1), "col", scatter_dimension=0, tiled=True
+        )
+    late = jnp.concatenate([shared_sum, late[:, STATES + PAIR :]], axis=1)
     shared_width = pair_width + state_width
     cuts = [shared_width]
     for width in (channels, channels, units * HEAD_SIZE, units * STEP_WIDTH):

time: 668 us -> 668 us (level)
  waiting for transfers between devices: 222 us -> 201 us
  local copies, waits for them, and re-layouts: 106 us -> 126 us
    unnamed x330 -> x346, local copies, waits for them, and re-layouts: 78.9 us -> 89.2 us
    all_gather x4, waiting for transfers between devices: 23.6 us -> 16.5 us  [gather_weight(): return (lax.all_gather(shards[-1], 'row', axis=0),)]
    ppermute x54 -> x55, waiting for transfers between devices: 139 us -> 132 us  [flip(): return lax.ppermute(values, 'col', [(i, i ^ mask) for i in range(4)])]
    ppermute x54 -> x55, starting transfers between devices: 61.1 us -> 59 us  [flip(): return lax.ppermute(values, 'col', [(i, i ^ mask) for i in range(4)])]
    pallas_call x8 -> x6, Pallas kernels: 38.1 us -> 37.4 us  [collect_blocks(): pl.pallas_call(functools.partial(collect_kernel, masks, len(gathered)), i...]
  transfers between devices with their start and end apart: 65 -> 66, of which waited for: 29 -> 26; matrix products, arithmetic and copies ran while one was open for 13% -> 15% of each run, Pallas kernels for 24% -> 24%
where the time goes in v6:
time: 668 us; the launch traced here: 659 us
  waiting for transfers between devices  201 us (30%)
  Pallas kernels  173 us (26%)
  local copies, waits for them, and re-layouts  126 us (19%)
  starting transfers between devices  78.2 us (12%)
  other arithmetic  36.4 us (5%)
  matrix products  26.5 us (4%)
  between operations  18.2 us (3%)
    ppermute x55, waiting for transfers between devices, flip(): return lax.ppermute(values, 'col', [(i, i ^ mask) for i in range(4)])  132 us
    unnamed x346, local copies, waits for them, and re-layouts  89.2 us
    pallas_call x16, Pallas kernels, spread_block(): pl.pallas_call(functools.partial(spread_kernel, mask, len(gathered)), in_...  71 us
    ppermute x55, starting transfers between devices, flip(): return lax.ppermute(values, 'col', [(i, i ^ mask) for i in range(4)])  59 us
    all_to_all x4, waiting for transfers between devices, local(): lax.all_to_all(values, ALL_AXES, split_axis=0, concat_axis=0, tiled=True)  40.1 us
    pallas_call x6, Pallas kernels, collect_blocks(): pl.pallas_call(functools.partial(collect_kernel, masks, len(gathered)), i...  37.4 us
    pallas_call x1, Pallas kernels, scan_backward(): pl.pallas_call(scan_backward_kernel, grid=(blocks,), in_specs=scan_specs(...  27.8 us
    dot_general x12, matrix products, contract_first(): lax.dot_general(left, right, (((0,), (0,)), ((), ())), preferred_element_...  19.9 us
  transfers between devices with their start and end apart: 66, of which 26 were waited for; matrix products, arithmetic and copies ran while one was open for 15% of the time, Pallas kernels for 24%

profile of v6, /device:TPU:0, one launch (start us, length us, event | category | flops | bytes accessed | tf_op | source)
XLA Modules:
  0.0 659.3 jit_solution(2549404970529680164)
XLA Ops:
  23.1 7.3 %all-to-all-start = ((bf16[32,8,2176]{2,1,0:T(8,128)(2,1)}), bf16[32,8,2176]{2,1,0:T(8,128)(2,1)S(1)}, u32[]{:S(2)}, u32[]{:S(2)}) async-start(bf16[32,8,2176]{2,1,0:T(8,128)(2,1)} %bitcast.185), calls=%async_computation | async-start | bytes 2228224 | tf_op jit(solution)/shard_map/all_to_all | solution.py:1094
  30.5 12.0 %all-gather.11.cloned.1.call-done = bf16[2304,256]{1,0:T(8,128)(2,1)} async-done(((bf16[288,256]{1,0:T(8,128)(2,1)}), bf16[2304,256]{1,0:T(8,128)(2,1)}) %all-gather.11.cloned.1.call-update) | async-done | bytes 1179664 | tf_op jit(solution)/shard_map/all_gather | solution.py:1119
  48.1 24.5 %all-to-all-done = bf16[32,8,2176]{2,1,0:T(8,128)(2,1)S(1)} async-done(((bf16[32,8,2176]{2,1,0:T(8,128)(2,1)}), bf16[32,8,2176]{2,1,0:T(8,128)(2,1)S(1)}, u32[]{:S(2)}, u32[]{:S(2)}) %all-to-all-start) | async-done | bytes 1114144 | tf_op jit(solution)/shard_map/all_to_all | solution.py:1094
  96.1 12.7 %collective-permute-done.4.right_ref = bf16[256,1024]{1,0:T(8,128)(2,1)S(1)} collective-permute-done((bf16[256,1024]{1,0:T(8,128)(2,1)}, bf16[256,1024]{1,0:T(8,128)(2,1)S(1)}, u32[]{:S(2)}, u32[]{:S(2)}) %collective-permute-start.4) | collective-permute-done | bytes 524320 | tf_op jit(solution)/shard_map/ppermute | solution.py:951
  109.7 12.2 %collective-permute-done.2.left_ref = bf16[256,1024]{1,0:T(8,128)(2,1)} collective-permute-done((bf16[256,1024]{1,0:T(8,128)(2,1)}, bf16[256,1024]{1,0:T(8,128)(2,1)}, u32[]{:S(2)}, u32[]{:S(2)}) %collective-permute-start.2) | collective-permute-done | bytes 524320 | tf_op jit(solution)/shard_map/ppermute | solution.py:951
  139.8 7.5 %spread_block.16 = (bf16[1024,2688]{1,0:T(8,128)(2,1)S(1)}, bf16[1024,128]{1,0:T(8,128)(2,1)S(1)}) custom-call(bf16[256,1024]{1,0:T(8,128)(2,1)} %get-tuple-element.134.left_ref, bf16[256,1024]{1,0:T(8,128)(2,1)} %get-tuple-element.135.right_ref, f32[1024,128]{1,0:T(8,128)S(1)} %compare_convert_fusion.chosen_ref, bf16[8,272,768]{2,1,0:T(8,128)(2,1)S(1)} %copy-done.14, ...), custom_call_target="tpu_custom_call" | custom-call | flops 184549376 | bytes 151552 | tf_op jit(solution)/shard_map/spread_block/pallas_call | solution.py:670
  147.2 7.1 %spread_block.17 = (bf16[1024,2688]{1,0:T(8,128)(2,1)S(1)}, bf16[1024,128]{1,0:T(8,128)(2,1)S(1)}) custom-call(bf16[256,1024]{1,0:T(8,128)(2,1)} %collective-permute-done.9.left_ref, bf16[256,1024]{1,0:T(8,128)(2,1)S(1)} %collective-permute-done.4.right_ref, ...), custom_call_target="tpu_custom_call", output_to_operand_aliasing={{0}: (5, {}), {1}: (6, {})} | custom-call | flops 184549376 | bytes 151552 | tf_op jit(solution)/shard_map/spread_block/pallas_call | solution.py:670
  154.4 7.5 %spread_block.18 = (bf16[1024,2688]{1,0:T(8,128)(2,1)S(1)}, bf16[1024,128]{1,0:T(8,128)(2,1)S(1)}) custom-call(bf16[256,1024]{1,0:T(8,128)(2,1)} %collective-permute-done.2.left_ref, bf16[256,1024]{1,0:T(8,128)(2,1)S(1)} %collective-permute-done.8.right_ref, ...), custom_call_target="tpu_custom_call", output_to_operand_aliasing={{0}: (5, {}), {1}: (6, {})} | custom-call | flops 184549376 | bytes 151552 | tf_op jit(solution)/shard_map/spread_block/pallas_call | solution.py:670
  161.9 7.3 %spread_block.19 = (bf16[1024,2688]{1,0:T(8,128)(2,1)S(1)}, bf16[1024,128]{1,0:T(8,128)(2,1)S(1)}) custom-call(bf16[256,1024]{1,0:T(8,128)(2,1)} %collective-permute-done.3.left_ref, bf16[256,1024]{1,0:T(8,128)(2,1)} %collective-permute-done.5.right_ref, ...), custom_call_target="tpu_custom_call", output_to_operand_aliasing={{0}: (5, {}), {1}: (6, {})} | custom-call | flops 184549376 | bytes 151552 | tf_op jit(solution)/shard_map/spread_block/pallas_call | solution.py:670
  189.9 12.9 %scan_forward.1 = (bf16[1024,1024]{1,0:T(8,128)(2,1)S(1)}, f32[1024,768]{1,0:T(8,128)S(1)}, bf16[4,256,768]{2,1,0:T(8,128)(2,1)S(1)}) custom-call(bf16[1024,2688]{1,0:T(8,128)(2,1)S(1)} %copy-done.3, bf16[1024,2688]{1,0:T(8,128)(2,1)S(1)} %copy-done.3, bf16[1024,2688]{1,0:T(8,128)(2,1)S(1)} %copy-done.3, ...), custom_call_target="tpu_custom_call", output_to_operand_aliasing={{0}: (12, {})} | custom-call | flops 83886080 | bytes 589824 | tf_op jit(solution)/shard_map/scan_forward/pallas_call | solution.py:377
  243.0 17.3 %collective-permute-done.15.second_far = bf16[256,1024]{1,0:T(8,128)(2,1)} collective-permute-done((bf16[256,1024]{1,0:T(8,128)(2,1)}, bf16[256,1024]{1,0:T(8,128)(2,1)}, u32[]{:S(2)}, u32[]{:S(2)}) %collective-permute-start.15) | collective-permute-done | bytes 524320 | tf_op jit(solution)/shard_map/ppermute | solution.py:951
  272.9 6.7 %collective-permute-done.16.left_ref = bf16[256,1024]{1,0:T(8,128)(2,1)S(1)} collective-permute-done((bf16[256,1024]{1,0:T(8,128)(2,1)S(1)}, bf16[256,1024]{1,0:T(8,128)(2,1)S(1)}, u32[]{:S(2)}, u32[]{:S(2)}) %collective-permute-start.16) | collective-permute-done | bytes 524320 | tf_op jit(solution)/shard_map/ppermute | solution.py:951
  283.3 7.6 %collective-permute-done.22.left_ref = bf16[256,1024]{1,0:T(8,128)(2,1)} collective-permute-done((bf16[256,1024]{1,0:T(8,128)(2,1)}, bf16[256,1024]{1,0:T(8,128)(2,1)}, u32[]{:S(2)}, u32[]{:S(2)}) %collective-permute-start.22) | collective-permute-done | bytes 524320 | tf_op jit(solution)/shard_map/ppermute | solution.py:951
  295.3 6.9 %collective-permute-done.20.right_ref = bf16[256,1024]{1,0:T(8,128)(2,1)S(1)} collective-permute-done((bf16[256,1024]{1,0:T(8,128)(2,1)S(1)}, bf16[256,1024]{1,0:T(8,128)(2,1)S(1)}, u32[]{:S(2)}, u32[]{:S(2)}) %collective-permute-start.20) | collective-permute-done | bytes 524320 | tf_op jit(solution)/shard_map/ppermute | solution.py:951
  332.4 10.8 %all-gather.19.cloned.1.call-done = bf16[2176,1152]{1,0:T(8,128)(2,1)} async-done(((bf16[272,1152]{1,0:T(8,128)(2,1)}), bf16[2176,1152]{1,0:T(8,128)(2,1)}) %all-gather.19.cloned.1.call-update) | async-done | bytes 5013520 | tf_op jit(solution)/shard_map/all_gather | solution.py:1104
  374.2 7.5 %collect_blocks.10 = (bf16[256,1152]{1,0:T(8,128)(2,1)S(1)}, f32[256,1024]{1,0:T(8,128)S(1)}, f32[256,1152]{1,0:T(8,128)S(1)}, bf16[256,1024]{1,0:T(8,128)(2,1)S...) custom-call(bf16[1024,2048]{1,0:T(8,128)(2,1)S(1)} %copy-done.28, bf16[8,272,2176]{2,1,0:T(8,128)(2,1)S(1)} %bitcast.160), custom_call_target="tpu_custom_call" | custom-call | flops 402653184 | bytes 589824 | tf_op jit(solution)/shard_map/collect_blocks/pallas_call | solution.py:733
  396.9 13.6 %collective-permute-done.33.second_far = bf16[256,1024]{1,0:T(8,128)(2,1)S(1)} collective-permute-done((bf16[256,1024]{1,0:T(8,128)(2,1)S(1)}, bf16[256,1024]{1,0:T(8,128)(2,1)S(1)}, u32[]{:S(2)}, u32[]{:S(2)}) %collective-permute-start.33) | collective-permute-done | bytes 524320 | tf_op jit(solution)/shard_map/ppermute | solution.py:951
  422.1 8.2 %collective-permute-done.34.left_ref = bf16[256,1024]{1,0:T(8,128)(2,1)S(1)} collective-permute-done((bf16[256,1024]{1,0:T(8,128)(2,1)S(1)}, bf16[256,1024]{1,0:T(8,128)(2,1)S(1)}, u32[]{:S(2)}, u32[]{:S(2)}) %collective-permute-start.34) | collective-permute-done | bytes 524320 | tf_op jit(solution)/shard_map/ppermute | solution.py:951
  477.6 27.8 %scan_backward.1.held_ref = bf16[1024,2688]{1,0:T(8,128)(2,1)S(1)} custom-call(bf16[1024,2688]{1,0:T(8,128)(2,1)S(1)} %bitcast.152, bf16[1024,2688]{1,0:T(8,128)(2,1)S(1)} %bitcast.152, bf16[1024,2688]{1,0:T(8,128)(2,1)S(1)} %bitcast.152, bf16[1024,2688]{1,0:T(8,128)(2,1)S(1)} %bitcast.152, bf16[1024,2688]{1,0:T(8,128)(2,1)S(1)} %bitcast.152, ...), custom_call_target="tpu_custom_call" | custom-call | flops 167772160 | bytes 1179648 | tf_op jit(solution)/shard_map/scan_backward/pallas_call | solution.py:404
  521.8 7.5 %attention_backward.1.values_ref = bf16[1024,2688]{1,0:T(8,128)(2,1)S(1)} custom-call(bf16[1024,2688]{1,0:T(8,128)(2,1)S(1)} %copy-done.4, bf16[1024,2688]{1,0:T(8,128)(2,1)S(1)} %copy-done.4, bf16[1024,2688]{1,0:T(8,128)(2,1)S(1)} %copy-done.4, f32[1024,128]{1,0:T(8,128)S(1)} %copy-done.44, ...), custom_call_target="tpu_custom_call", output_to_operand_aliasing={{}: (8, {})} | custom-call | flops 100663296 | bytes 393216 | tf_op jit(solution)/shard_map/attention_backward/pallas_call | solution.py:551
  532.9 14.6 %collect_blocks.11 = (bf16[256,1152]{1,0:T(8,128)(2,1)}, bf16[256,1024]{1,0:T(8,128)(2,1)}, bf16[256,1152]{1,0:T(8,128)(2,1)}, f32[256,1024]{1,0:T(8,128)S(1)}, ...) custom-call(bf16[1024,2688]{1,0:T(8,128)(2,1)S(1)} %attention_backward.1, ...), custom_call_target="tpu_custom_call" | custom-call | flops 704643072 | bytes 868352 | tf_op jit(solution)/shard_map/collect_blocks/pallas_call | solution.py:733
  574.9 12.8 %collective-permute-done.51.second_far = bf16[256,1024]{1,0:T(8,128)(2,1)} collective-permute-done((bf16[256,1024]{1,0:T(8,128)(2,1)}, bf16[256,1024]{1,0:T(8,128)(2,1)}, u32[]{:S(2)}, u32[]{:S(2)}) %collective-permute-start.51) | collective-permute-done | bytes 524320 | tf_op jit(solution)/shard_map/ppermute | solution.py:951
  587.7 15.0 %collective-permute-done.50.second_near = bf16[256,1024]{1,0:T(8,128)(2,1)} collective-permute-done((bf16[256,1024]{1,0:T(8,128)(2,1)}, bf16[256,1024]{1,0:T(8,128)(2,1)}, u32[]{:S(2)}, u32[]{:S(2)}) %collective-permute-start.50) | collective-permute-done | bytes 524320 | tf_op jit(solution)/shard_map/ppermute | solution.py:951
  633.9 15.6 %all-to-all-done.3 = bf16[32,8,2304]{2,1,0:T(8,128)(2,1)S(1)} async-done(((bf16[32,8,2304]{2,1,0:T(8,128)(2,1)}), bf16[32,8,2304]{2,1,0:T(8,128)(2,1)S(1)}, u32[]{:S(2)}, u32[]{:S(2)}) %all-to-all-start.3) | async-done | bytes 1179680 | tf_op jit(solution)/shard_map/all_to_all | solution.py:1094
  (656 shorter events, 358.0 us)
Async XLA Ops:
  12.7 121.6 %all-gather.13.cloned.1.call-start = ((), (), s32[]{:S(2)}) async-start(), calls=%async_computation.9 | async-start | bytes 10027008 | tf_op jit(solution)/shard_map/all_gather | solution.py:1104
  21.3 185.7 %all-gather.15.cloned.1.call-start = ((), (), s32[]{:S(2)}) async-start(), calls=%async_computation.10 | async-start | bytes 5640192 | tf_op jit(solution)/shard_map/all_gather | solution.py:1104
  23.1 49.4 %all-to-all-start = ((bf16[32,8,2176]{2,1,0:T(8,128)(2,1)}), bf16[32,8,2176]{2,1,0:T(8,128)(2,1)S(1)}, u32[]{:S(2)}, u32[]{:S(2)}) async-start(bf16[32,8,2176]{2,1,0:T(8,128)(2,1)} %bitcast.185), calls=%async_computation | async-start | bytes 2228224 | tf_op jit(solution)/shard_map/all_to_all | solution.py:1094
  30.4 277.0 %all-gather.17.cloned.1.call-start = ((), (), s32[]{:S(2)}) async-start(), calls=%async_computation.11 | async-start | bytes 10653696 | tf_op jit(solution)/shard_map/all_gather | solution.py:1104
  78.8 264.4 %all-gather.19.cloned.1.call-start = ((), (), s32[]{:S(2)}) async-start(), calls=%async_computation.12 | async-start | bytes 5640192 | tf_op jit(solution)/shard_map/all_gather | solution.py:1104
  82.3 40.7 %collective-permute-start.7 = (bf16[4,288,256]{2,1,0:T(8,128)(2,1)S(1)}, bf16[4,288,256]{2,1,0:T(8,128)(2,1)S(1)}, u32[]{:S(2)}, u32[]{:S(2)}) collective-permute-start(bf16[4,288,256]{2,1,0:T(8,128)(2,1)S(1)} %slice.439), channel_id=1, source_target_pairs={{0,1},{1,0},{2,3},{3,2},{4,5},{5,4},{6,7},{7,6},{8,9},{9,8},{10,11... | collective-permute-start | bytes 1769480 | tf_op jit(solution)/shard_map/ppermute | solution.py:951
  84.4 40.0 %collective-permute-start.6 = (bf16[4,288,256]{2,1,0:T(8,128)(2,1)S(1)}, bf16[4,288,256]{2,1,0:T(8,128)(2,1)S(1)}, u32[]{:S(2)}, u32[]{:S(2)}) collective-permute-start(bf16[4,288,256]{2,1,0:T(8,128)(2,1)S(1)} %slice.438), channel_id=1, source_target_pairs={{0,2},{1,3},{2,0},{3,1},{4,6},{5,7},{6,4},{7,5},{8,10},{9,11},{10,... | collective-permute-start | bytes 1769480 | tf_op jit(solution)/shard_map/ppermute | solution.py:951
  90.0 64.4 %collective-permute-start.8 = (bf16[256,1024]{1,0:T(8,128)(2,1)}, bf16[256,1024]{1,0:T(8,128)(2,1)S(1)}, u32[]{:S(2)}, u32[]{:S(2)}) collective-permute-start(bf16[256,1024]{1,0:T(8,128)(2,1)} %get-tuple-element.135.right_ref), channel_id=1, source_target_pairs={{0,2},{1,3},{2,0},{3,1},{4,6},{5,7},{6,4},{7,5},{8,10},{9,11},{10,... | collective-permute-start | bytes 1572872 | tf_op jit(solution)/shard_map/ppermute | solution.py:951
  121.9 40.0 %collective-permute-start.5 = (bf16[256,1024]{1,0:T(8,128)(2,1)S(1)}, bf16[256,1024]{1,0:T(8,128)(2,1)}, u32[]{:S(2)}, u32[]{:S(2)}) collective-permute-start(bf16[256,1024]{1,0:T(8,128)(2,1)S(1)} %collective-permute-done.4.right_ref), channel_id=1, source_target_pairs={{0,2},{1,3},{2,0},{3,1},{4,6},{5,7},{6,4},{7,5},{8,10},{9,11},{10,... | collective-permute-start | bytes 1572872 | tf_op jit(solution)/shard_map/ppermute | solution.py:951
  123.0 38.9 %collective-permute-start.3 = (bf16[256,1024]{1,0:T(8,128)(2,1)}, bf16[256,1024]{1,0:T(8,128)(2,1)}, u32[]{:S(2)}, u32[]{:S(2)}) collective-permute-start(bf16[256,1024]{1,0:T(8,128)(2,1)} %collective-permute-done.2.left_ref), channel_id=1, source_target_pairs={{0,1},{1,0},{2,3},{3,2},{4,5},{5,4},{6,7},{7,6},{8,9},{9,8},{10,11... | collective-permute-start | bytes 1572872 | tf_op jit(solution)/shard_map/ppermute | solution.py:951
  177.0 60.1 %all-to-all-start.1 = ((bf16[32,8,2048]{2,1,0:T(8,128)(2,1)}), bf16[32,8,2048]{2,1,0:T(8,128)(2,1)}, u32[]{:S(2)}, u32[]{:S(2)}) async-start(bf16[32,8,2048]{2,1,0:T(8,128)(2,1)} %fusion.9), calls=%async_computation.1 | async-start | bytes 2097152 | tf_op jit(solution)/shard_map/all_to_all | solution.py:1094
  180.8 433.4 %reduce-scatter.3.cloned.1.call-start = ((), (), s32[]{:S(2)}) async-start(), calls=%async_computation.6 | async-start | bytes 1179648 | tf_op jit(solution)/shard_map/reduce_scatter | solution.py:1285
  282.8 42.4 %collective-permute-start.19 = (bf16[256,1024]{1,0:T(8,128)(2,1)}, bf16[256,1024]{1,0:T(8,128)(2,1)}, u32[]{:S(2)}, u32[]{:S(2)}) collective-permute-start(bf16[256,1024]{1,0:T(8,128)(2,1)} %collective-permute-done.18.right_ref), channel_id=1, source_target_pairs={{0,2},{1,3},{2,0},{3,1},{4,6},{5,7},{6,4},{7,5},{8,10},{9,11},{10,... | collective-permute-start | bytes 1572872 | tf_op jit(solution)/shard_map/ppermute | solution.py:951
  291.0 57.8 %collective-permute-start.27 = (bf16[256,1024]{1,0:T(8,128)(2,1)}, bf16[256,1024]{1,0:T(8,128)(2,1)}, u32[]{:S(2)}, u32[]{:S(2)}) collective-permute-start(bf16[256,1024]{1,0:T(8,128)(2,1)} %get-tuple-element.268.left_ref), channel_id=1, source_target_pairs={{0,1},{1,0},{2,3},{3,2},{4,5},{5,4},{6,7},{7,6},{8,9},{9,8},{10,11... | collective-permute-start | bytes 1572872 | tf_op jit(solution)/shard_map/ppermute | solution.py:951
  294.7 57.2 %collective-permute-start.26 = (bf16[256,1024]{1,0:T(8,128)(2,1)}, bf16[256,1024]{1,0:T(8,128)(2,1)}, u32[]{:S(2)}, u32[]{:S(2)}) collective-permute-start(bf16[256,1024]{1,0:T(8,128)(2,1)} %get-tuple-element.267.right_ref), channel_id=1, source_target_pairs={{0,2},{1,3},{2,0},{3,1},{4,6},{5,7},{6,4},{7,5},{8,10},{9,11},{10,... | collective-permute-start | bytes 1572872 | tf_op jit(solution)/shard_map/ppermute | solution.py:951
  302.9 52.2 %collective-permute-start.25 = (bf16[256,1024]{1,0:T(8,128)(2,1)}, bf16[256,1024]{1,0:T(8,128)(2,1)}, u32[]{:S(2)}, u32[]{:S(2)}) collective-permute-start(bf16[256,1024]{1,0:T(8,128)(2,1)} %collective-permute-done.24.right_ref), channel_id=1, source_target_pairs={{0,2},{1,3},{2,0},{3,1},{4,6},{5,7},{6,4},{7,5},{8,10},{9,11},{10,... | collective-permute-start | bytes 1572872 | tf_op jit(solution)/shard_map/ppermute | solution.py:951
  305.9 49.1 %collective-permute-start.23 = (bf16[256,1024]{1,0:T(8,128)(2,1)}, bf16[256,1024]{1,0:T(8,128)(2,1)}, u32[]{:S(2)}, u32[]{:S(2)}) collective-permute-start(bf16[256,1024]{1,0:T(8,128)(2,1)} %collective-permute-done.22.left_ref), channel_id=1, source_target_pairs={{0,1},{1,0},{2,3},{3,2},{4,5},{5,4},{6,7},{7,6},{8,9},{9,8},{10,11... | collective-permute-start | bytes 1572872 | tf_op jit(solution)/shard_map/ppermute | solution.py:951
  420.0 43.1 %collective-permute-start.39 = (bf16[256,1024]{1,0:T(8,128)(2,1)S(1)}, bf16[256,1024]{1,0:T(8,128)(2,1)}, u32[]{:S(2)}, u32[]{:S(2)}) collective-permute-start(bf16[256,1024]{1,0:T(8,128)(2,1)S(1)} %get-tuple-element.196.left_ref), channel_id=1, source_target_pairs={{0,1},{1,0},{2,3},{3,2},{4,5},{5,4},{6,7},{7,6},{8,9},{9,8},{10,11... | collective-permute-start | bytes 1572872 | tf_op jit(solution)/shard_map/ppermute | solution.py:951
  421.5 44.7 %collective-permute-start.38 = (bf16[256,1024]{1,0:T(8,128)(2,1)}, bf16[256,1024]{1,0:T(8,128)(2,1)}, u32[]{:S(2)}, u32[]{:S(2)}) collective-permute-start(bf16[256,1024]{1,0:T(8,128)(2,1)} %get-tuple-element.197.right_ref), channel_id=1, source_target_pairs={{0,2},{1,3},{2,0},{3,1},{4,6},{5,7},{6,4},{7,5},{8,10},{9,11},{10,... | collective-permute-start | bytes 1572872 | tf_op jit(solution)/shard_map/ppermute | solution.py:951
  430.3 39.1 %collective-permute-start.35 = (bf16[256,1024]{1,0:T(8,128)(2,1)S(1)}, bf16[256,1024]{1,0:T(8,128)(2,1)}, u32[]{:S(2)}, u32[]{:S(2)}) collective-permute-start(bf16[256,1024]{1,0:T(8,128)(2,1)S(1)} %collective-permute-done.34.left_ref), channel_id=1, source_target_pairs={{0,1},{1,0},{2,3},{3,2},{4,5},{5,4},{6,7},{7,6},{8,9},{9,8},{10,11... | collective-permute-start | bytes 1572872 | tf_op jit(solution)/shard_map/ppermute | solution.py:951
  475.4 38.8 %collective-permute-start.43 = (bf16[256,1024]{1,0:T(8,128)(2,1)}, bf16[256,1024]{1,0:T(8,128)(2,1)}, u32[]{:S(2)}, u32[]{:S(2)}) collective-permute-start(bf16[256,1024]{1,0:T(8,128)(2,1)} %get-tuple-element.217), channel_id=1, source_target_pairs={{0,2},{1,3},{2,0},{3,1},{4,6},{5,7},{6,4},{7,5},{8,10},{9,11},{10,... | collective-permute-start | bytes 1572872 | tf_op jit(solution)/shard_map/ppermute | solution.py:951
  510.1 39.8 %collective-permute-start.42 = (bf16[256,1152]{1,0:T(8,128)(2,1)}, bf16[256,1152]{1,0:T(8,128)(2,1)}, u32[]{:S(2)}, u32[]{:S(2)}) collective-permute-start(bf16[256,1152]{1,0:T(8,128)(2,1)} %add_convert_fusion.1), channel_id=1, source_target_pairs={{0,2},{1,3},{2,0},{3,1},{4,6},{5,7},{6,4},{7,5},{8,10},{9,11},{10,... | collective-permute-start | bytes 1769480 | tf_op jit(solution)/shard_map/ppermute | solution.py:951
  556.4 59.7 %all-to-all-start.2 = ((bf16[32,8,2816]{2,1,0:T(8,128)(2,1)}), bf16[32,8,2816]{2,1,0:T(8,128)(2,1)}, u32[]{:S(2)}, u32[]{:S(2)}) async-start(bf16[32,8,2816]{2,1,0:T(8,128)(2,1)} %pad_maximum_fusion.1), calls=%async_computation.2 | async-start | bytes 2883584 | tf_op jit(solution)/shard_map/all_to_all | solution.py:1094
  560.0 55.2 %reduce-scatter.5.cloned.1.call-start = ((), (), s32[]{:S(2)}) async-start(), calls=%async_computation.7 | async-start | bytes 774144 | tf_op jit(solution)/shard_map/reduce_scatter | solution.py:1285
  (204 other events, 3143.6 us)
Sparse Core Ops, SparseCore 0:
  12.8 29.6 all-gather.10
  44.1 90.1 all-gather.12
  136.5 57.7 all-gather.14
  195.8 93.0 all-gather.16
  290.4 52.7 all-gather.18
  514.3 30.3 reduce-scatter.2
  572.7 34.1 reduce-scatter.4

commit v7 on v6

--- a/solution.py
+++ b/solution.py
@@ -66,6 +66,7 @@
 ESTIMATE = 16
 SCAN_BYTES = 32 * 1024 * 1024
 DENSE_BYTES = 16 * 1024 * 1024
+FINISH_BYTES = 32 * 1024 * 1024
 LANES = 128
 
 
@@ -240,13 +241,15 @@
 
 def scan_backward_kernel(
     gate_ref, conv_ref, before_ref, state_ref, state_before_ref, step_ref, meta_ref, segment_ref, taps_ref,
-    state_taps_ref, head_ref, skip_ref, scanned_ref, states_ref, grad_ref, out_ref, state_grad, later, state_later,
+    state_taps_ref, head_ref, skip_ref, scanned_ref, states_ref, grad_ref, query_grad_ref, shared_grad_ref, *rest,
 ):
+    out_ref, *running = rest[-4:]
+    state_grad, later, state_later = running
+
     @pl.when(pl.program_id(0) == 0)
     def _():
-        state_grad[...] = jnp.zeros_like(state_grad)
-        later[...] = jnp.zeros_like(later)
-        state_later[...] = jnp.zeros_like(state_later)
+        for at, ref in enumerate(running):
+            ref[...] = rest[1 + at][...] if len(rest) > 4 else jnp.zeros_like(ref)
 
     block = scan_block(
         conv_ref, before_ref, state_ref, state_before_ref, step_ref, meta_ref, segment_ref, taps_ref, state_taps_ref,
@@ -325,9 +328,12 @@
     conv_pre = conv_back(inputs_grad * silu_slope(block["summed"], block["conv_gate"]), later, taps_ref, meta)
     out_ref[:, : 2 * NSTATE] = state_pre.astype(BFLOAT)
     start = 2 * NSTATE + 2 * HEAD_SIZE
+    end = out_ref.shape[1] - LANES
+    out_ref[:, 2 * NSTATE : start] = shared_grad_ref[...]
+    out_ref[:, start + 2 * channels : end] = query_grad_ref[...]
     out_ref[:, start : start + channels] = gate_grad.astype(BFLOAT)
     out_ref[:, start + channels : start + 2 * channels] = conv_pre.astype(BFLOAT)
-    out_ref[:, out_ref.shape[1] - LANES :] = raw_grad.astype(BFLOAT)
+    out_ref[:, end:] = raw_grad.astype(BFLOAT)
 
 
 STATES = 2 * NSTATE
@@ -396,31 +402,41 @@
     )(*scan_operands(projected, tables), mixed)
 
 
-def scan_backward(projected, tables, scanned, carried, mixed_grad):
+def scan_backward(projected, tables, scanned, carried, mixed_grad, attended_grads, part, parts, before):
     tokens, width = projected.shape
     channels = tables["taps"].shape[1]
     blocks = tokens // SSD_BLOCK
-    back = lambda i: (blocks - 1 - i, 0)
+    last = blocks - 1 - part * (blocks // parts)
+    back = lambda i: (last - i, 0)
+    running = [(NSTATE, channels), (8, channels), (8, STATES)]
+    query_grad, shared_grad = attended_grads
+    operands = [*scan_operands(projected, tables), scanned, carried, mixed_grad, query_grad, shared_grad]
+    in_specs = scan_specs(channels, lambda i: last - i) + [
+        pl.BlockSpec((SSD_BLOCK, channels), back),
+        pl.BlockSpec((1, NSTATE, channels), lambda i: (last - i, 0, 0)),
+        pl.BlockSpec((SSD_BLOCK, channels), back),
+        pl.BlockSpec((SSD_BLOCK, query_grad.shape[1]), back),
+        pl.BlockSpec((SSD_BLOCK, PAIR), back),
+    ]
+    aliases = {}
+    if before is not None:
+        aliases = {len(operands): 0}
+        operands += list(before)
+        in_specs += [pl.BlockSpec(memory_space=pl.ANY), *[whole(shape) for shape in running]]
     return pl.pallas_call(
         scan_backward_kernel,
-        grid=(blocks,),
-        in_specs=scan_specs(channels, lambda i: blocks - 1 - i)
-        + [
-            pl.BlockSpec((SSD_BLOCK, channels), back),
-            pl.BlockSpec((1, NSTATE, channels), lambda i: (blocks - 1 - i, 0, 0)),
-            pl.BlockSpec((SSD_BLOCK, channels), back),
+        grid=(blocks // parts,),
+        in_specs=in_specs,
+        out_specs=[pl.BlockSpec((SSD_BLOCK, width), back), *[whole(shape) for shape in running]],
+        out_shape=[
+            jax.ShapeDtypeStruct((tokens, width), BFLOAT),
+            *[jax.ShapeDtypeStruct(shape, FLOAT) for shape in running],
         ],
-        out_specs=pl.BlockSpec((SSD_BLOCK, width), back),
-        out_shape=jax.ShapeDtypeStruct((tokens, width), BFLOAT),
-        scratch_shapes=[
-            pltpu.VMEM((NSTATE, channels), FLOAT),
-            pltpu.VMEM((8, channels), FLOAT),
-            pltpu.VMEM((8, STATES), FLOAT),
-        ],
+        input_output_aliases=aliases,
         compiler_params=pltpu.CompilerParams(vmem_limit_bytes=SCAN_BYTES),
         cost_estimate=scan_cost(tokens, channels, 2),
         name="scan_backward",
-    )(*scan_operands(projected, tables), scanned, carried, mixed_grad)
+    )(*operands)
 
 
 def turned(values, cosine, sine):
@@ -462,10 +478,9 @@
 
 
 def attention_backward_kernel(
-    query_ref, key_ref, value_ref, cosine_ref, sine_ref, meta_ref, segment_ref, grad_ref, held_ref,
-    out_ref, keys, key_sum, value_sum, query_grad_ref, shared_grad_ref, sems,
+    query_ref, key_ref, value_ref, cosine_ref, sine_ref, meta_ref, segment_ref, grad_ref,
+    query_grad_ref, shared_grad_ref, keys, key_sum, value_sum,
 ):
-    del held_ref
     tokens = key_ref.shape[0]
     scale = 1.0 / math.sqrt(HEAD_SIZE)
     keys[...] = turned(key_ref[...].astype(FLOAT), cosine_ref[...], sine_ref[...])
@@ -489,16 +504,6 @@
             query_grad_ref[here, span] = turned_back(query_grad, cosine_ref[here], sine_ref[here]).astype(BFLOAT)
     shared_grad_ref[:, :HEAD_SIZE] = turned_back(key_sum[...], cosine_ref[...], sine_ref[...]).astype(BFLOAT)
     shared_grad_ref[:, HEAD_SIZE:] = value_sum[...].astype(BFLOAT)
-    end = out_ref.shape[1] - LANES
-    width = query_grad_ref.shape[1]
-    copies = [
-        pltpu.make_async_copy(query_grad_ref, out_ref.at[:, end - width : end], sems.at[0]),
-        pltpu.make_async_copy(shared_grad_ref, out_ref.at[:, STATES : STATES + PAIR], sems.at[1]),
-    ]
-    for copy in copies:
-        copy.start()
-    for copy in copies:
-        copy.wait()
 
 
 def attention_cost(tokens, width, factor):
@@ -544,7 +549,7 @@
     )(*attention_operands(projected, tables))
 
 
-def attention_backward(projected, tables, mixed_grad, projected_grad):
+def attention_backward(projected, tables, mixed_grad):
     tokens = projected.shape[0]
     channels = tables["taps"].shape[1]
     width = channels * QUERY_HEADS // DSSM * HEAD_SIZE
@@ -552,22 +557,18 @@
         attention_backward_kernel,
         grid=(1,),
         in_specs=attention_specs(tokens, channels)
-        + [pl.BlockSpec((tokens, width), lambda *_: (0, channels // width)), pl.BlockSpec(memory_space=pl.ANY)],
-        out_specs=pl.BlockSpec(memory_space=pl.ANY),
-        out_shape=jax.ShapeDtypeStruct(projected_grad.shape, BFLOAT),
+        + [pl.BlockSpec((tokens, width), lambda *_: (0, channels // width))],
+        out_specs=[whole((tokens, width)), whole((tokens, PAIR))],
+        out_shape=[jax.ShapeDtypeStruct((tokens, width), BFLOAT), jax.ShapeDtypeStruct((tokens, PAIR), BFLOAT)],
         scratch_shapes=[
             pltpu.VMEM((tokens, HEAD_SIZE), BFLOAT),
             pltpu.VMEM((tokens, HEAD_SIZE), FLOAT),
             pltpu.VMEM((tokens, HEAD_SIZE), FLOAT),
-            pltpu.VMEM((tokens, width), BFLOAT),
-            pltpu.VMEM((tokens, PAIR), BFLOAT),
-            pltpu.SemaphoreType.DMA((2,)),
         ],
-        input_output_aliases={8: 0},
         compiler_params=pltpu.CompilerParams(vmem_limit_bytes=SCAN_BYTES),
         cost_estimate=attention_cost(tokens, width, 3),
         name="attention_backward",
-    )(*attention_operands(projected, tables), mixed_grad, projected_grad)
+    )(*attention_operands(projected, tables), mixed_grad)
 
 
 def mixer_tables(lengths, segment, position, conv_values, conv_states, scan_params):
@@ -750,9 +751,28 @@
     return lax.rsqrt(jnp.mean(values * values, axis=1, keepdims=True) + EPSILON)
 
 
+def packed_grad(narrow, values, choose):
+    half = LANES // 2
+    chosen = dot(narrow, choose, (1, 0)).astype(BFLOAT)
+    grad = dot(chosen, values, (0, 0))
+    low = lax.broadcasted_iota(jnp.int32, (8, LANES), 1) < half
+    devices = []
+    for start in range(0, grad.shape[1], LANES):
+        own = grad[:, start : start + LANES]
+        turned_own = pltpu.roll(own, half, 1)
+        for first, second in ((own, turned_own), (turned_own, own)):
+            devices.append(
+                jnp.concatenate(
+                    [jnp.where(low, first[at : at + 8], second[at + 8 : at + 16]) for at in (0, 16)], axis=1
+                )
+            )
+    return jnp.concatenate(devices, axis=0).astype(BFLOAT)
+
+
 def finish_kernel(kind, first_own, first_near, first_far, second_own, second_near, second_far, lower_ref, chosen_ref,
                   *refs):
     half = second_own.shape[1]
+    model = HALVES * half
     wide = lambda ref: ref[...].astype(FLOAT)
     first = wide(first_own) + wide(first_near) + wide(first_far)
     second = wide(second_own) + wide(second_near) + wide(second_far)
@@ -761,30 +781,36 @@
         inner, matrix_rows(lower_ref[...]), (1, 1)
     )
     if kind == "output":
-        residual_ref, out_ref, inner_ref = refs
-        inner_ref[...] = inner
-        out_ref[...] = (residual_ref[...] + summed).astype(BFLOAT)
+        residual_ref, place_ref, choose_ref, branch_ref, early_ref, out_ref = refs
+        result = (residual_ref[...] + summed).astype(BFLOAT)
+        out_ref[:, :model] = dot(place_ref[...], result, (0, 0)).astype(BFLOAT)
+        out_ref[:, model : model + 2 * LANES] = packed_grad(inner, branch_ref[...], choose_ref[...])
+        out_ref[:, model + 2 * LANES :] = early_ref[...]
         return
     if kind == "forward":
         residual_ref, gain_ref, out_ref, inner_ref, left_ref, right_ref = refs
         hidden = residual_ref[...] + summed
         normed = (hidden * root_mean(hidden) * gain_ref[0:1, :]).astype(BFLOAT)
-        out_ref[...] = hidden
     else:
-        values_ref, upstream_ref, gain_ref = refs[:3]
+        values_ref, upstream_ref, gain_ref, choose_ref, normed_left, normed_right = refs[:6]
         values = values_ref[...]
         scale = root_mean(values)
         weighted = summed * gain_ref[0:1, :]
         mean = jnp.mean(weighted * values, axis=1, keepdims=True)
         hidden = upstream_ref[...].astype(FLOAT) + scale * weighted - values * (scale * scale * scale * mean)
         normed = hidden.astype(BFLOAT)
+        packed = packed_grad(
+            inner, jnp.concatenate([normed_left[...], normed_right[...]], axis=1), choose_ref[...]
+        )
         if kind == "input":
-            out_ref, inner_ref = refs[3:]
-            inner_ref[...] = inner
-            out_ref[...] = normed
+            place_ref, out_ref = refs[6:]
+            out_ref[:, :model] = dot(place_ref[...], normed, (0, 0)).astype(BFLOAT)
+            out_ref[:, model:] = packed
             return
-        out_ref, inner_ref, left_ref, right_ref = refs[3:]
-        out_ref[...] = hidden
+        given_ref, out_ref, inner_ref, left_ref, right_ref, packed_ref = refs[6:]
+        packed_ref[:, : 2 * LANES] = packed
+        packed_ref[:, 2 * LANES :] = packed_grad(given_ref[...], normed, choose_ref[...])
+    out_ref[...] = hidden
     inner_ref[...] = inner
     left_ref[...] = normed[:, :half]
     right_ref[...] = normed[:, half:]
@@ -796,24 +822,44 @@
     shards = gathered[-1].shape[0]
     model = HALVES * half
     lower = gathered[-1][:, : model // shards, -LANES:]
-    result = BFLOAT if kind in ("output", "input") else FLOAT
-    out_shape = [jax.ShapeDtypeStruct((rows, model), result), jax.ShapeDtypeStruct((rows, LANES), BFLOAT)]
-    if kind in ("forward", "backward"):
-        out_shape += [jax.ShapeDtypeStruct((rows, half), BFLOAT)] * 2
+    shaped = jax.ShapeDtypeStruct
+    if kind in ("output", "input"):
+        out_shape = shaped((rows, model + 2 * LANES * (3 if kind == "output" else 1)), BFLOAT)
+        out_specs = whole(out_shape.shape)
+    else:
+        out_shape = [shaped((rows, model), FLOAT), shaped((rows, LANES), BFLOAT)]
+        out_shape += [shaped((rows, half), BFLOAT)] * 2
+        out_shape += [shaped((rows, 4 * LANES), BFLOAT)] * (kind == "backward")
+        out_specs = [whole(shape.shape) for shape in out_shape]
     given = [*parts, lower, own_selector, *operands]
-    in_specs = [whole(value.shape) for value in given]
     return pl.pallas_call(
         functools.partial(finish_kernel, kind),
         grid=(1,),
-        in_specs=in_specs,
-        out_specs=[whole(shape.shape) for shape in out_shape],
+        in_specs=[whole(value.shape) for value in given],
+        out_specs=out_specs,
         out_shape=out_shape,
-        compiler_params=pltpu.CompilerParams(vmem_limit_bytes=DENSE_BYTES),
+        compiler_params=pltpu.CompilerParams(vmem_limit_bytes=FINISH_BYTES),
         cost_estimate=estimate(
             flops=2 * rows * model * LANES, bytes_accessed=rows * model * 20, transcendentals=0
         ),
         name="finish_" + kind,
     )(*given)
+
+
+def onward_kernel(first_kept, first_part, second_kept, second_part, first_ref, second_ref):
+    first_ref[...] = (first_kept[...] + first_part[...].astype(FLOAT)).astype(BFLOAT)
+    second_ref[...] = (second_kept[...] + second_part[...].astype(FLOAT)).astype(BFLOAT)
+
+
+def sum_onward(first_kept, first_part, second_kept, second_part):
+    return pl.pallas_call(
+        onward_kernel,
+        in_specs=[pl.BlockSpec(memory_space=pltpu.VMEM)] * 4,
+        out_specs=[pl.BlockSpec(memory_space=pltpu.VMEM)] * 2,
+        out_shape=[jax.ShapeDtypeStruct(part.shape, BFLOAT) for part in (first_part, second_part)],
+        compiler_params=pltpu.CompilerParams(vmem_limit_bytes=DENSE_BYTES),
+        name="sum_onward",
+    )(first_kept, first_part, second_kept, second_part)
 
 
 def send_kernel(target_column, target_row, tokens_ref, adapter_ref, sent_ref, matrix_ref):
@@ -947,6 +993,18 @@
     return lax.axis_size("col") == 4 and lax.axis_size("row") == 8 and rows == 256
 
 
+def spread_early(halves, gathered, selector):
+    left, right = halves
+    far_left, near_right = flip(left, 2), flip(right, 1)
+    near_left, far_right = flip(left, 1), flip(right, 2)
+    held = spread_block(0, halves, gathered, selector, None)
+    onward_left, onward_right = after_all((far_left, near_right), held[1])
+    corner = flip(onward_left, 1), flip(onward_right, 2)
+    held = spread_block(1, (near_left, near_right), gathered, selector, held)
+    held = spread_block(2, (far_left, far_right), gathered, selector, held)
+    return spread_block(3, corner, gathered, selector, held)
+
+
 def flip(values, mask):
     return lax.ppermute(values, "col", [(i, i ^ mask) for i in range(4)])
 
@@ -1006,10 +1064,7 @@
 
 def collect_middle(started):
     own, near_first, far_second, far_first, near_second, arriving = started
-    onward = [
-        (kept + part.astype(FLOAT)).astype(BFLOAT) for kept, part in zip((far_first, near_second), arriving)
-    ]
-    return (own, near_first, far_second), onward
+    return (own, near_first, far_second), sum_onward(far_first, arriving[0], near_second, arriving[1])
 
 
 def collect_onward(onward):
@@ -1188,18 +1243,34 @@
         chosen = (jnp.arange(NADAPT * RANK, dtype=jnp.int32)[:, None] == adapter_row[None, :]).astype(BFLOAT)
         return product(chosen, dealt)
 
-    def send_back(values, grads, earlier=()):
+    def send_back(values, grads):
         back = contract_first(place_matrix, values).astype(BFLOAT).reshape(devices, peer, model)
-        payload = jnp.concatenate([back, *grads], axis=2)
-        payload = after(payload, *earlier) if earlier else payload
-        payloads.append(payload)
-        return exchange(payload)
-
-    payloads = []
+        return exchange(jnp.concatenate([back, *grads], axis=2))
+
+    def expand_packed(dealt, count):
+        slots = dealt.shape[0] * peer
+        block = jnp.arange(2 * LANES // (model // devices), dtype=jnp.int32)[:, None, None]
+        row = jnp.arange(peer, dtype=jnp.int32)[None, None, :]
+        place = block * peer + row
+        adapter = jnp.where(place < RANK, source_adapters[None, :, 0:1], source_adapters[None, :, 1:2])
+        adapter_row = (adapter * RANK + place % RANK).reshape(block.shape[0], 1, slots)
+        chosen = (jnp.arange(NADAPT * RANK, dtype=jnp.int32)[None, :, None] == adapter_row).astype(BFLOAT)
+        sums = product(chosen.reshape(-1, slots), dealt.reshape(slots, dealt.shape[2]))
+        sums = sums.reshape(block.shape[0], NADAPT * RANK, dealt.shape[2])
+        width = model // devices
+        return [
+            sum(
+                sums[at, :, grad * 2 * LANES + at * width : grad * 2 * LANES + (at + 1) * width]
+                for at in range(block.shape[0])
+            )
+            for grad in range(count)
+        ]
 
     def take_back(dealt, count):
         returned = contract_first(send_matrix, dealt[:, :, :model].reshape(rows, model)).astype(BFLOAT)
-        width = (dealt.shape[2] - model) // max(count, 1)
+        if fast:
+            return returned, expand_packed(dealt[:, :, model:], count)
+        width = (dealt.shape[2] - model) // count
         return returned, [
             expand_grad(dealt[:, :, model + at * width : model + (at + 1) * width]) for at in range(count)
         ]
@@ -1225,10 +1296,14 @@
     feed_grad = jnp.concatenate(
         [wide_grad * up_part * (gate * (1.0 + gate_part * (1.0 - gate))), wide_grad * silu], axis=1
     ).astype(BFLOAT)
+    choose = (
+        jnp.arange(NADAPT * RANK, dtype=jnp.int32)[:, None]
+        == (adapters[:, None] * RANK + jnp.arange(RANK, dtype=jnp.int32)[None, :]).reshape(1, -1)
+    ).astype(BFLOAT)
     if fast:
         pieces = collect_pieces(after(activated, feed_grad), weights_down, True)
         kept, onward = collect_middle(collect_send(collect_pieces(feed_grad, weights_feed, False)))
-        hidden_grad, narrow_three, *branch_one = collect_end(
+        hidden_grad, narrow_three, left, right, early_grads = collect_end(
             kept,
             collect_onward(onward),
             "backward",
@@ -1237,20 +1312,15 @@
             after(hidden, pieces[3][0]),
             branch_two,
             gains[1],
+            choose,
+            *normed_two,
+            inner_out,
         )
-        blocks_branch = gather_blocks(branch_one)
+        mixed_grad, narrow_one = spread_early((left, right), weights_mix, selector)
     else:
         hidden_grad, narrow_three, *branch_one = collect_project(
             feed_grad, weights_feed, "backward", own_selector, hidden, branch_two, gains[1]
         )
-    early_grads = [
-        compact_grad(narrow_three, jnp.concatenate(normed_two, axis=1)),
-        compact_grad(inner_out, jnp.concatenate(branch_one, axis=1)),
-    ]
-    if fast:
-        blocks_branch[3] = (3, after_all(blocks_branch[3][1], *early_grads))
-        mixed_grad, narrow_one = spread_gathered(blocks_branch, weights_mix, selector)
-    else:
         mixed_grad, narrow_one = spread_project(branch_one, weights_mix, selector)
 
     if fast:
@@ -1258,28 +1328,41 @@
         started = collect_send(
             [near_parts[:2], (near_parts[2], pieces[1][1]), (pieces[2][0], near_parts[3]), pieces[3]], False
         )
-        projected_grad = scan_backward(projected, tables, scanned, carried, after(mixed_grad, near_parts[0]))
-        kept, onward = collect_middle((*started[:5], [after(part, projected_grad) for part in started[5]]))
-        projected_grad = attention_backward(
-            projected, tables, mixed_grad, after(projected_grad, *onward, *kept[1:])
+        attended_grads = attention_backward(projected, tables, after(mixed_grad, near_parts[0]))
+        kept, onward = collect_middle((*started[:5], after_all(started[5], attended_grads[1])))
+        scan_inputs = (projected, tables, scanned, carried, after(mixed_grad, *onward), attended_grads)
+        scan_part = list(scan_backward(*scan_inputs, 0, 2, None))
+        payload = collect_end(
+            kept,
+            collect_onward(onward),
+            "output",
+            weights_down,
+            own_selector,
+            after(hidden, scan_part[2]),
+            place_matrix,
+            choose,
+            branch_two,
+            early_grads,
         )
-        last = collect_onward(onward)
+        dealt_out = exchange(payload.reshape(devices, peer, -1))
+        scan_part[2] = after(scan_part[2], payload)
+        projected_grad = scan_backward(*scan_inputs, 1, 2, scan_part)[0]
         started_in = collect_send(collect_pieces(projected_grad, weights_in, True))
         kept_in, onward_in = collect_middle(started_in)
-        block_out, inner_down = collect_end(
-            kept, last, "output", weights_down, own_selector, after(hidden, started_in[0][0])
-        )
     else:
         block_out, inner_down = collect_project(activated, weights_down, "output", own_selector, hidden)
-        projected_grad = scan_backward(projected, tables, scanned, carried, mixed_grad)
-        projected_grad = attention_backward(projected, tables, mixed_grad, projected_grad)
-    dealt_out = send_back(
-        block_out,
-        [
-            compact_grad(inner_down, branch_two),
-            *early_grads,
-        ],
-    )
+        attended_grads = attention_backward(projected, tables, mixed_grad)
+        projected_grad = scan_backward(
+            projected, tables, scanned, carried, mixed_grad, attended_grads, 0, 1, None
+        )[0]
+        dealt_out = send_back(
+            block_out,
+            [
+                compact_grad(inner_down, branch_two),
+                compact_grad(narrow_three, jnp.concatenate(normed_two, axis=1)),
+                compact_grad(inner_out, jnp.concatenate(branch_one, axis=1)),
+            ],
+        )
 
     def sum_rows(values):
         return lax.psum_scatter(values.astype(BFLOAT), "row", scatter_dimension=0, tiled=True).astype(FLOAT)
@@ -1295,24 +1378,27 @@
     late = sum_rows(raise_grad)
 
     if fast:
-        input_grad, narrow_four = collect_end(
+        payload = collect_end(
             kept_in,
             collect_onward(onward_in),
             "input",
             weights_in,
             own_selector,
             own_input,
-            after(hidden_grad, payloads[0]),
+            after(hidden_grad, dealt_out),
             gains[0],
+            choose,
+            *normed_one,
+            place_matrix,
         )
+        dealt_grad = exchange(payload.reshape(devices, peer, -1))
     else:
         input_grad, narrow_four = collect_project(
             projected_grad, weights_in, "input", own_selector, own_input, hidden_grad, gains[0]
         )
-    dealt_grad = send_back(
-        input_grad, [compact_grad(narrow_four, jnp.concatenate(normed_one, axis=1))], [dealt_out]
-    )
-    dealt_out, early, late = after_all((dealt_out, early, late), payloads[-1])
+        dealt_grad = send_back(input_grad, [compact_grad(narrow_four, jnp.concatenate(normed_one, axis=1))])
+        payload = input_grad
+    dealt_out, early, late = after_all((dealt_out, early, late), payload)
     early_cuts = [0, early_parts[0].shape[1]]
     early_cuts.append(early_cuts[1] + early_parts[1].shape[1])
     grad_mix_lower = join_halves(early[:, : early_cuts[1]], units, GATE_WIDTH, 1).T

time: 668 us -> 660 us (0.988)
  waiting for transfers between devices: 201 us -> 216 us
  other arithmetic: 36.4 us -> 22.4 us
  matrix products: 26.5 us -> 12.7 us
    reduce_scatter x2, waiting for transfers between devices: 0.02 us -> 23.3 us  [sum_rows(): lax.psum_scatter(values.astype(BFLOAT), 'row', scatter_dimension=0, tiled...]
    ppermute x55, waiting for transfers between devices: 132 us -> 118 us  [flip(): return lax.ppermute(values, 'col', [(i, i ^ mask) for i in range(4)])]
    unnamed x346 -> x358, local copies, waits for them, and re-layouts: 89.2 us -> 102 us
    dot_general x12 -> x6, matrix products: 19.9 us -> 7.87 us  [contract_first(): lax.dot_general(left, right, (((0,), (0,)), ((), ())), preferred_element_...]
    convert_element_type x9 -> x2, other arithmetic: 10.9 us -> 0.02 us  [the longest x1 0.02 us: local(): choose = (jnp.arange(NADAPT * RANK, dtype=jnp.int32)[:, None] == (adapter...]
    reshape x14 -> x0, local copies, waits for them, and re-layouts: 9.19 us -> none  [the longest x6 5.43 us: compact_grad(): grad = grad.reshape(kept, devices, model // devices).transpose(1, 0, 2)]
    ppermute x55, starting transfers between devices: 59 us -> 66 us  [flip(): return lax.ppermute(values, 'col', [(i, i ^ mask) for i in range(4)])]
    pallas_call x1 -> x6, Pallas kernels: 27.8 us -> 33.1 us  [the longest x2 28.7 us: scan_backward(): pl.pallas_call(scan_backward_kernel, grid=(blocks // parts,), in_specs=in...]
  transfers between devices with their start and end apart: 66 -> 66, of which waited for: 26 -> 27; matrix products, arithmetic and copies ran while one was open for 15% -> 9% of each run, Pallas kernels for 24% -> 25%
where the time goes in v7:
time: 660 us; the launch traced here: 651 us
  waiting for transfers between devices  216 us (33%)
  Pallas kernels  175 us (27%)
  local copies, waits for them, and re-layouts  124 us (19%)
  starting transfers between devices  83.7 us (13%)
  other arithmetic  22.4 us (3%)
  between operations  17.2 us (3%)
  matrix products  12.7 us (2%)
    ppermute x55, waiting for transfers between devices, flip(): return lax.ppermute(values, 'col', [(i, i ^ mask) for i in range(4)])  118 us
    unnamed x358, local copies, waits for them, and re-layouts  102 us
    pallas_call x16, Pallas kernels, spread_block(): pl.pallas_call(functools.partial(spread_kernel, mask, len(gathered)), in_...  66.6 us
    ppermute x55, starting transfers between devices, flip(): return lax.ppermute(values, 'col', [(i, i ^ mask) for i in range(4)])  66 us
    all_to_all x4, waiting for transfers between devices, local(): lax.all_to_all(values, ALL_AXES, split_axis=0, concat_axis=0, tiled=True)  40.7 us
    pallas_call x6, Pallas kernels, collect_blocks(): pl.pallas_call(functools.partial(collect_kernel, masks, len(gathered)), i...  37.3 us
    pallas_call x2, Pallas kernels, scan_backward(): pl.pallas_call(scan_backward_kernel, grid=(blocks // parts,), in_specs=in...  28.7 us
    reduce_scatter x2, waiting for transfers between devices, sum_rows(): lax.psum_scatter(values.astype(BFLOAT), 'row', scatter_dimension=0, tiled...  23.3 us
  transfers between devices with their start and end apart: 66, of which 27 were waited for; matrix products, arithmetic and copies ran while one was open for 9% of the time, Pallas kernels for 25%

profile of v7, /device:TPU:0, one launch (start us, length us, event | category | flops | bytes accessed | tf_op | source)
XLA Modules:
  0.0 651.2 jit_solution(1072968088886678516)
XLA Ops:
  23.1 7.3 %all-to-all-start = ((bf16[32,8,2176]{2,1,0:T(8,128)(2,1)}), bf16[32,8,2176]{2,1,0:T(8,128)(2,1)S(1)}, u32[]{:S(2)}, u32[]{:S(2)}) async-start(bf16[32,8,2176]{2,1,0:T(8,128)(2,1)} %bitcast.192), calls=%async_computation | async-start | bytes 2228224 | tf_op jit(solution)/shard_map/all_to_all | solution.py:1149
  30.5 12.0 %all-gather.11.cloned.1.call-done = bf16[2304,256]{1,0:T(8,128)(2,1)} async-done(((bf16[288,256]{1,0:T(8,128)(2,1)}), bf16[2304,256]{1,0:T(8,128)(2,1)}) %all-gather.11.cloned.1.call-update) | async-done | bytes 1179664 | tf_op jit(solution)/shard_map/all_gather | solution.py:1174
  48.1 24.5 %all-to-all-done = bf16[32,8,2176]{2,1,0:T(8,128)(2,1)S(1)} async-done(((bf16[32,8,2176]{2,1,0:T(8,128)(2,1)}), bf16[32,8,2176]{2,1,0:T(8,128)(2,1)S(1)}, u32[]{:S(2)}, u32[]{:S(2)}) %all-to-all-start) | async-done | bytes 1114144 | tf_op jit(solution)/shard_map/all_to_all | solution.py:1149
  95.6 12.6 %collective-permute-done.4.right_ref = bf16[256,1024]{1,0:T(8,128)(2,1)S(1)} collective-permute-done((bf16[256,1024]{1,0:T(8,128)(2,1)}, bf16[256,1024]{1,0:T(8,128)(2,1)S(1)}, u32[]{:S(2)}, u32[]{:S(2)}) %collective-permute-start.4) | collective-permute-done | bytes 524320 | tf_op jit(solution)/shard_map/ppermute | solution.py:1009
  109.1 12.3 %collective-permute-done.2.left_ref = bf16[256,1024]{1,0:T(8,128)(2,1)} collective-permute-done((bf16[256,1024]{1,0:T(8,128)(2,1)}, bf16[256,1024]{1,0:T(8,128)(2,1)}, u32[]{:S(2)}, u32[]{:S(2)}) %collective-permute-start.2) | collective-permute-done | bytes 524320 | tf_op jit(solution)/shard_map/ppermute | solution.py:1009
  139.8 7.5 %spread_block.16 = (bf16[1024,2688]{1,0:T(8,128)(2,1)S(1)}, bf16[1024,128]{1,0:T(8,128)(2,1)S(1)}) custom-call(bf16[256,1024]{1,0:T(8,128)(2,1)} %get-tuple-element.144.left_ref.refs_4_, bf16[256,1024]{1,0:T(8,128)(2,1)} %get-tuple-element.145.right_ref.refs_5_, f32[1024,128]{1,0:T(8,128)S(1)} %compare_convert_fusion.chosen_ref, ...), custom_call_target="tpu_custom_call" | custom-call | flops 184549376 | bytes 151552 | tf_op jit(solution)/shard_map/spread_block/pallas_call | solution.py:671
  147.2 7.1 %spread_block.17 = (bf16[1024,2688]{1,0:T(8,128)(2,1)S(1)}, bf16[1024,128]{1,0:T(8,128)(2,1)S(1)}) custom-call(bf16[256,1024]{1,0:T(8,128)(2,1)} %collective-permute-done.9.left_ref, bf16[256,1024]{1,0:T(8,128)(2,1)S(1)} %collective-permute-done.4.right_ref, ...), custom_call_target="tpu_custom_call", output_to_operand_aliasing={{0}: (5, {}), {1}: (6, {})} | custom-call | flops 184549376 | bytes 151552 | tf_op jit(solution)/shard_map/spread_block/pallas_call | solution.py:671
  154.4 7.5 %spread_block.18 = (bf16[1024,2688]{1,0:T(8,128)(2,1)S(1)}, bf16[1024,128]{1,0:T(8,128)(2,1)S(1)}) custom-call(bf16[256,1024]{1,0:T(8,128)(2,1)} %collective-permute-done.2.left_ref, bf16[256,1024]{1,0:T(8,128)(2,1)S(1)} %collective-permute-done.8.right_ref, ...), custom_call_target="tpu_custom_call", output_to_operand_aliasing={{0}: (5, {}), {1}: (6, {})} | custom-call | flops 184549376 | bytes 151552 | tf_op jit(solution)/shard_map/spread_block/pallas_call | solution.py:671
  161.9 7.3 %spread_block.19 = (bf16[1024,2688]{1,0:T(8,128)(2,1)S(1)}, bf16[1024,128]{1,0:T(8,128)(2,1)S(1)}) custom-call(bf16[256,1024]{1,0:T(8,128)(2,1)} %collective-permute-done.3.left_ref, bf16[256,1024]{1,0:T(8,128)(2,1)} %collective-permute-done.5.right_ref, ...), custom_call_target="tpu_custom_call", output_to_operand_aliasing={{0}: (5, {}), {1}: (6, {})} | custom-call | flops 184549376 | bytes 151552 | tf_op jit(solution)/shard_map/spread_block/pallas_call | solution.py:671
  189.9 12.9 %scan_forward.1 = (bf16[1024,1024]{1,0:T(8,128)(2,1)S(1)}, f32[1024,768]{1,0:T(8,128)S(1)}, bf16[4,256,768]{2,1,0:T(8,128)(2,1)S(1)}) custom-call(bf16[1024,2688]{1,0:T(8,128)(2,1)S(1)} %copy-done.3, bf16[1024,2688]{1,0:T(8,128)(2,1)S(1)} %copy-done.3, bf16[1024,2688]{1,0:T(8,128)(2,1)S(1)} %copy-done.3, ...), custom_call_target="tpu_custom_call", output_to_operand_aliasing={{0}: (12, {})} | custom-call | flops 83886080 | bytes 589824 | tf_op jit(solution)/shard_map/scan_forward/pallas_call | solution.py:383
  241.0 17.4 %collective-permute-done.14.second_near = bf16[256,1024]{1,0:T(8,128)(2,1)} collective-permute-done((bf16[256,1024]{1,0:T(8,128)(2,1)}, bf16[256,1024]{1,0:T(8,128)(2,1)}, u32[]{:S(2)}, u32[]{:S(2)}) %collective-permute-start.14) | collective-permute-done | bytes 524320 | tf_op jit(solution)/shard_map/ppermute | solution.py:1009
  281.6 7.6 %collective-permute-done.22.left_ref = bf16[256,1024]{1,0:T(8,128)(2,1)} collective-permute-done((bf16[256,1024]{1,0:T(8,128)(2,1)}, bf16[256,1024]{1,0:T(8,128)(2,1)}, u32[]{:S(2)}, u32[]{:S(2)}) %collective-permute-start.22) | collective-permute-done | bytes 524320 | tf_op jit(solution)/shard_map/ppermute | solution.py:1009
  293.5 6.8 %collective-permute-done.20.right_ref = bf16[256,1024]{1,0:T(8,128)(2,1)S(1)} collective-permute-done((bf16[256,1024]{1,0:T(8,128)(2,1)S(1)}, bf16[256,1024]{1,0:T(8,128)(2,1)S(1)}, u32[]{:S(2)}, u32[]{:S(2)}) %collective-permute-start.20) | collective-permute-done | bytes 524320 | tf_op jit(solution)/shard_map/ppermute | solution.py:1009
  329.0 15.3 %all-gather.19.cloned.1.call-done = bf16[2176,1152]{1,0:T(8,128)(2,1)} async-done(((bf16[272,1152]{1,0:T(8,128)(2,1)}), bf16[2176,1152]{1,0:T(8,128)(2,1)}) %all-gather.19.cloned.1.call-update) | async-done | bytes 5013520 | tf_op jit(solution)/shard_map/all_gather | solution.py:1159
  371.2 8.3 %collect_blocks.10 = (bf16[256,1152]{1,0:T(8,128)(2,1)}, f32[256,1024]{1,0:T(8,128)S(1)}, f32[256,1152]{1,0:T(8,128)S(1)}, bf16[256,1024]{1,0:T(8,128)(2,1)}, f3...) custom-call(bf16[1024,2048]{1,0:T(8,128)(2,1)S(1)} %pad_maximum_fusion.values_ref, bf16[8,272,2176]{2,1,0:T(8,128)(2,1)S(1)} %bitcast.165), custom_call_target="tpu_custom_call" | custom-call | flops 402653184 | bytes 589824 | tf_op jit(solution)/shard_map/collect_blocks/pallas_call | solution.py:734
  422.2 8.8 %collective-permute-done.34.left_ref = bf16[256,1024]{1,0:T(8,128)(2,1)S(1)} collective-permute-done((bf16[256,1024]{1,0:T(8,128)(2,1)S(1)}, bf16[256,1024]{1,0:T(8,128)(2,1)S(1)}, u32[]{:S(2)}, u32[]{:S(2)}) %collective-permute-start.34) | collective-permute-done | bytes 524320 | tf_op jit(solution)/shard_map/ppermute | solution.py:1009
  435.7 7.1 %collective-permute-done.39.left_ref = bf16[256,1024]{1,0:T(8,128)(2,1)S(1)} collective-permute-done((bf16[256,1024]{1,0:T(8,128)(2,1)S(1)}, bf16[256,1024]{1,0:T(8,128)(2,1)S(1)}, u32[]{:S(2)}, u32[]{:S(2)}) %collective-permute-start.39) | collective-permute-done | bytes 524320 | tf_op jit(solution)/shard_map/ppermute | solution.py:1009
  464.2 7.2 %attention_backward.1 = (bf16[1024,256]{1,0:T(8,128)(2,1)S(1)}, bf16[1024,256]{1,0:T(8,128)(2,1)S(1)}) custom-call(bf16[1024,2688]{1,0:T(8,128)(2,1)S(1)} %copy-done.4, bf16[1024,2688]{1,0:T(8,128)(2,1)S(1)} %copy-done.4, bf16[1024,2688]{1,0:T(8,128)(2,1)S(1)} %copy-done.4, f32[1024,128]{1,0:T(8,128)S(1)} %copy-done.49, f32[1024,128]{1,0:T(8,128)S(1)} %copy-done.47, ...), custom_call_target="tpu_custom_call" | custom-call | flops 100663296 | bytes 393216 | tf_op jit(solution)/shard_map/attention_backward/pallas_call | solution.py:556
  478.2 13.9 %scan_backward.2 = (bf16[1024,2688]{1,0:T(8,128)(2,1)S(1)}, f32[256,768]{1,0:T(8,128)S(1)}, f32[8,768]{1,0:T(8,128)S(1)}, f32[8,512]{1,0:T(8,128)S(1)}) custom-call(bf16[1024,2688]{1,0:T(8,128)(2,1)S(1)} %copy-done.4, bf16[1024,2688]{1,0:T(8,128)(2,1)S(1)} %copy-done.4, bf16[1024,2688]{1,0:T(8,128)(2,1)S(1)} %copy-done.4, bf16[1024,2688]{1,0:T(8,128)(2,1)S(1)} %copy-done.4, ...), custom_call_target="tpu_custom_call" | custom-call | flops 167772160 | bytes 1179648 | tf_op jit(solution)/shard_map/scan_backward/pallas_call | solution.py:426
  512.4 14.8 %scan_backward.3 = (bf16[1024,2688]{1,0:T(8,128)(2,1)S(1)}, f32[256,768]{1,0:T(8,128)}, f32[8,768]{1,0:T(8,128)}, f32[8,512]{1,0:T(8,128)}) custom-call(bf16[1024,2688]{1,0:T(8,128)(2,1)S(1)} %copy-done.5, bf16[1024,2688]{1,0:T(8,128)(2,1)S(1)} %copy-done.5, bf16[1024,2688]{1,0:T(8,128)(2,1)S(1)} %copy-done.5, ...), custom_call_target="tpu_custom_call", output_to_operand_aliasing={{0}: (17, {})} | custom-call | flops 167772160 | bytes 1179648 | tf_op jit(solution)/shard_map/scan_backward/pallas_call | solution.py:426
  529.2 13.5 %collect_blocks.11 = (bf16[256,1152]{1,0:T(8,128)(2,1)S(1)}, bf16[256,1024]{1,0:T(8,128)(2,1)S(1)}, bf16[256,1152]{1,0:T(8,128)(2,1)S(1)}, f32[256,1024]{1,0:T(8...) custom-call(bf16[1024,2688]{1,0:T(8,128)(2,1)S(1)} %get-tuple-elemen, ...), custom_call_target="tpu_custom_call" | custom-call | flops 704643072 | bytes 868352 | tf_op jit(solution)/shard_map/collect_blocks/pallas_call | solution.py:734
  545.9 12.2 %collective-permute-done.47.second_part = bf16[256,1024]{1,0:T(8,128)(2,1)S(1)} collective-permute-done((bf16[256,1024]{1,0:T(8,128)(2,1)S(1)}, bf16[256,1024]{1,0:T(8,128)(2,1)S(1)}, u32[]{:S(2)}, u32[]{:S(2)}) %collective-permute-start.47) | collective-permute-done | bytes 524320 | tf_op jit(solution)/shard_map/ppermute | solution.py:1009
  571.7 23.3 %reduce-scatter.5.cloned.1.call-done = bf16[16,2688]{1,0:T(8,128)(2,1)} async-done(((bf16[128,2688]{1,0:T(8,128)(2,1)}), bf16[16,2688]{1,0:T(8,128)(2,1)}) %reduce-scatter.5.cloned.1.call-update) | async-done | bytes 86032 | tf_op jit(solution)/shard_map/reduce_scatter | solution.py:1368
  625.1 16.2 %all-to-all-done.3 = bf16[32,8,2304]{2,1,0:T(8,128)(2,1)S(1)} async-done(((bf16[32,8,2304]{2,1,0:T(8,128)(2,1)}), bf16[32,8,2304]{2,1,0:T(8,128)(2,1)S(1)}, u32[]{:S(2)}, u32[]{:S(2)}) %all-to-all-start.3) | async-done | bytes 1179680 | tf_op jit(solution)/shard_map/all_to_all | solution.py:1149
  (641 shorter events, 350.6 us)
Async XLA Ops:
  7.2 35.2 %all-gather.11.cloned.1.call-start = ((), (), s32[]{:S(2)}) async-start(), calls=%async_computation.8 | async-start | bytes 1327104 | tf_op jit(solution)/shard_map/all_gather | solution.py:1174
  12.7 121.6 %all-gather.13.cloned.1.call-start = ((), (), s32[]{:S(2)}) async-start(), calls=%async_computation.9 | async-start | bytes 10027008 | tf_op jit(solution)/shard_map/all_gather | solution.py:1159
  21.3 185.6 %all-gather.15.cloned.1.call-start = ((), (), s32[]{:S(2)}) async-start(), calls=%async_computation.10 | async-start | bytes 5640192 | tf_op jit(solution)/shard_map/all_gather | solution.py:1159
  23.1 49.4 %all-to-all-start = ((bf16[32,8,2176]{2,1,0:T(8,128)(2,1)}), bf16[32,8,2176]{2,1,0:T(8,128)(2,1)S(1)}, u32[]{:S(2)}, u32[]{:S(2)}) async-start(bf16[32,8,2176]{2,1,0:T(8,128)(2,1)} %bitcast.192), calls=%async_computation | async-start | bytes 2228224 | tf_op jit(solution)/shard_map/all_to_all | solution.py:1149
  30.4 274.3 %all-gather.17.cloned.1.call-start = ((), (), s32[]{:S(2)}) async-start(), calls=%async_computation.11 | async-start | bytes 10653696 | tf_op jit(solution)/shard_map/all_gather | solution.py:1159
  42.4 33.6 %collective-permute-start.1 = (bf16[8,288,256]{2,1,0:T(8,128)(2,1)}, bf16[8,288,256]{2,1,0:T(8,128)(2,1)}, u32[]{:S(2)}, u32[]{:S(2)}) collective-permute-start(bf16[8,288,256]{2,1,0:T(8,128)(2,1)} %bitcast.194), channel_id=1, source_target_pairs={{0,2},{1,3},{2,0},{3,1},{4,6},{5,7},{6,4},{7,5},{8,10},{9,11},{10,... | collective-permute-start | bytes 3538952 | tf_op jit(solution)/shard_map/ppermute | solution.py:1009
  78.8 265.4 %all-gather.19.cloned.1.call-start = ((), (), s32[]{:S(2)}) async-start(), calls=%async_computation.12 | async-start | bytes 5640192 | tf_op jit(solution)/shard_map/all_gather | solution.py:1159
  81.7 40.7 %collective-permute-start.7 = (bf16[4,288,256]{2,1,0:T(8,128)(2,1)S(1)}, bf16[4,288,256]{2,1,0:T(8,128)(2,1)S(1)}, u32[]{:S(2)}, u32[]{:S(2)}) collective-permute-start(bf16[4,288,256]{2,1,0:T(8,128)(2,1)S(1)} %slice.489), channel_id=1, source_target_pairs={{0,1},{1,0},{2,3},{3,2},{4,5},{5,4},{6,7},{7,6},{8,9},{9,8},{10,11... | collective-permute-start | bytes 1769480 | tf_op jit(solution)/shard_map/ppermute | solution.py:1009
  83.8 40.0 %collective-permute-start.6 = (bf16[4,288,256]{2,1,0:T(8,128)(2,1)S(1)}, bf16[4,288,256]{2,1,0:T(8,128)(2,1)S(1)}, u32[]{:S(2)}, u32[]{:S(2)}) collective-permute-start(bf16[4,288,256]{2,1,0:T(8,128)(2,1)S(1)} %slice.488), channel_id=1, source_target_pairs={{0,2},{1,3},{2,0},{3,1},{4,6},{5,7},{6,4},{7,5},{8,10},{9,11},{10,... | collective-permute-start | bytes 1769480 | tf_op jit(solution)/shard_map/ppermute | solution.py:1009
  89.3 65.0 %collective-permute-start.8 = (bf16[256,1024]{1,0:T(8,128)(2,1)}, bf16[256,1024]{1,0:T(8,128)(2,1)S(1)}, u32[]{:S(2)}, u32[]{:S(2)}) collective-permute-start(bf16[256,1024]{1,0:T(8,128)(2,1)} %get-tuple-element.145.right_ref.refs_5_), channel_id=1, source_target_pairs={{0,2},{1,3},{2,0},{3,1},{4,6},{5,7},{6,4},{7,5},{8,10},{9,11},{10,... | collective-permute-start | bytes 1572872 | tf_op jit(solution)/shard_map/ppermute | solution.py:1009
  108.2 39.0 %collective-permute-start.9 = (bf16[256,1024]{1,0:T(8,128)(2,1)}, bf16[256,1024]{1,0:T(8,128)(2,1)}, u32[]{:S(2)}, u32[]{:S(2)}) collective-permute-start(bf16[256,1024]{1,0:T(8,128)(2,1)} %get-tuple-element.144.left_ref.refs_4_), channel_id=1, source_target_pairs={{0,1},{1,0},{2,3},{3,2},{4,5},{5,4},{6,7},{7,6},{8,9},{9,8},{10,11... | collective-permute-start | bytes 1572872 | tf_op jit(solution)/shard_map/ppermute | solution.py:1009
  121.4 40.5 %collective-permute-start.5 = (bf16[256,1024]{1,0:T(8,128)(2,1)S(1)}, bf16[256,1024]{1,0:T(8,128)(2,1)}, u32[]{:S(2)}, u32[]{:S(2)}) collective-permute-start(bf16[256,1024]{1,0:T(8,128)(2,1)S(1)} %collective-permute-done.4.right_ref), channel_id=1, source_target_pairs={{0,2},{1,3},{2,0},{3,1},{4,6},{5,7},{6,4},{7,5},{8,10},{9,11},{10,... | collective-permute-start | bytes 1572872 | tf_op jit(solution)/shard_map/ppermute | solution.py:1009
  122.4 39.5 %collective-permute-start.3 = (bf16[256,1024]{1,0:T(8,128)(2,1)}, bf16[256,1024]{1,0:T(8,128)(2,1)}, u32[]{:S(2)}, u32[]{:S(2)}) collective-permute-start(bf16[256,1024]{1,0:T(8,128)(2,1)} %collective-permute-done.2.left_ref), channel_id=1, source_target_pairs={{0,1},{1,0},{2,3},{3,2},{4,5},{5,4},{6,7},{7,6},{8,9},{9,8},{10,11... | collective-permute-start | bytes 1572872 | tf_op jit(solution)/shard_map/ppermute | solution.py:1009
  175.1 59.9 %all-to-all-start.1 = ((bf16[32,8,2048]{2,1,0:T(8,128)(2,1)}), bf16[32,8,2048]{2,1,0:T(8,128)(2,1)}, u32[]{:S(2)}, u32[]{:S(2)}) async-start(bf16[32,8,2048]{2,1,0:T(8,128)(2,1)} %fusion.9), calls=%async_computation.1 | async-start | bytes 2097152 | tf_op jit(solution)/shard_map/all_to_all | solution.py:1149
  178.9 391.2 %reduce-scatter.3.cloned.1.call-start = ((), (), s32[]{:S(2)}) async-start(), calls=%async_computation.6 | async-start | bytes 1179648 | tf_op jit(solution)/shard_map/reduce_scatter | solution.py:1368
  279.9 42.6 %collective-permute-start.19 = (bf16[256,1024]{1,0:T(8,128)(2,1)}, bf16[256,1024]{1,0:T(8,128)(2,1)}, u32[]{:S(2)}, u32[]{:S(2)}) collective-permute-start(bf16[256,1024]{1,0:T(8,128)(2,1)} %collective-permute-done.18.right_ref), channel_id=1, source_target_pairs={{0,2},{1,3},{2,0},{3,1},{4,6},{5,7},{6,4},{7,5},{8,10},{9,11},{10,... | collective-permute-start | bytes 1572872 | tf_op jit(solution)/shard_map/ppermute | solution.py:1009
  289.2 60.6 %collective-permute-start.27 = (bf16[256,1024]{1,0:T(8,128)(2,1)}, bf16[256,1024]{1,0:T(8,128)(2,1)}, u32[]{:S(2)}, u32[]{:S(2)}) collective-permute-start(bf16[256,1024]{1,0:T(8,128)(2,1)} %get-tuple-element.338.left_ref), channel_id=1, source_target_pairs={{0,1},{1,0},{2,3},{3,2},{4,5},{5,4},{6,7},{7,6},{8,9},{9,8},{10,11... | collective-permute-start | bytes 1572872 | tf_op jit(solution)/shard_map/ppermute | solution.py:1009
  291.8 61.1 %collective-permute-start.26 = (bf16[256,1024]{1,0:T(8,128)(2,1)}, bf16[256,1024]{1,0:T(8,128)(2,1)}, u32[]{:S(2)}, u32[]{:S(2)}) collective-permute-start(bf16[256,1024]{1,0:T(8,128)(2,1)} %get-tuple-element.337.right_ref), channel_id=1, source_target_pairs={{0,2},{1,3},{2,0},{3,1},{4,6},{5,7},{6,4},{7,5},{8,10},{9,11},{10,... | collective-permute-start | bytes 1572872 | tf_op jit(solution)/shard_map/ppermute | solution.py:1009
  301.1 55.0 %collective-permute-start.25 = (bf16[256,1024]{1,0:T(8,128)(2,1)}, bf16[256,1024]{1,0:T(8,128)(2,1)}, u32[]{:S(2)}, u32[]{:S(2)}) collective-permute-start(bf16[256,1024]{1,0:T(8,128)(2,1)} %collective-permute-done.24.right_ref), channel_id=1, source_target_pairs={{0,2},{1,3},{2,0},{3,1},{4,6},{5,7},{6,4},{7,5},{8,10},{9,11},{10,... | collective-permute-start | bytes 1572872 | tf_op jit(solution)/shard_map/ppermute | solution.py:1009
  303.3 52.9 %collective-permute-start.23 = (bf16[256,1024]{1,0:T(8,128)(2,1)}, bf16[256,1024]{1,0:T(8,128)(2,1)}, u32[]{:S(2)}, u32[]{:S(2)}) collective-permute-start(bf16[256,1024]{1,0:T(8,128)(2,1)} %collective-permute-done.22.left_ref), channel_id=1, source_target_pairs={{0,1},{1,0},{2,3},{3,2},{4,5},{5,4},{6,7},{7,6},{8,9},{9,8},{10,11... | collective-permute-start | bytes 1572872 | tf_op jit(solution)/shard_map/ppermute | solution.py:1009
  459.2 37.0 %collective-permute-start.40 = (bf16[256,1152]{1,0:T(8,128)(2,1)}, bf16[256,1152]{1,0:T(8,128)(2,1)S(1)}, u32[]{:S(2)}, u32[]{:S(2)}) collective-permute-start(bf16[256,1152]{1,0:T(8,128)(2,1)} %copy-done.123), channel_id=1, source_target_pairs={{0,1},{1,0},{2,3},{3,2},{4,5},{5,4},{6,7},{7,6},{8,9},{9,8},{10,11... | collective-permute-start | bytes 1769480 | tf_op jit(solution)/shard_map/ppermute | solution.py:1009
  498.7 97.8 %all-to-all-start.2 = ((bf16[32,8,2816]{2,1,0:T(8,128)(2,1)}), bf16[32,8,2816]{2,1,0:T(8,128)(2,1)}, u32[]{:S(2)}, u32[]{:S(2)}) async-start(bf16[32,8,2816]{2,1,0:T(8,128)(2,1)} %bitcast.40), calls=%async_computation.2 | async-start | bytes 2883584 | tf_op jit(solution)/shard_map/all_to_all | solution.py:1149
  502.3 92.7 %reduce-scatter.5.cloned.1.call-start = ((), (), s32[]{:S(2)}) async-start(), calls=%async_computation.7 | async-start | bytes 774144 | tf_op jit(solution)/shard_map/reduce_scatter | solution.py:1368
  562.1 34.5 %collective-permute-start.49 = (bf16[256,1152]{1,0:T(8,128)(2,1)}, bf16[256,1152]{1,0:T(8,128)(2,1)S(1)}, u32[]{:S(2)}, u32[]{:S(2)}) collective-permute-start(bf16[256,1152]{1,0:T(8,128)(2,1)} %copy-done.125), channel_id=1, source_target_pairs={{0,2},{1,3},{2,0},{3,1},{4,6},{5,7},{6,4},{7,5},{8,10},{9,11},{10,... | collective-permute-start | bytes 1769480 | tf_op jit(solution)/shard_map/ppermute | solution.py:1009
  (208 other events, 2860.1 us)
Sparse Core Ops, SparseCore 0:
  12.8 29.6 all-gather.10
  44.1 90.1 all-gather.12
  136.5 60.8 all-gather.14
  198.9 91.1 all-gather.16
  291.6 52.5 all-gather.18
  459.3 29.3 reduce-scatter.2
  562.2 32.7 reduce-scatter.4

commit v8 on v7

--- a/solution.py
+++ b/solution.py
@@ -65,6 +65,7 @@
 
 ESTIMATE = 16
 SCAN_BYTES = 32 * 1024 * 1024
+ALONE_BYTES = 56 * 1024 * 1024
 DENSE_BYTES = 16 * 1024 * 1024
 FINISH_BYTES = 32 * 1024 * 1024
 LANES = 128
@@ -433,7 +434,7 @@
             *[jax.ShapeDtypeStruct(shape, FLOAT) for shape in running],
         ],
         input_output_aliases=aliases,
-        compiler_params=pltpu.CompilerParams(vmem_limit_bytes=SCAN_BYTES),
+        compiler_params=pltpu.CompilerParams(vmem_limit_bytes=ALONE_BYTES),
         cost_estimate=scan_cost(tokens, channels, 2),
         name="scan_backward",
     )(*operands)
@@ -619,34 +620,37 @@
     return [(low, min(low + tile, width)) for low in range(0, width, tile)]
 
 
-def spread_kernel(mask, count, left_ref, right_ref, chosen_ref, *rest):
-    weights, (out_ref, narrow_ref, out_tile, narrow, sems) = rest[:count], rest[-5:]
-    rows = left_ref.shape[0]
+def spread_kernel(masks, count, chosen_ref, *rest):
+    halves, weights = rest[: 2 * len(masks)], rest[2 * len(masks) : 2 * len(masks) + count]
+    out_ref, narrow_ref, out_tile, narrow, sems = rest[-5:]
+    rows = halves[0].shape[0]
     shards = weights[0].shape[0]
     depth = shards // HALVES
-    start = pl.multiple_of((lax.axis_index("col") ^ mask) * rows, rows)
-    here = pl.ds(start, rows)
-
-    def through(ref, low, high):
-        return dot(left_ref[...], matrix_rows(ref[:depth, :rows, low:high]), (1, 0)) + dot(
-            right_ref[...], matrix_rows(ref[depth:, :rows, low:high]), (1, 0)
-        )
-
     lower = weights[-1].shape[2] - LANES
-    narrow[...] = (chosen_ref[here, :] * through(weights[-1], lower, lower + LANES)).astype(BFLOAT)
-    copies = [pltpu.make_async_copy(narrow, narrow_ref.at[here, :], sems.at[0])]
-    copies[0].start()
-    column = 0
-    for ref in weights:
-        for low, high in cut_tiles(ref.shape[2] - (LANES if ref is weights[-1] else 0), DENSE_TILE):
-            span = slice(column, column + high - low)
-            column += high - low
-            raised = matrix_rows(ref[:, rows : rows + NADAPT * RANK // shards, low:high])
-            out_tile[:, span] = (through(ref, low, high) + dot(narrow[...], raised, (1, 0))).astype(BFLOAT)
-            copies.append(
-                pltpu.make_async_copy(out_tile.at[:, span], out_ref.at[here, span], sems.at[len(copies)])
+    copies = []
+    for at, mask in enumerate(masks):
+        left_ref, right_ref = halves[2 * at : 2 * at + 2]
+        here = pl.ds(pl.multiple_of((lax.axis_index("col") ^ mask) * rows, rows), rows)
+
+        def through(ref, low, high):
+            return dot(left_ref[...], matrix_rows(ref[:depth, :rows, low:high]), (1, 0)) + dot(
+                right_ref[...], matrix_rows(ref[depth:, :rows, low:high]), (1, 0)
             )
+
+        def send(tile, target):
+            copies.append(pltpu.make_async_copy(tile, target, sems.at[len(copies)]))
             copies[-1].start()
+
+        narrow[at] = (chosen_ref[here, :] * through(weights[-1], lower, lower + LANES)).astype(BFLOAT)
+        send(narrow.at[at], narrow_ref.at[here, :])
+        column = 0
+        for ref in weights:
+            for low, high in cut_tiles(ref.shape[2] - (LANES if ref is weights[-1] else 0), DENSE_TILE):
+                span = slice(column, column + high - low)
+                column += high - low
+                raised = matrix_rows(ref[:, rows : rows + NADAPT * RANK // shards, low:high])
+                out_tile[at, :, span] = (through(ref, low, high) + dot(narrow[at], raised, (1, 0))).astype(BFLOAT)
+                send(out_tile.at[at, :, span], out_ref.at[here, span])
     for copy in copies:
         copy.wait()
 
@@ -655,21 +659,22 @@
     return sum(part.shape[2] for part in gathered) - LANES
 
 
-def spread_block(mask, halves, gathered, selector, held):
-    rows, half = halves[0].shape
+def spread_blocks(blocks, gathered, selector, held):
+    masks = [mask for mask, _ in blocks]
+    rows, half = blocks[0][1][0].shape
     width = weights_width(gathered)
     total = selector.shape[0]
     fast, free = pl.BlockSpec(memory_space=pltpu.VMEM), pl.BlockSpec(memory_space=pl.ANY)
-    operands = [*halves, selector, *gathered]
+    operands = [selector, *[part for _, halves in blocks for part in halves], *gathered]
     in_specs = [fast] * len(operands)
     aliases = {}
     if held is not None:
         aliases = {len(operands): 0, len(operands) + 1: 1}
         operands += list(held)
         in_specs += [free] * 2
-    copies = 1 + sum(-(-part.shape[2] // DENSE_TILE) for part in gathered)
+    copies = len(masks) * (1 + sum(-(-part.shape[2] // DENSE_TILE) for part in gathered))
     return pl.pallas_call(
-        functools.partial(spread_kernel, mask, len(gathered)),
+        functools.partial(spread_kernel, masks, len(gathered)),
         in_specs=in_specs,
         out_specs=[free] * 2,
         out_shape=[
@@ -677,16 +682,18 @@
             jax.ShapeDtypeStruct((total, LANES), BFLOAT),
         ],
         scratch_shapes=[
-            pltpu.VMEM((rows, width), BFLOAT),
-            pltpu.VMEM((rows, LANES), BFLOAT),
+            pltpu.VMEM((len(masks), rows, width), BFLOAT),
+            pltpu.VMEM((len(masks), rows, LANES), BFLOAT),
             pltpu.SemaphoreType.DMA((copies,)),
         ],
         input_output_aliases=aliases,
         compiler_params=pltpu.CompilerParams(vmem_limit_bytes=DENSE_BYTES),
         cost_estimate=estimate(
-            flops=4 * rows * half * (width + LANES), bytes_accessed=2 * rows * (2 * half + width), transcendentals=0
+            flops=4 * len(masks) * rows * half * (width + LANES),
+            bytes_accessed=2 * len(masks) * rows * (2 * half + width),
+            transcendentals=0,
         ),
-        name="spread_block",
+        name="spread_blocks",
     )(*operands)
 
 
@@ -997,12 +1004,12 @@
     left, right = halves
     far_left, near_right = flip(left, 2), flip(right, 1)
     near_left, far_right = flip(left, 1), flip(right, 2)
-    held = spread_block(0, halves, gathered, selector, None)
+    held = spread_blocks([(0, halves)], gathered, selector, None)
     onward_left, onward_right = after_all((far_left, near_right), held[1])
     corner = flip(onward_left, 1), flip(onward_right, 2)
-    held = spread_block(1, (near_left, near_right), gathered, selector, held)
-    held = spread_block(2, (far_left, far_right), gathered, selector, held)
-    return spread_block(3, corner, gathered, selector, held)
+    held = spread_blocks([(1, (near_left, near_right))], gathered, selector, held)
+    held = spread_blocks([(2, (far_left, far_right))], gathered, selector, held)
+    return spread_blocks([(3, corner)], gathered, selector, held)
 
 
 def flip(values, mask):
@@ -1028,8 +1035,8 @@
 
 def spread_gathered(blocks, gathered, selector):
     held = None
-    for mask, values in blocks:
-        held = spread_block(mask, values, gathered, selector, held)
+    for block in blocks:
+        held = spread_blocks([block], gathered, selector, held)
     return held
 
 
@@ -1275,7 +1282,10 @@
             expand_grad(dealt[:, :, model + at * width : model + (at + 1) * width]) for at in range(count)
         ]
 
-    projected, inner_in = (spread_gathered if fast else spread_project)(blocks_one, weights_in, selector)
+    if fast:
+        projected, inner_in = spread_blocks(blocks_one, weights_in, selector, None)
+    else:
+        projected, inner_in = spread_project(blocks_one, weights_in, selector)
 
     sent_grad = product(send_matrix, cotangent).astype(BFLOAT).reshape(devices, peer, model)
     arrived_grad = exchange(after(sent_grad, normed_one[0])).reshape(rows, model)
@@ -1286,7 +1296,11 @@
     mixed_out, scanned, carried = scan_forward(projected, tables, mixed_out)
     hidden, inner_out, *normed_two = collect_project(mixed_out, weights_mix, "forward", own_selector, own_input, gains[1])
     gate_up, inner_feed = spread_project(normed_two, weights_feed, selector)
-    act_grad, narrow_two = spread_project(cut_halves(after(branch_two, projected)), weights_down, selector)
+    branch_halves = cut_halves(after(branch_two, projected))
+    if fast:
+        act_grad, narrow_two = spread_blocks(gather_blocks(branch_halves), weights_down, selector, None)
+    else:
+        act_grad, narrow_two = spread_project(branch_halves, weights_down, selector)
     half_feed = units * UNIT_FF
     gate_part, up_part = gate_up[:, :half_feed].astype(FLOAT), gate_up[:, half_feed:].astype(FLOAT)
     gate = jax.nn.sigmoid(gate_part)
@@ -1347,6 +1361,8 @@
         dealt_out = exchange(payload.reshape(devices, peer, -1))
         scan_part[2] = after(scan_part[2], payload)
         projected_grad = scan_backward(*scan_inputs, 1, 2, scan_part)[0]
+        raise_grad = contract_first(inner_in, projected_grad).astype(BFLOAT)
+        projected_grad = after(projected_grad, raise_grad)
         started_in = collect_send(collect_pieces(projected_grad, weights_in, True))
         kept_in, onward_in = collect_middle(started_in)
     else:
@@ -1374,8 +1390,7 @@
     ]
     early = sum_rows(jnp.concatenate(early_parts, axis=1))
 
-    raise_grad = contract_first(inner_in, after(projected_grad, *onward_in) if fast else projected_grad)
-    late = sum_rows(raise_grad)
+    late = sum_rows(raise_grad if fast else contract_first(inner_in, projected_grad))
 
     if fast:
         payload = collect_end(

time: 660 us -> 664 us (level)
    ppermute x55, waiting for transfers between devices: 118 us -> 163 us  [flip(): return lax.ppermute(values, 'col', [(i, i ^ mask) for i in range(4)])]
    reduce_scatter x2, waiting for transfers between devices: 23.3 us -> 1.97 us  [sum_rows(): lax.psum_scatter(values.astype(BFLOAT), 'row', scatter_dimension=0, tiled...]
    all_to_all x4, waiting for transfers between devices: 40.7 us -> 22.9 us  [local(): lax.all_to_all(values, ALL_AXES, split_axis=0, concat_axis=0, tiled=True)]
    all_gather x4, waiting for transfers between devices: 21.6 us -> 5.63 us  [gather_weight(): return (lax.all_gather(shards[-1], 'row', axis=0),)]
    all_gather x1, waiting for transfers between devices: 12 us -> 24 us  [local(): shared = lax.all_gather(shared_shard, 'row', axis=0)]
    pallas_call x16 -> x10, Pallas kernels: 66.6 us -> 60.4 us  [spread_blocks(): pl.pallas_call(functools.partial(spread_kernel, masks, len(gathered)), in...]
    unnamed x358 -> x362, local copies, waits for them, and re-layouts: 102 us -> 102 us
  transfers between devices with their start and end apart: 66 -> 66, of which waited for: 27 -> 29; matrix products, arithmetic and copies ran while one was open for 9% -> 8% of each run, Pallas kernels for 25% -> 24%
where the time goes in v8:
time: 664 us; the launch traced here: 655 us
  waiting for transfers between devices  218 us (33%)
  Pallas kernels  176 us (27%)
  local copies, waits for them, and re-layouts  124 us (19%)
  starting transfers between devices  82.6 us (12%)
  other arithmetic  22.7 us (3%)
  between operations  17.2 us (3%)
  matrix products  14.9 us (2%)
    ppermute x55, waiting for transfers between devices, flip(): return lax.ppermute(values, 'col', [(i, i ^ mask) for i in range(4)])  163 us
    unnamed x362, local copies, waits for them, and re-layouts  102 us
    ppermute x55, starting transfers between devices, flip(): return lax.ppermute(values, 'col', [(i, i ^ mask) for i in range(4)])  62 us
    pallas_call x10, Pallas kernels, spread_blocks(): pl.pallas_call(functools.partial(spread_kernel, masks, len(gathered)), in...  60.4 us
    pallas_call x6, Pallas kernels, collect_blocks(): pl.pallas_call(functools.partial(collect_kernel, masks, len(gathered)), i...  38.2 us
    pallas_call x2, Pallas kernels, scan_backward(): pl.pallas_call(scan_backward_kernel, grid=(blocks // parts,), in_specs=in...  33.8 us
    all_gather x1, waiting for transfers between devices, local(): shared = lax.all_gather(shared_shard, 'row', axis=0)  24 us
    all_to_all x4, waiting for transfers between devices, local(): lax.all_to_all(values, ALL_AXES, split_axis=0, concat_axis=0, tiled=True)  22.9 us
  transfers between devices with their start and end apart: 66, of which 29 were waited for; matrix products, arithmetic and copies ran while one was open for 8% of the time, Pallas kernels for 24%

profile of v8, /device:TPU:0, one launch (start us, length us, event | category | flops | bytes accessed | tf_op | source)
XLA Modules:
  0.0 655.3 jit_solution(6156100761341046390)
XLA Ops:
  18.6 7.3 %all-to-all-start = ((bf16[32,8,2176]{2,1,0:T(8,128)(2,1)}), bf16[32,8,2176]{2,1,0:T(8,128)(2,1)S(1)}, u32[]{:S(2)}, u32[]{:S(2)}) async-start(bf16[32,8,2176]{2,1,0:T(8,128)(2,1)} %bitcast.184), calls=%async_computation | async-start | bytes 2228224 | tf_op jit(solution)/shard_map/all_to_all | solution.py:1156
  26.0 24.0 %all-gather.11.cloned.1.call-done = bf16[2304,256]{1,0:T(8,128)(2,1)} async-done(((bf16[288,256]{1,0:T(8,128)(2,1)}), bf16[2304,256]{1,0:T(8,128)(2,1)}) %all-gather.11.cloned.1.call-update) | async-done | bytes 1179664 | tf_op jit(solution)/shard_map/all_gather | solution.py:1181
  55.3 6.6 %all-to-all-done = bf16[32,8,2176]{2,1,0:T(8,128)(2,1)S(1)} async-done(((bf16[32,8,2176]{2,1,0:T(8,128)(2,1)}), bf16[32,8,2176]{2,1,0:T(8,128)(2,1)S(1)}, u32[]{:S(2)}, u32[]{:S(2)}) %all-to-all-start) | async-done | bytes 1114144 | tf_op jit(solution)/shard_map/all_to_all | solution.py:1156
  61.9 18.6 %collective-permute-done.1 = bf16[8,288,256]{2,1,0:T(8,128)(2,1)} collective-permute-done((bf16[8,288,256]{2,1,0:T(8,128)(2,1)}, bf16[8,288,256]{2,1,0:T(8,128)(2,1)}, u32[]{:S(2)}, u32[]{:S(2)}) %collective-permute-start.1) | collective-permute-done | bytes 1179680 | tf_op jit(solution)/shard_map/ppermute | solution.py:1016
  100.3 14.0 %collective-permute-done.3.rest_3_ = bf16[256,1024]{1,0:T(8,128)(2,1)S(1)} collective-permute-done((bf16[256,1024]{1,0:T(8,128)(2,1)S(1)}, bf16[256,1024]{1,0:T(8,128)(2,1)S(1)}, u32[]{:S(2)}, u32[]{:S(2)}) %collective-permute-start.3) | collective-permute-done | bytes 524320 | tf_op jit(solution)/shard_map/ppermute | solution.py:1016
  114.8 12.1 %collective-permute-done.4.rest_4_ = bf16[256,1024]{1,0:T(8,128)(2,1)S(1)} collective-permute-done((bf16[256,1024]{1,0:T(8,128)(2,1)S(1)}, bf16[256,1024]{1,0:T(8,128)(2,1)S(1)}, u32[]{:S(2)}, u32[]{:S(2)}) %collective-permute-start.4) | collective-permute-done | bytes 524320 | tf_op jit(solution)/shard_map/ppermute | solution.py:1016
  152.2 26.2 %spread_blocks.10 = (bf16[1024,2688]{1,0:T(8,128)(2,1)S(1)}, bf16[1024,128]{1,0:T(8,128)(2,1)S(1)}) custom-call(f32[1024,128]{1,0:T(8,128)S(1)} %compare_convert_fusion.chosen_ref, bf16[256,1024]{1,0:T(8,128)(2,1)S(1)} %get-tuple-element.132.rest_0_.refs_4_, bf16[256,1024]{1,0:T(8,128)(2,1)S(1)} %copy-done.49, bf16[256,1024]{1,0:T(8,128)(2,1)S(1)} %copy-done.104, ...), custom_call_target="tpu_custom_call" | custom-call | flops 738197504 | bytes 606208 | tf_op jit(solution)/shard_map/spread_blocks/pallas_call | solution.py:676
  200.7 12.9 %scan_forward.1 = (bf16[1024,1024]{1,0:T(8,128)(2,1)S(1)}, f32[1024,768]{1,0:T(8,128)S(1)}, bf16[4,256,768]{2,1,0:T(8,128)(2,1)S(1)}) custom-call(bf16[1024,2688]{1,0:T(8,128)(2,1)S(1)} %copy-done.3, bf16[1024,2688]{1,0:T(8,128)(2,1)S(1)} %copy-done.3, bf16[1024,2688]{1,0:T(8,128)(2,1)S(1)} %copy-done.3, ...), custom_call_target="tpu_custom_call", output_to_operand_aliasing={{0}: (12, {})} | custom-call | flops 83886080 | bytes 589824 | tf_op jit(solution)/shard_map/scan_forward/pallas_call | solution.py:384
  250.1 18.2 %collective-permute-done.14.second_near = bf16[256,1024]{1,0:T(8,128)(2,1)S(1)} collective-permute-done((bf16[256,1024]{1,0:T(8,128)(2,1)}, bf16[256,1024]{1,0:T(8,128)(2,1)S(1)}, u32[]{:S(2)}, u32[]{:S(2)}) %collective-permute-start.14) | collective-permute-done | bytes 524320 | tf_op jit(solution)/shard_map/ppermute | solution.py:1016
  280.8 8.5 %collective-permute-done.16.rest_0_ = bf16[256,1024]{1,0:T(8,128)(2,1)S(1)} collective-permute-done((bf16[256,1024]{1,0:T(8,128)(2,1)S(1)}, bf16[256,1024]{1,0:T(8,128)(2,1)S(1)}, u32[]{:S(2)}, u32[]{:S(2)}) %collective-permute-start.16) | collective-permute-done | bytes 524320 | tf_op jit(solution)/shard_map/ppermute | solution.py:1016
  291.9 8.7 %collective-permute-done.24.rest_4_ = bf16[256,1024]{1,0:T(8,128)(2,1)} collective-permute-done((bf16[256,1024]{1,0:T(8,128)(2,1)S(1)}, bf16[256,1024]{1,0:T(8,128)(2,1)}, u32[]{:S(2)}, u32[]{:S(2)}) %collective-permute-start.24) | collective-permute-done | bytes 524320 | tf_op jit(solution)/shard_map/ppermute | solution.py:1016
  303.6 8.2 %collective-permute-done.20.rest_1_ = bf16[256,1024]{1,0:T(8,128)(2,1)S(1)} collective-permute-done((bf16[256,1024]{1,0:T(8,128)(2,1)S(1)}, bf16[256,1024]{1,0:T(8,128)(2,1)S(1)}, u32[]{:S(2)}, u32[]{:S(2)}) %collective-permute-start.20) | collective-permute-done | bytes 524320 | tf_op jit(solution)/shard_map/ppermute | solution.py:1016
  351.0 9.8 %spread_blocks.15 = (bf16[1024,1024]{1,0:T(8,128)(2,1)S(1)}, bf16[1024,128]{1,0:T(8,128)(2,1)S(1)}) custom-call(f32[1024,128]{1,0:T(8,128)S(1)} %compare_convert_fusion.chosen_ref, bf16[256,1024]{1,0:T(8,128)(2,1)S(1)} %get-tuple-element.314.rest_0_, bf16[256,1024]{1,0:T(8,128)(2,1)S(1)} %get-tuple-element.313.rest_1_, ...), custom_call_target="tpu_custom_call" | custom-call | flops 301989888 | bytes 393216 | tf_op jit(solution)/shard_map/spread_blocks/pallas_call | solution.py:676
  373.5 8.3 %collect_blocks.10 = (bf16[256,1152]{1,0:T(8,128)(2,1)}, f32[256,1024]{1,0:T(8,128)S(1)}, f32[256,1152]{1,0:T(8,128)S(1)}, bf16[256,1024]{1,0:T(8,128)(2,1)}, f3...) custom-call(bf16[1024,2048]{1,0:T(8,128)(2,1)S(1)} %pad_maximum_fusion.values_ref, bf16[8,272,2176]{2,1,0:T(8,128)(2,1)S(1)} %bitcast.165), custom_call_target="tpu_custom_call" | custom-call | flops 402653184 | bytes 589824 | tf_op jit(solution)/shard_map/collect_blocks/pallas_call | solution.py:741
  406.0 8.5 %collective-permute-done.30.first_near = bf16[256,1152]{1,0:T(8,128)(2,1)} collective-permute-done((bf16[256,1152]{1,0:T(8,128)(2,1)}, bf16[256,1152]{1,0:T(8,128)(2,1)}, u32[]{:S(2)}, u32[]{:S(2)}) %collective-permute-start.30) | collective-permute-done | bytes 589856 | tf_op jit(solution)/shard_map/ppermute | solution.py:1016
  424.4 8.8 %collective-permute-done.34.rest_0_ = bf16[256,1024]{1,0:T(8,128)(2,1)S(1)} collective-permute-done((bf16[256,1024]{1,0:T(8,128)(2,1)S(1)}, bf16[256,1024]{1,0:T(8,128)(2,1)S(1)}, u32[]{:S(2)}, u32[]{:S(2)}) %collective-permute-start.34) | collective-permute-done | bytes 524320 | tf_op jit(solution)/shard_map/ppermute | solution.py:1016
  438.0 7.0 %collective-permute-done.39.rest_0_ = bf16[256,1024]{1,0:T(8,128)(2,1)S(1)} collective-permute-done((bf16[256,1024]{1,0:T(8,128)(2,1)S(1)}, bf16[256,1024]{1,0:T(8,128)(2,1)S(1)}, u32[]{:S(2)}, u32[]{:S(2)}) %collective-permute-start.39) | collective-permute-done | bytes 524320 | tf_op jit(solution)/shard_map/ppermute | solution.py:1016
  464.5 7.2 %attention_backward.1 = (bf16[1024,256]{1,0:T(8,128)(2,1)S(1)}, bf16[1024,256]{1,0:T(8,128)(2,1)S(1)}) custom-call(bf16[1024,2688]{1,0:T(8,128)(2,1)S(1)} %copy-done.4, bf16[1024,2688]{1,0:T(8,128)(2,1)S(1)} %copy-done.4, bf16[1024,2688]{1,0:T(8,128)(2,1)S(1)} %copy-done.4, f32[1024,128]{1,0:T(8,128)S(1)} %copy-done.43, f32[1024,128]{1,0:T(8,128)S(1)} %copy-done.41, ...), custom_call_target="tpu_custom_call" | custom-call | flops 100663296 | bytes 393216 | tf_op jit(solution)/shard_map/attention_backward/pallas_call | solution.py:557
  479.3 16.7 %scan_backward.2 = (bf16[1024,2688]{1,0:T(8,128)(2,1)}, f32[256,768]{1,0:T(8,128)}, f32[8,768]{1,0:T(8,128)}, f32[8,512]{1,0:T(8,128)}) custom-call(bf16[1024,2688]{1,0:T(8,128)(2,1)} %copy-done.2, bf16[1024,2688]{1,0:T(8,128)(2,1)} %copy-done.2, bf16[1024,2688]{1,0:T(8,128)(2,1)} %copy-done.2, bf16[1024,2688]{1,0:T(8,128)(2,1)} %copy-done.2, ...), custom_call_target="tpu_custom_call" | custom-call | flops 167772160 | bytes 1179648 | tf_op jit(solution)/shard_map/scan_backward/pallas_call | solution.py:427
  504.4 17.1 %scan_backward.3 = (bf16[1024,2688]{1,0:T(8,128)(2,1)}, f32[256,768]{1,0:T(8,128)}, f32[8,768]{1,0:T(8,128)}, f32[8,512]{1,0:T(8,128)}) custom-call(bf16[1024,2688]{1,0:T(8,128)(2,1)} %copy-done.2, bf16[1024,2688]{1,0:T(8,128)(2,1)} %copy-done.2, bf16[1024,2688]{1,0:T(8,128)(2,1)} %copy-done.2, ...), custom_call_target="tpu_custom_call", output_to_operand_aliasing={{0}: (17, {})} | custom-call | flops 167772160 | bytes 1179648 | tf_op jit(solution)/shard_map/scan_backward/pallas_call | solution.py:427
  533.9 14.2 %collect_blocks.11 = (bf16[256,1152]{1,0:T(8,128)(2,1)S(1)}, bf16[256,1024]{1,0:T(8,128)(2,1)S(1)}, bf16[256,1152]{1,0:T(8,128)(2,1)}, f32[256,1024]{1,0:T(8,128...) custom-call(bf16[1024,2688]{1,0:T(8,128)(2,1)S(1)} %copy-done.17, ...), custom_call_target="tpu_custom_call" | custom-call | flops 704643072 | bytes 868352 | tf_op jit(solution)/shard_map/collect_blocks/pallas_call | solution.py:741
  555.1 12.2 %collective-permute-done.47.second_part = bf16[256,1024]{1,0:T(8,128)(2,1)S(1)} collective-permute-done((bf16[256,1024]{1,0:T(8,128)(2,1)S(1)}, bf16[256,1024]{1,0:T(8,128)(2,1)S(1)}, u32[]{:S(2)}, u32[]{:S(2)}) %collective-permute-start.47) | collective-permute-done | bytes 524320 | tf_op jit(solution)/shard_map/ppermute | solution.py:1016
  586.9 13.0 %collective-permute-done.50.second_near = bf16[256,1024]{1,0:T(8,128)(2,1)} collective-permute-done((bf16[256,1024]{1,0:T(8,128)(2,1)}, bf16[256,1024]{1,0:T(8,128)(2,1)}, u32[]{:S(2)}, u32[]{:S(2)}) %collective-permute-start.50) | collective-permute-done | bytes 524320 | tf_op jit(solution)/shard_map/ppermute | solution.py:1016
  629.3 16.2 %all-to-all-done.3 = bf16[32,8,2304]{2,1,0:T(8,128)(2,1)S(1)} async-done(((bf16[32,8,2304]{2,1,0:T(8,128)(2,1)}), bf16[32,8,2304]{2,1,0:T(8,128)(2,1)S(1)}, u32[]{:S(2)}, u32[]{:S(2)}) %all-to-all-start.3) | async-done | bytes 1179680 | tf_op jit(solution)/shard_map/all_to_all | solution.py:1156
  (638 shorter events, 333.7 us)
Async XLA Ops:
  7.2 42.7 %all-gather.11.cloned.1.call-start = ((), (), s32[]{:S(2)}) async-start(), calls=%async_computation.8 | async-start | bytes 1327104 | tf_op jit(solution)/shard_map/all_gather | solution.py:1181
  14.6 126.7 %all-gather.13.cloned.1.call-start = ((), (), s32[]{:S(2)}) async-start(), calls=%async_computation.9 | async-start | bytes 10027008 | tf_op jit(solution)/shard_map/all_gather | solution.py:1166
  16.7 200.9 %all-gather.15.cloned.1.call-start = ((), (), s32[]{:S(2)}) async-start(), calls=%async_computation.10 | async-start | bytes 5640192 | tf_op jit(solution)/shard_map/all_gather | solution.py:1166
  18.6 43.3 %all-to-all-start = ((bf16[32,8,2176]{2,1,0:T(8,128)(2,1)}), bf16[32,8,2176]{2,1,0:T(8,128)(2,1)S(1)}, u32[]{:S(2)}, u32[]{:S(2)}) async-start(bf16[32,8,2176]{2,1,0:T(8,128)(2,1)} %bitcast.184), calls=%async_computation | async-start | bytes 2228224 | tf_op jit(solution)/shard_map/all_to_all | solution.py:1156
  25.9 288.5 %all-gather.17.cloned.1.call-start = ((), (), s32[]{:S(2)}) async-start(), calls=%async_computation.11 | async-start | bytes 10653696 | tf_op jit(solution)/shard_map/all_gather | solution.py:1166
  49.9 30.7 %collective-permute-start.1 = (bf16[8,288,256]{2,1,0:T(8,128)(2,1)}, bf16[8,288,256]{2,1,0:T(8,128)(2,1)}, u32[]{:S(2)}, u32[]{:S(2)}) collective-permute-start(bf16[8,288,256]{2,1,0:T(8,128)(2,1)} %bitcast.186), channel_id=1, source_target_pairs={{0,2},{1,3},{2,0},{3,1},{4,6},{5,7},{6,4},{7,5},{8,10},{9,11},{10,... | collective-permute-start | bytes 3538952 | tf_op jit(solution)/shard_map/ppermute | solution.py:1016
  50.9 30.7 %collective-permute-start = (bf16[8,288,256]{2,1,0:T(8,128)(2,1)}, bf16[8,288,256]{2,1,0:T(8,128)(2,1)}, u32[]{:S(2)}, u32[]{:S(2)}) collective-permute-start(bf16[8,288,256]{2,1,0:T(8,128)(2,1)} %bitcast.187), channel_id=1, source_target_pairs={{0,1},{1,0},{2,3},{3,2},{4,5},{5,4},{6,7},{7,6},{8,9},{9,8},{10,11... | collective-permute-start | bytes 3538952 | tf_op jit(solution)/shard_map/ppermute | solution.py:1016
  84.0 264.6 %all-gather.19.cloned.1.call-start = ((), (), s32[]{:S(2)}) async-start(), calls=%async_computation.12 | async-start | bytes 5640192 | tf_op jit(solution)/shard_map/all_gather | solution.py:1166
  88.2 40.3 %collective-permute-start.9 = (bf16[4,288,256]{2,1,0:T(8,128)(2,1)S(1)}, bf16[4,288,256]{2,1,0:T(8,128)(2,1)S(1)}, u32[]{:S(2)}, u32[]{:S(2)}) collective-permute-start(bf16[4,288,256]{2,1,0:T(8,128)(2,1)S(1)} %slice.489), channel_id=1, source_target_pairs={{0,1},{1,0},{2,3},{3,2},{4,5},{5,4},{6,7},{7,6},{8,9},{9,8},{10,11... | collective-permute-start | bytes 1769480 | tf_op jit(solution)/shard_map/ppermute | solution.py:1016
  90.3 38.5 %collective-permute-start.8 = (bf16[4,288,256]{2,1,0:T(8,128)(2,1)S(1)}, bf16[4,288,256]{2,1,0:T(8,128)(2,1)S(1)}, u32[]{:S(2)}, u32[]{:S(2)}) collective-permute-start(bf16[4,288,256]{2,1,0:T(8,128)(2,1)S(1)} %slice.488), channel_id=1, source_target_pairs={{0,2},{1,3},{2,0},{3,1},{4,6},{5,7},{6,4},{7,5},{8,10},{9,11},{10,... | collective-permute-start | bytes 1769480 | tf_op jit(solution)/shard_map/ppermute | solution.py:1016
  94.9 38.1 %collective-permute-start.5 = (bf16[256,1024]{1,0:T(8,128)(2,1)S(1)}, bf16[256,1024]{1,0:T(8,128)(2,1)S(1)}, u32[]{:S(2)}, u32[]{:S(2)}) collective-permute-start(bf16[256,1024]{1,0:T(8,128)(2,1)S(1)} %get-tuple-element.133.rest_1_.refs_5_), channel_id=1, source_target_pairs={{0,2},{1,3},{2,0},{3,1},{4,6},{5,7},{6,4},{7,5},{8,10},{9,11},{10,... | collective-permute-start | bytes 1572872 | tf_op jit(solution)/shard_map/ppermute | solution.py:1016
  184.9 60.1 %all-to-all-start.1 = ((bf16[32,8,2048]{2,1,0:T(8,128)(2,1)}), bf16[32,8,2048]{2,1,0:T(8,128)(2,1)}, u32[]{:S(2)}, u32[]{:S(2)}) async-start(bf16[32,8,2048]{2,1,0:T(8,128)(2,1)} %fusion.9), calls=%async_computation.1 | async-start | bytes 2097152 | tf_op jit(solution)/shard_map/all_to_all | solution.py:1156
  189.7 392.1 %reduce-scatter.3.cloned.1.call-start = ((), (), s32[]{:S(2)}) async-start(), calls=%async_computation.6 | async-start | bytes 1179648 | tf_op jit(solution)/shard_map/reduce_scatter | solution.py:1384
  248.4 30.1 %collective-permute-start.23 = (bf16[256,1024]{1,0:T(8,128)(2,1)S(1)}, bf16[256,1024]{1,0:T(8,128)(2,1)}, u32[]{:S(2)}, u32[]{:S(2)}) collective-permute-start(bf16[256,1024]{1,0:T(8,128)(2,1)S(1)} %get-tuple-element.313.rest_1_), channel_id=1, source_target_pairs={{0,1},{1,0},{2,3},{3,2},{4,5},{5,4},{6,7},{7,6},{8,9},{9,8},{10,11... | collective-permute-start | bytes 1572872 | tf_op jit(solution)/shard_map/ppermute | solution.py:1016
  278.5 33.3 %collective-permute-start.20 = (bf16[256,1024]{1,0:T(8,128)(2,1)S(1)}, bf16[256,1024]{1,0:T(8,128)(2,1)S(1)}, u32[]{:S(2)}, u32[]{:S(2)}) collective-permute-start(bf16[256,1024]{1,0:T(8,128)(2,1)S(1)} %get-tuple-element.152.rest_1_.refs_5_), channel_id=1, source_target_pairs={{0,2},{1,3},{2,0},{3,1},{4,6},{5,7},{6,4},{7,5},{8,10},{9,11},{10,... | collective-permute-start | bytes 1572872 | tf_op jit(solution)/shard_map/ppermute | solution.py:1016
  290.9 40.2 %collective-permute-start.19 = (bf16[256,1024]{1,0:T(8,128)(2,1)}, bf16[256,1024]{1,0:T(8,128)(2,1)}, u32[]{:S(2)}, u32[]{:S(2)}) collective-permute-start(bf16[256,1024]{1,0:T(8,128)(2,1)} %collective-permute-done.18.rest_1_), channel_id=1, source_target_pairs={{0,2},{1,3},{2,0},{3,1},{4,6},{5,7},{6,4},{7,5},{8,10},{9,11},{10,... | collective-permute-start | bytes 1572872 | tf_op jit(solution)/shard_map/ppermute | solution.py:1016
  300.7 36.9 %collective-permute-start.25 = (bf16[256,1024]{1,0:T(8,128)(2,1)S(1)}, bf16[256,1024]{1,0:T(8,128)(2,1)}, u32[]{:S(2)}, u32[]{:S(2)}) collective-permute-start(bf16[256,1024]{1,0:T(8,128)(2,1)S(1)} %get-tuple-element.313.rest_1_), channel_id=1, source_target_pairs={{0,2},{1,3},{2,0},{3,1},{4,6},{5,7},{6,4},{7,5},{8,10},{9,11},{10,... | collective-permute-start | bytes 1572872 | tf_op jit(solution)/shard_map/ppermute | solution.py:1016
  303.0 34.6 %collective-permute-start.22 = (bf16[256,1024]{1,0:T(8,128)(2,1)S(1)}, bf16[256,1024]{1,0:T(8,128)(2,1)}, u32[]{:S(2)}, u32[]{:S(2)}) collective-permute-start(bf16[256,1024]{1,0:T(8,128)(2,1)S(1)} %get-tuple-element.314.rest_0_), channel_id=1, source_target_pairs={{0,1},{1,0},{2,3},{3,2},{4,5},{5,4},{6,7},{7,6},{8,9},{9,8},{10,11... | collective-permute-start | bytes 1572872 | tf_op jit(solution)/shard_map/ppermute | solution.py:1016
  312.6 30.4 %collective-permute-start.27 = (bf16[256,1024]{1,0:T(8,128)(2,1)}, bf16[256,1024]{1,0:T(8,128)(2,1)}, u32[]{:S(2)}, u32[]{:S(2)}) collective-permute-start(bf16[256,1024]{1,0:T(8,128)(2,1)} %collective-permute-done.23.rest_3_), channel_id=1, source_target_pairs={{0,2},{1,3},{2,0},{3,1},{4,6},{5,7},{6,4},{7,5},{8,10},{9,11},{10,... | collective-permute-start | bytes 1572872 | tf_op jit(solution)/shard_map/ppermute | solution.py:1016
  460.2 37.1 %collective-permute-start.40 = (bf16[256,1152]{1,0:T(8,128)(2,1)}, bf16[256,1152]{1,0:T(8,128)(2,1)}, u32[]{:S(2)}, u32[]{:S(2)}) collective-permute-start(bf16[256,1152]{1,0:T(8,128)(2,1)} %copy-done.131), channel_id=1, source_target_pairs={{0,1},{1,0},{2,3},{3,2},{4,5},{5,4},{6,7},{7,6},{8,9},{9,8},{10,11... | collective-permute-start | bytes 1769480 | tf_op jit(solution)/shard_map/ppermute | solution.py:1016
  500.9 86.0 %all-to-all-start.2 = ((bf16[32,8,2816]{2,1,0:T(8,128)(2,1)}), bf16[32,8,2816]{2,1,0:T(8,128)(2,1)}, u32[]{:S(2)}, u32[]{:S(2)}) async-start(bf16[32,8,2816]{2,1,0:T(8,128)(2,1)} %bitcast.40), calls=%async_computation.2 | async-start | bytes 2883584 | tf_op jit(solution)/shard_map/all_to_all | solution.py:1156
  504.3 81.0 %reduce-scatter.5.cloned.1.call-start = ((), (), s32[]{:S(2)}) async-start(), calls=%async_computation.7 | async-start | bytes 774144 | tf_op jit(solution)/shard_map/reduce_scatter | solution.py:1384
  568.2 31.6 %collective-permute-start.48 = (bf16[256,1152]{1,0:T(8,128)(2,1)}, bf16[256,1152]{1,0:T(8,128)(2,1)}, u32[]{:S(2)}, u32[]{:S(2)}) collective-permute-start(bf16[256,1152]{1,0:T(8,128)(2,1)} %get-tuple-element.234), channel_id=1, source_target_pairs={{0,1},{1,0},{2,3},{3,2},{4,5},{5,4},{6,7},{7,6},{8,9},{9,8},{10,11... | collective-permute-start | bytes 1769480 | tf_op jit(solution)/shard_map/ppermute | solution.py:1016
  611.6 33.9 %all-to-all-start.3 = ((bf16[32,8,2304]{2,1,0:T(8,128)(2,1)}), bf16[32,8,2304]{2,1,0:T(8,128)(2,1)S(1)}, u32[]{:S(2)}, u32[]{:S(2)}) async-start(bf16[32,8,2304]{2,1,0:T(8,128)(2,1)} %bitcast.181), calls=%async_computation.5 | async-start | bytes 2359296 | tf_op jit(solution)/shard_map/all_to_all | solution.py:1156
  (210 other events, 3029.0 us)
Sparse Core Ops, SparseCore 0:
  14.7 35.1 all-gather.10
  51.6 87.9 all-gather.12
  141.8 52.6 all-gather.14
  196.0 97.8 all-gather.16
  295.4 53.1 all-gather.18
  460.4 29.5 reduce-scatter.2
  553.7 31.5 reduce-scatter.4

commit v9 on v8

--- a/solution.py
+++ b/solution.py
@@ -65,7 +65,6 @@
 
 ESTIMATE = 16
 SCAN_BYTES = 32 * 1024 * 1024
-ALONE_BYTES = 56 * 1024 * 1024
 DENSE_BYTES = 16 * 1024 * 1024
 FINISH_BYTES = 32 * 1024 * 1024
 LANES = 128
@@ -434,7 +433,7 @@
             *[jax.ShapeDtypeStruct(shape, FLOAT) for shape in running],
         ],
         input_output_aliases=aliases,
-        compiler_params=pltpu.CompilerParams(vmem_limit_bytes=ALONE_BYTES),
+        compiler_params=pltpu.CompilerParams(vmem_limit_bytes=SCAN_BYTES),
         cost_estimate=scan_cost(tokens, channels, 2),
         name="scan_backward",
     )(*operands)
@@ -620,14 +619,23 @@
     return [(low, min(low + tile, width)) for low in range(0, width, tile)]
 
 
-def spread_kernel(masks, count, chosen_ref, *rest):
+def spread_kernel(masks, count, times, chosen_ref, *rest):
     halves, weights = rest[: 2 * len(masks)], rest[2 * len(masks) : 2 * len(masks) + count]
-    out_ref, narrow_ref, out_tile, narrow, sems = rest[-5:]
+    factors = rest[2 * len(masks) + count : 2 * len(masks) + count + times]
+    out_ref, narrow_ref, out_tile, narrow, sems, factor_tile, factor_sems = rest[-7:]
     rows = halves[0].shape[0]
     shards = weights[0].shape[0]
     depth = shards // HALVES
     lower = weights[-1].shape[2] - LANES
     copies = []
+    fetches = []
+    for at, mask in enumerate(masks):
+        here = pl.ds(pl.multiple_of((lax.axis_index("col") ^ mask) * rows, rows), rows)
+        for place, factor in enumerate(factors):
+            fetches.append(
+                pltpu.make_async_copy(factor.at[here, :], factor_tile.at[at, place], factor_sems.at[at, place])
+            )
+            fetches[-1].start()
     for at, mask in enumerate(masks):
         left_ref, right_ref = halves[2 * at : 2 * at + 2]
         here = pl.ds(pl.multiple_of((lax.axis_index("col") ^ mask) * rows, rows), rows)
@@ -649,8 +657,17 @@
                 span = slice(column, column + high - low)
                 column += high - low
                 raised = matrix_rows(ref[:, rows : rows + NADAPT * RANK // shards, low:high])
-                out_tile[at, :, span] = (through(ref, low, high) + dot(narrow[at], raised, (1, 0))).astype(BFLOAT)
-                send(out_tile.at[at, :, span], out_ref.at[here, span])
+                result = (through(ref, low, high) + dot(narrow[at], raised, (1, 0))).astype(BFLOAT)
+                if not factors:
+                    out_tile[at, :, span] = result
+                    send(out_tile.at[at, :, span], out_ref.at[here, span])
+                for place, factor in enumerate(factors):
+                    if low == 0:
+                        fetches[at * times + place].wait()
+                    shift = place * factor.shape[1]
+                    wide = slice(span.start + shift, span.stop + shift)
+                    out_tile[at, :, wide] = (result.astype(FLOAT) * factor_tile[at, place, :, span]).astype(BFLOAT)
+                    send(out_tile.at[at, :, wide], out_ref.at[here, wide])
     for copy in copies:
         copy.wait()
 
@@ -659,35 +676,40 @@
     return sum(part.shape[2] for part in gathered) - LANES
 
 
-def spread_blocks(blocks, gathered, selector, held):
+def spread_blocks(blocks, gathered, selector, held, factors=()):
     masks = [mask for mask, _ in blocks]
     rows, half = blocks[0][1][0].shape
     width = weights_width(gathered)
     total = selector.shape[0]
     fast, free = pl.BlockSpec(memory_space=pltpu.VMEM), pl.BlockSpec(memory_space=pl.ANY)
     operands = [selector, *[part for _, halves in blocks for part in halves], *gathered]
-    in_specs = [fast] * len(operands)
+    wide = width * max(len(factors), 1)
+    in_specs = [fast] * len(operands) + [free] * len(factors)
+    operands += list(factors)
     aliases = {}
     if held is not None:
         aliases = {len(operands): 0, len(operands) + 1: 1}
         operands += list(held)
         in_specs += [free] * 2
-    copies = len(masks) * (1 + sum(-(-part.shape[2] // DENSE_TILE) for part in gathered))
+    tiles = sum(-(-part.shape[2] // DENSE_TILE) for part in gathered)
+    copies = len(masks) * (1 + tiles * max(len(factors), 1))
     return pl.pallas_call(
-        functools.partial(spread_kernel, masks, len(gathered)),
+        functools.partial(spread_kernel, masks, len(gathered), len(factors)),
         in_specs=in_specs,
         out_specs=[free] * 2,
         out_shape=[
-            jax.ShapeDtypeStruct((total, width), BFLOAT),
+            jax.ShapeDtypeStruct((total, wide), BFLOAT),
             jax.ShapeDtypeStruct((total, LANES), BFLOAT),
         ],
         scratch_shapes=[
-            pltpu.VMEM((len(masks), rows, width), BFLOAT),
+            pltpu.VMEM((len(masks), rows, wide), BFLOAT),
             pltpu.VMEM((len(masks), rows, LANES), BFLOAT),
             pltpu.SemaphoreType.DMA((copies,)),
+            pltpu.VMEM((len(masks), len(factors), rows, width) if factors else (1, 1, 8, LANES), FLOAT),
+            pltpu.SemaphoreType.DMA((len(masks), max(len(factors), 1))),
         ],
         input_output_aliases=aliases,
-        compiler_params=pltpu.CompilerParams(vmem_limit_bytes=DENSE_BYTES),
+        compiler_params=pltpu.CompilerParams(vmem_limit_bytes=FINISH_BYTES if factors else DENSE_BYTES),
         cost_estimate=estimate(
             flops=4 * len(masks) * rows * half * (width + LANES),
             bytes_accessed=2 * len(masks) * rows * (2 * half + width),
@@ -1283,7 +1305,7 @@
         ]
 
     if fast:
-        projected, inner_in = spread_blocks(blocks_one, weights_in, selector, None)
+        projected, inner_in = spread_gathered(blocks_one, weights_in, selector)
     else:
         projected, inner_in = spread_project(blocks_one, weights_in, selector)
 
@@ -1296,20 +1318,21 @@
     mixed_out, scanned, carried = scan_forward(projected, tables, mixed_out)
     hidden, inner_out, *normed_two = collect_project(mixed_out, weights_mix, "forward", own_selector, own_input, gains[1])
     gate_up, inner_feed = spread_project(normed_two, weights_feed, selector)
-    branch_halves = cut_halves(after(branch_two, projected))
-    if fast:
-        act_grad, narrow_two = spread_blocks(gather_blocks(branch_halves), weights_down, selector, None)
-    else:
-        act_grad, narrow_two = spread_project(branch_halves, weights_down, selector)
     half_feed = units * UNIT_FF
     gate_part, up_part = gate_up[:, :half_feed].astype(FLOAT), gate_up[:, half_feed:].astype(FLOAT)
     gate = jax.nn.sigmoid(gate_part)
     silu = gate_part * gate
     activated = (silu * up_part).astype(BFLOAT)
-    wide_grad = act_grad.astype(FLOAT)
-    feed_grad = jnp.concatenate(
-        [wide_grad * up_part * (gate * (1.0 + gate_part * (1.0 - gate))), wide_grad * silu], axis=1
-    ).astype(BFLOAT)
+    slope = up_part * (gate * (1.0 + gate_part * (1.0 - gate)))
+    branch_halves = cut_halves(after(branch_two, projected))
+    if fast:
+        feed_grad, narrow_two = spread_blocks(
+            gather_blocks(branch_halves), weights_down, selector, None, [slope, silu]
+        )
+    else:
+        act_grad, narrow_two = spread_project(branch_halves, weights_down, selector)
+        wide_grad = act_grad.astype(FLOAT)
+        feed_grad = jnp.concatenate([wide_grad * slope, wide_grad * silu], axis=1).astype(BFLOAT)
     choose = (
         jnp.arange(NADAPT * RANK, dtype=jnp.int32)[:, None]
         == (adapters[:, None] * RANK + jnp.arange(RANK, dtype=jnp.int32)[None, :]).reshape(1, -1)
@@ -1363,7 +1386,7 @@
         projected_grad = scan_backward(*scan_inputs, 1, 2, scan_part)[0]
         raise_grad = contract_first(inner_in, projected_grad).astype(BFLOAT)
         projected_grad = after(projected_grad, raise_grad)
-        started_in = collect_send(collect_pieces(projected_grad, weights_in, True))
+        started_in = collect_send(collect_pieces(projected_grad, weights_in, True), False)
         kept_in, onward_in = collect_middle(started_in)
     else:
         block_out, inner_down = collect_project(activated, weights_down, "output", own_selector, hidden)

time: 664 us -> 675 us (1.017)
  local copies, waits for them, and re-layouts: 124 us -> 150 us
  waiting for transfers between devices: 218 us -> 202 us
    ppermute x55, waiting for transfers between devices: 163 us -> 139 us  [flip(): return lax.ppermute(values, 'col', [(i, i ^ mask) for i in range(4)])]
    unnamed x362 -> x346, local copies, waits for them, and re-layouts: 102 us -> 125 us
    all_to_all x4, waiting for transfers between devices: 22.9 us -> 38.1 us  [local(): lax.all_to_all(values, ALL_AXES, split_axis=0, concat_axis=0, tiled=True)]
    all_gather x1, waiting for transfers between devices: 24 us -> 12 us  [local(): shared = lax.all_gather(shared_shard, 'row', axis=0)]
    pallas_call x10 -> x13, Pallas kernels: 60.4 us -> 67.8 us  [spread_blocks(): pl.pallas_call(functools.partial(spread_kernel, masks, len(gathered), len...]
  transfers between devices with their start and end apart: 66 -> 66, of which waited for: 29 -> 28; matrix products, arithmetic and copies ran while one was open for 8% -> 10% of each run, Pallas kernels for 24% -> 23%
where the time goes in v9:
time: 675 us; the launch traced here: 666 us
  waiting for transfers between devices  202 us (30%)
  Pallas kernels  177 us (26%)
  local copies, waits for them, and re-layouts  150 us (22%)
  starting transfers between devices  84.3 us (12%)
  other arithmetic  23.9 us (4%)
  between operations  16.9 us (3%)
  matrix products  12.3 us (2%)
    ppermute x55, waiting for transfers between devices, flip(): return lax.ppermute(values, 'col', [(i, i ^ mask) for i in range(4)])  139 us
    unnamed x346, local copies, waits for them, and re-layouts  125 us
    pallas_call x13, Pallas kernels, spread_blocks(): pl.pallas_call(functools.partial(spread_kernel, masks, len(gathered), len...  67.8 us
    ppermute x55, starting transfers between devices, flip(): return lax.ppermute(values, 'col', [(i, i ^ mask) for i in range(4)])  63.4 us
    all_to_all x4, waiting for transfers between devices, local(): lax.all_to_all(values, ALL_AXES, split_axis=0, concat_axis=0, tiled=True)  38.1 us
    pallas_call x6, Pallas kernels, collect_blocks(): pl.pallas_call(functools.partial(collect_kernel, masks, len(gathered)), i...  37 us
    pallas_call x2, Pallas kernels, scan_backward(): pl.pallas_call(scan_backward_kernel, grid=(blocks // parts,), in_specs=in...  28.7 us
    all_to_all x4, starting transfers between devices, local(): lax.all_to_all(values, ALL_AXES, split_axis=0, concat_axis=0, tiled=True)  20.6 us
  transfers between devices with their start and end apart: 66, of which 28 were waited for; matrix products, arithmetic and copies ran while one was open for 10% of the time, Pallas kernels for 23%

profile of v9, /device:TPU:0, one launch (start us, length us, event | category | flops | bytes accessed | tf_op | source)
XLA Modules:
  0.0 665.6 jit_solution(16458644898650645117)
XLA Ops:
  23.1 7.3 %all-to-all-start = ((bf16[32,8,2176]{2,1,0:T(8,128)(2,1)}), bf16[32,8,2176]{2,1,0:T(8,128)(2,1)S(1)}, u32[]{:S(2)}, u32[]{:S(2)}) async-start(bf16[32,8,2176]{2,1,0:T(8,128)(2,1)} %bitcast.187), calls=%async_computation | async-start | bytes 2228224 | tf_op jit(solution)/shard_map/all_to_all | solution.py:1178
  30.4 12.0 %all-gather.11.cloned.1.call-done = bf16[2304,256]{1,0:T(8,128)(2,1)} async-done(((bf16[288,256]{1,0:T(8,128)(2,1)}), bf16[2304,256]{1,0:T(8,128)(2,1)}) %all-gather.11.cloned.1.call-update) | async-done | bytes 1179664 | tf_op jit(solution)/shard_map/all_gather | solution.py:1203
  48.1 21.9 %all-to-all-done = bf16[32,8,2176]{2,1,0:T(8,128)(2,1)S(1)} async-done(((bf16[32,8,2176]{2,1,0:T(8,128)(2,1)}), bf16[32,8,2176]{2,1,0:T(8,128)(2,1)S(1)}, u32[]{:S(2)}, u32[]{:S(2)}) %all-to-all-start) | async-done | bytes 1114144 | tf_op jit(solution)/shard_map/all_to_all | solution.py:1178
  96.2 12.7 %collective-permute-done.4.rest_1_ = bf16[256,1024]{1,0:T(8,128)(2,1)S(1)} collective-permute-done((bf16[256,1024]{1,0:T(8,128)(2,1)}, bf16[256,1024]{1,0:T(8,128)(2,1)S(1)}, u32[]{:S(2)}, u32[]{:S(2)}) %collective-permute-start.4) | collective-permute-done | bytes 524320 | tf_op jit(solution)/shard_map/ppermute | solution.py:1038
  109.7 12.2 %collective-permute-done.2.rest_0_ = bf16[256,1024]{1,0:T(8,128)(2,1)} collective-permute-done((bf16[256,1024]{1,0:T(8,128)(2,1)}, bf16[256,1024]{1,0:T(8,128)(2,1)}, u32[]{:S(2)}, u32[]{:S(2)}) %collective-permute-start.2) | collective-permute-done | bytes 524320 | tf_op jit(solution)/shard_map/ppermute | solution.py:1038
  139.8 7.5 %spread_blocks.13 = (bf16[1024,2688]{1,0:T(8,128)(2,1)S(1)}, bf16[1024,128]{1,0:T(8,128)(2,1)S(1)}) custom-call(f32[1024,128]{1,0:T(8,128)S(1)} %compare_convert_fusion.chosen_ref, bf16[256,1024]{1,0:T(8,128)(2,1)} %get-tuple-element.136.rest_0_.refs_4_, bf16[256,1024]{1,0:T(8,128)(2,1)} %get-tuple-element.137.rest_1_.refs_5_, ...), custom_call_target="tpu_custom_call" | custom-call | flops 184549376 | bytes 151552 | tf_op jit(solution)/shard_map/spread_blocks/pallas_call | solution.py:696
  147.3 7.1 %spread_blocks.14 = (bf16[1024,2688]{1,0:T(8,128)(2,1)S(1)}, bf16[1024,128]{1,0:T(8,128)(2,1)S(1)}) custom-call(f32[1024,128]{1,0:T(8,128)S(1)} %compare_convert_fusion.chosen_ref, bf16[256,1024]{1,0:T(8,128)(2,1)} %collective-permute-done.9.rest_0_, ...), custom_call_target="tpu_custom_call", output_to_operand_aliasing={{0}: (5, {}), {1}: (6, {})} | custom-call | flops 184549376 | bytes 151552 | tf_op jit(solution)/shard_map/spread_blocks/pallas_call | solution.py:696
  154.4 7.5 %spread_blocks.15 = (bf16[1024,2688]{1,0:T(8,128)(2,1)S(1)}, bf16[1024,128]{1,0:T(8,128)(2,1)S(1)}) custom-call(f32[1024,128]{1,0:T(8,128)S(1)} %compare_convert_fusion.chosen_ref, bf16[256,1024]{1,0:T(8,128)(2,1)} %collective-permute-done.2.rest_0_, ...), custom_call_target="tpu_custom_call", output_to_operand_aliasing={{0}: (5, {}), {1}: (6, {})} | custom-call | flops 184549376 | bytes 151552 | tf_op jit(solution)/shard_map/spread_blocks/pallas_call | solution.py:696
  162.0 7.3 %spread_blocks.16 = (bf16[1024,2688]{1,0:T(8,128)(2,1)S(1)}, bf16[1024,128]{1,0:T(8,128)(2,1)S(1)}) custom-call(f32[1024,128]{1,0:T(8,128)S(1)} %compare_convert_fusion.chosen_ref, bf16[256,1024]{1,0:T(8,128)(2,1)} %collective-permute-done.3.rest_0_, bf16[256,1024]{1,0:T(8,128)(2,1)} %collective-permute-done.5.rest_1_, ...), custom_call_target="tpu_custom_call", output_to_operand_aliasing={{0}: (5, {}), {1}: (6, {})} | custom-call | flops 184549376 | bytes 151552 | tf_op jit(solution)/shard_map/spread_blocks/pallas_call | solution.py:696
  191.1 12.9 %scan_forward.1 = (bf16[1024,1024]{1,0:T(8,128)(2,1)S(1)}, f32[1024,768]{1,0:T(8,128)S(1)}, bf16[4,256,768]{2,1,0:T(8,128)(2,1)S(1)}) custom-call(bf16[1024,2688]{1,0:T(8,128)(2,1)S(1)} %copy-done.3, bf16[1024,2688]{1,0:T(8,128)(2,1)S(1)} %copy-done.3, bf16[1024,2688]{1,0:T(8,128)(2,1)S(1)} %copy-done.3, ...), custom_call_target="tpu_custom_call", output_to_operand_aliasing={{0}: (12, {})} | custom-call | flops 83886080 | bytes 589824 | tf_op jit(solution)/shard_map/scan_forward/pallas_call | solution.py:383
  235.7 22.3 %collective-permute-done.14.second_near = bf16[256,1024]{1,0:T(8,128)(2,1)S(1)} collective-permute-done((bf16[256,1024]{1,0:T(8,128)(2,1)}, bf16[256,1024]{1,0:T(8,128)(2,1)S(1)}, u32[]{:S(2)}, u32[]{:S(2)}) %collective-permute-start.14) | collective-permute-done | bytes 524320 | tf_op jit(solution)/shard_map/ppermute | solution.py:1038
  275.3 7.3 %collective-permute-done.21.rest_0_ = bf16[256,1024]{1,0:T(8,128)(2,1)S(1)} collective-permute-done((bf16[256,1024]{1,0:T(8,128)(2,1)S(1)}, bf16[256,1024]{1,0:T(8,128)(2,1)S(1)}, u32[]{:S(2)}, u32[]{:S(2)}) %collective-permute-start.21) | collective-permute-done | bytes 524320 | tf_op jit(solution)/shard_map/ppermute | solution.py:1038
  285.1 8.8 %collective-permute-done.18.rest_1_ = bf16[256,1024]{1,0:T(8,128)(2,1)} collective-permute-done((bf16[256,1024]{1,0:T(8,128)(2,1)}, bf16[256,1024]{1,0:T(8,128)(2,1)}, u32[]{:S(2)}, u32[]{:S(2)}) %collective-permute-start.18) | collective-permute-done | bytes 524320 | tf_op jit(solution)/shard_map/ppermute | solution.py:1038
  354.2 11.2 %spread_blocks.21 = (bf16[1024,2048]{1,0:T(8,128)(2,1)S(1)}, bf16[1024,128]{1,0:T(8,128)(2,1)S(1)}) custom-call(f32[1024,128]{1,0:T(8,128)S(1)} %compare_convert_fusion.chosen_ref, bf16[256,1024]{1,0:T(8,128)(2,1)} %get-tuple-element.322.rest_0_, bf16[256,1024]{1,0:T(8,128)(2,1)} %get-tuple-element.321.rest_1_, bf16[256,1024]{1,0:T(8,128)(2,1)S(1)} %copy-done.109, ...), custom_call_target="tpu_custom_call" | custom-call | flops 301989888 | bytes 393216 | tf_op jit(solution)/shard_map/spread_blocks/pallas_call | solution.py:696
  376.2 8.3 %collect_blocks.10 = (bf16[256,1152]{1,0:T(8,128)(2,1)}, f32[256,1024]{1,0:T(8,128)S(1)}, f32[256,1152]{1,0:T(8,128)S(1)}, bf16[256,1024]{1,0:T(8,128)(2,1)}, f3...) custom-call(bf16[1024,2048]{1,0:T(8,128)(2,1)S(1)} %get-tuple-element.183.values_ref, bf16[8,272,2176]{2,1,0:T(8,128)(2,1)S(1)} %bitcast.164), custom_call_target="tpu_custom_call" | custom-call | flops 402653184 | bytes 589824 | tf_op jit(solution)/shard_map/collect_blocks/pallas_call | solution.py:763
  427.4 8.8 %collective-permute-done.34.rest_0_ = bf16[256,1024]{1,0:T(8,128)(2,1)S(1)} collective-permute-done((bf16[256,1024]{1,0:T(8,128)(2,1)S(1)}, bf16[256,1024]{1,0:T(8,128)(2,1)S(1)}, u32[]{:S(2)}, u32[]{:S(2)}) %collective-permute-start.34) | collective-permute-done | bytes 524320 | tf_op jit(solution)/shard_map/ppermute | solution.py:1038
  440.9 7.0 %collective-permute-done.39.rest_0_ = bf16[256,1024]{1,0:T(8,128)(2,1)S(1)} collective-permute-done((bf16[256,1024]{1,0:T(8,128)(2,1)S(1)}, bf16[256,1024]{1,0:T(8,128)(2,1)S(1)}, u32[]{:S(2)}, u32[]{:S(2)}) %collective-permute-start.39) | collective-permute-done | bytes 524320 | tf_op jit(solution)/shard_map/ppermute | solution.py:1038
  469.5 7.2 %attention_backward.1 = (bf16[1024,256]{1,0:T(8,128)(2,1)S(1)}, bf16[1024,256]{1,0:T(8,128)(2,1)S(1)}) custom-call(bf16[1024,2688]{1,0:T(8,128)(2,1)S(1)} %copy-done.4, bf16[1024,2688]{1,0:T(8,128)(2,1)S(1)} %copy-done.4, bf16[1024,2688]{1,0:T(8,128)(2,1)S(1)} %copy-done.4, f32[1024,128]{1,0:T(8,128)S(1)} %copy-done.53, f32[1024,128]{1,0:T(8,128)S(1)} %copy-done.51, ...), custom_call_target="tpu_custom_call" | custom-call | flops 100663296 | bytes 393216 | tf_op jit(solution)/shard_map/attention_backward/pallas_call | solution.py:556
  483.5 13.9 %scan_backward.2 = (bf16[1024,2688]{1,0:T(8,128)(2,1)S(1)}, f32[256,768]{1,0:T(8,128)S(1)}, f32[8,768]{1,0:T(8,128)S(1)}, f32[8,512]{1,0:T(8,128)S(1)}) custom-call(bf16[1024,2688]{1,0:T(8,128)(2,1)S(1)} %copy-done.4, bf16[1024,2688]{1,0:T(8,128)(2,1)S(1)} %copy-done.4, bf16[1024,2688]{1,0:T(8,128)(2,1)S(1)} %copy-done.4, bf16[1024,2688]{1,0:T(8,128)(2,1)S(1)} %copy-done.4, ...), custom_call_target="tpu_custom_call" | custom-call | flops 167772160 | bytes 1179648 | tf_op jit(solution)/shard_map/scan_backward/pallas_call | solution.py:426
  519.1 14.9 %scan_backward.3 = (bf16[1024,2688]{1,0:T(8,128)(2,1)S(1)}, f32[256,768]{1,0:T(8,128)}, f32[8,768]{1,0:T(8,128)}, f32[8,512]{1,0:T(8,128)}) custom-call(bf16[1024,2688]{1,0:T(8,128)(2,1)S(1)} %copy-done.5, bf16[1024,2688]{1,0:T(8,128)(2,1)S(1)} %copy-done.5, bf16[1024,2688]{1,0:T(8,128)(2,1)S(1)} %copy-done.5, ...), custom_call_target="tpu_custom_call", output_to_operand_aliasing={{0}: (17, {})} | custom-call | flops 167772160 | bytes 1179648 | tf_op jit(solution)/shard_map/scan_backward/pallas_call | solution.py:426
  546.2 14.2 %collect_blocks.11 = (bf16[256,1152]{1,0:T(8,128)(2,1)S(1)}, bf16[256,1024]{1,0:T(8,128)(2,1)S(1)}, bf16[256,1152]{1,0:T(8,128)(2,1)}, f32[256,1024]{1,0:T(8,128...) custom-call(bf16[1024,2688]{1,0:T(8,128)(2,1)S(1)} %copy-done.22, ...), custom_call_target="tpu_custom_call" | custom-call | flops 704643072 | bytes 868352 | tf_op jit(solution)/shard_map/collect_blocks/pallas_call | solution.py:763
  568.0 11.7 %collective-permute-done.48.second_part = bf16[256,1024]{1,0:T(8,128)(2,1)S(1)} collective-permute-done((bf16[256,1024]{1,0:T(8,128)(2,1)S(1)}, bf16[256,1024]{1,0:T(8,128)(2,1)S(1)}, u32[]{:S(2)}, u32[]{:S(2)}) %collective-permute-start.48) | collective-permute-done | bytes 524320 | tf_op jit(solution)/shard_map/ppermute | solution.py:1038
  599.3 11.5 %collective-permute-done.50.second_near = bf16[256,1024]{1,0:T(8,128)(2,1)} collective-permute-done((bf16[256,1024]{1,0:T(8,128)(2,1)}, bf16[256,1024]{1,0:T(8,128)(2,1)}, u32[]{:S(2)}, u32[]{:S(2)}) %collective-permute-start.50) | collective-permute-done | bytes 524320 | tf_op jit(solution)/shard_map/ppermute | solution.py:1038
  639.6 16.2 %all-to-all-done.3 = bf16[32,8,2304]{2,1,0:T(8,128)(2,1)S(1)} async-done(((bf16[32,8,2304]{2,1,0:T(8,128)(2,1)}), bf16[32,8,2304]{2,1,0:T(8,128)(2,1)S(1)}, u32[]{:S(2)}, u32[]{:S(2)}) %all-to-all-start.3) | async-done | bytes 1179680 | tf_op jit(solution)/shard_map/all_to_all | solution.py:1178
  (623 shorter events, 376.8 us)
Async XLA Ops:
  7.2 35.3 %all-gather.11.cloned.1.call-start = ((), (), s32[]{:S(2)}) async-start(), calls=%async_computation.8 | async-start | bytes 1327104 | tf_op jit(solution)/shard_map/all_gather | solution.py:1203
  12.7 121.6 %all-gather.13.cloned.1.call-start = ((), (), s32[]{:S(2)}) async-start(), calls=%async_computation.9 | async-start | bytes 10027008 | tf_op jit(solution)/shard_map/all_gather | solution.py:1188
  21.2 186.8 %all-gather.15.cloned.1.call-start = ((), (), s32[]{:S(2)}) async-start(), calls=%async_computation.10 | async-start | bytes 5640192 | tf_op jit(solution)/shard_map/all_gather | solution.py:1188
  23.1 46.9 %all-to-all-start = ((bf16[32,8,2176]{2,1,0:T(8,128)(2,1)}), bf16[32,8,2176]{2,1,0:T(8,128)(2,1)S(1)}, u32[]{:S(2)}, u32[]{:S(2)}) async-start(bf16[32,8,2176]{2,1,0:T(8,128)(2,1)} %bitcast.187), calls=%async_computation | async-start | bytes 2228224 | tf_op jit(solution)/shard_map/all_to_all | solution.py:1178
  30.4 265.0 %all-gather.17.cloned.1.call-start = ((), (), s32[]{:S(2)}) async-start(), calls=%async_computation.11 | async-start | bytes 10653696 | tf_op jit(solution)/shard_map/all_gather | solution.py:1188
  42.5 33.6 %collective-permute-start.1 = (bf16[8,288,256]{2,1,0:T(8,128)(2,1)}, bf16[8,288,256]{2,1,0:T(8,128)(2,1)}, u32[]{:S(2)}, u32[]{:S(2)}) collective-permute-start(bf16[8,288,256]{2,1,0:T(8,128)(2,1)} %bitcast.189), channel_id=1, source_target_pairs={{0,2},{1,3},{2,0},{3,1},{4,6},{5,7},{6,4},{7,5},{8,10},{9,11},{10,... | collective-permute-start | bytes 3538952 | tf_op jit(solution)/shard_map/ppermute | solution.py:1038
  42.9 33.5 %collective-permute-start = (bf16[8,288,256]{2,1,0:T(8,128)(2,1)}, bf16[8,288,256]{2,1,0:T(8,128)(2,1)}, u32[]{:S(2)}, u32[]{:S(2)}) collective-permute-start(bf16[8,288,256]{2,1,0:T(8,128)(2,1)} %bitcast.190), channel_id=1, source_target_pairs={{0,1},{1,0},{2,3},{3,2},{4,5},{5,4},{6,7},{7,6},{8,9},{9,8},{10,11... | collective-permute-start | bytes 3538952 | tf_op jit(solution)/shard_map/ppermute | solution.py:1038
  78.8 264.4 %all-gather.19.cloned.1.call-start = ((), (), s32[]{:S(2)}) async-start(), calls=%async_computation.12 | async-start | bytes 5640192 | tf_op jit(solution)/shard_map/all_gather | solution.py:1188
  82.4 40.7 %collective-permute-start.7 = (bf16[4,288,256]{2,1,0:T(8,128)(2,1)S(1)}, bf16[4,288,256]{2,1,0:T(8,128)(2,1)S(1)}, u32[]{:S(2)}, u32[]{:S(2)}) collective-permute-start(bf16[4,288,256]{2,1,0:T(8,128)(2,1)S(1)} %slice.489), channel_id=1, source_target_pairs={{0,1},{1,0},{2,3},{3,2},{4,5},{5,4},{6,7},{7,6},{8,9},{9,8},{10,11... | collective-permute-start | bytes 1769480 | tf_op jit(solution)/shard_map/ppermute | solution.py:1038
  84.4 40.1 %collective-permute-start.6 = (bf16[4,288,256]{2,1,0:T(8,128)(2,1)S(1)}, bf16[4,288,256]{2,1,0:T(8,128)(2,1)S(1)}, u32[]{:S(2)}, u32[]{:S(2)}) collective-permute-start(bf16[4,288,256]{2,1,0:T(8,128)(2,1)S(1)} %slice.488), channel_id=1, source_target_pairs={{0,2},{1,3},{2,0},{3,1},{4,6},{5,7},{6,4},{7,5},{8,10},{9,11},{10,... | collective-permute-start | bytes 1769480 | tf_op jit(solution)/shard_map/ppermute | solution.py:1038
  90.0 64.4 %collective-permute-start.8 = (bf16[256,1024]{1,0:T(8,128)(2,1)}, bf16[256,1024]{1,0:T(8,128)(2,1)S(1)}, u32[]{:S(2)}, u32[]{:S(2)}) collective-permute-start(bf16[256,1024]{1,0:T(8,128)(2,1)} %get-tuple-element.137.rest_1_.refs_5_), channel_id=1, source_target_pairs={{0,2},{1,3},{2,0},{3,1},{4,6},{5,7},{6,4},{7,5},{8,10},{9,11},{10,... | collective-permute-start | bytes 1572872 | tf_op jit(solution)/shard_map/ppermute | solution.py:1038
  108.9 38.4 %collective-permute-start.9 = (bf16[256,1024]{1,0:T(8,128)(2,1)}, bf16[256,1024]{1,0:T(8,128)(2,1)}, u32[]{:S(2)}, u32[]{:S(2)}) collective-permute-start(bf16[256,1024]{1,0:T(8,128)(2,1)} %get-tuple-element.136.rest_0_.refs_4_), channel_id=1, source_target_pairs={{0,1},{1,0},{2,3},{3,2},{4,5},{5,4},{6,7},{7,6},{8,9},{9,8},{10,11... | collective-permute-start | bytes 1572872 | tf_op jit(solution)/shard_map/ppermute | solution.py:1038
  121.9 40.0 %collective-permute-start.5 = (bf16[256,1024]{1,0:T(8,128)(2,1)S(1)}, bf16[256,1024]{1,0:T(8,128)(2,1)}, u32[]{:S(2)}, u32[]{:S(2)}) collective-permute-start(bf16[256,1024]{1,0:T(8,128)(2,1)S(1)} %collective-permute-done.4.rest_1_), channel_id=1, source_target_pairs={{0,2},{1,3},{2,0},{3,1},{4,6},{5,7},{6,4},{7,5},{8,10},{9,11},{10,... | collective-permute-start | bytes 1572872 | tf_op jit(solution)/shard_map/ppermute | solution.py:1038
  123.0 38.9 %collective-permute-start.3 = (bf16[256,1024]{1,0:T(8,128)(2,1)}, bf16[256,1024]{1,0:T(8,128)(2,1)}, u32[]{:S(2)}, u32[]{:S(2)}) collective-permute-start(bf16[256,1024]{1,0:T(8,128)(2,1)} %collective-permute-done.2.rest_0_), channel_id=1, source_target_pairs={{0,1},{1,0},{2,3},{3,2},{4,5},{5,4},{6,7},{7,6},{8,9},{9,8},{10,11... | collective-permute-start | bytes 1572872 | tf_op jit(solution)/shard_map/ppermute | solution.py:1038
  177.9 93.3 %all-to-all-start.1 = ((bf16[32,8,2048]{2,1,0:T(8,128)(2,1)}), bf16[32,8,2048]{2,1,0:T(8,128)(2,1)}, u32[]{:S(2)}, u32[]{:S(2)}) async-start(bf16[32,8,2048]{2,1,0:T(8,128)(2,1)} %fusion.6), calls=%async_computation.1 | async-start | bytes 2097152 | tf_op jit(solution)/shard_map/all_to_all | solution.py:1178
  181.7 412.7 %reduce-scatter.3.cloned.1.call-start = ((), (), s32[]{:S(2)}) async-start(), calls=%async_computation.6 | async-start | bytes 1179648 | tf_op jit(solution)/shard_map/reduce_scatter | solution.py:1407
  273.0 37.3 %collective-permute-start.20 = (bf16[256,1024]{1,0:T(8,128)(2,1)}, bf16[256,1024]{1,0:T(8,128)(2,1)}, u32[]{:S(2)}, u32[]{:S(2)}) collective-permute-start(bf16[256,1024]{1,0:T(8,128)(2,1)} %get-tuple-element.162.rest_1_.refs_5_), channel_id=1, source_target_pairs={{0,2},{1,3},{2,0},{3,1},{4,6},{5,7},{6,4},{7,5},{8,10},{9,11},{10,... | collective-permute-start | bytes 1572872 | tf_op jit(solution)/shard_map/ppermute | solution.py:1038
  274.7 41.0 %collective-permute-start.23 = (bf16[256,1024]{1,0:T(8,128)(2,1)}, bf16[256,1024]{1,0:T(8,128)(2,1)}, u32[]{:S(2)}, u32[]{:S(2)}) collective-permute-start(bf16[256,1024]{1,0:T(8,128)(2,1)} %get-tuple-element.321.rest_1_), channel_id=1, source_target_pairs={{0,1},{1,0},{2,3},{3,2},{4,5},{5,4},{6,7},{7,6},{8,9},{9,8},{10,11... | collective-permute-start | bytes 1572872 | tf_op jit(solution)/shard_map/ppermute | solution.py:1038
  283.4 32.7 %collective-permute-start.24 = (bf16[256,1024]{1,0:T(8,128)(2,1)}, bf16[256,1024]{1,0:T(8,128)(2,1)}, u32[]{:S(2)}, u32[]{:S(2)}) collective-permute-start(bf16[256,1024]{1,0:T(8,128)(2,1)} %get-tuple-element.322.rest_0_), channel_id=1, source_target_pairs={{0,2},{1,3},{2,0},{3,1},{4,6},{5,7},{6,4},{7,5},{8,10},{9,11},{10,... | collective-permute-start | bytes 1572872 | tf_op jit(solution)/shard_map/ppermute | solution.py:1038
  464.5 36.9 %collective-permute-start.40 = (bf16[256,1152]{1,0:T(8,128)(2,1)}, bf16[256,1152]{1,0:T(8,128)(2,1)S(1)}, u32[]{:S(2)}, u32[]{:S(2)}) collective-permute-start(bf16[256,1152]{1,0:T(8,128)(2,1)} %copy-done.128), channel_id=1, source_target_pairs={{0,1},{1,0},{2,3},{3,2},{4,5},{5,4},{6,7},{7,6},{8,9},{9,8},{10,11... | collective-permute-start | bytes 1769480 | tf_op jit(solution)/shard_map/ppermute | solution.py:1038
  504.0 95.3 %all-to-all-start.2 = ((bf16[32,8,2816]{2,1,0:T(8,128)(2,1)}), bf16[32,8,2816]{2,1,0:T(8,128)(2,1)}, u32[]{:S(2)}, u32[]{:S(2)}) async-start(bf16[32,8,2816]{2,1,0:T(8,128)(2,1)} %bitcast.183), calls=%async_computation.2 | async-start | bytes 2883584 | tf_op jit(solution)/shard_map/all_to_all | solution.py:1178
  507.5 90.2 %reduce-scatter.5.cloned.1.call-start = ((), (), s32[]{:S(2)}) async-start(), calls=%async_computation.7 | async-start | bytes 774144 | tf_op jit(solution)/shard_map/reduce_scatter | solution.py:1407
  567.5 43.3 %collective-permute-start.46 = (bf16[256,1152]{1,0:T(8,128)(2,1)}, bf16[256,1152]{1,0:T(8,128)(2,1)}, u32[]{:S(2)}, u32[]{:S(2)}) collective-permute-start(bf16[256,1152]{1,0:T(8,128)(2,1)} %get-tuple-element.240), channel_id=1, source_target_pairs={{0,1},{1,0},{2,3},{3,2},{4,5},{5,4},{6,7},{7,6},{8,9},{9,8},{10,11... | collective-permute-start | bytes 1769480 | tf_op jit(solution)/shard_map/ppermute | solution.py:1038
  620.8 35.0 %all-to-all-start.3 = ((bf16[32,8,2304]{2,1,0:T(8,128)(2,1)}), bf16[32,8,2304]{2,1,0:T(8,128)(2,1)S(1)}, u32[]{:S(2)}, u32[]{:S(2)}) async-start(bf16[32,8,2304]{2,1,0:T(8,128)(2,1)} %bitcast.184), calls=%async_computation.5 | async-start | bytes 2359296 | tf_op jit(solution)/shard_map/all_to_all | solution.py:1178
  (202 other events, 2382.0 us)
Sparse Core Ops, SparseCore 0:
  12.8 29.6 all-gather.10
  44.1 90.1 all-gather.12
  136.5 55.7 all-gather.14
  193.8 94.9 all-gather.16
  290.3 52.8 all-gather.18
  464.6 29.3 reduce-scatter.2
  566.0 31.5 reduce-scatter.4

commit v10 on v8

--- a/solution.py
+++ b/solution.py
@@ -65,7 +65,6 @@
 
 ESTIMATE = 16
 SCAN_BYTES = 32 * 1024 * 1024
-ALONE_BYTES = 56 * 1024 * 1024
 DENSE_BYTES = 16 * 1024 * 1024
 FINISH_BYTES = 32 * 1024 * 1024
 LANES = 128
@@ -434,7 +433,7 @@
             *[jax.ShapeDtypeStruct(shape, FLOAT) for shape in running],
         ],
         input_output_aliases=aliases,
-        compiler_params=pltpu.CompilerParams(vmem_limit_bytes=ALONE_BYTES),
+        compiler_params=pltpu.CompilerParams(vmem_limit_bytes=SCAN_BYTES),
         cost_estimate=scan_cost(tokens, channels, 2),
         name="scan_backward",
     )(*operands)
@@ -699,6 +698,9 @@
 
 def collect_kernel(masks, count, values_ref, *refs):
     weights, outs = refs[:count], refs[count:]
+    if len(outs) > 2 * len(masks):
+        inner_ref, *outs, raise_ref = outs
+        raise_ref[...] = dot(inner_ref[...], values_ref[...], (0, 0)).astype(BFLOAT)
     rows = values_ref.shape[0] // 4
     shards = weights[0].shape[0]
     half = shards // HALVES * rows
@@ -730,7 +732,7 @@
         ).astype(first.dtype)
 
 
-def collect_blocks(masks, values, gathered, types):
+def collect_blocks(masks, values, gathered, types, inner=()):
     rows = values.shape[0] // 4
     half = gathered[0].shape[0] // HALVES * rows
     fast = pl.BlockSpec(memory_space=pltpu.VMEM)
@@ -738,9 +740,10 @@
     for pair in types:
         out_shape.append(jax.ShapeDtypeStruct((rows, half + LANES), pair[0]))
         out_shape.append(jax.ShapeDtypeStruct((rows, half), pair[1]))
+    out_shape += [jax.ShapeDtypeStruct((LANES, values.shape[1]), BFLOAT) for _ in inner]
     outs = pl.pallas_call(
         functools.partial(collect_kernel, masks, len(gathered)),
-        in_specs=[fast] * (1 + len(gathered)),
+        in_specs=[fast] * (1 + len(gathered) + len(inner)),
         out_specs=[fast] * len(out_shape),
         out_shape=out_shape,
         compiler_params=pltpu.CompilerParams(vmem_limit_bytes=DENSE_BYTES),
@@ -750,8 +753,8 @@
             transcendentals=0,
         ),
         name="collect_blocks",
-    )(values, *gathered)
-    return [tuple(outs[2 * at : 2 * at + 2]) for at in range(len(masks))]
+    )(values, *gathered, *inner)
+    return [tuple(outs[2 * at : 2 * at + 2]) for at in range(len(masks))] + list(outs[2 * len(masks) :])
 
 
 def root_mean(values):
@@ -1282,10 +1285,7 @@
             expand_grad(dealt[:, :, model + at * width : model + (at + 1) * width]) for at in range(count)
         ]
 
-    if fast:
-        projected, inner_in = spread_blocks(blocks_one, weights_in, selector, None)
-    else:
-        projected, inner_in = spread_project(blocks_one, weights_in, selector)
+    projected, inner_in = (spread_gathered if fast else spread_project)(blocks_one, weights_in, selector)
 
     sent_grad = product(send_matrix, cotangent).astype(BFLOAT).reshape(devices, peer, model)
     arrived_grad = exchange(after(sent_grad, normed_one[0])).reshape(rows, model)
@@ -1361,9 +1361,8 @@
         dealt_out = exchange(payload.reshape(devices, peer, -1))
         scan_part[2] = after(scan_part[2], payload)
         projected_grad = scan_backward(*scan_inputs, 1, 2, scan_part)[0]
-        raise_grad = contract_first(inner_in, projected_grad).astype(BFLOAT)
-        projected_grad = after(projected_grad, raise_grad)
-        started_in = collect_send(collect_pieces(projected_grad, weights_in, True))
+        *pieces_in, raise_grad = collect_blocks([3, 1, 2, 0], projected_grad, weights_in, PIECE_TYPES, [inner_in])
+        started_in = collect_send(pieces_in)
         kept_in, onward_in = collect_middle(started_in)
     else:
         block_out, inner_down = collect_project(activated, weights_down, "output", own_selector, hidden)

time: 664 us -> 657 us (0.989)
  waiting for transfers between devices: 218 us -> 206 us
    ppermute x55, waiting for transfers between devices: 163 us -> 133 us  [flip(): return lax.ppermute(values, 'col', [(i, i ^ mask) for i in range(4)])]
    all_to_all x4, waiting for transfers between devices: 22.9 us -> 40.8 us  [local(): lax.all_to_all(values, ALL_AXES, split_axis=0, concat_axis=0, tiled=True)]
    all_gather x4, waiting for transfers between devices: 5.63 us -> 19.2 us  [gather_weight(): return (lax.all_gather(shards[-1], 'row', axis=0),)]
    all_gather x1, waiting for transfers between devices: 24 us -> 12 us  [local(): shared = lax.all_gather(shared_shard, 'row', axis=0)]
    unnamed x362 -> x358, local copies, waits for them, and re-layouts: 102 us -> 106 us
    pallas_call x10 -> x13, Pallas kernels: 60.4 us -> 63.9 us  [spread_blocks(): pl.pallas_call(functools.partial(spread_kernel, masks, len(gathered)), in...]
  transfers between devices with their start and end apart: 66 -> 66, of which waited for: 29 -> 29; matrix products, arithmetic and copies ran while one was open for 8% -> 9% of each run, Pallas kernels for 24% -> 24%
where the time goes in v10:
time: 657 us; the launch traced here: 648 us
  waiting for transfers between devices  206 us (31%)
  Pallas kernels  175 us (27%)
  local copies, waits for them, and re-layouts  130 us (20%)
  starting transfers between devices  86.5 us (13%)
  other arithmetic  22.5 us (3%)
  between operations  17.1 us (3%)
  matrix products  10.5 us (2%)
    ppermute x55, waiting for transfers between devices, flip(): return lax.ppermute(values, 'col', [(i, i ^ mask) for i in range(4)])  133 us
    unnamed x358, local copies, waits for them, and re-layouts  106 us
    ppermute x55, starting transfers between devices, flip(): return lax.ppermute(values, 'col', [(i, i ^ mask) for i in range(4)])  66.7 us
    pallas_call x13, Pallas kernels, spread_blocks(): pl.pallas_call(functools.partial(spread_kernel, masks, len(gathered)), in...  63.9 us
    all_to_all x4, waiting for transfers between devices, local(): lax.all_to_all(values, ALL_AXES, split_axis=0, concat_axis=0, tiled=True)  40.8 us
    pallas_call x6, Pallas kernels, collect_blocks(): pl.pallas_call(functools.partial(collect_kernel, masks, len(gathered)), i...  38.9 us
    pallas_call x2, Pallas kernels, scan_backward(): pl.pallas_call(scan_backward_kernel, grid=(blocks // parts,), in_specs=in...  28.8 us
    all_to_all x4, starting transfers between devices, local(): lax.all_to_all(values, ALL_AXES, split_axis=0, concat_axis=0, tiled=True)  19.5 us
  transfers between devices with their start and end apart: 66, of which 29 were waited for; matrix products, arithmetic and copies ran while one was open for 9% of the time, Pallas kernels for 24%

profile of v10, /device:TPU:0, one launch (start us, length us, event | category | flops | bytes accessed | tf_op | source)
XLA Modules:
  0.0 647.9 jit_solution(10782200612378969129)
XLA Ops:
  23.1 7.3 %all-to-all-start = ((bf16[32,8,2176]{2,1,0:T(8,128)(2,1)}), bf16[32,8,2176]{2,1,0:T(8,128)(2,1)S(1)}, u32[]{:S(2)}, u32[]{:S(2)}) async-start(bf16[32,8,2176]{2,1,0:T(8,128)(2,1)} %bitcast.187), calls=%async_computation | async-start | bytes 2228224 | tf_op jit(solution)/shard_map/all_to_all | solution.py:1159
  30.5 12.0 %all-gather.11.cloned.1.call-done = bf16[2304,256]{1,0:T(8,128)(2,1)} async-done(((bf16[288,256]{1,0:T(8,128)(2,1)}), bf16[2304,256]{1,0:T(8,128)(2,1)}) %all-gather.11.cloned.1.call-update) | async-done | bytes 1179664 | tf_op jit(solution)/shard_map/all_gather | solution.py:1184
  48.0 24.5 %all-to-all-done = bf16[32,8,2176]{2,1,0:T(8,128)(2,1)S(1)} async-done(((bf16[32,8,2176]{2,1,0:T(8,128)(2,1)}), bf16[32,8,2176]{2,1,0:T(8,128)(2,1)S(1)}, u32[]{:S(2)}, u32[]{:S(2)}) %all-to-all-start) | async-done | bytes 1114144 | tf_op jit(solution)/shard_map/all_to_all | solution.py:1159
  95.6 12.5 %collective-permute-done.4.rest_1_ = bf16[256,1024]{1,0:T(8,128)(2,1)S(1)} collective-permute-done((bf16[256,1024]{1,0:T(8,128)(2,1)}, bf16[256,1024]{1,0:T(8,128)(2,1)S(1)}, u32[]{:S(2)}, u32[]{:S(2)}) %collective-permute-start.4) | collective-permute-done | bytes 524320 | tf_op jit(solution)/shard_map/ppermute | solution.py:1019
  109.1 12.3 %collective-permute-done.2.rest_0_ = bf16[256,1024]{1,0:T(8,128)(2,1)} collective-permute-done((bf16[256,1024]{1,0:T(8,128)(2,1)}, bf16[256,1024]{1,0:T(8,128)(2,1)}, u32[]{:S(2)}, u32[]{:S(2)}) %collective-permute-start.2) | collective-permute-done | bytes 524320 | tf_op jit(solution)/shard_map/ppermute | solution.py:1019
  139.7 7.5 %spread_blocks.13 = (bf16[1024,2688]{1,0:T(8,128)(2,1)S(1)}, bf16[1024,128]{1,0:T(8,128)(2,1)S(1)}) custom-call(f32[1024,128]{1,0:T(8,128)S(1)} %compare_convert_fusion.chosen_ref, bf16[256,1024]{1,0:T(8,128)(2,1)} %get-tuple-element.138.rest_0_.refs_4_, bf16[256,1024]{1,0:T(8,128)(2,1)} %get-tuple-element.139.rest_1_.refs_5_, ...), custom_call_target="tpu_custom_call" | custom-call | flops 184549376 | bytes 151552 | tf_op jit(solution)/shard_map/spread_blocks/pallas_call | solution.py:675
  147.2 7.1 %spread_blocks.14 = (bf16[1024,2688]{1,0:T(8,128)(2,1)S(1)}, bf16[1024,128]{1,0:T(8,128)(2,1)S(1)}) custom-call(f32[1024,128]{1,0:T(8,128)S(1)} %compare_convert_fusion.chosen_ref, bf16[256,1024]{1,0:T(8,128)(2,1)} %collective-permute-done.9.rest_0_, ...), custom_call_target="tpu_custom_call", output_to_operand_aliasing={{0}: (5, {}), {1}: (6, {})} | custom-call | flops 184549376 | bytes 151552 | tf_op jit(solution)/shard_map/spread_blocks/pallas_call | solution.py:675
  154.4 7.5 %spread_blocks.15 = (bf16[1024,2688]{1,0:T(8,128)(2,1)S(1)}, bf16[1024,128]{1,0:T(8,128)(2,1)S(1)}) custom-call(f32[1024,128]{1,0:T(8,128)S(1)} %compare_convert_fusion.chosen_ref, bf16[256,1024]{1,0:T(8,128)(2,1)} %collective-permute-done.2.rest_0_, ...), custom_call_target="tpu_custom_call", output_to_operand_aliasing={{0}: (5, {}), {1}: (6, {})} | custom-call | flops 184549376 | bytes 151552 | tf_op jit(solution)/shard_map/spread_blocks/pallas_call | solution.py:675
  161.9 7.3 %spread_blocks.16 = (bf16[1024,2688]{1,0:T(8,128)(2,1)S(1)}, bf16[1024,128]{1,0:T(8,128)(2,1)S(1)}) custom-call(f32[1024,128]{1,0:T(8,128)S(1)} %compare_convert_fusion.chosen_ref, bf16[256,1024]{1,0:T(8,128)(2,1)} %collective-permute-done.3.rest_0_, bf16[256,1024]{1,0:T(8,128)(2,1)} %collective-permute-done.5.rest_1_, ...), custom_call_target="tpu_custom_call", output_to_operand_aliasing={{0}: (5, {}), {1}: (6, {})} | custom-call | flops 184549376 | bytes 151552 | tf_op jit(solution)/shard_map/spread_blocks/pallas_call | solution.py:675
  189.9 12.9 %scan_forward.1 = (bf16[1024,1024]{1,0:T(8,128)(2,1)S(1)}, f32[1024,768]{1,0:T(8,128)S(1)}, bf16[4,256,768]{2,1,0:T(8,128)(2,1)S(1)}) custom-call(bf16[1024,2688]{1,0:T(8,128)(2,1)S(1)} %copy-done.3, bf16[1024,2688]{1,0:T(8,128)(2,1)S(1)} %copy-done.3, bf16[1024,2688]{1,0:T(8,128)(2,1)S(1)} %copy-done.3, ...), custom_call_target="tpu_custom_call", output_to_operand_aliasing={{0}: (12, {})} | custom-call | flops 83886080 | bytes 589824 | tf_op jit(solution)/shard_map/scan_forward/pallas_call | solution.py:383
  241.0 17.4 %collective-permute-done.14.second_near = bf16[256,1024]{1,0:T(8,128)(2,1)} collective-permute-done((bf16[256,1024]{1,0:T(8,128)(2,1)}, bf16[256,1024]{1,0:T(8,128)(2,1)}, u32[]{:S(2)}, u32[]{:S(2)}) %collective-permute-start.14) | collective-permute-done | bytes 524320 | tf_op jit(solution)/shard_map/ppermute | solution.py:1019
  281.6 7.6 %collective-permute-done.24.rest_4_ = bf16[256,1024]{1,0:T(8,128)(2,1)} collective-permute-done((bf16[256,1024]{1,0:T(8,128)(2,1)}, bf16[256,1024]{1,0:T(8,128)(2,1)}, u32[]{:S(2)}, u32[]{:S(2)}) %collective-permute-start.24) | collective-permute-done | bytes 524320 | tf_op jit(solution)/shard_map/ppermute | solution.py:1019
  331.4 12.9 %all-gather.19.cloned.1.call-done = bf16[2176,1152]{1,0:T(8,128)(2,1)} async-done(((bf16[272,1152]{1,0:T(8,128)(2,1)}), bf16[2176,1152]{1,0:T(8,128)(2,1)}) %all-gather.19.cloned.1.call-update) | async-done | bytes 5013520 | tf_op jit(solution)/shard_map/all_gather | solution.py:1169
  346.6 10.1 %spread_blocks.21 = (bf16[1024,1024]{1,0:T(8,128)(2,1)S(1)}, bf16[1024,128]{1,0:T(8,128)(2,1)S(1)}) custom-call(f32[1024,128]{1,0:T(8,128)S(1)} %compare_convert_fusion.chosen_ref, bf16[256,1024]{1,0:T(8,128)(2,1)} %get-tuple-element.326.rest_0_, bf16[256,1024]{1,0:T(8,128)(2,1)} %get-tuple-element.325.rest_1_, ...), custom_call_target="tpu_custom_call" | custom-call | flops 301989888 | bytes 393216 | tf_op jit(solution)/shard_map/spread_blocks/pallas_call | solution.py:675
  369.1 8.3 %collect_blocks.10 = (bf16[256,1152]{1,0:T(8,128)(2,1)}, f32[256,1024]{1,0:T(8,128)S(1)}, f32[256,1152]{1,0:T(8,128)S(1)}, bf16[256,1024]{1,0:T(8,128)(2,1)}, f3...) custom-call(bf16[1024,2048]{1,0:T(8,128)(2,1)S(1)} %pad_maximum_fusion.values_ref, bf16[8,272,2176]{2,1,0:T(8,128)(2,1)S(1)} %bitcast.163), custom_call_target="tpu_custom_call" | custom-call | flops 402653184 | bytes 589824 | tf_op jit(solution)/shard_map/collect_blocks/pallas_call | solution.py:744
  420.0 8.8 %collective-permute-done.34.rest_0_ = bf16[256,1024]{1,0:T(8,128)(2,1)S(1)} collective-permute-done((bf16[256,1024]{1,0:T(8,128)(2,1)S(1)}, bf16[256,1024]{1,0:T(8,128)(2,1)S(1)}, u32[]{:S(2)}, u32[]{:S(2)}) %collective-permute-start.34) | collective-permute-done | bytes 524320 | tf_op jit(solution)/shard_map/ppermute | solution.py:1019
  433.5 7.1 %collective-permute-done.39.rest_0_ = bf16[256,1024]{1,0:T(8,128)(2,1)S(1)} collective-permute-done((bf16[256,1024]{1,0:T(8,128)(2,1)S(1)}, bf16[256,1024]{1,0:T(8,128)(2,1)S(1)}, u32[]{:S(2)}, u32[]{:S(2)}) %collective-permute-start.39) | collective-permute-done | bytes 524320 | tf_op jit(solution)/shard_map/ppermute | solution.py:1019
  462.1 7.2 %attention_backward.1 = (bf16[1024,256]{1,0:T(8,128)(2,1)S(1)}, bf16[1024,256]{1,0:T(8,128)(2,1)S(1)}) custom-call(bf16[1024,2688]{1,0:T(8,128)(2,1)S(1)} %copy-done.4, bf16[1024,2688]{1,0:T(8,128)(2,1)S(1)} %copy-done.4, bf16[1024,2688]{1,0:T(8,128)(2,1)S(1)} %copy-done.4, f32[1024,128]{1,0:T(8,128)S(1)} %copy-done.49, f32[1024,128]{1,0:T(8,128)S(1)} %copy-done.47, ...), custom_call_target="tpu_custom_call" | custom-call | flops 100663296 | bytes 393216 | tf_op jit(solution)/shard_map/attention_backward/pallas_call | solution.py:556
  476.1 13.9 %scan_backward.2 = (bf16[1024,2688]{1,0:T(8,128)(2,1)S(1)}, f32[256,768]{1,0:T(8,128)S(1)}, f32[8,768]{1,0:T(8,128)S(1)}, f32[8,512]{1,0:T(8,128)S(1)}) custom-call(bf16[1024,2688]{1,0:T(8,128)(2,1)S(1)} %copy-done.4, bf16[1024,2688]{1,0:T(8,128)(2,1)S(1)} %copy-done.4, bf16[1024,2688]{1,0:T(8,128)(2,1)S(1)} %copy-done.4, bf16[1024,2688]{1,0:T(8,128)(2,1)S(1)} %copy-done.4, ...), custom_call_target="tpu_custom_call" | custom-call | flops 167772160 | bytes 1179648 | tf_op jit(solution)/shard_map/scan_backward/pallas_call | solution.py:426
  510.2 14.9 %scan_backward.3 = (bf16[1024,2688]{1,0:T(8,128)(2,1)S(1)}, f32[256,768]{1,0:T(8,128)}, f32[8,768]{1,0:T(8,128)}, f32[8,512]{1,0:T(8,128)}) custom-call(bf16[1024,2688]{1,0:T(8,128)(2,1)S(1)} %copy-done.5, bf16[1024,2688]{1,0:T(8,128)(2,1)S(1)} %copy-done.5, bf16[1024,2688]{1,0:T(8,128)(2,1)S(1)} %copy-done.5, ...), custom_call_target="tpu_custom_call", output_to_operand_aliasing={{0}: (17, {})} | custom-call | flops 167772160 | bytes 1179648 | tf_op jit(solution)/shard_map/scan_backward/pallas_call | solution.py:426
  527.1 15.0 %collect_blocks.11 = (bf16[256,1152]{1,0:T(8,128)(2,1)S(1)}, bf16[256,1024]{1,0:T(8,128)(2,1)S(1)}, bf16[256,1152]{1,0:T(8,128)(2,1)}, f32[256,1024]{1,0:T(8,128...) custom-call(bf16[1024,2688]{1,0:T(8,128)(2,1)S(1)} %get-tuple-elemen, ...), custom_call_target="tpu_custom_call" | custom-call | flops 704643072 | bytes 868352 | tf_op jit(solution)/shard_map/collect_blocks/pallas_call | solution.py:744
  549.1 12.2 %collective-permute-done.47.second_part = bf16[256,1024]{1,0:T(8,128)(2,1)S(1)} collective-permute-done((bf16[256,1024]{1,0:T(8,128)(2,1)S(1)}, bf16[256,1024]{1,0:T(8,128)(2,1)S(1)}, u32[]{:S(2)}, u32[]{:S(2)}) %collective-permute-start.47) | collective-permute-done | bytes 524320 | tf_op jit(solution)/shard_map/ppermute | solution.py:1019
  580.9 13.3 %collective-permute-done.50.second_near = bf16[256,1024]{1,0:T(8,128)(2,1)} collective-permute-done((bf16[256,1024]{1,0:T(8,128)(2,1)}, bf16[256,1024]{1,0:T(8,128)(2,1)}, u32[]{:S(2)}, u32[]{:S(2)}) %collective-permute-start.50) | collective-permute-done | bytes 524320 | tf_op jit(solution)/shard_map/ppermute | solution.py:1019
  621.9 16.2 %all-to-all-done.3 = bf16[32,8,2304]{2,1,0:T(8,128)(2,1)S(1)} async-done(((bf16[32,8,2304]{2,1,0:T(8,128)(2,1)}), bf16[32,8,2304]{2,1,0:T(8,128)(2,1)S(1)}, u32[]{:S(2)}, u32[]{:S(2)}) %all-to-all-start.3) | async-done | bytes 1179680 | tf_op jit(solution)/shard_map/all_to_all | solution.py:1159
  (637 shorter events, 355.0 us)
Async XLA Ops:
  7.2 35.2 %all-gather.11.cloned.1.call-start = ((), (), s32[]{:S(2)}) async-start(), calls=%async_computation.8 | async-start | bytes 1327104 | tf_op jit(solution)/shard_map/all_gather | solution.py:1184
  12.7 121.6 %all-gather.13.cloned.1.call-start = ((), (), s32[]{:S(2)}) async-start(), calls=%async_computation.9 | async-start | bytes 10027008 | tf_op jit(solution)/shard_map/all_gather | solution.py:1169
  21.2 185.6 %all-gather.15.cloned.1.call-start = ((), (), s32[]{:S(2)}) async-start(), calls=%async_computation.10 | async-start | bytes 5640192 | tf_op jit(solution)/shard_map/all_gather | solution.py:1169
  23.1 49.4 %all-to-all-start = ((bf16[32,8,2176]{2,1,0:T(8,128)(2,1)}), bf16[32,8,2176]{2,1,0:T(8,128)(2,1)S(1)}, u32[]{:S(2)}, u32[]{:S(2)}) async-start(bf16[32,8,2176]{2,1,0:T(8,128)(2,1)} %bitcast.187), calls=%async_computation | async-start | bytes 2228224 | tf_op jit(solution)/shard_map/all_to_all | solution.py:1159
  30.4 274.4 %all-gather.17.cloned.1.call-start = ((), (), s32[]{:S(2)}) async-start(), calls=%async_computation.11 | async-start | bytes 10653696 | tf_op jit(solution)/shard_map/all_gather | solution.py:1169
  42.4 33.7 %collective-permute-start.1 = (bf16[8,288,256]{2,1,0:T(8,128)(2,1)}, bf16[8,288,256]{2,1,0:T(8,128)(2,1)}, u32[]{:S(2)}, u32[]{:S(2)}) collective-permute-start(bf16[8,288,256]{2,1,0:T(8,128)(2,1)} %bitcast.189), channel_id=1, source_target_pairs={{0,2},{1,3},{2,0},{3,1},{4,6},{5,7},{6,4},{7,5},{8,10},{9,11},{10,... | collective-permute-start | bytes 3538952 | tf_op jit(solution)/shard_map/ppermute | solution.py:1019
  42.9 33.4 %collective-permute-start = (bf16[8,288,256]{2,1,0:T(8,128)(2,1)}, bf16[8,288,256]{2,1,0:T(8,128)(2,1)}, u32[]{:S(2)}, u32[]{:S(2)}) collective-permute-start(bf16[8,288,256]{2,1,0:T(8,128)(2,1)} %bitcast.190), channel_id=1, source_target_pairs={{0,1},{1,0},{2,3},{3,2},{4,5},{5,4},{6,7},{7,6},{8,9},{9,8},{10,11... | collective-permute-start | bytes 3538952 | tf_op jit(solution)/shard_map/ppermute | solution.py:1019
  78.8 265.4 %all-gather.19.cloned.1.call-start = ((), (), s32[]{:S(2)}) async-start(), calls=%async_computation.12 | async-start | bytes 5640192 | tf_op jit(solution)/shard_map/all_gather | solution.py:1169
  81.7 40.7 %collective-permute-start.7 = (bf16[4,288,256]{2,1,0:T(8,128)(2,1)S(1)}, bf16[4,288,256]{2,1,0:T(8,128)(2,1)S(1)}, u32[]{:S(2)}, u32[]{:S(2)}) collective-permute-start(bf16[4,288,256]{2,1,0:T(8,128)(2,1)S(1)} %slice.489), channel_id=1, source_target_pairs={{0,1},{1,0},{2,3},{3,2},{4,5},{5,4},{6,7},{7,6},{8,9},{9,8},{10,11... | collective-permute-start | bytes 1769480 | tf_op jit(solution)/shard_map/ppermute | solution.py:1019
  83.7 40.0 %collective-permute-start.6 = (bf16[4,288,256]{2,1,0:T(8,128)(2,1)S(1)}, bf16[4,288,256]{2,1,0:T(8,128)(2,1)S(1)}, u32[]{:S(2)}, u32[]{:S(2)}) collective-permute-start(bf16[4,288,256]{2,1,0:T(8,128)(2,1)S(1)} %slice.488), channel_id=1, source_target_pairs={{0,2},{1,3},{2,0},{3,1},{4,6},{5,7},{6,4},{7,5},{8,10},{9,11},{10,... | collective-permute-start | bytes 1769480 | tf_op jit(solution)/shard_map/ppermute | solution.py:1019
  89.4 65.0 %collective-permute-start.8 = (bf16[256,1024]{1,0:T(8,128)(2,1)}, bf16[256,1024]{1,0:T(8,128)(2,1)S(1)}, u32[]{:S(2)}, u32[]{:S(2)}) collective-permute-start(bf16[256,1024]{1,0:T(8,128)(2,1)} %get-tuple-element.139.rest_1_.refs_5_), channel_id=1, source_target_pairs={{0,2},{1,3},{2,0},{3,1},{4,6},{5,7},{6,4},{7,5},{8,10},{9,11},{10,... | collective-permute-start | bytes 1572872 | tf_op jit(solution)/shard_map/ppermute | solution.py:1019
  108.2 39.0 %collective-permute-start.9 = (bf16[256,1024]{1,0:T(8,128)(2,1)}, bf16[256,1024]{1,0:T(8,128)(2,1)}, u32[]{:S(2)}, u32[]{:S(2)}) collective-permute-start(bf16[256,1024]{1,0:T(8,128)(2,1)} %get-tuple-element.138.rest_0_.refs_4_), channel_id=1, source_target_pairs={{0,1},{1,0},{2,3},{3,2},{4,5},{5,4},{6,7},{7,6},{8,9},{9,8},{10,11... | collective-permute-start | bytes 1572872 | tf_op jit(solution)/shard_map/ppermute | solution.py:1019
  121.4 40.5 %collective-permute-start.5 = (bf16[256,1024]{1,0:T(8,128)(2,1)S(1)}, bf16[256,1024]{1,0:T(8,128)(2,1)}, u32[]{:S(2)}, u32[]{:S(2)}) collective-permute-start(bf16[256,1024]{1,0:T(8,128)(2,1)S(1)} %collective-permute-done.4.rest_1_), channel_id=1, source_target_pairs={{0,2},{1,3},{2,0},{3,1},{4,6},{5,7},{6,4},{7,5},{8,10},{9,11},{10,... | collective-permute-start | bytes 1572872 | tf_op jit(solution)/shard_map/ppermute | solution.py:1019
  122.4 39.5 %collective-permute-start.3 = (bf16[256,1024]{1,0:T(8,128)(2,1)}, bf16[256,1024]{1,0:T(8,128)(2,1)}, u32[]{:S(2)}, u32[]{:S(2)}) collective-permute-start(bf16[256,1024]{1,0:T(8,128)(2,1)} %collective-permute-done.2.rest_0_), channel_id=1, source_target_pairs={{0,1},{1,0},{2,3},{3,2},{4,5},{5,4},{6,7},{7,6},{8,9},{9,8},{10,11... | collective-permute-start | bytes 1572872 | tf_op jit(solution)/shard_map/ppermute | solution.py:1019
  175.1 59.9 %all-to-all-start.1 = ((bf16[32,8,2048]{2,1,0:T(8,128)(2,1)}), bf16[32,8,2048]{2,1,0:T(8,128)(2,1)}, u32[]{:S(2)}, u32[]{:S(2)}) async-start(bf16[32,8,2048]{2,1,0:T(8,128)(2,1)} %fusion.9), calls=%async_computation.1 | async-start | bytes 2097152 | tf_op jit(solution)/shard_map/all_to_all | solution.py:1159
  178.9 397.1 %reduce-scatter.3.cloned.1.call-start = ((), (), s32[]{:S(2)}) async-start(), calls=%async_computation.6 | async-start | bytes 1179648 | tf_op jit(solution)/shard_map/reduce_scatter | solution.py:1383
  279.9 42.6 %collective-permute-start.19 = (bf16[256,1024]{1,0:T(8,128)(2,1)}, bf16[256,1024]{1,0:T(8,128)(2,1)}, u32[]{:S(2)}, u32[]{:S(2)}) collective-permute-start(bf16[256,1024]{1,0:T(8,128)(2,1)} %collective-permute-done.18.rest_1_), channel_id=1, source_target_pairs={{0,2},{1,3},{2,0},{3,1},{4,6},{5,7},{6,4},{7,5},{8,10},{9,11},{10,... | collective-permute-start | bytes 1572872 | tf_op jit(solution)/shard_map/ppermute | solution.py:1019
  289.2 39.8 %collective-permute-start.25 = (bf16[256,1024]{1,0:T(8,128)(2,1)}, bf16[256,1024]{1,0:T(8,128)(2,1)}, u32[]{:S(2)}, u32[]{:S(2)}) collective-permute-start(bf16[256,1024]{1,0:T(8,128)(2,1)} %get-tuple-element.325.rest_1_), channel_id=1, source_target_pairs={{0,2},{1,3},{2,0},{3,1},{4,6},{5,7},{6,4},{7,5},{8,10},{9,11},{10,... | collective-permute-start | bytes 1572872 | tf_op jit(solution)/shard_map/ppermute | solution.py:1019
  291.9 37.1 %collective-permute-start.22 = (bf16[256,1024]{1,0:T(8,128)(2,1)}, bf16[256,1024]{1,0:T(8,128)(2,1)}, u32[]{:S(2)}, u32[]{:S(2)}) collective-permute-start(bf16[256,1024]{1,0:T(8,128)(2,1)} %get-tuple-element.326.rest_0_), channel_id=1, source_target_pairs={{0,1},{1,0},{2,3},{3,2},{4,5},{5,4},{6,7},{7,6},{8,9},{9,8},{10,11... | collective-permute-start | bytes 1572872 | tf_op jit(solution)/shard_map/ppermute | solution.py:1019
  457.0 37.0 %collective-permute-start.40 = (bf16[256,1152]{1,0:T(8,128)(2,1)}, bf16[256,1152]{1,0:T(8,128)(2,1)S(1)}, u32[]{:S(2)}, u32[]{:S(2)}) collective-permute-start(bf16[256,1152]{1,0:T(8,128)(2,1)} %copy-done.125), channel_id=1, source_target_pairs={{0,1},{1,0},{2,3},{3,2},{4,5},{5,4},{6,7},{7,6},{8,9},{9,8},{10,11... | collective-permute-start | bytes 1769480 | tf_op jit(solution)/shard_map/ppermute | solution.py:1019
  496.6 84.4 %all-to-all-start.2 = ((bf16[32,8,2816]{2,1,0:T(8,128)(2,1)}), bf16[32,8,2816]{2,1,0:T(8,128)(2,1)}, u32[]{:S(2)}, u32[]{:S(2)}) async-start(bf16[32,8,2816]{2,1,0:T(8,128)(2,1)} %bitcast.40), calls=%async_computation.2 | async-start | bytes 2883584 | tf_op jit(solution)/shard_map/all_to_all | solution.py:1159
  500.1 79.2 %reduce-scatter.5.cloned.1.call-start = ((), (), s32[]{:S(2)}) async-start(), calls=%async_computation.7 | async-start | bytes 774144 | tf_op jit(solution)/shard_map/reduce_scatter | solution.py:1383
  562.2 32.0 %collective-permute-start.48 = (bf16[256,1152]{1,0:T(8,128)(2,1)}, bf16[256,1152]{1,0:T(8,128)(2,1)}, u32[]{:S(2)}, u32[]{:S(2)}) collective-permute-start(bf16[256,1152]{1,0:T(8,128)(2,1)} %get-tuple-element.246), channel_id=1, source_target_pairs={{0,1},{1,0},{2,3},{3,2},{4,5},{5,4},{6,7},{7,6},{8,9},{9,8},{10,11... | collective-permute-start | bytes 1769480 | tf_op jit(solution)/shard_map/ppermute | solution.py:1019
  604.2 33.9 %all-to-all-start.3 = ((bf16[32,8,2304]{2,1,0:T(8,128)(2,1)}), bf16[32,8,2304]{2,1,0:T(8,128)(2,1)S(1)}, u32[]{:S(2)}, u32[]{:S(2)}) async-start(bf16[32,8,2304]{2,1,0:T(8,128)(2,1)} %bitcast.184), calls=%async_computation.5 | async-start | bytes 2359296 | tf_op jit(solution)/shard_map/all_to_all | solution.py:1159
  (208 other events, 2772.8 us)
Sparse Core Ops, SparseCore 0:
  12.8 29.6 all-gather.10
  44.1 90.1 all-gather.12
  136.5 60.8 all-gather.14
  198.8 91.2 all-gather.16
  291.6 52.5 all-gather.18
  457.1 29.3 reduce-scatter.2
  547.7 31.6 reduce-scatter.4

commit v11 on v10

--- a/solution.py
+++ b/solution.py
@@ -910,6 +910,50 @@
     )
 
 
+def shards_kernel(given_ref, lower_ref, taps_ref, own_ref, shared_ref):
+    half = LANES // 2
+    given = given_ref[...].astype(FLOAT)
+    tall, width = given.shape
+    second = pltpu.roll(given, width - UNIT_IN, 1)
+    gate = DSSM // QUERY_HEADS
+    pair_at = 2 * gate + HEAD_SIZE
+    start = 0
+    for low, high in ((0, gate), (gate, 2 * gate), (2 * gate, pair_at)):
+        for unit in (given, second):
+            own_ref[:, start : start + high - low] = unit[:, low:high].astype(BFLOAT)
+            start += high - low
+    lane = lax.broadcasted_iota(jnp.int32, (tall, LANES), 1)
+    heads = NH // QUERY_HEADS
+    steps_at = pair_at + LANES
+    other = pltpu.roll(second[:, steps_at : steps_at + LANES], heads, 1)
+    steps = jnp.where(lane < heads, given[:, steps_at : steps_at + LANES], jnp.where(lane < 2 * heads, other, 0.0))
+    own_ref[:, start : start + LANES] = steps.astype(BFLOAT)
+    rows = lower_ref.shape[0]
+    own_ref[:rows, start + LANES :] = lower_ref[...]
+    own_ref[rows:, start + LANES :] = jnp.zeros((tall - rows, LANES), BFLOAT)
+    first_tile, second_tile = given[:, pair_at:steps_at], second[:, pair_at:steps_at]
+    shared_ref[:tall, :LANES] = jnp.where(lane < half, first_tile, pltpu.roll(second_tile, half, 1)).astype(BFLOAT)
+    shared_ref[:tall, LANES:] = jnp.where(lane < half, pltpu.roll(first_tile, half, 1), second_tile).astype(BFLOAT)
+    shared_ref[tall:, :LANES] = jnp.zeros(taps_ref.shape, BFLOAT)
+    shared_ref[tall:, LANES:] = taps_ref[...]
+
+
+def make_shards(given, lower, taps):
+    tall = given.shape[0]
+    own = 2 * (2 * DSSM // QUERY_HEADS + HEAD_SIZE) + 2 * LANES
+    return pl.pallas_call(
+        shards_kernel,
+        in_specs=[pl.BlockSpec(memory_space=pltpu.VMEM)] * 3,
+        out_specs=[pl.BlockSpec(memory_space=pltpu.VMEM)] * 2,
+        out_shape=[
+            jax.ShapeDtypeStruct((tall, own), BFLOAT),
+            jax.ShapeDtypeStruct((tall + taps.shape[0], 2 * LANES), BFLOAT),
+        ],
+        compiler_params=pltpu.CompilerParams(vmem_limit_bytes=DENSE_BYTES),
+        name="make_shards",
+    )(given, lower, taps)
+
+
 def arrive_kernel(arrived_ref, gain_ref, own_ref, matrix_ref, left_ref, right_ref):
     rows, model = own_ref.shape
     slots = arrived_ref[:, model:].astype(FLOAT).T[0:1, :]
@@ -1173,16 +1217,19 @@
     depth = weight_in.shape[0]
     height = depth + in_raise.shape[0]
     given = after(jnp.concatenate([weight_in, in_raise], axis=0), send_matrix)
-    gates, convs, queries, pairs, states, steps = unit_parts(given, units)
-    pair_width, state_width = pairs.shape[1], states.shape[1]
-    taps = jnp.concatenate([jnp.zeros((KCONV + 1, pair_width), BFLOAT), conv_states], axis=1)
-    taps = jnp.pad(taps, ((0, 16 - KCONV - 1), (0, 0)))
-    shared = jnp.concatenate([jnp.concatenate([pairs, states], axis=1), taps], axis=0)
-    own_columns = jnp.concatenate([gates, convs, queries, pad_columns(steps, LANES)], axis=1)
+    pair_width, state_width = units * PAIR_WIDTH, units * STATE_WIDTH
+    taps = jnp.pad(conv_states, ((0, 16 - KCONV - 1), (0, 0)))
     if fast:
-        shared_shard = shared
+        full = -(-given.shape[1] // LANES) * LANES
+        own_shard, shared_shard = make_shards(pad_columns(given, full), in_lower, taps)
         shared = lax.all_gather(shared_shard, "row", axis=0)
-        weights_own = gather_weight(own_columns[:depth], in_lower, own_columns[depth:])
+        shards.append(own_shard)
+        weights_own = (lax.all_gather(own_shard, "row", axis=0),)
+    else:
+        gates, convs, queries, pairs, states, steps = unit_parts(given, units)
+        taps = jnp.concatenate([jnp.zeros((taps.shape[0], pair_width), BFLOAT), taps], axis=1)
+        shared = jnp.concatenate([jnp.concatenate([pairs, states], axis=1), taps], axis=0)
+        own_columns = jnp.concatenate([gates, convs, queries, pad_columns(steps, LANES)], axis=1)
     arrived = exchange(sent)
     gains = jnp.broadcast_to(norm_gains.astype(FLOAT)[:, None, :], (2, 8, model))
     if fast:

time: 657 us -> 660 us (level)
  waiting for transfers between devices: 206 us -> 218 us
  local copies, waits for them, and re-layouts: 130 us -> 122 us
    all_to_all x4, waiting for transfers between devices: 40.8 us -> 20 us  [local(): lax.all_to_all(values, ALL_AXES, split_axis=0, concat_axis=0, tiled=True)]
    ppermute x55, waiting for transfers between devices: 133 us -> 150 us  [flip(): return lax.ppermute(values, 'col', [(i, i ^ mask) for i in range(4)])]
    all_gather x1, waiting for transfers between devices: 12 us -> 27 us  [local(): shared = lax.all_gather(shared_shard, 'row', axis=0)]
    all_gather x4 -> x3, waiting for transfers between devices: 19.2 us -> 12.7 us  [gather_weight(): return (lax.all_gather(shards[-1], 'row', axis=0),)]
    unnamed x358 -> x350, local copies, waits for them, and re-layouts: 106 us -> 100 us
  transfers between devices with their start and end apart: 66 -> 66, of which waited for: 29 -> 29; matrix products, arithmetic and copies ran while one was open for 9% -> 8% of each run, Pallas kernels for 24% -> 23%
where the time goes in v11:
time: 660 us; the launch traced here: 652 us
  waiting for transfers between devices  218 us (33%)
  Pallas kernels  177 us (27%)
  local copies, waits for them, and re-layouts  122 us (18%)
  starting transfers between devices  86.7 us (13%)
  other arithmetic  20.3 us (3%)
  between operations  17.1 us (3%)
  matrix products  10.5 us (2%)
    ppermute x55, waiting for transfers between devices, flip(): return lax.ppermute(values, 'col', [(i, i ^ mask) for i in range(4)])  150 us
    unnamed x350, local copies, waits for them, and re-layouts  100 us
    ppermute x55, starting transfers between devices, flip(): return lax.ppermute(values, 'col', [(i, i ^ mask) for i in range(4)])  67.4 us
    pallas_call x13, Pallas kernels, spread_blocks(): pl.pallas_call(functools.partial(spread_kernel, masks, len(gathered)), in...  64 us
    pallas_call x6, Pallas kernels, collect_blocks(): pl.pallas_call(functools.partial(collect_kernel, masks, len(gathered)), i...  38.9 us
    pallas_call x2, Pallas kernels, scan_backward(): pl.pallas_call(scan_backward_kernel, grid=(blocks // parts,), in_specs=in...  28.7 us
    all_gather x1, waiting for transfers between devices, local(): shared = lax.all_gather(shared_shard, 'row', axis=0)  27 us
    all_to_all x4, waiting for transfers between devices, local(): lax.all_to_all(values, ALL_AXES, split_axis=0, concat_axis=0, tiled=True)  20 us
  transfers between devices with their start and end apart: 66, of which 29 were waited for; matrix products, arithmetic and copies ran while one was open for 8% of the time, Pallas kernels for 23%

profile of v11, /device:TPU:0, one launch (start us, length us, event | category | flops | bytes accessed | tf_op | source)
XLA Modules:
  0.0 652.0 jit_solution(3699657864529580400)
XLA Ops:
  16.0 7.3 %all-to-all-start = ((bf16[32,8,2176]{2,1,0:T(8,128)(2,1)}), bf16[32,8,2176]{2,1,0:T(8,128)(2,1)S(1)}, u32[]{:S(2)}, u32[]{:S(2)}) async-start(bf16[32,8,2176]{2,1,0:T(8,128)(2,1)} %bitcast.187), calls=%async_computation | async-start | bytes 2228224 | tf_op jit(solution)/shard_map/all_to_all | solution.py:1203
  23.4 27.0 %all-gather.11.cloned.1.call-done = bf16[2304,256]{1,0:T(8,128)(2,1)} async-done(((bf16[288,256]{1,0:T(8,128)(2,1)}), bf16[2304,256]{1,0:T(8,128)(2,1)}) %all-gather.11.cloned.1.call-update) | async-done | bytes 1179664 | tf_op jit(solution)/shard_map/all_gather | solution.py:1225
  60.5 20.1 %collective-permute-done.1 = bf16[8,288,256]{2,1,0:T(8,128)(2,1)} collective-permute-done((bf16[8,288,256]{2,1,0:T(8,128)(2,1)}, bf16[8,288,256]{2,1,0:T(8,128)(2,1)}, u32[]{:S(2)}, u32[]{:S(2)}) %collective-permute-start.1) | collective-permute-done | bytes 1179680 | tf_op jit(solution)/shard_map/ppermute | solution.py:1063
  100.8 12.4 %collective-permute-done.4.rest_1_ = bf16[256,1024]{1,0:T(8,128)(2,1)S(1)} collective-permute-done((bf16[256,1024]{1,0:T(8,128)(2,1)}, bf16[256,1024]{1,0:T(8,128)(2,1)S(1)}, u32[]{:S(2)}, u32[]{:S(2)}) %collective-permute-start.4) | collective-permute-done | bytes 524320 | tf_op jit(solution)/shard_map/ppermute | solution.py:1063
  114.8 12.2 %collective-permute-done.2.rest_0_ = bf16[256,1024]{1,0:T(8,128)(2,1)} collective-permute-done((bf16[256,1024]{1,0:T(8,128)(2,1)}, bf16[256,1024]{1,0:T(8,128)(2,1)}, u32[]{:S(2)}, u32[]{:S(2)}) %collective-permute-start.2) | collective-permute-done | bytes 524320 | tf_op jit(solution)/shard_map/ppermute | solution.py:1063
  144.6 7.5 %spread_blocks.13 = (bf16[1024,2688]{1,0:T(8,128)(2,1)S(1)}, bf16[1024,128]{1,0:T(8,128)(2,1)S(1)}) custom-call(f32[1024,128]{1,0:T(8,128)S(1)} %compare_convert_fusion.chosen_ref, bf16[256,1024]{1,0:T(8,128)(2,1)} %get-tuple-element.142.rest_0_.refs_4_, bf16[256,1024]{1,0:T(8,128)(2,1)} %get-tuple-element.143.rest_1_.refs_5_, ...), custom_call_target="tpu_custom_call" | custom-call | flops 184549376 | bytes 151552 | tf_op jit(solution)/shard_map/spread_blocks/pallas_call | solution.py:675
  152.1 7.1 %spread_blocks.14 = (bf16[1024,2688]{1,0:T(8,128)(2,1)S(1)}, bf16[1024,128]{1,0:T(8,128)(2,1)S(1)}) custom-call(f32[1024,128]{1,0:T(8,128)S(1)} %compare_convert_fusion.chosen_ref, bf16[256,1024]{1,0:T(8,128)(2,1)} %collective-permute-done.9.rest_0_, ...), custom_call_target="tpu_custom_call", output_to_operand_aliasing={{0}: (5, {}), {1}: (6, {})} | custom-call | flops 184549376 | bytes 151552 | tf_op jit(solution)/shard_map/spread_blocks/pallas_call | solution.py:675
  159.2 7.5 %spread_blocks.15 = (bf16[1024,2688]{1,0:T(8,128)(2,1)S(1)}, bf16[1024,128]{1,0:T(8,128)(2,1)S(1)}) custom-call(f32[1024,128]{1,0:T(8,128)S(1)} %compare_convert_fusion.chosen_ref, bf16[256,1024]{1,0:T(8,128)(2,1)} %collective-permute-done.2.rest_0_, ...), custom_call_target="tpu_custom_call", output_to_operand_aliasing={{0}: (5, {}), {1}: (6, {})} | custom-call | flops 184549376 | bytes 151552 | tf_op jit(solution)/shard_map/spread_blocks/pallas_call | solution.py:675
  166.8 7.3 %spread_blocks.16 = (bf16[1024,2688]{1,0:T(8,128)(2,1)S(1)}, bf16[1024,128]{1,0:T(8,128)(2,1)S(1)}) custom-call(f32[1024,128]{1,0:T(8,128)S(1)} %compare_convert_fusion.chosen_ref, bf16[256,1024]{1,0:T(8,128)(2,1)} %collective-permute-done.3.rest_0_, bf16[256,1024]{1,0:T(8,128)(2,1)} %collective-permute-done.5.rest_1_, ...), custom_call_target="tpu_custom_call", output_to_operand_aliasing={{0}: (5, {}), {1}: (6, {})} | custom-call | flops 184549376 | bytes 151552 | tf_op jit(solution)/shard_map/spread_blocks/pallas_call | solution.py:675
  194.3 12.9 %scan_forward.1 = (bf16[1024,1024]{1,0:T(8,128)(2,1)S(1)}, f32[1024,768]{1,0:T(8,128)S(1)}, bf16[4,256,768]{2,1,0:T(8,128)(2,1)S(1)}) custom-call(bf16[1024,2688]{1,0:T(8,128)(2,1)S(1)} %copy-done.3, bf16[1024,2688]{1,0:T(8,128)(2,1)S(1)} %copy-done.3, bf16[1024,2688]{1,0:T(8,128)(2,1)S(1)} %copy-done.3, ...), custom_call_target="tpu_custom_call", output_to_operand_aliasing={{0}: (12, {})} | custom-call | flops 83886080 | bytes 589824 | tf_op jit(solution)/shard_map/scan_forward/pallas_call | solution.py:383
  245.4 17.4 %collective-permute-done.14.second_near = bf16[256,1024]{1,0:T(8,128)(2,1)} collective-permute-done((bf16[256,1024]{1,0:T(8,128)(2,1)}, bf16[256,1024]{1,0:T(8,128)(2,1)}, u32[]{:S(2)}, u32[]{:S(2)}) %collective-permute-start.14) | collective-permute-done | bytes 524320 | tf_op jit(solution)/shard_map/ppermute | solution.py:1063
  286.0 7.5 %collective-permute-done.24.rest_4_ = bf16[256,1024]{1,0:T(8,128)(2,1)} collective-permute-done((bf16[256,1024]{1,0:T(8,128)(2,1)}, bf16[256,1024]{1,0:T(8,128)(2,1)}, u32[]{:S(2)}, u32[]{:S(2)}) %collective-permute-start.24) | collective-permute-done | bytes 524320 | tf_op jit(solution)/shard_map/ppermute | solution.py:1063
  335.6 12.7 %all-gather.19.cloned.1.call-done = bf16[2176,1152]{1,0:T(8,128)(2,1)} async-done(((bf16[272,1152]{1,0:T(8,128)(2,1)}), bf16[2176,1152]{1,0:T(8,128)(2,1)}) %all-gather.19.cloned.1.call-update) | async-done | bytes 5013520 | tf_op jit(solution)/shard_map/all_gather | solution.py:1213
  350.8 10.1 %spread_blocks.21 = (bf16[1024,1024]{1,0:T(8,128)(2,1)S(1)}, bf16[1024,128]{1,0:T(8,128)(2,1)S(1)}) custom-call(f32[1024,128]{1,0:T(8,128)S(1)} %compare_convert_fusion.chosen_ref, bf16[256,1024]{1,0:T(8,128)(2,1)} %get-tuple-element.314.rest_0_, bf16[256,1024]{1,0:T(8,128)(2,1)} %get-tuple-element.313.rest_1_, ...), custom_call_target="tpu_custom_call" | custom-call | flops 301989888 | bytes 393216 | tf_op jit(solution)/shard_map/spread_blocks/pallas_call | solution.py:675
  373.2 8.3 %collect_blocks.10 = (bf16[256,1152]{1,0:T(8,128)(2,1)}, f32[256,1024]{1,0:T(8,128)S(1)}, f32[256,1152]{1,0:T(8,128)S(1)}, bf16[256,1024]{1,0:T(8,128)(2,1)}, f3...) custom-call(bf16[1024,2048]{1,0:T(8,128)(2,1)S(1)} %pad_maximum_fusion.values_ref, bf16[8,272,2176]{2,1,0:T(8,128)(2,1)S(1)} %bitcast.163), custom_call_target="tpu_custom_call" | custom-call | flops 402653184 | bytes 589824 | tf_op jit(solution)/shard_map/collect_blocks/pallas_call | solution.py:744
  424.2 8.8 %collective-permute-done.34.rest_0_ = bf16[256,1024]{1,0:T(8,128)(2,1)S(1)} collective-permute-done((bf16[256,1024]{1,0:T(8,128)(2,1)S(1)}, bf16[256,1024]{1,0:T(8,128)(2,1)S(1)}, u32[]{:S(2)}, u32[]{:S(2)}) %collective-permute-start.34) | collective-permute-done | bytes 524320 | tf_op jit(solution)/shard_map/ppermute | solution.py:1063
  437.7 7.0 %collective-permute-done.39.rest_0_ = bf16[256,1024]{1,0:T(8,128)(2,1)S(1)} collective-permute-done((bf16[256,1024]{1,0:T(8,128)(2,1)S(1)}, bf16[256,1024]{1,0:T(8,128)(2,1)S(1)}, u32[]{:S(2)}, u32[]{:S(2)}) %collective-permute-start.39) | collective-permute-done | bytes 524320 | tf_op jit(solution)/shard_map/ppermute | solution.py:1063
  466.3 7.2 %attention_backward.1 = (bf16[1024,256]{1,0:T(8,128)(2,1)S(1)}, bf16[1024,256]{1,0:T(8,128)(2,1)S(1)}) custom-call(bf16[1024,2688]{1,0:T(8,128)(2,1)S(1)} %copy-done.4, bf16[1024,2688]{1,0:T(8,128)(2,1)S(1)} %copy-done.4, bf16[1024,2688]{1,0:T(8,128)(2,1)S(1)} %copy-done.4, f32[1024,128]{1,0:T(8,128)S(1)} %copy-done.49, f32[1024,128]{1,0:T(8,128)S(1)} %copy-done.47, ...), custom_call_target="tpu_custom_call" | custom-call | flops 100663296 | bytes 393216 | tf_op jit(solution)/shard_map/attention_backward/pallas_call | solution.py:556
  480.3 13.9 %scan_backward.2 = (bf16[1024,2688]{1,0:T(8,128)(2,1)S(1)}, f32[256,768]{1,0:T(8,128)S(1)}, f32[8,768]{1,0:T(8,128)S(1)}, f32[8,512]{1,0:T(8,128)S(1)}) custom-call(bf16[1024,2688]{1,0:T(8,128)(2,1)S(1)} %copy-done.4, bf16[1024,2688]{1,0:T(8,128)(2,1)S(1)} %copy-done.4, bf16[1024,2688]{1,0:T(8,128)(2,1)S(1)} %copy-done.4, bf16[1024,2688]{1,0:T(8,128)(2,1)S(1)} %copy-done.4, ...), custom_call_target="tpu_custom_call" | custom-call | flops 167772160 | bytes 1179648 | tf_op jit(solution)/shard_map/scan_backward/pallas_call | solution.py:426
  514.4 14.9 %scan_backward.3 = (bf16[1024,2688]{1,0:T(8,128)(2,1)S(1)}, f32[256,768]{1,0:T(8,128)}, f32[8,768]{1,0:T(8,128)}, f32[8,512]{1,0:T(8,128)}) custom-call(bf16[1024,2688]{1,0:T(8,128)(2,1)S(1)} %copy-done.5, bf16[1024,2688]{1,0:T(8,128)(2,1)S(1)} %copy-done.5, bf16[1024,2688]{1,0:T(8,128)(2,1)S(1)} %copy-done.5, ...), custom_call_target="tpu_custom_call", output_to_operand_aliasing={{0}: (17, {})} | custom-call | flops 167772160 | bytes 1179648 | tf_op jit(solution)/shard_map/scan_backward/pallas_call | solution.py:426
  531.2 15.0 %collect_blocks.11 = (bf16[256,1152]{1,0:T(8,128)(2,1)S(1)}, bf16[256,1024]{1,0:T(8,128)(2,1)S(1)}, bf16[256,1152]{1,0:T(8,128)(2,1)}, f32[256,1024]{1,0:T(8,128...) custom-call(bf16[1024,2688]{1,0:T(8,128)(2,1)S(1)} %get-tuple-elemen, ...), custom_call_target="tpu_custom_call" | custom-call | flops 704643072 | bytes 868352 | tf_op jit(solution)/shard_map/collect_blocks/pallas_call | solution.py:744
  553.2 12.2 %collective-permute-done.47.second_part = bf16[256,1024]{1,0:T(8,128)(2,1)S(1)} collective-permute-done((bf16[256,1024]{1,0:T(8,128)(2,1)S(1)}, bf16[256,1024]{1,0:T(8,128)(2,1)S(1)}, u32[]{:S(2)}, u32[]{:S(2)}) %collective-permute-start.47) | collective-permute-done | bytes 524320 | tf_op jit(solution)/shard_map/ppermute | solution.py:1063
  585.0 13.3 %collective-permute-done.50.second_near = bf16[256,1024]{1,0:T(8,128)(2,1)} collective-permute-done((bf16[256,1024]{1,0:T(8,128)(2,1)}, bf16[256,1024]{1,0:T(8,128)(2,1)}, u32[]{:S(2)}, u32[]{:S(2)}) %collective-permute-start.50) | collective-permute-done | bytes 524320 | tf_op jit(solution)/shard_map/ppermute | solution.py:1063
  626.0 16.2 %all-to-all-done.3 = bf16[32,8,2304]{2,1,0:T(8,128)(2,1)S(1)} async-done(((bf16[32,8,2304]{2,1,0:T(8,128)(2,1)}), bf16[32,8,2304]{2,1,0:T(8,128)(2,1)S(1)}, u32[]{:S(2)}, u32[]{:S(2)}) %all-to-all-start.3) | async-done | bytes 1179680 | tf_op jit(solution)/shard_map/all_to_all | solution.py:1203
  (625 shorter events, 349.0 us)
Async XLA Ops:
  7.2 43.2 %all-gather.11.cloned.1.call-start = ((), (), s32[]{:S(2)}) async-start(), calls=%async_computation.8 | async-start | bytes 1327104 | tf_op jit(solution)/shard_map/all_gather | solution.py:1225
  13.4 125.7 %all-gather.13.cloned.1.call-start = ((), (), s32[]{:S(2)}) async-start(), calls=%async_computation.9 | async-start | bytes 10027008 | tf_op jit(solution)/shard_map/all_gather | solution.py:1227
  14.2 197.1 %all-gather.15.cloned.1.call-start = ((), (), s32[]{:S(2)}) async-start(), calls=%async_computation.10 | async-start | bytes 5640192 | tf_op jit(solution)/shard_map/all_gather | solution.py:1213
  16.0 44.4 %all-to-all-start = ((bf16[32,8,2176]{2,1,0:T(8,128)(2,1)}), bf16[32,8,2176]{2,1,0:T(8,128)(2,1)S(1)}, u32[]{:S(2)}, u32[]{:S(2)}) async-start(bf16[32,8,2176]{2,1,0:T(8,128)(2,1)} %bitcast.187), calls=%async_computation | async-start | bytes 2228224 | tf_op jit(solution)/shard_map/all_to_all | solution.py:1203
  23.3 285.8 %all-gather.17.cloned.1.call-start = ((), (), s32[]{:S(2)}) async-start(), calls=%async_computation.11 | async-start | bytes 10653696 | tf_op jit(solution)/shard_map/all_gather | solution.py:1213
  50.4 30.2 %collective-permute-start.1 = (bf16[8,288,256]{2,1,0:T(8,128)(2,1)}, bf16[8,288,256]{2,1,0:T(8,128)(2,1)}, u32[]{:S(2)}, u32[]{:S(2)}) collective-permute-start(bf16[8,288,256]{2,1,0:T(8,128)(2,1)} %bitcast.189), channel_id=1, source_target_pairs={{0,2},{1,3},{2,0},{3,1},{4,6},{5,7},{6,4},{7,5},{8,10},{9,11},{10,... | collective-permute-start | bytes 3538952 | tf_op jit(solution)/shard_map/ppermute | solution.py:1063
  84.4 263.9 %all-gather.19.cloned.1.call-start = ((), (), s32[]{:S(2)}) async-start(), calls=%async_computation.12 | async-start | bytes 5640192 | tf_op jit(solution)/shard_map/all_gather | solution.py:1213
  87.4 40.3 %collective-permute-start.7 = (bf16[4,288,256]{2,1,0:T(8,128)(2,1)S(1)}, bf16[4,288,256]{2,1,0:T(8,128)(2,1)S(1)}, u32[]{:S(2)}, u32[]{:S(2)}) collective-permute-start(bf16[4,288,256]{2,1,0:T(8,128)(2,1)S(1)} %slice.431), channel_id=1, source_target_pairs={{0,1},{1,0},{2,3},{3,2},{4,5},{5,4},{6,7},{7,6},{8,9},{9,8},{10,11... | collective-permute-start | bytes 1769480 | tf_op jit(solution)/shard_map/ppermute | solution.py:1063
  90.1 38.7 %collective-permute-start.6 = (bf16[4,288,256]{2,1,0:T(8,128)(2,1)S(1)}, bf16[4,288,256]{2,1,0:T(8,128)(2,1)S(1)}, u32[]{:S(2)}, u32[]{:S(2)}) collective-permute-start(bf16[4,288,256]{2,1,0:T(8,128)(2,1)S(1)} %slice.430), channel_id=1, source_target_pairs={{0,2},{1,3},{2,0},{3,1},{4,6},{5,7},{6,4},{7,5},{8,10},{9,11},{10,... | collective-permute-start | bytes 1769480 | tf_op jit(solution)/shard_map/ppermute | solution.py:1063
  95.0 64.2 %collective-permute-start.8 = (bf16[256,1024]{1,0:T(8,128)(2,1)}, bf16[256,1024]{1,0:T(8,128)(2,1)S(1)}, u32[]{:S(2)}, u32[]{:S(2)}) collective-permute-start(bf16[256,1024]{1,0:T(8,128)(2,1)} %get-tuple-element.143.rest_1_.refs_5_), channel_id=1, source_target_pairs={{0,2},{1,3},{2,0},{3,1},{4,6},{5,7},{6,4},{7,5},{8,10},{9,11},{10,... | collective-permute-start | bytes 1572872 | tf_op jit(solution)/shard_map/ppermute | solution.py:1063
  113.2 38.9 %collective-permute-start.9 = (bf16[256,1024]{1,0:T(8,128)(2,1)}, bf16[256,1024]{1,0:T(8,128)(2,1)}, u32[]{:S(2)}, u32[]{:S(2)}) collective-permute-start(bf16[256,1024]{1,0:T(8,128)(2,1)} %get-tuple-element.142.rest_0_.refs_4_), channel_id=1, source_target_pairs={{0,1},{1,0},{2,3},{3,2},{4,5},{5,4},{6,7},{7,6},{8,9},{9,8},{10,11... | collective-permute-start | bytes 1572872 | tf_op jit(solution)/shard_map/ppermute | solution.py:1063
  127.0 39.7 %collective-permute-start.5 = (bf16[256,1024]{1,0:T(8,128)(2,1)S(1)}, bf16[256,1024]{1,0:T(8,128)(2,1)}, u32[]{:S(2)}, u32[]{:S(2)}) collective-permute-start(bf16[256,1024]{1,0:T(8,128)(2,1)S(1)} %collective-permute-done.4.rest_1_), channel_id=1, source_target_pairs={{0,2},{1,3},{2,0},{3,1},{4,6},{5,7},{6,4},{7,5},{8,10},{9,11},{10,... | collective-permute-start | bytes 1572872 | tf_op jit(solution)/shard_map/ppermute | solution.py:1063
  127.7 39.1 %collective-permute-start.3 = (bf16[256,1024]{1,0:T(8,128)(2,1)}, bf16[256,1024]{1,0:T(8,128)(2,1)}, u32[]{:S(2)}, u32[]{:S(2)}) collective-permute-start(bf16[256,1024]{1,0:T(8,128)(2,1)} %collective-permute-done.2.rest_0_), channel_id=1, source_target_pairs={{0,1},{1,0},{2,3},{3,2},{4,5},{5,4},{6,7},{7,6},{8,9},{9,8},{10,11... | collective-permute-start | bytes 1572872 | tf_op jit(solution)/shard_map/ppermute | solution.py:1063
  180.0 59.4 %all-to-all-start.1 = ((bf16[32,8,2048]{2,1,0:T(8,128)(2,1)}), bf16[32,8,2048]{2,1,0:T(8,128)(2,1)}, u32[]{:S(2)}, u32[]{:S(2)}) async-start(bf16[32,8,2048]{2,1,0:T(8,128)(2,1)} %fusion.9), calls=%async_computation.1 | async-start | bytes 2097152 | tf_op jit(solution)/shard_map/all_to_all | solution.py:1203
  183.4 396.8 %reduce-scatter.3.cloned.1.call-start = ((), (), s32[]{:S(2)}) async-start(), calls=%async_computation.6 | async-start | bytes 1179648 | tf_op jit(solution)/shard_map/reduce_scatter | solution.py:1430
  273.1 31.6 %collective-permute-start.20 = (bf16[256,1024]{1,0:T(8,128)(2,1)S(1)}, bf16[256,1024]{1,0:T(8,128)(2,1)S(1)}, u32[]{:S(2)}, u32[]{:S(2)}) collective-permute-start(bf16[256,1024]{1,0:T(8,128)(2,1)S(1)} %get-tuple-element.168.rest_1_.refs_5_), channel_id=1, source_target_pairs={{0,2},{1,3},{2,0},{3,1},{4,6},{5,7},{6,4},{7,5},{8,10},{9,11},{10,... | collective-permute-start | bytes 1572872 | tf_op jit(solution)/shard_map/ppermute | solution.py:1063
  284.3 42.6 %collective-permute-start.19 = (bf16[256,1024]{1,0:T(8,128)(2,1)}, bf16[256,1024]{1,0:T(8,128)(2,1)}, u32[]{:S(2)}, u32[]{:S(2)}) collective-permute-start(bf16[256,1024]{1,0:T(8,128)(2,1)} %collective-permute-done.18.rest_1_), channel_id=1, source_target_pairs={{0,2},{1,3},{2,0},{3,1},{4,6},{5,7},{6,4},{7,5},{8,10},{9,11},{10,... | collective-permute-start | bytes 1572872 | tf_op jit(solution)/shard_map/ppermute | solution.py:1063
  293.5 39.8 %collective-permute-start.25 = (bf16[256,1024]{1,0:T(8,128)(2,1)}, bf16[256,1024]{1,0:T(8,128)(2,1)}, u32[]{:S(2)}, u32[]{:S(2)}) collective-permute-start(bf16[256,1024]{1,0:T(8,128)(2,1)} %get-tuple-element.313.rest_1_), channel_id=1, source_target_pairs={{0,2},{1,3},{2,0},{3,1},{4,6},{5,7},{6,4},{7,5},{8,10},{9,11},{10,... | collective-permute-start | bytes 1572872 | tf_op jit(solution)/shard_map/ppermute | solution.py:1063
  296.3 37.1 %collective-permute-start.22 = (bf16[256,1024]{1,0:T(8,128)(2,1)}, bf16[256,1024]{1,0:T(8,128)(2,1)}, u32[]{:S(2)}, u32[]{:S(2)}) collective-permute-start(bf16[256,1024]{1,0:T(8,128)(2,1)} %get-tuple-element.314.rest_0_), channel_id=1, source_target_pairs={{0,1},{1,0},{2,3},{3,2},{4,5},{5,4},{6,7},{7,6},{8,9},{9,8},{10,11... | collective-permute-start | bytes 1572872 | tf_op jit(solution)/shard_map/ppermute | solution.py:1063
  461.2 36.9 %collective-permute-start.40 = (bf16[256,1152]{1,0:T(8,128)(2,1)}, bf16[256,1152]{1,0:T(8,128)(2,1)S(1)}, u32[]{:S(2)}, u32[]{:S(2)}) collective-permute-start(bf16[256,1152]{1,0:T(8,128)(2,1)} %copy-done.126), channel_id=1, source_target_pairs={{0,1},{1,0},{2,3},{3,2},{4,5},{5,4},{6,7},{7,6},{8,9},{9,8},{10,11... | collective-permute-start | bytes 1769480 | tf_op jit(solution)/shard_map/ppermute | solution.py:1063
  500.7 84.3 %all-to-all-start.2 = ((bf16[32,8,2816]{2,1,0:T(8,128)(2,1)}), bf16[32,8,2816]{2,1,0:T(8,128)(2,1)}, u32[]{:S(2)}, u32[]{:S(2)}) async-start(bf16[32,8,2816]{2,1,0:T(8,128)(2,1)} %bitcast.40), calls=%async_computation.2 | async-start | bytes 2883584 | tf_op jit(solution)/shard_map/all_to_all | solution.py:1203
  504.3 79.2 %reduce-scatter.5.cloned.1.call-start = ((), (), s32[]{:S(2)}) async-start(), calls=%async_computation.7 | async-start | bytes 774144 | tf_op jit(solution)/shard_map/reduce_scatter | solution.py:1430
  566.3 32.0 %collective-permute-start.48 = (bf16[256,1152]{1,0:T(8,128)(2,1)}, bf16[256,1152]{1,0:T(8,128)(2,1)}, u32[]{:S(2)}, u32[]{:S(2)}) collective-permute-start(bf16[256,1152]{1,0:T(8,128)(2,1)} %get-tuple-element.250), channel_id=1, source_target_pairs={{0,1},{1,0},{2,3},{3,2},{4,5},{5,4},{6,7},{7,6},{8,9},{9,8},{10,11... | collective-permute-start | bytes 1769480 | tf_op jit(solution)/shard_map/ppermute | solution.py:1063
  608.4 33.9 %all-to-all-start.3 = ((bf16[32,8,2304]{2,1,0:T(8,128)(2,1)}), bf16[32,8,2304]{2,1,0:T(8,128)(2,1)S(1)}, u32[]{:S(2)}, u32[]{:S(2)}) async-start(bf16[32,8,2304]{2,1,0:T(8,128)(2,1)} %bitcast.184), calls=%async_computation.5 | async-start | bytes 2359296 | tf_op jit(solution)/shard_map/all_to_all | solution.py:1203
  (207 other events, 2793.3 us)
Sparse Core Ops, SparseCore 0:
  13.5 36.7 all-gather.10
  52.0 87.0 all-gather.12
  141.3 60.2 all-gather.14
  203.1 91.0 all-gather.16
  295.7 52.5 all-gather.18
  461.3 29.3 reduce-scatter.2
  551.8 31.5 reduce-scatter.4

commit v12 on v11

--- a/solution.py
+++ b/solution.py
@@ -1230,7 +1230,7 @@
         taps = jnp.concatenate([jnp.zeros((taps.shape[0], pair_width), BFLOAT), taps], axis=1)
         shared = jnp.concatenate([jnp.concatenate([pairs, states], axis=1), taps], axis=0)
         own_columns = jnp.concatenate([gates, convs, queries, pad_columns(steps, LANES)], axis=1)
-    arrived = exchange(sent)
+    arrived = exchange(after(sent, shared) if fast else sent)
     gains = jnp.broadcast_to(norm_gains.astype(FLOAT)[:, None, :], (2, 8, model))
     if fast:
         near, far = flip(shared, 1), flip(shared, 2)

time: 660 us -> 666 us (level)
  waiting for transfers between devices: 218 us -> 227 us
    all_to_all x4, waiting for transfers between devices: 20 us -> 28.2 us  [local(): lax.all_to_all(values, ALL_AXES, split_axis=0, concat_axis=0, tiled=True)]
    unnamed x350 -> x354, local copies, waits for them, and re-layouts: 100 us -> 98.8 us
  transfers between devices with their start and end apart: 66 -> 66, of which waited for: 29 -> 30; matrix products, arithmetic and copies ran while one was open for 8% -> 7% of each run, Pallas kernels for 23% -> 23%
where the time goes in v12:
time: 666 us; the launch traced here: 658 us
  waiting for transfers between devices  227 us (34%)
  Pallas kernels  177 us (27%)
  local copies, waits for them, and re-layouts  120 us (18%)
  starting transfers between devices  84.9 us (13%)
  other arithmetic  20.7 us (3%)
  between operations  17.1 us (3%)
  matrix products  10.5 us (2%)
    ppermute x55, waiting for transfers between devices, flip(): return lax.ppermute(values, 'col', [(i, i ^ mask) for i in range(4)])  156 us
    unnamed x354, local copies, waits for them, and re-layouts  98.8 us
    ppermute x55, starting transfers between devices, flip(): return lax.ppermute(values, 'col', [(i, i ^ mask) for i in range(4)])  68.2 us
    pallas_call x13, Pallas kernels, spread_blocks(): pl.pallas_call(functools.partial(spread_kernel, masks, len(gathered)), in...  63.9 us
    pallas_call x6, Pallas kernels, collect_blocks(): pl.pallas_call(functools.partial(collect_kernel, masks, len(gathered)), i...  38.9 us
    pallas_call x2, Pallas kernels, scan_backward(): pl.pallas_call(scan_backward_kernel, grid=(blocks // parts,), in_specs=in...  28.8 us
    all_to_all x4, waiting for transfers between devices, local(): lax.all_to_all(values, ALL_AXES, split_axis=0, concat_axis=0, tiled=True)  28.2 us
    all_gather x1, waiting for transfers between devices, local(): shared = lax.all_gather(shared_shard, 'row', axis=0)  22.9 us
  transfers between devices with their start and end apart: 66, of which 30 were waited for; matrix products, arithmetic and copies ran while one was open for 7% of the time, Pallas kernels for 23%

profile of v12, /device:TPU:0, one launch (start us, length us, event | category | flops | bytes accessed | tf_op | source)
XLA Modules:
  0.0 658.0 jit_solution(11889463923465325951)
XLA Ops:
  16.0 22.9 %all-gather.11.cloned.1.call-done = bf16[2304,256]{1,0:T(8,128)(2,1)} async-done(((bf16[288,256]{1,0:T(8,128)(2,1)}), bf16[2304,256]{1,0:T(8,128)(2,1)}) %all-gather.11.cloned.1.call-update) | async-done | bytes 1179664 | tf_op jit(solution)/shard_map/all_gather | solution.py:1225
  49.2 33.1 %collective-permute-done.1 = bf16[8,288,256]{2,1,0:T(8,128)(2,1)S(1)} collective-permute-done((bf16[8,288,256]{2,1,0:T(8,128)(2,1)}, bf16[8,288,256]{2,1,0:T(8,128)(2,1)S(1)}, u32[]{:S(2)}, u32[]{:S(2)}) %collective-permute-start.1) | collective-permute-done | bytes 1179680 | tf_op jit(solution)/shard_map/ppermute | solution.py:1063
  83.4 12.0 %all-to-all-done = bf16[32,8,2176]{2,1,0:T(8,128)(2,1)S(1)} async-done(((bf16[32,8,2176]{2,1,0:T(8,128)(2,1)}), bf16[32,8,2176]{2,1,0:T(8,128)(2,1)S(1)}, u32[]{:S(2)}, u32[]{:S(2)}) %all-to-all-start) | async-done | bytes 1114144 | tf_op jit(solution)/shard_map/all_to_all | solution.py:1203
  124.9 10.3 %collective-permute-done.4.rest_1_ = bf16[256,1024]{1,0:T(8,128)(2,1)S(1)} collective-permute-done((bf16[256,1024]{1,0:T(8,128)(2,1)}, bf16[256,1024]{1,0:T(8,128)(2,1)S(1)}, u32[]{:S(2)}, u32[]{:S(2)}) %collective-permute-start.4) | collective-permute-done | bytes 524320 | tf_op jit(solution)/shard_map/ppermute | solution.py:1063
  150.0 7.5 %spread_blocks.13 = (bf16[1024,2688]{1,0:T(8,128)(2,1)S(1)}, bf16[1024,128]{1,0:T(8,128)(2,1)S(1)}) custom-call(f32[1024,128]{1,0:T(8,128)S(1)} %compare_convert_fusion.chosen_ref, bf16[256,1024]{1,0:T(8,128)(2,1)} %get-tuple-element.144.rest_0_.refs_4_, bf16[256,1024]{1,0:T(8,128)(2,1)} %get-tuple-element.145.rest_1_.refs_5_, ...), custom_call_target="tpu_custom_call" | custom-call | flops 184549376 | bytes 151552 | tf_op jit(solution)/shard_map/spread_blocks/pallas_call | solution.py:675
  157.5 7.1 %spread_blocks.14 = (bf16[1024,2688]{1,0:T(8,128)(2,1)S(1)}, bf16[1024,128]{1,0:T(8,128)(2,1)S(1)}) custom-call(f32[1024,128]{1,0:T(8,128)S(1)} %compare_convert_fusion.chosen_ref, bf16[256,1024]{1,0:T(8,128)(2,1)} %collective-permute-done.9.rest_0_, ...), custom_call_target="tpu_custom_call", output_to_operand_aliasing={{0}: (5, {}), {1}: (6, {})} | custom-call | flops 184549376 | bytes 151552 | tf_op jit(solution)/shard_map/spread_blocks/pallas_call | solution.py:675
  164.6 7.5 %spread_blocks.15 = (bf16[1024,2688]{1,0:T(8,128)(2,1)S(1)}, bf16[1024,128]{1,0:T(8,128)(2,1)S(1)}) custom-call(f32[1024,128]{1,0:T(8,128)S(1)} %compare_convert_fusion.chosen_ref, bf16[256,1024]{1,0:T(8,128)(2,1)S(1)} %collective-permute-done.2.rest_0_, ...), custom_call_target="tpu_custom_call", output_to_operand_aliasing={{0}: (5, {}), {1}: (6, {})} | custom-call | flops 184549376 | bytes 151552 | tf_op jit(solution)/shard_map/spread_blocks/pallas_call | solution.py:675
  172.2 7.3 %spread_blocks.16 = (bf16[1024,2688]{1,0:T(8,128)(2,1)S(1)}, bf16[1024,128]{1,0:T(8,128)(2,1)S(1)}) custom-call(f32[1024,128]{1,0:T(8,128)S(1)} %compare_convert_fusion.chosen_ref, bf16[256,1024]{1,0:T(8,128)(2,1)} %collective-permute-done.3.rest_0_, bf16[256,1024]{1,0:T(8,128)(2,1)} %collective-permute-done.5.rest_1_, ...), custom_call_target="tpu_custom_call", output_to_operand_aliasing={{0}: (5, {}), {1}: (6, {})} | custom-call | flops 184549376 | bytes 151552 | tf_op jit(solution)/shard_map/spread_blocks/pallas_call | solution.py:675
  200.0 12.9 %scan_forward.1 = (bf16[1024,1024]{1,0:T(8,128)(2,1)S(1)}, f32[1024,768]{1,0:T(8,128)S(1)}, bf16[4,256,768]{2,1,0:T(8,128)(2,1)S(1)}) custom-call(bf16[1024,2688]{1,0:T(8,128)(2,1)S(1)} %copy-done.3, bf16[1024,2688]{1,0:T(8,128)(2,1)S(1)} %copy-done.3, bf16[1024,2688]{1,0:T(8,128)(2,1)S(1)} %copy-done.3, ...), custom_call_target="tpu_custom_call", output_to_operand_aliasing={{0}: (12, {})} | custom-call | flops 83886080 | bytes 589824 | tf_op jit(solution)/shard_map/scan_forward/pallas_call | solution.py:383
  251.2 17.4 %collective-permute-done.14.second_near = bf16[256,1024]{1,0:T(8,128)(2,1)} collective-permute-done((bf16[256,1024]{1,0:T(8,128)(2,1)}, bf16[256,1024]{1,0:T(8,128)(2,1)}, u32[]{:S(2)}, u32[]{:S(2)}) %collective-permute-start.14) | collective-permute-done | bytes 524320 | tf_op jit(solution)/shard_map/ppermute | solution.py:1063
  291.7 7.5 %collective-permute-done.24.rest_4_ = bf16[256,1024]{1,0:T(8,128)(2,1)} collective-permute-done((bf16[256,1024]{1,0:T(8,128)(2,1)}, bf16[256,1024]{1,0:T(8,128)(2,1)}, u32[]{:S(2)}, u32[]{:S(2)}) %collective-permute-start.24) | collective-permute-done | bytes 524320 | tf_op jit(solution)/shard_map/ppermute | solution.py:1063
  303.7 6.7 %collective-permute-done.20.rest_1_ = bf16[256,1024]{1,0:T(8,128)(2,1)S(1)} collective-permute-done((bf16[256,1024]{1,0:T(8,128)(2,1)S(1)}, bf16[256,1024]{1,0:T(8,128)(2,1)S(1)}, u32[]{:S(2)}, u32[]{:S(2)}) %collective-permute-start.20) | collective-permute-done | bytes 524320 | tf_op jit(solution)/shard_map/ppermute | solution.py:1063
  341.3 13.0 %all-gather.19.cloned.1.call-done = bf16[2176,1152]{1,0:T(8,128)(2,1)} async-done(((bf16[272,1152]{1,0:T(8,128)(2,1)}), bf16[2176,1152]{1,0:T(8,128)(2,1)}) %all-gather.19.cloned.1.call-update) | async-done | bytes 5013520 | tf_op jit(solution)/shard_map/all_gather | solution.py:1213
  356.8 10.1 %spread_blocks.21 = (bf16[1024,1024]{1,0:T(8,128)(2,1)S(1)}, bf16[1024,128]{1,0:T(8,128)(2,1)S(1)}) custom-call(f32[1024,128]{1,0:T(8,128)S(1)} %compare_convert_fusion.chosen_ref, bf16[256,1024]{1,0:T(8,128)(2,1)} %get-tuple-element.316.rest_0_, bf16[256,1024]{1,0:T(8,128)(2,1)} %get-tuple-element.315.rest_1_, ...), custom_call_target="tpu_custom_call" | custom-call | flops 301989888 | bytes 393216 | tf_op jit(solution)/shard_map/spread_blocks/pallas_call | solution.py:675
  379.2 8.3 %collect_blocks.10 = (bf16[256,1152]{1,0:T(8,128)(2,1)}, f32[256,1024]{1,0:T(8,128)S(1)}, f32[256,1152]{1,0:T(8,128)S(1)}, bf16[256,1024]{1,0:T(8,128)(2,1)}, f3...) custom-call(bf16[1024,2048]{1,0:T(8,128)(2,1)S(1)} %pad_maximum_fusion.values_ref, bf16[8,272,2176]{2,1,0:T(8,128)(2,1)S(1)} %bitcast.163), custom_call_target="tpu_custom_call" | custom-call | flops 402653184 | bytes 589824 | tf_op jit(solution)/shard_map/collect_blocks/pallas_call | solution.py:744
  430.1 8.8 %collective-permute-done.34.rest_0_ = bf16[256,1024]{1,0:T(8,128)(2,1)S(1)} collective-permute-done((bf16[256,1024]{1,0:T(8,128)(2,1)S(1)}, bf16[256,1024]{1,0:T(8,128)(2,1)S(1)}, u32[]{:S(2)}, u32[]{:S(2)}) %collective-permute-start.34) | collective-permute-done | bytes 524320 | tf_op jit(solution)/shard_map/ppermute | solution.py:1063
  443.7 7.1 %collective-permute-done.39.rest_0_ = bf16[256,1024]{1,0:T(8,128)(2,1)S(1)} collective-permute-done((bf16[256,1024]{1,0:T(8,128)(2,1)S(1)}, bf16[256,1024]{1,0:T(8,128)(2,1)S(1)}, u32[]{:S(2)}, u32[]{:S(2)}) %collective-permute-start.39) | collective-permute-done | bytes 524320 | tf_op jit(solution)/shard_map/ppermute | solution.py:1063
  472.2 7.2 %attention_backward.1 = (bf16[1024,256]{1,0:T(8,128)(2,1)S(1)}, bf16[1024,256]{1,0:T(8,128)(2,1)S(1)}) custom-call(bf16[1024,2688]{1,0:T(8,128)(2,1)S(1)} %copy-done.4, bf16[1024,2688]{1,0:T(8,128)(2,1)S(1)} %copy-done.4, bf16[1024,2688]{1,0:T(8,128)(2,1)S(1)} %copy-done.4, f32[1024,128]{1,0:T(8,128)S(1)} %copy-done.49, f32[1024,128]{1,0:T(8,128)S(1)} %copy-done.47, ...), custom_call_target="tpu_custom_call" | custom-call | flops 100663296 | bytes 393216 | tf_op jit(solution)/shard_map/attention_backward/pallas_call | solution.py:556
  486.2 13.9 %scan_backward.2 = (bf16[1024,2688]{1,0:T(8,128)(2,1)S(1)}, f32[256,768]{1,0:T(8,128)S(1)}, f32[8,768]{1,0:T(8,128)S(1)}, f32[8,512]{1,0:T(8,128)S(1)}) custom-call(bf16[1024,2688]{1,0:T(8,128)(2,1)S(1)} %copy-done.4, bf16[1024,2688]{1,0:T(8,128)(2,1)S(1)} %copy-done.4, bf16[1024,2688]{1,0:T(8,128)(2,1)S(1)} %copy-done.4, bf16[1024,2688]{1,0:T(8,128)(2,1)S(1)} %copy-done.4, ...), custom_call_target="tpu_custom_call" | custom-call | flops 167772160 | bytes 1179648 | tf_op jit(solution)/shard_map/scan_backward/pallas_call | solution.py:426
  520.3 14.9 %scan_backward.3 = (bf16[1024,2688]{1,0:T(8,128)(2,1)S(1)}, f32[256,768]{1,0:T(8,128)}, f32[8,768]{1,0:T(8,128)}, f32[8,512]{1,0:T(8,128)}) custom-call(bf16[1024,2688]{1,0:T(8,128)(2,1)S(1)} %copy-done.5, bf16[1024,2688]{1,0:T(8,128)(2,1)S(1)} %copy-done.5, bf16[1024,2688]{1,0:T(8,128)(2,1)S(1)} %copy-done.5, ...), custom_call_target="tpu_custom_call", output_to_operand_aliasing={{0}: (17, {})} | custom-call | flops 167772160 | bytes 1179648 | tf_op jit(solution)/shard_map/scan_backward/pallas_call | solution.py:426
  537.2 15.0 %collect_blocks.11 = (bf16[256,1152]{1,0:T(8,128)(2,1)S(1)}, bf16[256,1024]{1,0:T(8,128)(2,1)S(1)}, bf16[256,1152]{1,0:T(8,128)(2,1)}, f32[256,1024]{1,0:T(8,128...) custom-call(bf16[1024,2688]{1,0:T(8,128)(2,1)S(1)} %get-tuple-elemen, ...), custom_call_target="tpu_custom_call" | custom-call | flops 704643072 | bytes 868352 | tf_op jit(solution)/shard_map/collect_blocks/pallas_call | solution.py:744
  559.2 12.2 %collective-permute-done.47.second_part = bf16[256,1024]{1,0:T(8,128)(2,1)S(1)} collective-permute-done((bf16[256,1024]{1,0:T(8,128)(2,1)S(1)}, bf16[256,1024]{1,0:T(8,128)(2,1)S(1)}, u32[]{:S(2)}, u32[]{:S(2)}) %collective-permute-start.47) | collective-permute-done | bytes 524320 | tf_op jit(solution)/shard_map/ppermute | solution.py:1063
  591.0 13.3 %collective-permute-done.50.second_near = bf16[256,1024]{1,0:T(8,128)(2,1)} collective-permute-done((bf16[256,1024]{1,0:T(8,128)(2,1)}, bf16[256,1024]{1,0:T(8,128)(2,1)}, u32[]{:S(2)}, u32[]{:S(2)}) %collective-permute-start.50) | collective-permute-done | bytes 524320 | tf_op jit(solution)/shard_map/ppermute | solution.py:1063
  632.0 16.2 %all-to-all-done.3 = bf16[32,8,2304]{2,1,0:T(8,128)(2,1)S(1)} async-done(((bf16[32,8,2304]{2,1,0:T(8,128)(2,1)}), bf16[32,8,2304]{2,1,0:T(8,128)(2,1)S(1)}, u32[]{:S(2)}, u32[]{:S(2)}) %all-to-all-start.3) | async-done | bytes 1179680 | tf_op jit(solution)/shard_map/all_to_all | solution.py:1203
  (629 shorter events, 348.9 us)
Async XLA Ops:
  7.2 31.7 %all-gather.11.cloned.1.call-start = ((), (), s32[]{:S(2)}) async-start(), calls=%async_computation.8 | async-start | bytes 1327104 | tf_op jit(solution)/shard_map/all_gather | solution.py:1225
  13.4 131.1 %all-gather.13.cloned.1.call-start = ((), (), s32[]{:S(2)}) async-start(), calls=%async_computation.9 | async-start | bytes 10027008 | tf_op jit(solution)/shard_map/all_gather | solution.py:1227
  14.2 202.8 %all-gather.15.cloned.1.call-start = ((), (), s32[]{:S(2)}) async-start(), calls=%async_computation.10 | async-start | bytes 5640192 | tf_op jit(solution)/shard_map/all_gather | solution.py:1213
  38.9 56.4 %all-to-all-start = ((bf16[32,8,2176]{2,1,0:T(8,128)(2,1)}), bf16[32,8,2176]{2,1,0:T(8,128)(2,1)S(1)}, u32[]{:S(2)}, u32[]{:S(2)}) async-start(bf16[32,8,2176]{2,1,0:T(8,128)(2,1)} %bitcast.187), calls=%async_computation | async-start | bytes 2228224 | tf_op jit(solution)/shard_map/all_to_all | solution.py:1203
  43.3 271.6 %all-gather.17.cloned.1.call-start = ((), (), s32[]{:S(2)}) async-start(), calls=%async_computation.11 | async-start | bytes 10653696 | tf_op jit(solution)/shard_map/all_gather | solution.py:1213
  43.4 38.9 %collective-permute-start.1 = (bf16[8,288,256]{2,1,0:T(8,128)(2,1)}, bf16[8,288,256]{2,1,0:T(8,128)(2,1)S(1)}, u32[]{:S(2)}, u32[]{:S(2)}) collective-permute-start(bf16[8,288,256]{2,1,0:T(8,128)(2,1)} %bitcast.189), channel_id=1, source_target_pairs={{0,2},{1,3},{2,0},{3,1},{4,6},{5,7},{6,4},{7,5},{8,10},{9,11},{10,... | collective-permute-start | bytes 3538952 | tf_op jit(solution)/shard_map/ppermute | solution.py:1063
  45.2 38.2 %collective-permute-start = (bf16[8,288,256]{2,1,0:T(8,128)(2,1)}, bf16[8,288,256]{2,1,0:T(8,128)(2,1)}, u32[]{:S(2)}, u32[]{:S(2)}) collective-permute-start(bf16[8,288,256]{2,1,0:T(8,128)(2,1)} %bitcast.190), channel_id=1, source_target_pairs={{0,1},{1,0},{2,3},{3,2},{4,5},{5,4},{6,7},{7,6},{8,9},{9,8},{10,11... | collective-permute-start | bytes 3538952 | tf_op jit(solution)/shard_map/ppermute | solution.py:1063
  98.2 256.1 %all-gather.19.cloned.1.call-start = ((), (), s32[]{:S(2)}) async-start(), calls=%async_computation.12 | async-start | bytes 5640192 | tf_op jit(solution)/shard_map/all_gather | solution.py:1213
  123.0 34.5 %collective-permute-start.9 = (bf16[256,1024]{1,0:T(8,128)(2,1)}, bf16[256,1024]{1,0:T(8,128)(2,1)}, u32[]{:S(2)}, u32[]{:S(2)}) collective-permute-start(bf16[256,1024]{1,0:T(8,128)(2,1)} %get-tuple-element.144.rest_0_.refs_4_), channel_id=1, source_target_pairs={{0,1},{1,0},{2,3},{3,2},{4,5},{5,4},{6,7},{7,6},{8,9},{9,8},{10,11... | collective-permute-start | bytes 1572872 | tf_op jit(solution)/shard_map/ppermute | solution.py:1063
  124.6 40.1 %collective-permute-start.8 = (bf16[256,1024]{1,0:T(8,128)(2,1)}, bf16[256,1024]{1,0:T(8,128)(2,1)}, u32[]{:S(2)}, u32[]{:S(2)}) collective-permute-start(bf16[256,1024]{1,0:T(8,128)(2,1)} %get-tuple-element.145.rest_1_.refs_5_), channel_id=1, source_target_pairs={{0,2},{1,3},{2,0},{3,1},{4,6},{5,7},{6,4},{7,5},{8,10},{9,11},{10,... | collective-permute-start | bytes 1572872 | tf_op jit(solution)/shard_map/ppermute | solution.py:1063
  135.2 37.0 %collective-permute-start.5 = (bf16[256,1024]{1,0:T(8,128)(2,1)S(1)}, bf16[256,1024]{1,0:T(8,128)(2,1)}, u32[]{:S(2)}, u32[]{:S(2)}) collective-permute-start(bf16[256,1024]{1,0:T(8,128)(2,1)S(1)} %collective-permute-done.4.rest_1_), channel_id=1, source_target_pairs={{0,2},{1,3},{2,0},{3,1},{4,6},{5,7},{6,4},{7,5},{8,10},{9,11},{10,... | collective-permute-start | bytes 1572872 | tf_op jit(solution)/shard_map/ppermute | solution.py:1063
  136.9 35.2 %collective-permute-start.3 = (bf16[256,1024]{1,0:T(8,128)(2,1)S(1)}, bf16[256,1024]{1,0:T(8,128)(2,1)}, u32[]{:S(2)}, u32[]{:S(2)}) collective-permute-start(bf16[256,1024]{1,0:T(8,128)(2,1)S(1)} %collective-permute-done.2.rest_0_), channel_id=1, source_target_pairs={{0,1},{1,0},{2,3},{3,2},{4,5},{5,4},{6,7},{7,6},{8,9},{9,8},{10,11... | collective-permute-start | bytes 1572872 | tf_op jit(solution)/shard_map/ppermute | solution.py:1063
  185.3 59.8 %all-to-all-start.1 = ((bf16[32,8,2048]{2,1,0:T(8,128)(2,1)}), bf16[32,8,2048]{2,1,0:T(8,128)(2,1)}, u32[]{:S(2)}, u32[]{:S(2)}) async-start(bf16[32,8,2048]{2,1,0:T(8,128)(2,1)} %fusion.9), calls=%async_computation.1 | async-start | bytes 2097152 | tf_op jit(solution)/shard_map/all_to_all | solution.py:1203
  189.1 397.0 %reduce-scatter.3.cloned.1.call-start = ((), (), s32[]{:S(2)}) async-start(), calls=%async_computation.6 | async-start | bytes 1179648 | tf_op jit(solution)/shard_map/reduce_scatter | solution.py:1430
  278.9 31.5 %collective-permute-start.20 = (bf16[256,1024]{1,0:T(8,128)(2,1)S(1)}, bf16[256,1024]{1,0:T(8,128)(2,1)S(1)}, u32[]{:S(2)}, u32[]{:S(2)}) collective-permute-start(bf16[256,1024]{1,0:T(8,128)(2,1)S(1)} %get-tuple-element.170.rest_1_.refs_5_), channel_id=1, source_target_pairs={{0,2},{1,3},{2,0},{3,1},{4,6},{5,7},{6,4},{7,5},{8,10},{9,11},{10,... | collective-permute-start | bytes 1572872 | tf_op jit(solution)/shard_map/ppermute | solution.py:1063
  290.1 42.5 %collective-permute-start.19 = (bf16[256,1024]{1,0:T(8,128)(2,1)}, bf16[256,1024]{1,0:T(8,128)(2,1)}, u32[]{:S(2)}, u32[]{:S(2)}) collective-permute-start(bf16[256,1024]{1,0:T(8,128)(2,1)} %collective-permute-done.18.rest_1_), channel_id=1, source_target_pairs={{0,2},{1,3},{2,0},{3,1},{4,6},{5,7},{6,4},{7,5},{8,10},{9,11},{10,... | collective-permute-start | bytes 1572872 | tf_op jit(solution)/shard_map/ppermute | solution.py:1063
  299.2 39.9 %collective-permute-start.25 = (bf16[256,1024]{1,0:T(8,128)(2,1)}, bf16[256,1024]{1,0:T(8,128)(2,1)}, u32[]{:S(2)}, u32[]{:S(2)}) collective-permute-start(bf16[256,1024]{1,0:T(8,128)(2,1)} %get-tuple-element.315.rest_1_), channel_id=1, source_target_pairs={{0,2},{1,3},{2,0},{3,1},{4,6},{5,7},{6,4},{7,5},{8,10},{9,11},{10,... | collective-permute-start | bytes 1572872 | tf_op jit(solution)/shard_map/ppermute | solution.py:1063
  302.0 37.1 %collective-permute-start.22 = (bf16[256,1024]{1,0:T(8,128)(2,1)}, bf16[256,1024]{1,0:T(8,128)(2,1)}, u32[]{:S(2)}, u32[]{:S(2)}) collective-permute-start(bf16[256,1024]{1,0:T(8,128)(2,1)} %get-tuple-element.316.rest_0_), channel_id=1, source_target_pairs={{0,1},{1,0},{2,3},{3,2},{4,5},{5,4},{6,7},{7,6},{8,9},{9,8},{10,11... | collective-permute-start | bytes 1572872 | tf_op jit(solution)/shard_map/ppermute | solution.py:1063
  311.2 30.2 %collective-permute-start.27 = (bf16[256,1024]{1,0:T(8,128)(2,1)}, bf16[256,1024]{1,0:T(8,128)(2,1)}, u32[]{:S(2)}, u32[]{:S(2)}) collective-permute-start(bf16[256,1024]{1,0:T(8,128)(2,1)} %collective-permute-done.23.rest_3_), channel_id=1, source_target_pairs={{0,2},{1,3},{2,0},{3,1},{4,6},{5,7},{6,4},{7,5},{8,10},{9,11},{10,... | collective-permute-start | bytes 1572872 | tf_op jit(solution)/shard_map/ppermute | solution.py:1063
  467.2 36.9 %collective-permute-start.40 = (bf16[256,1152]{1,0:T(8,128)(2,1)}, bf16[256,1152]{1,0:T(8,128)(2,1)S(1)}, u32[]{:S(2)}, u32[]{:S(2)}) collective-permute-start(bf16[256,1152]{1,0:T(8,128)(2,1)} %copy-done.126), channel_id=1, source_target_pairs={{0,1},{1,0},{2,3},{3,2},{4,5},{5,4},{6,7},{7,6},{8,9},{9,8},{10,11... | collective-permute-start | bytes 1769480 | tf_op jit(solution)/shard_map/ppermute | solution.py:1063
  506.7 84.4 %all-to-all-start.2 = ((bf16[32,8,2816]{2,1,0:T(8,128)(2,1)}), bf16[32,8,2816]{2,1,0:T(8,128)(2,1)}, u32[]{:S(2)}, u32[]{:S(2)}) async-start(bf16[32,8,2816]{2,1,0:T(8,128)(2,1)} %bitcast.40), calls=%async_computation.2 | async-start | bytes 2883584 | tf_op jit(solution)/shard_map/all_to_all | solution.py:1203
  510.2 79.2 %reduce-scatter.5.cloned.1.call-start = ((), (), s32[]{:S(2)}) async-start(), calls=%async_computation.7 | async-start | bytes 774144 | tf_op jit(solution)/shard_map/reduce_scatter | solution.py:1430
  572.3 32.0 %collective-permute-start.48 = (bf16[256,1152]{1,0:T(8,128)(2,1)}, bf16[256,1152]{1,0:T(8,128)(2,1)}, u32[]{:S(2)}, u32[]{:S(2)}) collective-permute-start(bf16[256,1152]{1,0:T(8,128)(2,1)} %get-tuple-element.252), channel_id=1, source_target_pairs={{0,1},{1,0},{2,3},{3,2},{4,5},{5,4},{6,7},{7,6},{8,9},{9,8},{10,11... | collective-permute-start | bytes 1769480 | tf_op jit(solution)/shard_map/ppermute | solution.py:1063
  614.3 33.9 %all-to-all-start.3 = ((bf16[32,8,2304]{2,1,0:T(8,128)(2,1)}), bf16[32,8,2304]{2,1,0:T(8,128)(2,1)S(1)}, u32[]{:S(2)}, u32[]{:S(2)}) async-start(bf16[32,8,2304]{2,1,0:T(8,128)(2,1)} %bitcast.184), calls=%async_computation.5 | async-start | bytes 2359296 | tf_op jit(solution)/shard_map/all_to_all | solution.py:1203
  (209 other events, 2842.6 us)
Sparse Core Ops, SparseCore 0:
  13.5 25.3 all-gather.10
  40.6 103.9 all-gather.12
  146.7 60.6 all-gather.14
  209.0 91.2 all-gather.16
  301.7 52.5 all-gather.18
  467.3 29.1 reduce-scatter.2
  557.8 31.6 reduce-scatter.4

commit v13 on v10

--- a/solution.py
+++ b/solution.py
@@ -65,6 +65,7 @@
 
 ESTIMATE = 16
 SCAN_BYTES = 32 * 1024 * 1024
+ALONE_BYTES = 44 * 1024 * 1024
 DENSE_BYTES = 16 * 1024 * 1024
 FINISH_BYTES = 32 * 1024 * 1024
 LANES = 128
@@ -433,7 +434,7 @@
             *[jax.ShapeDtypeStruct(shape, FLOAT) for shape in running],
         ],
         input_output_aliases=aliases,
-        compiler_params=pltpu.CompilerParams(vmem_limit_bytes=SCAN_BYTES),
+        compiler_params=pltpu.CompilerParams(vmem_limit_bytes=ALONE_BYTES),
         cost_estimate=scan_cost(tokens, channels, 2),
         name="scan_backward",
     )(*operands)
@@ -565,7 +566,7 @@
             pltpu.VMEM((tokens, HEAD_SIZE), FLOAT),
             pltpu.VMEM((tokens, HEAD_SIZE), FLOAT),
         ],
-        compiler_params=pltpu.CompilerParams(vmem_limit_bytes=SCAN_BYTES),
+        compiler_params=pltpu.CompilerParams(vmem_limit_bytes=ALONE_BYTES),
         cost_estimate=attention_cost(tokens, width, 3),
         name="attention_backward",
     )(*attention_operands(projected, tables), mixed_grad)

time: 657 us -> 655 us (level)
    unnamed x358 -> x354, local copies, waits for them, and re-layouts: 106 us -> 102 us
where the time goes in v13:
time: 655 us; the launch traced here: 647 us
  waiting for transfers between devices  206 us (31%)
  Pallas kernels  178 us (27%)
  local copies, waits for them, and re-layouts  126 us (19%)
  starting transfers between devices  86.6 us (13%)
  other arithmetic  22.4 us (3%)
  between operations  17.1 us (3%)
  matrix products  10.5 us (2%)
    ppermute x55, waiting for transfers between devices, flip(): return lax.ppermute(values, 'col', [(i, i ^ mask) for i in range(4)])  135 us
    unnamed x354, local copies, waits for them, and re-layouts  102 us
    ppermute x55, starting transfers between devices, flip(): return lax.ppermute(values, 'col', [(i, i ^ mask) for i in range(4)])  66.9 us
    pallas_call x13, Pallas kernels, spread_blocks(): pl.pallas_call(functools.partial(spread_kernel, masks, len(gathered)), in...  63.9 us
    pallas_call x6, Pallas kernels, collect_blocks(): pl.pallas_call(functools.partial(collect_kernel, masks, len(gathered)), i...  38.9 us
    all_to_all x4, waiting for transfers between devices, local(): lax.all_to_all(values, ALL_AXES, split_axis=0, concat_axis=0, tiled=True)  38.1 us
    pallas_call x2, Pallas kernels, scan_backward(): pl.pallas_call(scan_backward_kernel, grid=(blocks // parts,), in_specs=in...  32.4 us
    all_to_all x4, starting transfers between devices, local(): lax.all_to_all(values, ALL_AXES, split_axis=0, concat_axis=0, tiled=True)  19.5 us
  transfers between devices with their start and end apart: 66, of which 29 were waited for; matrix products, arithmetic and copies ran while one was open for 9% of the time, Pallas kernels for 24%

profile of v13, /device:TPU:0, one launch (start us, length us, event | category | flops | bytes accessed | tf_op | source)
XLA Modules:
  0.0 646.7 jit_solution(2238930284050729343)
XLA Ops:
  23.1 7.3 %all-to-all-start = ((bf16[32,8,2176]{2,1,0:T(8,128)(2,1)}), bf16[32,8,2176]{2,1,0:T(8,128)(2,1)S(1)}, u32[]{:S(2)}, u32[]{:S(2)}) async-start(bf16[32,8,2176]{2,1,0:T(8,128)(2,1)} %bitcast.188), calls=%async_computation | async-start | bytes 2228224 | tf_op jit(solution)/shard_map/all_to_all | solution.py:1160
  30.5 12.0 %all-gather.11.cloned.1.call-done = bf16[2304,256]{1,0:T(8,128)(2,1)} async-done(((bf16[288,256]{1,0:T(8,128)(2,1)}), bf16[2304,256]{1,0:T(8,128)(2,1)}) %all-gather.11.cloned.1.call-update) | async-done | bytes 1179664 | tf_op jit(solution)/shard_map/all_gather | solution.py:1185
  48.0 21.9 %all-to-all-done = bf16[32,8,2176]{2,1,0:T(8,128)(2,1)S(1)} async-done(((bf16[32,8,2176]{2,1,0:T(8,128)(2,1)}), bf16[32,8,2176]{2,1,0:T(8,128)(2,1)S(1)}, u32[]{:S(2)}, u32[]{:S(2)}) %all-to-all-start) | async-done | bytes 1114144 | tf_op jit(solution)/shard_map/all_to_all | solution.py:1160
  95.6 12.6 %collective-permute-done.4.rest_1_ = bf16[256,1024]{1,0:T(8,128)(2,1)S(1)} collective-permute-done((bf16[256,1024]{1,0:T(8,128)(2,1)}, bf16[256,1024]{1,0:T(8,128)(2,1)S(1)}, u32[]{:S(2)}, u32[]{:S(2)}) %collective-permute-start.4) | collective-permute-done | bytes 524320 | tf_op jit(solution)/shard_map/ppermute | solution.py:1020
  109.1 12.3 %collective-permute-done.2.rest_0_ = bf16[256,1024]{1,0:T(8,128)(2,1)} collective-permute-done((bf16[256,1024]{1,0:T(8,128)(2,1)}, bf16[256,1024]{1,0:T(8,128)(2,1)}, u32[]{:S(2)}, u32[]{:S(2)}) %collective-permute-start.2) | collective-permute-done | bytes 524320 | tf_op jit(solution)/shard_map/ppermute | solution.py:1020
  139.8 7.5 %spread_blocks.13 = (bf16[1024,2688]{1,0:T(8,128)(2,1)S(1)}, bf16[1024,128]{1,0:T(8,128)(2,1)S(1)}) custom-call(f32[1024,128]{1,0:T(8,128)S(1)} %compare_convert_fusion.chosen_ref, bf16[256,1024]{1,0:T(8,128)(2,1)} %get-tuple-element.138.rest_0_.refs_4_, bf16[256,1024]{1,0:T(8,128)(2,1)} %get-tuple-element.139.rest_1_.refs_5_, ...), custom_call_target="tpu_custom_call" | custom-call | flops 184549376 | bytes 151552 | tf_op jit(solution)/shard_map/spread_blocks/pallas_call | solution.py:676
  147.3 7.1 %spread_blocks.14 = (bf16[1024,2688]{1,0:T(8,128)(2,1)S(1)}, bf16[1024,128]{1,0:T(8,128)(2,1)S(1)}) custom-call(f32[1024,128]{1,0:T(8,128)S(1)} %compare_convert_fusion.chosen_ref, bf16[256,1024]{1,0:T(8,128)(2,1)} %collective-permute-done.9.rest_0_, ...), custom_call_target="tpu_custom_call", output_to_operand_aliasing={{0}: (5, {}), {1}: (6, {})} | custom-call | flops 184549376 | bytes 151552 | tf_op jit(solution)/shard_map/spread_blocks/pallas_call | solution.py:676
  154.4 7.5 %spread_blocks.15 = (bf16[1024,2688]{1,0:T(8,128)(2,1)S(1)}, bf16[1024,128]{1,0:T(8,128)(2,1)S(1)}) custom-call(f32[1024,128]{1,0:T(8,128)S(1)} %compare_convert_fusion.chosen_ref, bf16[256,1024]{1,0:T(8,128)(2,1)} %collective-permute-done.2.rest_0_, ...), custom_call_target="tpu_custom_call", output_to_operand_aliasing={{0}: (5, {}), {1}: (6, {})} | custom-call | flops 184549376 | bytes 151552 | tf_op jit(solution)/shard_map/spread_blocks/pallas_call | solution.py:676
  162.0 7.3 %spread_blocks.16 = (bf16[1024,2688]{1,0:T(8,128)(2,1)S(1)}, bf16[1024,128]{1,0:T(8,128)(2,1)S(1)}) custom-call(f32[1024,128]{1,0:T(8,128)S(1)} %compare_convert_fusion.chosen_ref, bf16[256,1024]{1,0:T(8,128)(2,1)} %collective-permute-done.3.rest_0_, bf16[256,1024]{1,0:T(8,128)(2,1)} %collective-permute-done.5.rest_1_, ...), custom_call_target="tpu_custom_call", output_to_operand_aliasing={{0}: (5, {}), {1}: (6, {})} | custom-call | flops 184549376 | bytes 151552 | tf_op jit(solution)/shard_map/spread_blocks/pallas_call | solution.py:676
  189.9 12.9 %scan_forward.1 = (bf16[1024,1024]{1,0:T(8,128)(2,1)S(1)}, f32[1024,768]{1,0:T(8,128)S(1)}, bf16[4,256,768]{2,1,0:T(8,128)(2,1)S(1)}) custom-call(bf16[1024,2688]{1,0:T(8,128)(2,1)S(1)} %copy-done.3, bf16[1024,2688]{1,0:T(8,128)(2,1)S(1)} %copy-done.3, bf16[1024,2688]{1,0:T(8,128)(2,1)S(1)} %copy-done.3, ...), custom_call_target="tpu_custom_call", output_to_operand_aliasing={{0}: (12, {})} | custom-call | flops 83886080 | bytes 589824 | tf_op jit(solution)/shard_map/scan_forward/pallas_call | solution.py:384
  241.1 17.4 %collective-permute-done.14.second_near = bf16[256,1024]{1,0:T(8,128)(2,1)} collective-permute-done((bf16[256,1024]{1,0:T(8,128)(2,1)}, bf16[256,1024]{1,0:T(8,128)(2,1)}, u32[]{:S(2)}, u32[]{:S(2)}) %collective-permute-start.14) | collective-permute-done | bytes 524320 | tf_op jit(solution)/shard_map/ppermute | solution.py:1020
  281.6 7.6 %collective-permute-done.24.rest_4_ = bf16[256,1024]{1,0:T(8,128)(2,1)} collective-permute-done((bf16[256,1024]{1,0:T(8,128)(2,1)}, bf16[256,1024]{1,0:T(8,128)(2,1)}, u32[]{:S(2)}, u32[]{:S(2)}) %collective-permute-start.24) | collective-permute-done | bytes 524320 | tf_op jit(solution)/shard_map/ppermute | solution.py:1020
  331.4 12.9 %all-gather.19.cloned.1.call-done = bf16[2176,1152]{1,0:T(8,128)(2,1)} async-done(((bf16[272,1152]{1,0:T(8,128)(2,1)}), bf16[2176,1152]{1,0:T(8,128)(2,1)}) %all-gather.19.cloned.1.call-update) | async-done | bytes 5013520 | tf_op jit(solution)/shard_map/all_gather | solution.py:1170
  346.7 10.1 %spread_blocks.21 = (bf16[1024,1024]{1,0:T(8,128)(2,1)S(1)}, bf16[1024,128]{1,0:T(8,128)(2,1)S(1)}) custom-call(f32[1024,128]{1,0:T(8,128)S(1)} %compare_convert_fusion.chosen_ref, bf16[256,1024]{1,0:T(8,128)(2,1)} %get-tuple-element.326.rest_0_, bf16[256,1024]{1,0:T(8,128)(2,1)} %get-tuple-element.325.rest_1_, ...), custom_call_target="tpu_custom_call" | custom-call | flops 301989888 | bytes 393216 | tf_op jit(solution)/shard_map/spread_blocks/pallas_call | solution.py:676
  369.1 8.3 %collect_blocks.10 = (bf16[256,1152]{1,0:T(8,128)(2,1)}, f32[256,1024]{1,0:T(8,128)S(1)}, f32[256,1152]{1,0:T(8,128)S(1)}, bf16[256,1024]{1,0:T(8,128)(2,1)}, f3...) custom-call(bf16[1024,2048]{1,0:T(8,128)(2,1)S(1)} %pad_maximum_fusion.values_ref, bf16[8,272,2176]{2,1,0:T(8,128)(2,1)S(1)} %bitcast.163), custom_call_target="tpu_custom_call" | custom-call | flops 402653184 | bytes 589824 | tf_op jit(solution)/shard_map/collect_blocks/pallas_call | solution.py:745
  420.1 8.8 %collective-permute-done.34.rest_0_ = bf16[256,1024]{1,0:T(8,128)(2,1)S(1)} collective-permute-done((bf16[256,1024]{1,0:T(8,128)(2,1)S(1)}, bf16[256,1024]{1,0:T(8,128)(2,1)S(1)}, u32[]{:S(2)}, u32[]{:S(2)}) %collective-permute-start.34) | collective-permute-done | bytes 524320 | tf_op jit(solution)/shard_map/ppermute | solution.py:1020
  433.6 7.0 %collective-permute-done.39.rest_0_ = bf16[256,1024]{1,0:T(8,128)(2,1)S(1)} collective-permute-done((bf16[256,1024]{1,0:T(8,128)(2,1)S(1)}, bf16[256,1024]{1,0:T(8,128)(2,1)S(1)}, u32[]{:S(2)}, u32[]{:S(2)}) %collective-permute-start.39) | collective-permute-done | bytes 524320 | tf_op jit(solution)/shard_map/ppermute | solution.py:1020
  462.1 7.2 %attention_backward.1 = (bf16[1024,256]{1,0:T(8,128)(2,1)S(1)}, bf16[1024,256]{1,0:T(8,128)(2,1)S(1)}) custom-call(bf16[1024,2688]{1,0:T(8,128)(2,1)S(1)} %copy-done.4, bf16[1024,2688]{1,0:T(8,128)(2,1)S(1)} %copy-done.4, bf16[1024,2688]{1,0:T(8,128)(2,1)S(1)} %copy-done.4, f32[1024,128]{1,0:T(8,128)S(1)} %copy-done.48, f32[1024,128]{1,0:T(8,128)S(1)} %copy-done.46, ...), custom_call_target="tpu_custom_call" | custom-call | flops 100663296 | bytes 393216 | tf_op jit(solution)/shard_map/attention_backward/pallas_call | solution.py:557
  476.1 16.1 %scan_backward.2 = (bf16[1024,2688]{1,0:T(8,128)(2,1)}, f32[256,768]{1,0:T(8,128)S(1)}, f32[8,768]{1,0:T(8,128)S(1)}, f32[8,512]{1,0:T(8,128)S(1)}) custom-call(bf16[1024,2688]{1,0:T(8,128)(2,1)} %copy-done.2, bf16[1024,2688]{1,0:T(8,128)(2,1)} %copy-done.2, bf16[1024,2688]{1,0:T(8,128)(2,1)} %copy-done.2, bf16[1024,2688]{1,0:T(8,128)(2,1)} %copy-done.2, ...), custom_call_target="tpu_custom_call" | custom-call | flops 167772160 | bytes 1179648 | tf_op jit(solution)/shard_map/scan_backward/pallas_call | solution.py:427
  505.4 16.3 %scan_backward.3 = (bf16[1024,2688]{1,0:T(8,128)(2,1)}, f32[256,768]{1,0:T(8,128)}, f32[8,768]{1,0:T(8,128)}, f32[8,512]{1,0:T(8,128)}) custom-call(bf16[1024,2688]{1,0:T(8,128)(2,1)} %copy-done.2, bf16[1024,2688]{1,0:T(8,128)(2,1)} %copy-done.2, bf16[1024,2688]{1,0:T(8,128)(2,1)} %copy-done.2, ...), custom_call_target="tpu_custom_call", output_to_operand_aliasing={{0}: (17, {})} | custom-call | flops 167772160 | bytes 1179648 | tf_op jit(solution)/shard_map/scan_backward/pallas_call | solution.py:427
  526.2 15.0 %collect_blocks.11 = (bf16[256,1152]{1,0:T(8,128)(2,1)S(1)}, bf16[256,1024]{1,0:T(8,128)(2,1)S(1)}, bf16[256,1152]{1,0:T(8,128)(2,1)}, f32[256,1024]{1,0:T(8,128...) custom-call(bf16[1024,2688]{1,0:T(8,128)(2,1)S(1)} %copy-done.23, ...), custom_call_target="tpu_custom_call" | custom-call | flops 704643072 | bytes 868352 | tf_op jit(solution)/shard_map/collect_blocks/pallas_call | solution.py:745
  548.2 12.2 %collective-permute-done.47.second_part = bf16[256,1024]{1,0:T(8,128)(2,1)S(1)} collective-permute-done((bf16[256,1024]{1,0:T(8,128)(2,1)S(1)}, bf16[256,1024]{1,0:T(8,128)(2,1)S(1)}, u32[]{:S(2)}, u32[]{:S(2)}) %collective-permute-start.47) | collective-permute-done | bytes 524320 | tf_op jit(solution)/shard_map/ppermute | solution.py:1020
  580.0 13.0 %collective-permute-done.50.second_near = bf16[256,1024]{1,0:T(8,128)(2,1)} collective-permute-done((bf16[256,1024]{1,0:T(8,128)(2,1)}, bf16[256,1024]{1,0:T(8,128)(2,1)}, u32[]{:S(2)}, u32[]{:S(2)}) %collective-permute-start.50) | collective-permute-done | bytes 524320 | tf_op jit(solution)/shard_map/ppermute | solution.py:1020
  620.7 16.2 %all-to-all-done.3 = bf16[32,8,2304]{2,1,0:T(8,128)(2,1)S(1)} async-done(((bf16[32,8,2304]{2,1,0:T(8,128)(2,1)}), bf16[32,8,2304]{2,1,0:T(8,128)(2,1)S(1)}, u32[]{:S(2)}, u32[]{:S(2)}) %all-to-all-start.3) | async-done | bytes 1179680 | tf_op jit(solution)/shard_map/all_to_all | solution.py:1160
  (633 shorter events, 353.1 us)
Async XLA Ops:
  7.2 35.2 %all-gather.11.cloned.1.call-start = ((), (), s32[]{:S(2)}) async-start(), calls=%async_computation.8 | async-start | bytes 1327104 | tf_op jit(solution)/shard_map/all_gather | solution.py:1185
  12.7 121.6 %all-gather.13.cloned.1.call-start = ((), (), s32[]{:S(2)}) async-start(), calls=%async_computation.9 | async-start | bytes 10027008 | tf_op jit(solution)/shard_map/all_gather | solution.py:1170
  21.3 185.6 %all-gather.15.cloned.1.call-start = ((), (), s32[]{:S(2)}) async-start(), calls=%async_computation.10 | async-start | bytes 5640192 | tf_op jit(solution)/shard_map/all_gather | solution.py:1170
  23.1 46.8 %all-to-all-start = ((bf16[32,8,2176]{2,1,0:T(8,128)(2,1)}), bf16[32,8,2176]{2,1,0:T(8,128)(2,1)S(1)}, u32[]{:S(2)}, u32[]{:S(2)}) async-start(bf16[32,8,2176]{2,1,0:T(8,128)(2,1)} %bitcast.188), calls=%async_computation | async-start | bytes 2228224 | tf_op jit(solution)/shard_map/all_to_all | solution.py:1160
  30.4 274.4 %all-gather.17.cloned.1.call-start = ((), (), s32[]{:S(2)}) async-start(), calls=%async_computation.11 | async-start | bytes 10653696 | tf_op jit(solution)/shard_map/all_gather | solution.py:1170
  42.5 33.6 %collective-permute-start.1 = (bf16[8,288,256]{2,1,0:T(8,128)(2,1)}, bf16[8,288,256]{2,1,0:T(8,128)(2,1)}, u32[]{:S(2)}, u32[]{:S(2)}) collective-permute-start(bf16[8,288,256]{2,1,0:T(8,128)(2,1)} %bitcast.190), channel_id=1, source_target_pairs={{0,2},{1,3},{2,0},{3,1},{4,6},{5,7},{6,4},{7,5},{8,10},{9,11},{10,... | collective-permute-start | bytes 3538952 | tf_op jit(solution)/shard_map/ppermute | solution.py:1020
  42.9 33.5 %collective-permute-start = (bf16[8,288,256]{2,1,0:T(8,128)(2,1)}, bf16[8,288,256]{2,1,0:T(8,128)(2,1)}, u32[]{:S(2)}, u32[]{:S(2)}) collective-permute-start(bf16[8,288,256]{2,1,0:T(8,128)(2,1)} %bitcast.191), channel_id=1, source_target_pairs={{0,1},{1,0},{2,3},{3,2},{4,5},{5,4},{6,7},{7,6},{8,9},{9,8},{10,11... | collective-permute-start | bytes 3538952 | tf_op jit(solution)/shard_map/ppermute | solution.py:1020
  78.8 265.4 %all-gather.19.cloned.1.call-start = ((), (), s32[]{:S(2)}) async-start(), calls=%async_computation.12 | async-start | bytes 5640192 | tf_op jit(solution)/shard_map/all_gather | solution.py:1170
  81.7 40.7 %collective-permute-start.7 = (bf16[4,288,256]{2,1,0:T(8,128)(2,1)S(1)}, bf16[4,288,256]{2,1,0:T(8,128)(2,1)S(1)}, u32[]{:S(2)}, u32[]{:S(2)}) collective-permute-start(bf16[4,288,256]{2,1,0:T(8,128)(2,1)S(1)} %slice.489), channel_id=1, source_target_pairs={{0,1},{1,0},{2,3},{3,2},{4,5},{5,4},{6,7},{7,6},{8,9},{9,8},{10,11... | collective-permute-start | bytes 1769480 | tf_op jit(solution)/shard_map/ppermute | solution.py:1020
  83.7 40.1 %collective-permute-start.6 = (bf16[4,288,256]{2,1,0:T(8,128)(2,1)S(1)}, bf16[4,288,256]{2,1,0:T(8,128)(2,1)S(1)}, u32[]{:S(2)}, u32[]{:S(2)}) collective-permute-start(bf16[4,288,256]{2,1,0:T(8,128)(2,1)S(1)} %slice.488), channel_id=1, source_target_pairs={{0,2},{1,3},{2,0},{3,1},{4,6},{5,7},{6,4},{7,5},{8,10},{9,11},{10,... | collective-permute-start | bytes 1769480 | tf_op jit(solution)/shard_map/ppermute | solution.py:1020
  89.3 65.0 %collective-permute-start.8 = (bf16[256,1024]{1,0:T(8,128)(2,1)}, bf16[256,1024]{1,0:T(8,128)(2,1)S(1)}, u32[]{:S(2)}, u32[]{:S(2)}) collective-permute-start(bf16[256,1024]{1,0:T(8,128)(2,1)} %get-tuple-element.139.rest_1_.refs_5_), channel_id=1, source_target_pairs={{0,2},{1,3},{2,0},{3,1},{4,6},{5,7},{6,4},{7,5},{8,10},{9,11},{10,... | collective-permute-start | bytes 1572872 | tf_op jit(solution)/shard_map/ppermute | solution.py:1020
  108.3 39.0 %collective-permute-start.9 = (bf16[256,1024]{1,0:T(8,128)(2,1)}, bf16[256,1024]{1,0:T(8,128)(2,1)}, u32[]{:S(2)}, u32[]{:S(2)}) collective-permute-start(bf16[256,1024]{1,0:T(8,128)(2,1)} %get-tuple-element.138.rest_0_.refs_4_), channel_id=1, source_target_pairs={{0,1},{1,0},{2,3},{3,2},{4,5},{5,4},{6,7},{7,6},{8,9},{9,8},{10,11... | collective-permute-start | bytes 1572872 | tf_op jit(solution)/shard_map/ppermute | solution.py:1020
  121.4 40.5 %collective-permute-start.5 = (bf16[256,1024]{1,0:T(8,128)(2,1)S(1)}, bf16[256,1024]{1,0:T(8,128)(2,1)}, u32[]{:S(2)}, u32[]{:S(2)}) collective-permute-start(bf16[256,1024]{1,0:T(8,128)(2,1)S(1)} %collective-permute-done.4.rest_1_), channel_id=1, source_target_pairs={{0,2},{1,3},{2,0},{3,1},{4,6},{5,7},{6,4},{7,5},{8,10},{9,11},{10,... | collective-permute-start | bytes 1572872 | tf_op jit(solution)/shard_map/ppermute | solution.py:1020
  122.4 39.5 %collective-permute-start.3 = (bf16[256,1024]{1,0:T(8,128)(2,1)}, bf16[256,1024]{1,0:T(8,128)(2,1)}, u32[]{:S(2)}, u32[]{:S(2)}) collective-permute-start(bf16[256,1024]{1,0:T(8,128)(2,1)} %collective-permute-done.2.rest_0_), channel_id=1, source_target_pairs={{0,1},{1,0},{2,3},{3,2},{4,5},{5,4},{6,7},{7,6},{8,9},{9,8},{10,11... | collective-permute-start | bytes 1572872 | tf_op jit(solution)/shard_map/ppermute | solution.py:1020
  175.1 59.9 %all-to-all-start.1 = ((bf16[32,8,2048]{2,1,0:T(8,128)(2,1)}), bf16[32,8,2048]{2,1,0:T(8,128)(2,1)}, u32[]{:S(2)}, u32[]{:S(2)}) async-start(bf16[32,8,2048]{2,1,0:T(8,128)(2,1)} %fusion.9), calls=%async_computation.1 | async-start | bytes 2097152 | tf_op jit(solution)/shard_map/all_to_all | solution.py:1160
  179.0 395.9 %reduce-scatter.3.cloned.1.call-start = ((), (), s32[]{:S(2)}) async-start(), calls=%async_computation.6 | async-start | bytes 1179648 | tf_op jit(solution)/shard_map/reduce_scatter | solution.py:1384
  280.0 42.6 %collective-permute-start.19 = (bf16[256,1024]{1,0:T(8,128)(2,1)}, bf16[256,1024]{1,0:T(8,128)(2,1)}, u32[]{:S(2)}, u32[]{:S(2)}) collective-permute-start(bf16[256,1024]{1,0:T(8,128)(2,1)} %collective-permute-done.18.rest_1_), channel_id=1, source_target_pairs={{0,2},{1,3},{2,0},{3,1},{4,6},{5,7},{6,4},{7,5},{8,10},{9,11},{10,... | collective-permute-start | bytes 1572872 | tf_op jit(solution)/shard_map/ppermute | solution.py:1020
  289.2 39.8 %collective-permute-start.25 = (bf16[256,1024]{1,0:T(8,128)(2,1)}, bf16[256,1024]{1,0:T(8,128)(2,1)}, u32[]{:S(2)}, u32[]{:S(2)}) collective-permute-start(bf16[256,1024]{1,0:T(8,128)(2,1)} %get-tuple-element.325.rest_1_), channel_id=1, source_target_pairs={{0,2},{1,3},{2,0},{3,1},{4,6},{5,7},{6,4},{7,5},{8,10},{9,11},{10,... | collective-permute-start | bytes 1572872 | tf_op jit(solution)/shard_map/ppermute | solution.py:1020
  291.9 37.1 %collective-permute-start.22 = (bf16[256,1024]{1,0:T(8,128)(2,1)}, bf16[256,1024]{1,0:T(8,128)(2,1)}, u32[]{:S(2)}, u32[]{:S(2)}) collective-permute-start(bf16[256,1024]{1,0:T(8,128)(2,1)} %get-tuple-element.326.rest_0_), channel_id=1, source_target_pairs={{0,1},{1,0},{2,3},{3,2},{4,5},{5,4},{6,7},{7,6},{8,9},{9,8},{10,11... | collective-permute-start | bytes 1572872 | tf_op jit(solution)/shard_map/ppermute | solution.py:1020
  457.1 36.9 %collective-permute-start.40 = (bf16[256,1152]{1,0:T(8,128)(2,1)}, bf16[256,1152]{1,0:T(8,128)(2,1)S(1)}, u32[]{:S(2)}, u32[]{:S(2)}) collective-permute-start(bf16[256,1152]{1,0:T(8,128)(2,1)} %copy-done.123), channel_id=1, source_target_pairs={{0,1},{1,0},{2,3},{3,2},{4,5},{5,4},{6,7},{7,6},{8,9},{9,8},{10,11... | collective-permute-start | bytes 1769480 | tf_op jit(solution)/shard_map/ppermute | solution.py:1020
  496.6 83.4 %all-to-all-start.2 = ((bf16[32,8,2816]{2,1,0:T(8,128)(2,1)}), bf16[32,8,2816]{2,1,0:T(8,128)(2,1)}, u32[]{:S(2)}, u32[]{:S(2)}) async-start(bf16[32,8,2816]{2,1,0:T(8,128)(2,1)} %bitcast.184), calls=%async_computation.2 | async-start | bytes 2883584 | tf_op jit(solution)/shard_map/all_to_all | solution.py:1160
  500.1 78.3 %reduce-scatter.5.cloned.1.call-start = ((), (), s32[]{:S(2)}) async-start(), calls=%async_computation.7 | async-start | bytes 774144 | tf_op jit(solution)/shard_map/reduce_scatter | solution.py:1384
  561.3 31.7 %collective-permute-start.48 = (bf16[256,1152]{1,0:T(8,128)(2,1)}, bf16[256,1152]{1,0:T(8,128)(2,1)}, u32[]{:S(2)}, u32[]{:S(2)}) collective-permute-start(bf16[256,1152]{1,0:T(8,128)(2,1)} %get-tuple-element.246), channel_id=1, source_target_pairs={{0,1},{1,0},{2,3},{3,2},{4,5},{5,4},{6,7},{7,6},{8,9},{9,8},{10,11... | collective-permute-start | bytes 1769480 | tf_op jit(solution)/shard_map/ppermute | solution.py:1020
  603.0 33.9 %all-to-all-start.3 = ((bf16[32,8,2304]{2,1,0:T(8,128)(2,1)}), bf16[32,8,2304]{2,1,0:T(8,128)(2,1)S(1)}, u32[]{:S(2)}, u32[]{:S(2)}) async-start(bf16[32,8,2304]{2,1,0:T(8,128)(2,1)} %bitcast.185), calls=%async_computation.5 | async-start | bytes 2359296 | tf_op jit(solution)/shard_map/all_to_all | solution.py:1160
  (206 other events, 2757.0 us)
Sparse Core Ops, SparseCore 0:
  12.8 29.6 all-gather.10
  44.1 90.1 all-gather.12
  136.5 60.8 all-gather.14
  198.9 91.2 all-gather.16
  291.6 52.5 all-gather.18
  457.2 29.3 reduce-scatter.2
  546.8 31.5 reduce-scatter.4
